TPU v7x, 32 devices: a whole 2x2x4 slice. The times are simulated.
32 devices in a mesh: lon: 8 (over z, x), lat: 4 (over y, core).
Axes of the slice: x: 2, y: 2, z: 4, core: 2. Of those that a mesh axis runs over, the one named last changes fastest.
Arguments:
- first_block_input: bfloat16 [128, 256, 192], P('lat', 'lon'), may hold values from -6 to 6
- first_block_preactivation: bfloat16 [128, 256, 192], P('lat', 'lon'), may hold values from -8 to 8
- second_block_input: bfloat16 [128, 256, 192], P('lat', 'lon'), may hold values from -6 to 6
- second_block_preactivation: bfloat16 [128, 256, 192], P('lat', 'lon'), may hold values from -8 to 8
- output_gradient_final: bfloat16 [128, 256, 192], P('lat', 'lon'), may hold values from -6 to 6
- first_block_conv_one: bfloat16 [9, 192, 192], replicated, may hold values from -0.15625 to 0.15625
- first_block_conv_two: bfloat16 [9, 192, 192], replicated, may hold values from -0.15625 to 0.15625
- second_block_conv_one: bfloat16 [9, 192, 192], replicated, may hold values from -0.15625 to 0.15625
- second_block_conv_two: bfloat16 [9, 192, 192], replicated, may hold values from -0.15625 to 0.15625
Outputs:
- first_block_input_gradient: bfloat16 [128, 256, 192], P('lat', 'lon')
- first_block_conv_one_gradient: float32 [9, 192, 192], replicated
- first_block_conv_two_gradient: float32 [9, 192, 192], replicated
- second_block_conv_one_gradient: float32 [9, 192, 192], replicated
- second_block_conv_two_gradient: float32 [9, 192, 192], replicated
All inputs are finite; a program needn't handle non-finite values.
Results may differ from a plain program's by a relative error of at most 0.0061.
Values may be sent and summed in bfloat16 or wider, within the bound.
No kernel may reach another device: no remote copies, remote signals or barrier semaphores. Data moves between devices by JAX's collectives and lax.ppermute only.
A program may use at most 128 MiB of HBM per device.

v0:
```python
import jax
import jax.numpy as jnp
from jax import lax
from jax.sharding import PartitionSpec as P

DILATION_FIRST = 16
DILATION_SECOND = 32


tap_offsets = [(row_tap, col_tap) for row_tap in (-1, 0, 1) for col_tap in (-1, 0, 1)]


def with_halo(block, sides, width, periodic):
    for axis, dim in sides:
        count = lax.axis_size(axis)
        forward = [(i, i + 1) for i in range(count - 1)]
        if periodic:
            forward.append((count - 1, 0))
        backward = [(target, source) for source, target in forward]
        low = lax.ppermute(
            lax.slice_in_dim(block, block.shape[dim] - width, None, axis=dim), axis, forward
        )
        high = lax.ppermute(lax.slice_in_dim(block, 0, width, axis=dim), axis, backward)
        block = jnp.concatenate([low, block, high], axis=dim)
    return block


def widen_active(values, dilation):
    across = with_halo(values, (("lon", 1),), dilation, True)
    return with_halo(across, (("lat", 0),), dilation, False)


def widen_gradient(values, dilation):
    across = with_halo(values, (("lon", 1),), dilation, True)
    return with_halo(across, (("lat", 0),), dilation, False)


def window(widened, row_shift, col_shift, dilation, height, breadth):
    top = dilation + row_shift * dilation
    left = dilation + col_shift * dilation
    return widened[top : top + height, left : left + breadth]


def weight_grad(widened, gradient, dilation):
    height, breadth = (gradient.shape[0], gradient.shape[1])
    return jnp.stack(
        [
            lax.dot_general(
                window(widened, row_tap, col_tap, dilation, height, breadth),
                gradient,
                (((0, 1), (0, 1)), ((), ())),
                preferred_element_type=jnp.float32,
            )
            for row_tap, col_tap in tap_offsets
        ]
    )


def pulled(gradient, widened, weights, dilation):
    height, breadth = (gradient.shape[0], gradient.shape[1])
    widened = widen_gradient(gradient, dilation)
    total = jnp.zeros(gradient.shape, jnp.float32)
    for row_index, row_tap in enumerate((-1, 0, 1)):
        joined = jnp.concatenate(
            [
                window(widened, -row_tap, -col_tap, dilation, height, breadth)
                for col_tap in (-1, 0, 1)
            ],
            2,
        )
        stacked = jnp.concatenate([weights[3 * row_index + col_index] for col_index in range(3)], 1)
        total = total + lax.dot_general(
            joined, stacked, (((2,), (1,)), ((), ())), preferred_element_type=jnp.float32
        )
    return total


def transpose_conv(gradient, weights, dilation):
    return pulled(gradient, None, weights, dilation)


def residual_block_backward(entry, hidden_pre, gradient, first, second, dilation):
    pre = hidden_pre.astype(jnp.float32)
    sigma = jax.nn.sigmoid(pre)
    hidden = (pre * sigma).astype(jnp.bfloat16)
    grad_second = weight_grad(widen_active(hidden, dilation), gradient, dilation)
    grad_hidden = transpose_conv(gradient, second, dilation)
    grad_pre = (grad_hidden * sigma * (1.0 + pre * (1.0 - sigma))).astype(jnp.bfloat16)
    grad_first = weight_grad(widen_active(entry, dilation), grad_pre, dilation)
    first_block_input_gradient = (
        gradient.astype(jnp.float32) + transpose_conv(grad_pre, first, dilation)
    ).astype(jnp.bfloat16)
    return (first_block_input_gradient, grad_first, grad_second)


def settle(first_grad, second_grad):
    return lax.psum((first_grad, second_grad), ("lon", "lat"))


def local(
    first_block_input,
    first_block_preactivation,
    second_block_input,
    second_block_preactivation,
    output_gradient_final,
    first_block_conv_one,
    first_block_conv_two,
    second_block_conv_one,
    second_block_conv_two,
):
    between_blocks_gradient, second_block_conv_one_gradient, second_block_conv_two_gradient = (
        residual_block_backward(
            second_block_input,
            second_block_preactivation,
            output_gradient_final,
            second_block_conv_one,
            second_block_conv_two,
            DILATION_SECOND,
        )
    )
    second_block_conv_one_gradient, second_block_conv_two_gradient = settle(
        second_block_conv_one_gradient, second_block_conv_two_gradient
    )
    first_block_input_gradient, first_block_conv_one_gradient, first_block_conv_two_gradient = (
        residual_block_backward(
            first_block_input,
            first_block_preactivation,
            between_blocks_gradient,
            first_block_conv_one,
            first_block_conv_two,
            DILATION_FIRST,
        )
    )
    first_block_conv_one_gradient, first_block_conv_two_gradient = settle(
        first_block_conv_one_gradient, first_block_conv_two_gradient
    )
    return (
        first_block_input_gradient,
        first_block_conv_one_gradient,
        first_block_conv_two_gradient,
        second_block_conv_one_gradient,
        second_block_conv_two_gradient,
    )


def solution(mesh):
    in_specs = (
        P("lat", "lon", None),
        P("lat", "lon", None),
        P("lat", "lon", None),
        P("lat", "lon", None),
        P("lat", "lon", None),
        P(),
        P(),
        P(),
        P(),
    )
    out_specs = (P("lat", "lon", None), P(), P(), P(), P())
    return jax.shard_map(local, mesh=mesh, in_specs=in_specs, out_specs=out_specs, check_vma=False)
```

profile of v0, /device:TPU:0, one launch (start us, length us, event | category | flops | bytes accessed | tf_op | source)
XLA Modules:
  0.0 413.8 jit_solution(15439307799620587239)
XLA Ops:
  7.2 3.0 collective-permute-start
  10.2 3.1 collective-permute-start.1
  13.3 1.1 fusion.261
  14.5 4.7 %collective-permute-start.17 = (bf16[32,16,192]{2,1,0:T(8,128)(2,1)S(1)}, bf16[32,16,192]{2,1,0:T(8,128)(2,1)S(1)}, u32[]{:S(2)}, u32[]{:S(2)}) collective-permute-start(bf16[32,16,192]{2,1,0:T(8,128)(2,1)S(1)} %get-tuple-element.85), channel_id=1, source_target_pairs={{4,0},{8,4},{12,8},{16,12},{20,16},{24,20},{28,24},{0,28},{5,1},{9... | collective-permute-start | bytes 589832 | tf_op jit(solution)/shard_map/ppermute | solution.py:23
  19.2 1.4 fusion.143
  20.9 0.7 copy-done.13
  22.1 27.6 %collective-permute-done.16 = bf16[32,16,192]{2,1,0:T(8,128)(2,1)S(1)} collective-permute-done((bf16[32,16,192]{2,1,0:T(8,128)(2,1)S(1)}, bf16[32,16,192]{2,1,0:T(8,128)(2,1)S(1)}, u32[]{:S(2)}, u32[]{:S(2)}) %collective-permute-start.16) | collective-permute-done | bytes 196640 | tf_op jit(solution)/shard_map/ppermute | solution.py:20
  49.7 2.5 collective-permute-start.20
  53.1 4.2 %collective-permute-start.25 = (bf16[32,32,192]{2,1,0:T(8,128)(2,1)S(1)}, bf16[32,32,192]{2,1,0:T(8,128)(2,1)S(1)}, u32[]{:S(2)}, u32[]{:S(2)}) collective-permute-start(bf16[32,32,192]{2,1,0:T(8,128)(2,1)S(1)} %copy-done.1), channel_id=1, source_target_pairs={{4,0},{8,4},{12,8},{16,12},{20,16},{24,20},{28,24},{0,28},{5,1},{9... | collective-permute-start | bytes 1179656 | tf_op jit(solution)/shard_map/ppermute | solution.py:23
  57.3 18.5 %collective-permute-done.20 = bf16[32,16,192]{2,1,0:T(8,128)(2,1)S(1)} collective-permute-done((bf16[32,16,192]{2,1,0:T(8,128)(2,1)S(1)}, bf16[32,16,192]{2,1,0:T(8,128)(2,1)S(1)}, u32[]{:S(2)}, u32[]{:S(2)}) %collective-permute-start.20) | collective-permute-done | bytes 196640 | tf_op jit(solution)/shard_map/ppermute | solution.py:20
  75.8 5.5 %collective-permute-start.29 = (bf16[32,32,192]{2,1,0:T(8,128)(2,1)S(1)}, bf16[32,32,192]{2,1,0:T(8,128)(2,1)S(1)}, u32[]{:S(2)}, u32[]{:S(2)}) collective-permute-start(bf16[32,32,192]{2,1,0:T(8,128)(2,1)S(1)} %fusion.138), channel_id=1, source_target_pairs={{4,0},{8,4},{12,8},{16,12},{20,16},{24,20},{28,24},{0,28},{5,1},{9... | collective-permute-start | bytes 1179656 | tf_op jit(solution)/shard_map/ppermute | solution.py:23
  81.8 1.4 collective-permute-start.3
  83.2 9.4 %collective-permute-done.24 = bf16[32,32,192]{2,1,0:T(8,128)(2,1)S(1)} collective-permute-done((bf16[32,32,192]{2,1,0:T(8,128)(2,1)S(1)}, bf16[32,32,192]{2,1,0:T(8,128)(2,1)S(1)}, u32[]{:S(2)}, u32[]{:S(2)}) %collective-permute-start.24) | collective-permute-done | bytes 393248 | tf_op jit(solution)/shard_map/ppermute | solution.py:20
  92.6 1.3 collective-permute-start.2
  94.4 1.3 collective-permute-start.23
  95.7 9.7 %collective-permute-done.29 = bf16[32,32,192]{2,1,0:T(8,128)(2,1)S(1)} collective-permute-done((bf16[32,32,192]{2,1,0:T(8,128)(2,1)S(1)}, bf16[32,32,192]{2,1,0:T(8,128)(2,1)S(1)}, u32[]{:S(2)}, u32[]{:S(2)}) %collective-permute-start.29) | collective-permute-done | bytes 393248 | tf_op jit(solution)/shard_map/ppermute | solution.py:23
  105.4 1.8 collective-permute-start.22
  107.2 0.7 fusion.27
  107.9 3.7 collective-permute-start.18
  112.0 1.3 collective-permute-start.19
  113.3 10.5 %collective-permute-start.26 = (bf16[32,96,192]{2,1,0:T(8,128)(2,1)S(1)}, bf16[32,96,192]{2,1,0:T(8,128)(2,1)S(1)}, u32[]{:S(2)}, u32[]{:S(2)}) collective-permute-start(bf16[32,96,192]{2,1,0:T(8,128)(2,1)S(1)} %constant_dynamic-update-slice_fusion.6), channel_id=1, source_target_pairs={{0,1},{1,2},{2,3},{4,5},{5,6},{6,7},{8,9},{9,10},{10,11},{12,13},{... | collective-permute-start | bytes 3538952 | tf_op jit(solution)/shard_map/ppermute | solution.py:20
  123.8 1.1 pad_maximum_fusion.3
  124.9 1.3 collective-permute-start.27
  126.4 0.7 fusion.33
  127.1 4.3 %collective-permute-start.30 = (bf16[32,96,192]{2,1,0:T(8,128)(2,1)S(1)}, bf16[32,96,192]{2,1,0:T(8,128)(2,1)S(1)}, u32[]{:S(2)}, u32[]{:S(2)}) collective-permute-start(bf16[32,96,192]{2,1,0:T(8,128)(2,1)S(1)} %pad_maximum_fusion.4), channel_id=1, source_target_pairs={{0,1},{1,2},{2,3},{4,5},{5,6},{6,7},{8,9},{9,10},{10,11},{12,13},{... | collective-permute-start | bytes 3538952 | tf_op jit(solution)/shard_map/ppermute | solution.py:20
  131.5 1.0 fusion.95
  132.5 1.3 collective-permute-start.31
  135.8 5.6 %collective-permute-start.5 = (bf16[32,32,192]{2,1,0:T(8,128)(2,1)S(1)}, bf16[32,32,192]{2,1,0:T(8,128)(2,1)S(1)}, u32[]{:S(2)}, u32[]{:S(2)}) collective-permute-start(bf16[32,32,192]{2,1,0:T(8,128)(2,1)S(1)} %fusion.95), channel_id=1, source_target_pairs={{4,0},{8,4},{12,8},{16,12},{20,16},{24,20},{28,24},{0,28},{5,1},{9... | collective-permute-start | bytes 1179656 | tf_op jit(solution)/shard_map/ppermute | solution.py:23
  144.2 3.9 collective-permute-done.5
  148.1 6.2 %collective-permute-done.4 = bf16[32,32,192]{2,1,0:T(8,128)(2,1)S(1)} collective-permute-done((bf16[32,32,192]{2,1,0:T(8,128)(2,1)S(1)}, bf16[32,32,192]{2,1,0:T(8,128)(2,1)S(1)}, u32[]{:S(2)}, u32[]{:S(2)}) %collective-permute-start.4) | collective-permute-done | bytes 393248 | tf_op jit(solution)/shard_map/ppermute | solution.py:20
  154.7 19.1 %collective-permute-start.7 = (bf16[32,96,192]{2,1,0:T(8,128)(2,1)S(1)}, bf16[32,96,192]{2,1,0:T(8,128)(2,1)S(1)}, u32[]{:S(2)}, u32[]{:S(2)}) collective-permute-start(bf16[32,96,192]{2,1,0:T(8,128)(2,1)S(1)} %pad_maximum_fusion), channel_id=1, source_target_pairs={{0,1},{1,2},{2,3},{4,5},{5,6},{6,7},{8,9},{9,10},{10,11},{12,13},{... | collective-permute-start | bytes 3538952 | tf_op jit(solution)/shard_map/ppermute | solution.py:20
  174.5 1.3 collective-permute-start.6
  176.9 0.7 fusion.44
  178.2 0.7 fusion.50
  178.9 4.7 %collective-permute-done.6 = bf16[32,96,192]{2,1,0:T(8,128)(2,1)S(1)} collective-permute-done((bf16[32,96,192]{2,1,0:T(8,128)(2,1)S(1)}, bf16[32,96,192]{2,1,0:T(8,128)(2,1)S(1)}, u32[]{:S(2)}, u32[]{:S(2)}) %collective-permute-start.6) | collective-permute-done | bytes 1179680 | tf_op jit(solution)/shard_map/ppermute | solution.py:23
  183.8 0.7 fusion.92
  184.5 2.5 collective-permute-start.8
  187.1 3.2 collective-permute-start.9
  193.9 0.7 collective-permute-done.8
  194.7 1.6 collective-permute-done.9
  196.6 17.4 %collective-permute-start.11 = (bf16[16,64,192]{2,1,0:T(8,128)(2,1)S(1)}, bf16[16,64,192]{2,1,0:T(8,128)(2,1)S(1)}, u32[]{:S(2)}, u32[]{:S(2)}) collective-permute-start(bf16[16,64,192]{2,1,0:T(8,128)(2,1)S(1)} %get-tuple-element.45), channel_id=1, source_target_pairs={{0,1},{1,2},{2,3},{4,5},{5,6},{6,7},{8,9},{9,10},{10,11},{12,13},{... | collective-permute-start | bytes 1179656 | tf_op jit(solution)/shard_map/ppermute | solution.py:20
  214.0 1.5 collective-permute-start.10
  215.9 0.7 fusion.16
  217.1 1.5 collective-permute-done.10
  218.6 0.9 maximum_maximum_fusion
  220.0 0.7 fusion.58
  220.7 0.9 fusion.89
  225.0 1.2 copy-done.5
  226.3 4.7 %collective-permute-start.13 = (bf16[32,16,192]{2,1,0:T(8,128)(2,1)S(1)}, bf16[32,16,192]{2,1,0:T(8,128)(2,1)S(1)}, u32[]{:S(2)}, u32[]{:S(2)}) collective-permute-start(bf16[32,16,192]{2,1,0:T(8,128)(2,1)S(1)} %get-tuple-element.87), channel_id=1, source_target_pairs={{4,0},{8,4},{12,8},{16,12},{20,16},{24,20},{28,24},{0,28},{5,1},{9... | collective-permute-start | bytes 589832 | tf_op jit(solution)/shard_map/ppermute | solution.py:23
  231.0 4.5 %collective-permute-done.12 = bf16[32,16,192]{2,1,0:T(8,128)(2,1)S(1)} collective-permute-done((bf16[32,16,192]{2,1,0:T(8,128)(2,1)S(1)}, bf16[32,16,192]{2,1,0:T(8,128)(2,1)S(1)}, u32[]{:S(2)}, u32[]{:S(2)}) %collective-permute-start.12) | collective-permute-done | bytes 196640 | tf_op jit(solution)/shard_map/ppermute | solution.py:20
  235.9 12.5 %collective-permute-start.15 = (bf16[16,64,192]{2,1,0:T(8,128)(2,1)S(1)}, bf16[16,64,192]{2,1,0:T(8,128)(2,1)S(1)}, u32[]{:S(2)}, u32[]{:S(2)}) collective-permute-start(bf16[16,64,192]{2,1,0:T(8,128)(2,1)S(1)} %get-tuple-element.41), channel_id=1, source_target_pairs={{0,1},{1,2},{2,3},{4,5},{5,6},{6,7},{8,9},{9,10},{10,11},{12,13},{... | collective-permute-start | bytes 1179656 | tf_op jit(solution)/shard_map/ppermute | solution.py:20
  248.3 1.3 collective-permute-start.14
  249.7 0.7 fusion.9
  250.4 2.4 collective-permute-done.14
  252.9 1.2 maximum_maximum_fusion.1
  254.5 0.7 fusion.73
  255.2 1.5 fusion.86
  256.7 141.9 %all-reduce.3.cloned.1.call-done = (f32[9,192,192]{2,1,0:T(8,128)}, f32[9,192,192]{2,1,0:T(8,128)}, f32[9,192,192]{2,1,0:T(8,128)}, f32[9,192,192]{2,1,0:T(8,128)}) async-done(((f32[9,192,192]{2,1,0:T(8,128)}, f32[9,192,192]{2,1,0:T(8,128)}, f32[9,192,192]{2,1,0:T(8,128)}, f32[9,192,192]{2,1,0:T(8,128)}), (f32[9,192,192]{2,1,0:T(8,128)}, f32[9,192,192]{2,1,0:T(8,128)}, f32[9,192,192]{2,1,0:T(8,128)}, ...) | async-done | bytes 5308432 | tf_op jit(solution)/shard_map/psum | solution.py:97
  398.6 2.9 copy.68
  401.5 1.2 copy.69
  402.7 0.9 copy-done.7
  403.6 1.2 copy.70
  404.9 0.9 copy-done.6
  405.8 1.2 copy.71
  (125 shorter events, 20.4 us)
Async XLA Ops:
  7.2 13.6 %copy-start.9 = (bf16[9,192,192]{2,1,0:T(8,128)(2,1)S(1)}, bf16[9,192,192]{2,1,0:T(8,128)(2,1)}, u32[]{:S(2)}) copy-start(bf16[9,192,192]{2,1,0:T(8,128)(2,1)} %param.17) | copy-start | bytes 1990660
  7.2 391.4 %all-reduce.3.cloned.1.call-start = ((), (), s32[]{:S(2)}) async-start(), calls=%async_computation | async-start | bytes 14155776 | tf_op jit(solution)/shard_map/psum | solution.py:97
  7.2 74.3 %collective-permute-start = (bf16[32,32,192]{2,1,0:T(8,128)(2,1)}, bf16[32,32,192]{2,1,0:T(8,128)(2,1)S(1)}, u32[]{:S(2)}, u32[]{:S(2)}) collective-permute-start(bf16[32,32,192]{2,1,0:T(8,128)(2,1)} %param.13), channel_id=1, source_target_pairs={{0,4},{4,8},{8,12},{12,16},{16,20},{20,24},{24,28},{28,0},{1,5},{5... | collective-permute-start | bytes 1179656 | tf_op jit(solution)/shard_map/ppermute | solution.py:20
  10.2 71.5 %collective-permute-start.1 = (bf16[32,32,192]{2,1,0:T(8,128)(2,1)}, bf16[32,32,192]{2,1,0:T(8,128)(2,1)S(1)}, u32[]{:S(2)}, u32[]{:S(2)}) collective-permute-start(bf16[32,32,192]{2,1,0:T(8,128)(2,1)} %param.13), channel_id=1, source_target_pairs={{4,0},{8,4},{12,8},{16,12},{20,16},{24,20},{28,24},{0,28},{5,1},{9... | collective-permute-start | bytes 1179656 | tf_op jit(solution)/shard_map/ppermute | solution.py:23
  14.4 35.3 %collective-permute-start.16 = (bf16[32,16,192]{2,1,0:T(8,128)(2,1)S(1)}, bf16[32,16,192]{2,1,0:T(8,128)(2,1)S(1)}, u32[]{:S(2)}, u32[]{:S(2)}) collective-permute-start(bf16[32,16,192]{2,1,0:T(8,128)(2,1)S(1)} %get-tuple-element.86), channel_id=1, source_target_pairs={{0,4},{4,8},{8,12},{12,16},{16,20},{20,24},{24,28},{28,0},{1,5},{5... | collective-permute-start | bytes 589832 | tf_op jit(solution)/shard_map/ppermute | solution.py:20
  14.5 6.3 %copy-start.10 = (bf16[9,192,192]{2,1,0:T(8,128)(2,1)S(1)}, bf16[9,192,192]{2,1,0:T(8,128)(2,1)}, u32[]{:S(2)}) copy-start(bf16[9,192,192]{2,1,0:T(8,128)(2,1)} %param.16) | copy-start | bytes 1990660
  14.5 37.8 %collective-permute-start.17 = (bf16[32,16,192]{2,1,0:T(8,128)(2,1)S(1)}, bf16[32,16,192]{2,1,0:T(8,128)(2,1)S(1)}, u32[]{:S(2)}, u32[]{:S(2)}) collective-permute-start(bf16[32,16,192]{2,1,0:T(8,128)(2,1)S(1)} %get-tuple-element.85), channel_id=1, source_target_pairs={{4,0},{8,4},{12,8},{16,12},{20,16},{24,20},{28,24},{0,28},{5,1},{9... | collective-permute-start | bytes 589832 | tf_op jit(solution)/shard_map/ppermute | solution.py:23
  20.6 1.0 copy-start.13
  20.6 32.5 %collective-permute-start.21 = (bf16[32,16,192]{2,1,0:T(8,128)(2,1)S(1)}, bf16[32,16,192]{2,1,0:T(8,128)(2,1)S(1)}, u32[]{:S(2)}, u32[]{:S(2)}) collective-permute-start(bf16[32,16,192]{2,1,0:T(8,128)(2,1)S(1)} %get-tuple-element.84), channel_id=1, source_target_pairs={{4,0},{8,4},{12,8},{16,12},{20,16},{24,20},{28,24},{0,28},{5,1},{9... | collective-permute-start | bytes 589832 | tf_op jit(solution)/shard_map/ppermute | solution.py:23
  20.8 1.2 copy-start.11
  21.6 30.6 %copy-start = (bf16[32,32,192]{2,1,0:T(8,128)(2,1)S(1)}, bf16[32,32,192]{2,1,0:T(8,128)(2,1)}, u32[]{:S(2)}) copy-start(bf16[32,32,192]{2,1,0:T(8,128)(2,1)} %param.9) | copy-start | bytes 1179652
  22.0 30.3 %copy-start.1 = (bf16[32,32,192]{2,1,0:T(8,128)(2,1)S(1)}, bf16[32,32,192]{2,1,0:T(8,128)(2,1)}, u32[]{:S(2)}) copy-start(bf16[32,32,192]{2,1,0:T(8,128)(2,1)} %param.11) | copy-start | bytes 1179652
  49.7 26.1 %collective-permute-start.20 = (bf16[32,16,192]{2,1,0:T(8,128)(2,1)S(1)}, bf16[32,16,192]{2,1,0:T(8,128)(2,1)S(1)}, u32[]{:S(2)}, u32[]{:S(2)}) collective-permute-start(bf16[32,16,192]{2,1,0:T(8,128)(2,1)S(1)} %get-tuple-element.83), channel_id=1, source_target_pairs={{0,4},{4,8},{8,12},{12,16},{16,20},{20,24},{24,28},{28,0},{1,5},{5... | collective-permute-start | bytes 589832 | tf_op jit(solution)/shard_map/ppermute | solution.py:20
  52.3 40.4 %collective-permute-start.24 = (bf16[32,32,192]{2,1,0:T(8,128)(2,1)S(1)}, bf16[32,32,192]{2,1,0:T(8,128)(2,1)S(1)}, u32[]{:S(2)}, u32[]{:S(2)}) collective-permute-start(bf16[32,32,192]{2,1,0:T(8,128)(2,1)S(1)} %copy-done.1), channel_id=1, source_target_pairs={{0,4},{4,8},{8,12},{12,16},{16,20},{20,24},{24,28},{28,0},{1,5},{5... | collective-permute-start | bytes 1179656 | tf_op jit(solution)/shard_map/ppermute | solution.py:20
  53.0 28.6 %copy-start.14 = (bf16[32,32,192]{2,1,0:T(8,128)(2,1)S(1)}, bf16[32,32,192]{2,1,0:T(8,128)(2,1)}, u32[]{:S(2)}) copy-start(bf16[32,32,192]{2,1,0:T(8,128)(2,1)} %param.13) | copy-start | bytes 1179652
  53.1 41.4 %collective-permute-start.25 = (bf16[32,32,192]{2,1,0:T(8,128)(2,1)S(1)}, bf16[32,32,192]{2,1,0:T(8,128)(2,1)S(1)}, u32[]{:S(2)}, u32[]{:S(2)}) collective-permute-start(bf16[32,32,192]{2,1,0:T(8,128)(2,1)S(1)} %copy-done.1), channel_id=1, source_target_pairs={{4,0},{8,4},{12,8},{16,12},{20,16},{24,20},{28,24},{0,28},{5,1},{9... | collective-permute-start | bytes 1179656 | tf_op jit(solution)/shard_map/ppermute | solution.py:23
  75.8 29.6 %collective-permute-start.29 = (bf16[32,32,192]{2,1,0:T(8,128)(2,1)S(1)}, bf16[32,32,192]{2,1,0:T(8,128)(2,1)S(1)}, u32[]{:S(2)}, u32[]{:S(2)}) collective-permute-start(bf16[32,32,192]{2,1,0:T(8,128)(2,1)S(1)} %fusion.138), channel_id=1, source_target_pairs={{4,0},{8,4},{12,8},{16,12},{20,16},{24,20},{28,24},{0,28},{5,1},{9... | collective-permute-start | bytes 1179656 | tf_op jit(solution)/shard_map/ppermute | solution.py:23
  81.5 26.4 %collective-permute-start.28 = (bf16[32,32,192]{2,1,0:T(8,128)(2,1)S(1)}, bf16[32,32,192]{2,1,0:T(8,128)(2,1)S(1)}, u32[]{:S(2)}, u32[]{:S(2)}) collective-permute-start(bf16[32,32,192]{2,1,0:T(8,128)(2,1)S(1)} %fusion.138), channel_id=1, source_target_pairs={{0,4},{4,8},{8,12},{12,16},{16,20},{20,24},{24,28},{28,0},{1,5},{5... | collective-permute-start | bytes 1179656 | tf_op jit(solution)/shard_map/ppermute | solution.py:20
  81.8 43.2 %collective-permute-start.3 = (bf16[32,96,192]{2,1,0:T(8,128)(2,1)S(1)}, bf16[32,96,192]{2,1,0:T(8,128)(2,1)S(1)}, u32[]{:S(2)}, u32[]{:S(2)}) collective-permute-start(bf16[32,96,192]{2,1,0:T(8,128)(2,1)S(1)} %constant_dynamic-update-slice_fusion), channel_id=1, source_target_pairs={{0,1},{1,2},{2,3},{4,5},{5,6},{6,7},{8,9},{9,10},{10,11},{12,13},{... | collective-permute-start | bytes 3538952 | tf_op jit(solution)/shard_map/ppermute | solution.py:20
  92.6 34.4 %collective-permute-start.2 = (bf16[32,96,192]{2,1,0:T(8,128)(2,1)S(1)}, bf16[32,96,192]{2,1,0:T(8,128)(2,1)S(1)}, u32[]{:S(2)}, u32[]{:S(2)}) collective-permute-start(bf16[32,96,192]{2,1,0:T(8,128)(2,1)S(1)} %constant_dynamic-update-slice_fusion), channel_id=1, source_target_pairs={{1,0},{2,1},{3,2},{5,4},{6,5},{7,6},{9,8},{10,9},{11,10},{13,12},{... | collective-permute-start | bytes 3538952 | tf_op jit(solution)/shard_map/ppermute | solution.py:23
  94.4 17.5 %collective-permute-start.23 = (bf16[16,64,192]{2,1,0:T(8,128)(2,1)S(1)}, bf16[16,64,192]{2,1,0:T(8,128)(2,1)S(1)}, u32[]{:S(2)}, u32[]{:S(2)}) collective-permute-start(bf16[16,64,192]{2,1,0:T(8,128)(2,1)S(1)} %get-tuple-element.35), channel_id=1, source_target_pairs={{1,0},{2,1},{3,2},{5,4},{6,5},{7,6},{9,8},{10,9},{11,10},{13,12},{... | collective-permute-start | bytes 1179656 | tf_op jit(solution)/shard_map/ppermute | solution.py:23
  105.4 7.9 %collective-permute-start.22 = (bf16[16,64,192]{2,1,0:T(8,128)(2,1)S(1)}, bf16[16,64,192]{2,1,0:T(8,128)(2,1)S(1)}, u32[]{:S(2)}, u32[]{:S(2)}) collective-permute-start(bf16[16,64,192]{2,1,0:T(8,128)(2,1)S(1)} %get-tuple-element.36), channel_id=1, source_target_pairs={{0,1},{1,2},{2,3},{4,5},{5,6},{6,7},{8,9},{9,10},{10,11},{12,13},{... | collective-permute-start | bytes 1179656 | tf_op jit(solution)/shard_map/ppermute | solution.py:20
  107.9 113.7 %collective-permute-start.18 = (bf16[16,64,192]{2,1,0:T(8,128)(2,1)S(1)}, bf16[16,64,192]{2,1,0:T(8,128)(2,1)S(1)}, u32[]{:S(2)}, u32[]{:S(2)}) collective-permute-start(bf16[16,64,192]{2,1,0:T(8,128)(2,1)S(1)} %get-tuple-element.38), channel_id=1, source_target_pairs={{0,1},{1,2},{2,3},{4,5},{5,6},{6,7},{8,9},{9,10},{10,11},{12,13},{... | collective-permute-start | bytes 1179656 | tf_op jit(solution)/shard_map/ppermute | solution.py:20
  112.0 111.9 %collective-permute-start.19 = (bf16[16,64,192]{2,1,0:T(8,128)(2,1)S(1)}, bf16[16,64,192]{2,1,0:T(8,128)(2,1)S(1)}, u32[]{:S(2)}, u32[]{:S(2)}) collective-permute-start(bf16[16,64,192]{2,1,0:T(8,128)(2,1)S(1)} %get-tuple-element.37), channel_id=1, source_target_pairs={{1,0},{2,1},{3,2},{5,4},{6,5},{7,6},{9,8},{10,9},{11,10},{13,12},{... | collective-permute-start | bytes 1179656 | tf_op jit(solution)/shard_map/ppermute | solution.py:23
  113.3 19.2 %collective-permute-start.26 = (bf16[32,96,192]{2,1,0:T(8,128)(2,1)S(1)}, bf16[32,96,192]{2,1,0:T(8,128)(2,1)S(1)}, u32[]{:S(2)}, u32[]{:S(2)}) collective-permute-start(bf16[32,96,192]{2,1,0:T(8,128)(2,1)S(1)} %constant_dynamic-update-slice_fusion.6), channel_id=1, source_target_pairs={{0,1},{1,2},{2,3},{4,5},{5,6},{6,7},{8,9},{9,10},{10,11},{12,13},{... | collective-permute-start | bytes 3538952 | tf_op jit(solution)/shard_map/ppermute | solution.py:20
  124.9 10.9 %collective-permute-start.27 = (bf16[32,96,192]{2,1,0:T(8,128)(2,1)S(1)}, bf16[32,96,192]{2,1,0:T(8,128)(2,1)S(1)}, u32[]{:S(2)}, u32[]{:S(2)}) collective-permute-start(bf16[32,96,192]{2,1,0:T(8,128)(2,1)S(1)} %constant_dynamic-update-slice_fusion.6), channel_id=1, source_target_pairs={{1,0},{2,1},{3,2},{5,4},{6,5},{7,6},{9,8},{10,9},{11,10},{13,12},{... | collective-permute-start | bytes 3538952 | tf_op jit(solution)/shard_map/ppermute | solution.py:23
  127.1 15.0 %collective-permute-start.30 = (bf16[32,96,192]{2,1,0:T(8,128)(2,1)S(1)}, bf16[32,96,192]{2,1,0:T(8,128)(2,1)S(1)}, u32[]{:S(2)}, u32[]{:S(2)}) collective-permute-start(bf16[32,96,192]{2,1,0:T(8,128)(2,1)S(1)} %pad_maximum_fusion.4), channel_id=1, source_target_pairs={{0,1},{1,2},{2,3},{4,5},{5,6},{6,7},{8,9},{9,10},{10,11},{12,13},{... | collective-permute-start | bytes 3538952 | tf_op jit(solution)/shard_map/ppermute | solution.py:20
  132.5 43.4 %collective-permute-start.31 = (bf16[32,96,192]{2,1,0:T(8,128)(2,1)S(1)}, bf16[32,96,192]{2,1,0:T(8,128)(2,1)S(1)}, u32[]{:S(2)}, u32[]{:S(2)}) collective-permute-start(bf16[32,96,192]{2,1,0:T(8,128)(2,1)S(1)} %pad_maximum_fusion.4), channel_id=1, source_target_pairs={{1,0},{2,1},{3,2},{5,4},{6,5},{7,6},{9,8},{10,9},{11,10},{13,12},{... | collective-permute-start | bytes 3538952 | tf_op jit(solution)/shard_map/ppermute | solution.py:23
  135.8 12.3 %collective-permute-start.5 = (bf16[32,32,192]{2,1,0:T(8,128)(2,1)S(1)}, bf16[32,32,192]{2,1,0:T(8,128)(2,1)S(1)}, u32[]{:S(2)}, u32[]{:S(2)}) collective-permute-start(bf16[32,32,192]{2,1,0:T(8,128)(2,1)S(1)} %fusion.95), channel_id=1, source_target_pairs={{4,0},{8,4},{12,8},{16,12},{20,16},{24,20},{28,24},{0,28},{5,1},{9... | collective-permute-start | bytes 1179656 | tf_op jit(solution)/shard_map/ppermute | solution.py:23
  142.1 12.2 %collective-permute-start.4 = (bf16[32,32,192]{2,1,0:T(8,128)(2,1)S(1)}, bf16[32,32,192]{2,1,0:T(8,128)(2,1)S(1)}, u32[]{:S(2)}, u32[]{:S(2)}) collective-permute-start(bf16[32,32,192]{2,1,0:T(8,128)(2,1)S(1)} %fusion.95), channel_id=1, source_target_pairs={{0,4},{4,8},{8,12},{12,16},{16,20},{20,24},{24,28},{28,0},{1,5},{5... | collective-permute-start | bytes 1179656 | tf_op jit(solution)/shard_map/ppermute | solution.py:20
  154.7 23.4 %collective-permute-start.7 = (bf16[32,96,192]{2,1,0:T(8,128)(2,1)S(1)}, bf16[32,96,192]{2,1,0:T(8,128)(2,1)S(1)}, u32[]{:S(2)}, u32[]{:S(2)}) collective-permute-start(bf16[32,96,192]{2,1,0:T(8,128)(2,1)S(1)} %pad_maximum_fusion), channel_id=1, source_target_pairs={{0,1},{1,2},{2,3},{4,5},{5,6},{6,7},{8,9},{9,10},{10,11},{12,13},{... | collective-permute-start | bytes 3538952 | tf_op jit(solution)/shard_map/ppermute | solution.py:20
  174.1 2.0 copy-start.2
  174.5 9.1 %collective-permute-start.6 = (bf16[32,96,192]{2,1,0:T(8,128)(2,1)S(1)}, bf16[32,96,192]{2,1,0:T(8,128)(2,1)S(1)}, u32[]{:S(2)}, u32[]{:S(2)}) collective-permute-start(bf16[32,96,192]{2,1,0:T(8,128)(2,1)S(1)} %pad_maximum_fusion), channel_id=1, source_target_pairs={{1,0},{2,1},{3,2},{5,4},{6,5},{7,6},{9,8},{10,9},{11,10},{13,12},{... | collective-permute-start | bytes 3538952 | tf_op jit(solution)/shard_map/ppermute | solution.py:23
  176.9 1.2 copy-start.3
  184.5 10.1 %collective-permute-start.8 = (bf16[32,16,192]{2,1,0:T(8,128)(2,1)S(1)}, bf16[32,16,192]{2,1,0:T(8,128)(2,1)S(1)}, u32[]{:S(2)}, u32[]{:S(2)}) collective-permute-start(bf16[32,16,192]{2,1,0:T(8,128)(2,1)S(1)} %get-tuple-element.90), channel_id=1, source_target_pairs={{0,4},{4,8},{8,12},{12,16},{16,20},{20,24},{24,28},{28,0},{1,5},{5... | collective-permute-start | bytes 589832 | tf_op jit(solution)/shard_map/ppermute | solution.py:20
  187.1 9.2 %collective-permute-start.9 = (bf16[32,16,192]{2,1,0:T(8,128)(2,1)S(1)}, bf16[32,16,192]{2,1,0:T(8,128)(2,1)S(1)}, u32[]{:S(2)}, u32[]{:S(2)}) collective-permute-start(bf16[32,16,192]{2,1,0:T(8,128)(2,1)S(1)} %get-tuple-element.89), channel_id=1, source_target_pairs={{4,0},{8,4},{12,8},{16,12},{20,16},{24,20},{28,24},{0,28},{5,1},{9... | collective-permute-start | bytes 589832 | tf_op jit(solution)/shard_map/ppermute | solution.py:23
  191.3 1.0 copy-start.15
  196.6 20.5 %collective-permute-start.11 = (bf16[16,64,192]{2,1,0:T(8,128)(2,1)S(1)}, bf16[16,64,192]{2,1,0:T(8,128)(2,1)S(1)}, u32[]{:S(2)}, u32[]{:S(2)}) collective-permute-start(bf16[16,64,192]{2,1,0:T(8,128)(2,1)S(1)} %get-tuple-element.45), channel_id=1, source_target_pairs={{0,1},{1,2},{2,3},{4,5},{5,6},{6,7},{8,9},{9,10},{10,11},{12,13},{... | collective-permute-start | bytes 1179656 | tf_op jit(solution)/shard_map/ppermute | solution.py:20
  214.0 4.5 %collective-permute-start.10 = (bf16[16,64,192]{2,1,0:T(8,128)(2,1)S(1)}, bf16[16,64,192]{2,1,0:T(8,128)(2,1)S(1)}, u32[]{:S(2)}, u32[]{:S(2)}) collective-permute-start(bf16[16,64,192]{2,1,0:T(8,128)(2,1)S(1)} %get-tuple-element.46), channel_id=1, source_target_pairs={{1,0},{2,1},{3,2},{5,4},{6,5},{7,6},{9,8},{10,9},{11,10},{13,12},{... | collective-permute-start | bytes 1179656 | tf_op jit(solution)/shard_map/ppermute | solution.py:23
  215.9 1.2 copy-start.4
  225.0 1.2 copy-start.5
  226.2 9.2 %collective-permute-start.12 = (bf16[32,16,192]{2,1,0:T(8,128)(2,1)S(1)}, bf16[32,16,192]{2,1,0:T(8,128)(2,1)S(1)}, u32[]{:S(2)}, u32[]{:S(2)}) collective-permute-start(bf16[32,16,192]{2,1,0:T(8,128)(2,1)S(1)} %get-tuple-element.88), channel_id=1, source_target_pairs={{0,4},{4,8},{8,12},{12,16},{16,20},{20,24},{24,28},{28,0},{1,5},{5... | collective-permute-start | bytes 589832 | tf_op jit(solution)/shard_map/ppermute | solution.py:20
  226.3 23.3 %copy-start.12 = (bf16[9,192,192]{2,1,0:T(8,128)(2,1)S(1)}, bf16[9,192,192]{2,1,0:T(8,128)(2,1)}, u32[]{:S(2)}) copy-start(bf16[9,192,192]{2,1,0:T(8,128)(2,1)} %param.14) | copy-start | bytes 1990660
  226.3 9.2 %collective-permute-start.13 = (bf16[32,16,192]{2,1,0:T(8,128)(2,1)S(1)}, bf16[32,16,192]{2,1,0:T(8,128)(2,1)S(1)}, u32[]{:S(2)}, u32[]{:S(2)}) collective-permute-start(bf16[32,16,192]{2,1,0:T(8,128)(2,1)S(1)} %get-tuple-element.87), channel_id=1, source_target_pairs={{4,0},{8,4},{12,8},{16,12},{20,16},{24,20},{28,24},{0,28},{5,1},{9... | collective-permute-start | bytes 589832 | tf_op jit(solution)/shard_map/ppermute | solution.py:23
  235.9 14.5 %collective-permute-start.15 = (bf16[16,64,192]{2,1,0:T(8,128)(2,1)S(1)}, bf16[16,64,192]{2,1,0:T(8,128)(2,1)S(1)}, u32[]{:S(2)}, u32[]{:S(2)}) collective-permute-start(bf16[16,64,192]{2,1,0:T(8,128)(2,1)S(1)} %get-tuple-element.41), channel_id=1, source_target_pairs={{0,1},{1,2},{2,3},{4,5},{5,6},{6,7},{8,9},{9,10},{10,11},{12,13},{... | collective-permute-start | bytes 1179656 | tf_op jit(solution)/shard_map/ppermute | solution.py:20
  248.3 4.5 %collective-permute-start.14 = (bf16[16,64,192]{2,1,0:T(8,128)(2,1)S(1)}, bf16[16,64,192]{2,1,0:T(8,128)(2,1)S(1)}, u32[]{:S(2)}, u32[]{:S(2)}) collective-permute-start(bf16[16,64,192]{2,1,0:T(8,128)(2,1)S(1)} %get-tuple-element.42), channel_id=1, source_target_pairs={{1,0},{2,1},{3,2},{5,4},{6,5},{7,6},{9,8},{10,9},{11,10},{13,12},{... | collective-permute-start | bytes 1179656 | tf_op jit(solution)/shard_map/ppermute | solution.py:23
  398.6 2.9 copy-start.8
  401.5 2.1 copy-start.7
  403.6 2.1 copy-start.6
Sparse Core Ops, SparseCore 0:
  226.3 172.2 all-reduce.2
where the time goes:
time: 415 us; the launch traced here: 414 us
  waiting for transfers between devices  233 us (56%)
  starting transfers between devices  121 us (29%)
  matrix products  22.3 us (5%)
  local copies, waits for them, and re-layouts  15.7 us (4%)
  between operations  15.1 us (4%)
  other arithmetic  6.13 us (1%)
    psum x1, waiting for transfers between devices, settle(): return lax.psum((first_grad, second_grad), ('lon', 'lat'))  142 us
    ppermute x16, starting transfers between devices, with_halo(): lax.ppermute(lax.slice_in_dim(block, block.shape[dim] - width, None, axis...  79.7 us
    ppermute x16, waiting for transfers between devices, with_halo(): lax.ppermute(lax.slice_in_dim(block, block.shape[dim] - width, None, axis...  67 us
    ppermute x16, starting transfers between devices, with_halo(): lax.ppermute(lax.slice_in_dim(block, 0, width, axis=dim), axis, backward)  41.7 us
    ppermute x16, waiting for transfers between devices, with_halo(): lax.ppermute(lax.slice_in_dim(block, 0, width, axis=dim), axis, backward)  24.3 us
    dot_general x36, matrix products, weight_grad(): lax.dot_general(window(widened, row_tap, col_tap, dilation, height, bread...  12.7 us
    unnamed x42, local copies, waits for them, and re-layouts  12.3 us
    dot_general x12, matrix products, pulled(): lax.dot_general(joined, stacked, (((2,), (1,)), ((), ())), preferred_elem...  9.6 us
  transfers between devices with their start and end apart: 33, of which 15 were waited for; matrix products, arithmetic and copies ran while one was open for 7% of the time, Pallas kernels for 0%

commit v1 on v0

v1 whole, which is shorter than its diff:
```python
import jax
import jax.numpy as jnp
from jax import lax
from jax.experimental import pallas as pl
from jax.experimental.pallas import tpu as pltpu
from jax.sharding import Mesh
from jax.sharding import PartitionSpec as P


F32 = jnp.float32
BF16 = jnp.bfloat16
STRIDE = 16
TAPS = [(r, c) for r in (-1, 0, 1) for c in (-1, 0, 1)]
PLANE = ("x", "y", "c")
VMEM_LIMIT = 48 * 1024 * 1024


def call(body, outs, scratch, flops, *args):
    size = sum(a.size * a.dtype.itemsize for a in args)
    size += sum(o.size * o.dtype.itemsize for o in outs)
    return pl.pallas_call(
        body,
        out_shape=outs,
        scratch_shapes=scratch,
        compiler_params=pltpu.CompilerParams(vmem_limit_bytes=VMEM_LIMIT),
        cost_estimate=pl.CostEstimate(flops=flops, bytes_accessed=size, transcendentals=0),
    )(*args)


def class_column(ref, col):
    part = ref[col // 2, :, :, :, :, col % 2]
    return part.reshape((8, 2) + part.shape[-2:])


def class_flat(ref):
    cols = [class_column(ref, col) for col in range(4)]
    chan = cols[0].shape[-1]
    return jnp.concatenate([col.reshape(-1, chan) for col in cols], 0)


def fill(padded, pieces, step):
    rows = padded.shape[1] - 2 * step
    edge = jnp.zeros(padded.shape[:1] + (step,) + padded.shape[2:], BF16)
    padded[:, :step] = edge
    padded[:, step + rows :] = edge
    at = 0
    for ref in pieces:
        if len(ref.shape) == 8:
            for col in range(4):
                padded[at, step : step + rows] = class_column(ref, col)
                at += 1
        else:
            padded[at : at + ref.shape[0], step : step + rows] = ref[...]
            at += ref.shape[0]


def window(padded, tap, step):
    r, c = tap
    top, left = step - r * step, step - c * step
    part = padded[left : left + 4, top : top + 8]
    return part.reshape(-1, part.shape[-1])


def pulled(padded, weights, step):
    total = None
    for k, tap in enumerate(TAPS):
        term = lax.dot_general(
            window(padded, tap, step), weights[k], (((1,), (1,)), ((), ())), preferred_element_type=F32
        )
        total = term if total is None else total + term
    return total


def store(refs, value):
    value = value.astype(BF16)
    at = 0
    for ref in refs:
        if len(ref.shape) == 8:
            cols = value.reshape((4, 2, 2, 2, 2) + ref.shape[-2:])
            for col in range(4):
                ref[col // 2, :, :, :, :, col % 2] = cols[col]
        else:
            size = ref.size // ref.shape[-1]
            ref[...] = value[at : at + size].reshape(ref.shape)
            at += size


def flat(refs):
    if len(refs) == 1:
        return class_flat(refs[0])
    return jnp.concatenate([ref[...].reshape(-1, ref.shape[-1]) for ref in refs], 0)


def conv_two(field, act, weights, step, outs):
    n = len(field)

    def body(*refs):
        pieces, act_ref, w_ref = refs[:n], refs[n], refs[n + 1]
        out_refs, padded = refs[n + 2 : -1], refs[-1]
        fill(padded, pieces, step)
        grad = pulled(padded, w_ref, step)
        pre = class_flat(act_ref).astype(F32)
        sigma = jax.nn.sigmoid(pre)
        store(out_refs, grad * sigma * (1.0 + pre * (1.0 - sigma)))

    return call(body, outs, [padded_shape(field, step)], flops_of(act), *field, act, weights)


def conv_one(field, base, weights, step, outs):
    n, b = len(field), len(base)

    def body(*refs):
        pieces, base_refs, w_ref = refs[:n], refs[n : n + b], refs[n + b]
        out_refs, padded = refs[n + b + 1 : -1], refs[-1]
        fill(padded, pieces, step)
        grad = pulled(padded, w_ref, step)
        store(out_refs, flat(base_refs).astype(F32) + grad)

    total = flops_of(*base)
    return call(body, outs, [padded_shape(field, step)], total, *field, *base, weights)


def weight_grad(field, source, active, step):
    n = len(field)
    chan = source.shape[-1]

    def body(*refs):
        pieces, src_ref, out_ref, padded = refs[:n], refs[n], refs[n + 1], refs[n + 2]
        fill(padded, pieces, step)
        src = class_flat(src_ref)
        if active:
            pre = src.astype(F32)
            src = (pre * jax.nn.sigmoid(pre)).astype(BF16)
        turned = src.T
        for k, tap in enumerate(TAPS):
            out_ref[k] = jnp.dot(turned, window(padded, tap, step), preferred_element_type=F32)

    out = [jax.ShapeDtypeStruct((len(TAPS), chan, chan), F32)]
    return call(body, out, [padded_shape(field, step)], flops_of(source), *field, source)[0]


def flops_of(*arrays):
    size = sum(a.size for a in arrays)
    return 2 * len(TAPS) * size * arrays[0].shape[-1]


def padded_shape(field, step):
    chan = field[0].shape[-1]
    return pltpu.VMEM((4 + 2 * step, 8 + 2 * step, 2, STRIDE, chan), BF16)


def coarse(cols, chan):
    return jax.ShapeDtypeStruct((cols, 8, 2, STRIDE, chan), BF16)


def scatter_classes(value):
    height, breadth, chan = value.shape
    group = lax.axis_size(PLANE)
    parts = value.reshape(2, group, STRIDE // group, breadth, chan).transpose(1, 0, 2, 3, 4)
    parts = lax.all_to_all(parts, PLANE, 0, 0)
    return parts.reshape(2, 2, 2, 2, 2, 2, STRIDE, chan)


def gather_classes(value, height, breadth):
    chan = value.shape[-1]
    group = lax.axis_size(PLANE)
    parts = value.reshape(group, 2, STRIDE // group, breadth, chan)
    parts = lax.all_to_all(parts, PLANE, 0, 0)
    return parts.transpose(1, 0, 2, 3, 4).reshape(height, breadth, chan)


def ring(left_edge, right_edge):
    count = lax.axis_size("z")
    up = [(i, (i + 1) % count) for i in range(count)]
    down = [(b, a) for a, b in up]
    return lax.ppermute(right_edge, "z", up), lax.ppermute(left_edge, "z", down)


def xor(value, axis, k):
    count = lax.axis_size(axis)
    return lax.ppermute(value, axis, [(i, i ^ k) for i in range(count)])


def sum_weights(first, second):
    taps, chan, _ = first.shape
    core = lax.axis_index("c")
    mine = 2 * lax.axis_index("x") + lax.axis_index("y")
    first = first.reshape(4, -1, chan)
    second = second.reshape(4, -1, chan)
    keep = jnp.where(core == 0, first, second)
    give = jnp.where(core == 0, second, first).astype(BF16)
    total = keep + xor(give, "c", 1).astype(F32)
    sent = total.astype(BF16)
    got = [
        xor(lax.dynamic_index_in_dim(sent, mine ^ k, 0, keepdims=False), ("x", "y"), k) for k in (1, 2, 3)
    ]
    part = lax.dynamic_index_in_dim(total, mine, 0, keepdims=False)
    for term in got:
        part = part + term.astype(F32)
    part = part.astype(BF16)
    count = lax.axis_size("z")
    k = 1
    while k < count:
        near = part.astype(F32) + xor(part, "z", k).astype(F32)
        if 4 * k <= count:
            near = near + (xor(part, "z", 2 * k).astype(F32) + xor(part, "z", 3 * k).astype(F32))
            k = 4 * k
        else:
            k = 2 * k
        part = near.astype(BF16)
    quarters = jnp.stack([part] + [xor(part, ("x", "y"), k) for k in (1, 2, 3)])
    other = xor(quarters, "c", 1)
    place = jnp.stack([core, mine]).astype(jnp.int32)

    def body(place_ref, own_ref, other_ref, first_ref, second_ref):
        rows = own_ref.shape[1]

        def put(out_ref, parts_ref):
            for k in range(4):
                at = pl.multiple_of((place_ref[1] ^ k) * rows, 8)
                out_ref[pl.ds(at, rows)] = parts_ref[k].astype(F32)

        @pl.when(place_ref[0] == 0)
        def _():
            put(first_ref, own_ref)
            put(second_ref, other_ref)

        @pl.when(place_ref[0] != 0)
        def _():
            put(first_ref, other_ref)
            put(second_ref, own_ref)

    out = jax.ShapeDtypeStruct((taps * chan, chan), F32)
    vmem = pl.BlockSpec(memory_space=pltpu.VMEM)
    one, two = pl.pallas_call(
        body,
        out_shape=[out, out],
        in_specs=[pl.BlockSpec(memory_space=pltpu.SMEM), vmem, vmem],
        compiler_params=pltpu.CompilerParams(vmem_limit_bytes=VMEM_LIMIT),
    )(place, quarters, other)
    return one.reshape(taps, chan, chan), two.reshape(taps, chan, chan)


def local(
    first_block_input,
    first_block_preactivation,
    second_block_input,
    second_block_preactivation,
    output_gradient_final,
    first_block_conv_one,
    first_block_conv_two,
    second_block_conv_one,
    second_block_conv_two,
):
    height, breadth, chan = output_gradient_final.shape
    final = scatter_classes(output_gradient_final)
    low, high = ring(final[0].reshape(2, -1, breadth, chan), final[1].reshape(2, -1, breadth, chan))

    def halved(edge):
        return edge.reshape(8, 2, 2, STRIDE, chan).transpose(2, 0, 1, 3, 4)

    entry_two = scatter_classes(second_block_input)
    act_two = scatter_classes(second_block_preactivation)
    entry_one = scatter_classes(first_block_input)
    act_one = scatter_classes(first_block_preactivation)

    halves = [coarse(2, chan)] * 2
    thirds = [coarse(1, chan), coarse(2, chan), coarse(1, chan)]

    wide = [halved(low), final, halved(high)]
    pre = conv_two(wide, act_two, second_block_conv_two, 2, halves)
    low, high = ring(pre[0], pre[1])
    second_two = weight_grad(wide, act_two, True, 2)
    wide = [low, *pre, high]
    mid = conv_one(wide, [final], second_block_conv_one, 2, thirds)
    low, high = ring(mid[0], mid[2])
    second_one = weight_grad(wide, entry_two, False, 2)
    wide = [low, *mid, high]
    pre = conv_two(wide, act_one, first_block_conv_two, 1, thirds)
    low, high = ring(pre[0], pre[2])
    first_two = weight_grad(wide, act_one, True, 1)
    wide = [low, *pre, high]
    whole = [jax.ShapeDtypeStruct(final.shape, BF16)]
    out = conv_one(wide, mid, first_block_conv_one, 1, whole)[0]
    first_one = weight_grad(wide, entry_one, False, 1)
    second_two, second_one = sum_weights(second_two, second_one)
    first_two, first_one = sum_weights(first_two, first_one)
    out = gather_classes(out, height, breadth)
    return out, first_one, first_two, second_one, second_two


def solution(mesh):
    lon, lat = mesh.shape["lon"], mesh.shape["lat"]
    split = Mesh(mesh.devices.reshape(lon // 2, 2, lat // 2, 2), ("z", "x", "y", "c"))
    grid = P(("y", "c"), ("z", "x"), None)
    return jax.shard_map(
        local,
        mesh=split,
        in_specs=(grid,) * 5 + (P(),) * 4,
        out_specs=(grid, P(), P(), P(), P()),
        check_vma=False,
    )
```

time: 415 us -> 215 us (0.52)
  waiting for transfers between devices: 233 us -> 69.4 us
  starting transfers between devices: 121 us -> 69.1 us
  Pallas kernels: 0 us -> 23 us
  matrix products: 22.3 us -> 0 us
  local copies, waits for them, and re-layouts: 15.7 us -> 36.3 us
  between operations: 15.1 us -> 1.22 us
  other arithmetic: 6.13 us -> 14.7 us
    psum x1 -> x0, waiting for transfers between devices: 142 us -> none  [settle(): return lax.psum((first_grad, second_grad), ('lon', 'lat'))]
    ppermute x32 -> x30, starting transfers between devices: 121 us -> 45 us  [the longest x22 29.6 us: xor(): return lax.ppermute(value, axis, [(i, i ^ k) for i in range(count)])]
    ppermute x32 -> x30, waiting for transfers between devices: 91.3 us -> 44.8 us  [the longest x22 28.2 us: xor(): return lax.ppermute(value, axis, [(i, i ^ k) for i in range(count)])]
    all_to_all x0 -> x6, waiting for transfers between devices: none -> 24.6 us  [the longest x5 15.9 us: scatter_classes(): parts = lax.all_to_all(parts, PLANE, 0, 0)]
    all_to_all x0 -> x6, starting transfers between devices: none -> 24.1 us  [the longest x5 20.6 us: scatter_classes(): parts = lax.all_to_all(parts, PLANE, 0, 0)]
    pallas_call x0 -> x10, Pallas kernels: none -> 23 us  [the longest x8 17.8 us: call(): pl.pallas_call(body, out_shape=outs, scratch_shapes=scratch, compiler_par...]
    dot_general x48 -> x0, matrix products: 22.3 us -> none  [the longest x36 12.7 us: weight_grad(): lax.dot_general(window(widened, row_tap, col_tap, dilation, height, bread...]
    convert_element_type x2 -> x8, other arithmetic: 1.69 us -> 9.34 us  [the longest x2 3.38 us: sum_weights(): sent = total.astype(BF16)]
  transfers between devices with their start and end apart: 33 -> 36, of which waited for: 15 -> 20; matrix products, arithmetic and copies ran while one was open for 7% -> 18% of each run, Pallas kernels for 0% -> 10%
where the time goes in v1:
time: 215 us; the launch traced here: 214 us
  waiting for transfers between devices  69.4 us (32%)
  starting transfers between devices  69.1 us (32%)
  local copies, waits for them, and re-layouts  36.3 us (17%)
  Pallas kernels  23 us (11%)
  other arithmetic  14.7 us (7%)
    ppermute x22, starting transfers between devices, xor(): return lax.ppermute(value, axis, [(i, i ^ k) for i in range(count)])  29.6 us
    ppermute x22, waiting for transfers between devices, xor(): return lax.ppermute(value, axis, [(i, i ^ k) for i in range(count)])  28.2 us
    all_to_all x5, starting transfers between devices, scatter_classes(): parts = lax.all_to_all(parts, PLANE, 0, 0)  20.6 us
    pallas_call x8, Pallas kernels, call(): pl.pallas_call(body, out_shape=outs, scratch_shapes=scratch, compiler_par...  17.8 us
    all_to_all x5, waiting for transfers between devices, scatter_classes(): parts = lax.all_to_all(parts, PLANE, 0, 0)  15.9 us
    ppermute x4, starting transfers between devices, ring(): lax.ppermute(left_edge, 'z', down)  12.3 us
    unnamed x74, local copies, waits for them, and re-layouts  9.41 us
    all_to_all x1, waiting for transfers between devices, gather_classes(): parts = lax.all_to_all(parts, PLANE, 0, 0)  8.68 us
  transfers between devices with their start and end apart: 36, of which 20 were waited for; matrix products, arithmetic and copies ran while one was open for 18% of the time, Pallas kernels for 10%

profile of v1, /device:TPU:0, one launch (start us, length us, event | category | flops | bytes accessed | tf_op | source)
XLA Modules:
  0.0 213.8 jit_solution(8504433620103883911)
XLA Ops:
  0.6 1.9 copy.62
  2.6 5.3 %all-to-all-start.1 = ((bf16[8,2,2,32,192]{4,3,2,1,0:T(8,128)(2,1)}), bf16[8,2,2,32,192]{4,3,2,1,0:T(8,128)(2,1)S(1)}, u32[]{:S(2)}, u32[]{:S(2)}) async-start(bf16[8,2,2,32,192]{4,3,2,1,0:T(8,128)(2,1)} %bitcast.74), calls=%async_computation.1 | async-start | bytes 1048576 | tf_op jit(solution)/shard_map/all_to_all | solution.py:160
  8.7 8.0 %all-to-all-done.1 = bf16[8,2,2,32,192]{4,3,2,1,0:T(8,128)(2,1)S(1)} async-done(((bf16[8,2,2,32,192]{4,3,2,1,0:T(8,128)(2,1)}), bf16[8,2,2,32,192]{4,3,2,1,0:T(8,128)(2,1)S(1)}, u32[]{:S(2)}, u32[]{:S(2)}) %all-to-all-start.1) | async-done | bytes 393248 | tf_op jit(solution)/shard_map/all_to_all | solution.py:160
  16.7 3.5 %all-to-all-start = ((bf16[8,2,2,32,192]{4,3,2,1,0:T(8,128)(2,1)}), bf16[8,2,2,32,192]{4,3,2,1,0:T(8,128)(2,1)S(1)}, u32[]{:S(2)}, u32[]{:S(2)}) async-start(bf16[8,2,2,32,192]{4,3,2,1,0:T(8,128)(2,1)} %bitcast.75), calls=%async_computation | async-start | bytes 1048576 | tf_op jit(solution)/shard_map/all_to_all | solution.py:160
  21.1 7.9 %all-to-all-done = bf16[8,2,2,32,192]{4,3,2,1,0:T(8,128)(2,1)S(1)} async-done(((bf16[8,2,2,32,192]{4,3,2,1,0:T(8,128)(2,1)}), bf16[8,2,2,32,192]{4,3,2,1,0:T(8,128)(2,1)S(1)}, u32[]{:S(2)}, u32[]{:S(2)}) %all-to-all-start) | async-done | bytes 393248 | tf_op jit(solution)/shard_map/all_to_all | solution.py:160
  29.0 3.5 %all-to-all-start.5 = ((bf16[8,2,2,32,192]{4,3,2,1,0:T(8,128)(2,1)}), bf16[8,2,2,32,192]{4,3,2,1,0:T(8,128)(2,1)S(1)}, u32[]{:S(2)}, u32[]{:S(2)}) async-start(bf16[8,2,2,32,192]{4,3,2,1,0:T(8,128)(2,1)} %bitcast.71), calls=%async_computation.5 | async-start | bytes 1048576 | tf_op jit(solution)/shard_map/all_to_all | solution.py:160
  32.5 1.6 collective-permute-start
  34.2 2.2 %collective-permute-start.1 = (bf16[2,8,32,192]{3,2,1,0:T(8,128)(2,1)S(1)}, bf16[2,8,32,192]{3,2,1,0:T(8,128)(2,1)S(1)}, u32[]{:S(2)}, u32[]{:S(2)}) collective-permute-start(bf16[2,8,32,192]{3,2,1,0:T(8,128)(2,1)S(1)} %bitcast.104), channel_id=1, source_target_pairs={{8,0},{16,8},{24,16},{0,24},{9,1},{17,9},{25,17},{1,25},{10,2},{18... | collective-permute-start | bytes 589832 | tf_op jit(solution)/shard_map/ppermute | solution.py:176
  36.4 7.1 %collective-permute-done = bf16[2,8,32,192]{3,2,1,0:T(8,128)(2,1)S(1)} collective-permute-done((bf16[2,8,32,192]{3,2,1,0:T(8,128)(2,1)S(1)}, bf16[2,8,32,192]{3,2,1,0:T(8,128)(2,1)S(1)}, u32[]{:S(2)}, u32[]{:S(2)}) %collective-permute-start) | collective-permute-done | bytes 196640 | tf_op jit(solution)/shard_map/ppermute | solution.py:176
  43.6 4.6 %collective-permute-done.1 = bf16[2,8,32,192]{3,2,1,0:T(8,128)(2,1)S(1)} collective-permute-done((bf16[2,8,32,192]{3,2,1,0:T(8,128)(2,1)S(1)}, bf16[2,8,32,192]{3,2,1,0:T(8,128)(2,1)S(1)}, u32[]{:S(2)}, u32[]{:S(2)}) %collective-permute-start.1) | collective-permute-done | bytes 196640 | tf_op jit(solution)/shard_map/ppermute | solution.py:176
  48.2 1.5 shard_map.128
  50.9 2.7 %collective-permute-start.3 = (bf16[2,8,2,16,192]{4,3,2,1,0:T(8,128)(2,1)S(1)}, bf16[2,8,2,16,192]{4,3,2,1,0:T(8,128)(2,1)S(1)}, u32[]{:S(2)}, u32[]{:S(2)}) collective-permute-start(bf16[2,8,2,16,192]{4,3,2,1,0:T(8,128)(2,1)S(1)} %get-tuple-element.18.refs_1_), channel_id=1, source_target_pairs={{8,0},{16,8},{24,16},{0,24},{9,1},{17,9},{25,17},{1,25},{10,2},{18... | collective-permute-start | bytes 589832 | tf_op jit(solution)/shard_map/ppermute | solution.py:176
  54.5 4.2 %all-to-all-start.2 = ((bf16[8,2,2,32,192]{4,3,2,1,0:T(8,128)(2,1)}), bf16[8,2,2,32,192]{4,3,2,1,0:T(8,128)(2,1)}, u32[]{:S(2)}, u32[]{:S(2)}) async-start(bf16[8,2,2,32,192]{4,3,2,1,0:T(8,128)(2,1)} %bitcast.73), calls=%async_computation.2 | async-start | bytes 1048576 | tf_op jit(solution)/shard_map/all_to_all | solution.py:160
  59.5 1.3 collective-permute-done.2.refs_0_
  60.8 3.6 %collective-permute-done.3.refs_3_ = bf16[2,8,2,16,192]{4,3,2,1,0:T(8,128)(2,1)S(1)} collective-permute-done((bf16[2,8,2,16,192]{4,3,2,1,0:T(8,128)(2,1)S(1)}, bf16[2,8,2,16,192]{4,3,2,1,0:T(8,128)(2,1)S(1)}, u32[]{:S(2)}, u32[]{:S(2)}) %collective-permute-start.3) | collective-permute-done | bytes 196640 | tf_op jit(solution)/shard_map/ppermute | solution.py:176
  65.6 2.1 shard_map.129
  68.1 3.5 %collective-permute-start.5 = (bf16[1,8,2,16,192]{4,3,2,1,0:T(8,128)(2,1)}, bf16[1,8,2,16,192]{4,3,2,1,0:T(8,128)(2,1)}, u32[]{:S(2)}, u32[]{:S(2)}) collective-permute-start(bf16[1,8,2,16,192]{4,3,2,1,0:T(8,128)(2,1)} %get-tuple-element.20.refs_1_.refs_5_), channel_id=1, source_target_pairs={{8,0},{16,8},{24,16},{0,24},{9,1},{17,9},{25,17},{1,25},{10,2},{18... | collective-permute-start | bytes 294920 | tf_op jit(solution)/shard_map/ppermute | solution.py:176
  73.5 1.3 shard_map.135
  74.9 1.2 shard_map.136
  76.1 4.2 %all-to-all-start.4 = ((bf16[8,2,2,32,192]{4,3,2,1,0:T(8,128)(2,1)}), bf16[8,2,2,32,192]{4,3,2,1,0:T(8,128)(2,1)}, u32[]{:S(2)}, u32[]{:S(2)}) async-start(bf16[8,2,2,32,192]{4,3,2,1,0:T(8,128)(2,1)} %bitcast.92), calls=%async_computation.4 | async-start | bytes 1048576 | tf_op jit(solution)/shard_map/all_to_all | solution.py:160
  82.4 3.4 %shard_map.130 = (bf16[1,8,2,16,192]{4,3,2,1,0:T(8,128)(2,1)}, bf16[2,8,2,16,192]{4,3,2,1,0:T(8,128)(2,1)S(1)}, bf16[1,8,2,16,192]{4,3,2,1,0:T(8,128)(2,1)}) custom-call(bf16[1,8,2,16,192]{4,3,2,1,0:T(8,128)(2,1)} %collective-permute-done.4.refs_0_, bf16[1,8,2,16,192]{4,3,2,1,0:T(8,128)(2,1)} %get-tuple-element.20.refs_1_.refs_5_, ...), custom_call_target="tpu_custom_call" | custom-call | flops 679477248 | bytes 2039808 | tf_op jit(solution)/shard_map/pallas_call | solution.py:21
  85.8 3.8 %collective-permute-start.7 = (bf16[1,8,2,16,192]{4,3,2,1,0:T(8,128)(2,1)}, bf16[1,8,2,16,192]{4,3,2,1,0:T(8,128)(2,1)}, u32[]{:S(2)}, u32[]{:S(2)}) collective-permute-start(bf16[1,8,2,16,192]{4,3,2,1,0:T(8,128)(2,1)} %get-tuple-element.23.refs_1_), channel_id=1, source_target_pairs={{8,0},{16,8},{24,16},{0,24},{9,1},{17,9},{25,17},{1,25},{10,2},{18... | collective-permute-start | bytes 294920 | tf_op jit(solution)/shard_map/ppermute | solution.py:176
  90.8 2.2 %copy.44 = bf16[4,432,192]{1,2,0:T(8,128)(2,1)} copy(bf16[4,432,192]{2,1,0:T(8,128)(2,1)} %bitcast.90) | data formatting | bytes 1327104 | tf_op jit(solution)/shard_map/convert_element_type | solution.py:191
  93.9 2.5 %shard_map.132 = f32[9,192,192]{2,1,0:T(8,128)S(1)} custom-call(bf16[1,8,2,16,192]{4,3,2,1,0:T(8,128)(2,1)} %collective-permute-done.4.refs_0_, bf16[1,8,2,16,192]{4,3,2,1,0:T(8,128)(2,1)} %get-tuple-element.20.refs_1_.refs_5_, bf16[2,8,2,16,192]{4,3,2,1,0:T(8,128)(2,1)S(1)} %copy-done.11, bf16[1,8,2,16,192]{4,3,2,1,0:T(8,128)(2,1)} %get-tuple-element.19.refs_3_.refs_7_, ...), custom_call_target="tpu_custom_call" | custom-call | flops 679477248 | bytes 2310144 | tf_op jit(solution)/shard_map/pallas_call | solution.py:21
  96.4 1.2 copy-done
  98.7 2.5 %shard_map.133 = f32[9,192,192]{2,1,0:T(8,128)S(1)} custom-call(bf16[1,8,2,16,192]{4,3,2,1,0:T(8,128)(2,1)} %collective-permute-done.6.refs_0_, bf16[1,8,2,16,192]{4,3,2,1,0:T(8,128)(2,1)} %get-tuple-element.23.refs_1_, bf16[2,8,2,16,192]{4,3,2,1,0:T(8,128)(2,1)S(1)} %copy-done.14, bf16[1,8,2,16,192]{4,3,2,1,0:T(8,128)(2,1)} %get-tuple-element.22.refs_3_, ...), custom_call_target="tpu_custom_call" | custom-call | flops 679477248 | bytes 2310144 | tf_op jit(solution)/shard_map/pallas_call | solution.py:21
  101.2 1.3 select_convert_fusion.1
  102.7 2.2 %copy.35 = bf16[4,432,192]{1,2,0:T(8,128)(2,1)} copy(bf16[4,432,192]{2,1,0:T(8,128)(2,1)} %bitcast.91) | data formatting | bytes 1327104 | tf_op jit(solution)/shard_map/convert_element_type | solution.py:191
  105.4 3.7 %broadcast_select_fusion = (f32[9,192,192]{2,1,0:T(8,128)}, f32[9,192,192]{2,1,0:T(8,128)}) fusion(f32[9,192,192]{2,1,0:T(8,128)S(1)} %shard_map.135, f32[9,192,192]{2,1,0:T(8,128)S(1)} %shard_map.136, pred[]{:T(512)S(6)} %eq.2, f32[9,192,192]{2,1,0:T(8,128)} %copy-done, f32[9,192,192]{2,1,0:T(8,128)} %copy-done.2), kind=kLoop, calls=%fused_computation.6 | loop fusion | flops 663552 | bytes 7962625 | tf_op jit(solution)/shard_map/jit(_where)/select_n | solution.py:190
  109.1 2.8 %copy.45 = f32[4,432,192]{1,2,0:T(8,128)} copy(f32[4,432,192]{2,1,0:T(8,128)} %bitcast.89) | data formatting | bytes 2654208 | tf_op jit(solution)/shard_map/jit(_where)/select_n | solution.py:190
  112.7 1.9 fusion.6
  115.4 1.7 copy.47
  118.8 1.9 collective-permute-start.21
  120.7 1.4 collective-permute-start.22
  123.1 1.9 copy.46
  125.0 1.4 fusion.7
  127.0 2.0 collective-permute-start.10
  128.9 1.4 collective-permute-start.11
  130.5 3.0 %collective-permute-done.22 = bf16[432,192]{1,0:T(8,128)(2,1)} collective-permute-done((bf16[432,192]{1,0:T(8,128)(2,1)}, bf16[432,192]{1,0:T(8,128)(2,1)}, u32[]{:S(2)}, u32[]{:S(2)}) %collective-permute-start.22) | collective-permute-done | bytes 165920 | tf_op jit(solution)/shard_map/ppermute | solution.py:181
  133.5 1.8 collective-permute-done.20
  135.3 1.2 fusion.2
  136.9 4.3 %collective-permute-start.23 = (bf16[432,192]{1,0:T(8,128)(2,1)S(1)}, bf16[432,192]{1,0:T(8,128)(2,1)S(1)}, u32[]{:S(2)}, u32[]{:S(2)}) collective-permute-start(bf16[432,192]{1,0:T(8,128)(2,1)S(1)} %fusion.2), channel_id=1, source_target_pairs={{0,8},{8,0},{16,24},{24,16},{1,9},{9,1},{17,25},{25,17},{2,10},{10... | collective-permute-start | bytes 497672 | tf_op jit(solution)/shard_map/ppermute | solution.py:181
  142.1 1.3 collective-permute-done.9
  144.8 2.0 collective-permute-done.25
  146.8 11.5 %collective-permute-start.12 = (bf16[432,192]{1,0:T(8,128)(2,1)S(1)}, bf16[432,192]{1,0:T(8,128)(2,1)S(1)}, u32[]{:S(2)}, u32[]{:S(2)}) collective-permute-start(bf16[432,192]{1,0:T(8,128)(2,1)S(1)} %fusion.5), channel_id=1, source_target_pairs={{0,8},{8,0},{16,24},{24,16},{1,9},{9,1},{17,25},{25,17},{2,10},{10... | collective-permute-start | bytes 497672 | tf_op jit(solution)/shard_map/ppermute | solution.py:181
  158.2 8.0 %collective-permute-done.24 = bf16[432,192]{1,0:T(8,128)(2,1)} collective-permute-done((bf16[432,192]{1,0:T(8,128)(2,1)S(1)}, bf16[432,192]{1,0:T(8,128)(2,1)}, u32[]{:S(2)}, u32[]{:S(2)}) %collective-permute-start.24) | collective-permute-done | bytes 165920 | tf_op jit(solution)/shard_map/ppermute | solution.py:181
  167.2 1.5 collective-permute-start.28
  169.2 1.6 collective-permute-start.26
  170.8 1.5 collective-permute-done.13
  172.4 1.5 collective-permute-start.17
  174.3 1.6 collective-permute-done.28
  176.4 3.2 %collective-permute-done.27 = bf16[432,192]{1,0:T(8,128)(2,1)S(1)} collective-permute-done((bf16[432,192]{1,0:T(8,128)(2,1)S(1)}, bf16[432,192]{1,0:T(8,128)(2,1)S(1)}, u32[]{:S(2)}, u32[]{:S(2)}) %collective-permute-start.27) | collective-permute-done | bytes 165920 | tf_op jit(solution)/shard_map/ppermute | solution.py:181
  179.6 2.3 %collective-permute-done.26 = bf16[432,192]{1,0:T(8,128)(2,1)S(1)} collective-permute-done((bf16[432,192]{1,0:T(8,128)(2,1)S(1)}, bf16[432,192]{1,0:T(8,128)(2,1)S(1)}, u32[]{:S(2)}, u32[]{:S(2)}) %collective-permute-start.26) | collective-permute-done | bytes 165920 | tf_op jit(solution)/shard_map/ppermute | solution.py:181
  182.1 1.2 copy.50
  183.8 1.2 collective-permute-done.16
  186.7 1.3 pad_maximum_fusion.own_ref
  188.0 1.2 copy.41
  189.3 3.4 %shard_map.131 = bf16[2,2,2,2,2,2,16,192]{7,6,5,4,3,2,1,0:T(8,128)(2,1)} custom-call(bf16[1,8,2,16,192]{4,3,2,1,0:T(8,128)(2,1)} %collective-permute-done.6.refs_0_, bf16[1,8,2,16,192]{4,3,2,1,0:T(8,128)(2,1)} %get-tuple-element.23.refs_1_, bf16[2,8,2,16,192]{4,3,2,1,0:T(8,128)(2,1)S(1)} %copy-done.15, ...), custom_call_target="tpu_custom_call" | custom-call | flops 679477248 | bytes 2039808 | tf_op jit(solution)/shard_map/pallas_call | solution.py:21
  192.7 3.5 %all-to-all-start.3 = ((bf16[8,2,2,32,192]{4,3,2,1,0:T(8,128)(2,1)}), bf16[8,2,2,32,192]{4,3,2,1,0:T(8,128)(2,1)S(1)}, u32[]{:S(2)}, u32[]{:S(2)}) async-start(bf16[8,2,2,32,192]{4,3,2,1,0:T(8,128)(2,1)} %bitcast.15), calls=%async_computation.3 | async-start | bytes 1048576 | tf_op jit(solution)/shard_map/all_to_all | solution.py:168
  196.3 8.7 %all-to-all-done.3 = bf16[8,2,2,32,192]{4,3,2,1,0:T(8,128)(2,1)S(1)} async-done(((bf16[8,2,2,32,192]{4,3,2,1,0:T(8,128)(2,1)}), bf16[8,2,2,32,192]{4,3,2,1,0:T(8,128)(2,1)S(1)}, u32[]{:S(2)}, u32[]{:S(2)}) %all-to-all-start.3) | async-done | bytes 393248 | tf_op jit(solution)/shard_map/all_to_all | solution.py:168
  205.8 1.4 copy.51.other_ref
  207.2 2.6 %shard_map.137 = (f32[1728,192]{1,0:T(8,128)}, f32[1728,192]{1,0:T(8,128)}) custom-call(s32[2]{0:T(128)S(1)} %pad_add_fusion.place_ref, bf16[4,432,192]{2,1,0:T(8,128)(2,1)S(1)} %pad_maximum_fusion.1.own_ref, bf16[4,432,192]{2,1,0:T(8,128)(2,1)S(1)} %copy.51.other_ref), custom_call_target="tpu_custom_call" | custom-call | tf_op jit(solution)/shard_map/pallas_call | solution.py:235
  209.8 1.4 copy.42.other_ref
  211.2 2.6 %shard_map.134 = (f32[1728,192]{1,0:T(8,128)}, f32[1728,192]{1,0:T(8,128)}) custom-call(s32[2]{0:T(128)S(1)} %pad_add_fusion.place_ref, bf16[4,432,192]{2,1,0:T(8,128)(2,1)S(1)} %pad_maximum_fusion.own_ref, bf16[4,432,192]{2,1,0:T(8,128)(2,1)S(1)} %copy.42.other_ref), custom_call_target="tpu_custom_call" | custom-call | tf_op jit(solution)/shard_map/pallas_call | solution.py:235
  (133 shorter events, 27.0 us)
Async XLA Ops:
  0.6 7.3 %copy-start.30 = (bf16[32,32,192]{2,1,0:T(8,128)(2,1)S(1)}, bf16[32,32,192]{2,1,0:T(8,128)(2,1)}, u32[]{:S(2)}) copy-start(bf16[32,32,192]{2,1,0:T(8,128)(2,1)} %param.13) | copy-start | bytes 1179652
  2.6 17.7 %copy-start.31 = (bf16[32,32,192]{2,1,0:T(8,128)(2,1)S(1)}, bf16[32,32,192]{2,1,0:T(8,128)(2,1)}, u32[]{:S(2)}) copy-start(bf16[32,32,192]{2,1,0:T(8,128)(2,1)} %param.11) | copy-start | bytes 1179652
  2.6 14.1 %all-to-all-start.1 = ((bf16[8,2,2,32,192]{4,3,2,1,0:T(8,128)(2,1)}), bf16[8,2,2,32,192]{4,3,2,1,0:T(8,128)(2,1)S(1)}, u32[]{:S(2)}, u32[]{:S(2)}) async-start(bf16[8,2,2,32,192]{4,3,2,1,0:T(8,128)(2,1)} %bitcast.74), calls=%async_computation.1 | async-start | bytes 1048576 | tf_op jit(solution)/shard_map/all_to_all | solution.py:160
  16.7 12.3 %all-to-all-start = ((bf16[8,2,2,32,192]{4,3,2,1,0:T(8,128)(2,1)}), bf16[8,2,2,32,192]{4,3,2,1,0:T(8,128)(2,1)S(1)}, u32[]{:S(2)}, u32[]{:S(2)}) async-start(bf16[8,2,2,32,192]{4,3,2,1,0:T(8,128)(2,1)} %bitcast.75), calls=%async_computation | async-start | bytes 1048576 | tf_op jit(solution)/shard_map/all_to_all | solution.py:160
  21.1 27.1 %copy-start.25 = (bf16[9,192,192]{2,1,0:T(8,128)(2,1)S(1)}, bf16[9,192,192]{2,1,0:T(8,128)(2,1)}, u32[]{:S(2)}) copy-start(bf16[9,192,192]{2,1,0:T(8,128)(2,1)} %refs_4_.1) | copy-start | bytes 1990660
  29.0 25.5 %all-to-all-start.5 = ((bf16[8,2,2,32,192]{4,3,2,1,0:T(8,128)(2,1)}), bf16[8,2,2,32,192]{4,3,2,1,0:T(8,128)(2,1)S(1)}, u32[]{:S(2)}, u32[]{:S(2)}) async-start(bf16[8,2,2,32,192]{4,3,2,1,0:T(8,128)(2,1)} %bitcast.71), calls=%async_computation.5 | async-start | bytes 1048576 | tf_op jit(solution)/shard_map/all_to_all | solution.py:160
  32.5 11.0 %collective-permute-start = (bf16[2,8,32,192]{3,2,1,0:T(8,128)(2,1)S(1)}, bf16[2,8,32,192]{3,2,1,0:T(8,128)(2,1)S(1)}, u32[]{:S(2)}, u32[]{:S(2)}) collective-permute-start(bf16[2,8,32,192]{3,2,1,0:T(8,128)(2,1)S(1)} %bitcast.105), channel_id=1, source_target_pairs={{0,8},{8,16},{16,24},{24,0},{1,9},{9,17},{17,25},{25,1},{2,10},{10... | collective-permute-start | bytes 589832 | tf_op jit(solution)/shard_map/ppermute | solution.py:176
  34.2 14.0 %collective-permute-start.1 = (bf16[2,8,32,192]{3,2,1,0:T(8,128)(2,1)S(1)}, bf16[2,8,32,192]{3,2,1,0:T(8,128)(2,1)S(1)}, u32[]{:S(2)}, u32[]{:S(2)}) collective-permute-start(bf16[2,8,32,192]{3,2,1,0:T(8,128)(2,1)S(1)} %bitcast.104), channel_id=1, source_target_pairs={{8,0},{16,8},{24,16},{0,24},{9,1},{17,9},{25,17},{1,25},{10,2},{18... | collective-permute-start | bytes 589832 | tf_op jit(solution)/shard_map/ppermute | solution.py:176
  43.5 10.1 %copy-start.32 = (bf16[32,32,192]{2,1,0:T(8,128)(2,1)S(1)}, bf16[32,32,192]{2,1,0:T(8,128)(2,1)}, u32[]{:S(2)}) copy-start(bf16[32,32,192]{2,1,0:T(8,128)(2,1)} %param.10) | copy-start | bytes 1179652
  43.6 10.0 %copy-start.5 = (bf16[8,2,2,16,192]{4,3,1,0,2:T(8,128)(2,1)}, bf16[8,2,2,16,192]{4,3,1,0,2:T(8,128)(2,1)S(1)}, u32[]{:S(2)}) copy-start(bf16[8,2,2,16,192]{4,3,1,0,2:T(8,128)(2,1)S(1)} %copy.65) | copy-start | bytes 589828
  48.2 5.4 %copy-start.7 = (bf16[8,2,2,16,192]{4,3,1,0,2:T(8,128)(2,1)}, bf16[8,2,2,16,192]{4,3,1,0,2:T(8,128)(2,1)S(1)}, u32[]{:S(2)}) copy-start(bf16[8,2,2,16,192]{4,3,1,0,2:T(8,128)(2,1)S(1)} %copy.64) | copy-start | bytes 589828
  49.7 18.0 %copy-start.17 = (bf16[2,8,2,16,192]{4,3,2,1,0:T(8,128)(2,1)}, bf16[2,8,2,16,192]{4,3,2,1,0:T(8,128)(2,1)S(1)}, u32[]{:S(2)}) copy-start(bf16[2,8,2,16,192]{4,3,2,1,0:T(8,128)(2,1)S(1)} %get-tuple-element.18.refs_1_) | copy-start | bytes 589828
  49.7 18.0 %copy-start.19 = (bf16[2,8,2,16,192]{4,3,2,1,0:T(8,128)(2,1)}, bf16[2,8,2,16,192]{4,3,2,1,0:T(8,128)(2,1)S(1)}, u32[]{:S(2)}) copy-start(bf16[2,8,2,16,192]{4,3,2,1,0:T(8,128)(2,1)S(1)} %get-tuple-element.17.refs_2_) | copy-start | bytes 589828
  49.7 8.9 %copy-start.33 = (bf16[32,32,192]{2,1,0:T(8,128)(2,1)S(1)}, bf16[32,32,192]{2,1,0:T(8,128)(2,1)}, u32[]{:S(2)}) copy-start(bf16[32,32,192]{2,1,0:T(8,128)(2,1)} %param.9) | copy-start | bytes 1179652
  49.7 11.1 %collective-permute-start.2 = (bf16[2,8,2,16,192]{4,3,2,1,0:T(8,128)(2,1)S(1)}, bf16[2,8,2,16,192]{4,3,2,1,0:T(8,128)(2,1)S(1)}, u32[]{:S(2)}, u32[]{:S(2)}) collective-permute-start(bf16[2,8,2,16,192]{4,3,2,1,0:T(8,128)(2,1)S(1)} %get-tuple-element.17.refs_2_), channel_id=1, source_target_pairs={{0,8},{8,16},{16,24},{24,0},{1,9},{9,17},{17,25},{25,1},{2,10},{10... | collective-permute-start | bytes 589832 | tf_op jit(solution)/shard_map/ppermute | solution.py:176
  50.9 13.6 %collective-permute-start.3 = (bf16[2,8,2,16,192]{4,3,2,1,0:T(8,128)(2,1)S(1)}, bf16[2,8,2,16,192]{4,3,2,1,0:T(8,128)(2,1)S(1)}, u32[]{:S(2)}, u32[]{:S(2)}) collective-permute-start(bf16[2,8,2,16,192]{4,3,2,1,0:T(8,128)(2,1)S(1)} %get-tuple-element.18.refs_1_), channel_id=1, source_target_pairs={{8,0},{16,8},{24,16},{0,24},{9,1},{17,9},{25,17},{1,25},{10,2},{18... | collective-permute-start | bytes 589832 | tf_op jit(solution)/shard_map/ppermute | solution.py:176
  54.5 13.3 %copy-start.3 = (bf16[8,2,2,32,192]{4,3,2,1,0:T(8,128)(2,1)}, bf16[8,2,2,32,192]{4,3,2,1,0:T(8,128)(2,1)S(1)}, u32[]{:S(2)}) copy-start(bf16[8,2,2,32,192]{4,3,2,1,0:T(8,128)(2,1)S(1)} %all-to-all-done.5) | copy-start | bytes 1179652
  54.5 21.6 %all-to-all-start.2 = ((bf16[8,2,2,32,192]{4,3,2,1,0:T(8,128)(2,1)}), bf16[8,2,2,32,192]{4,3,2,1,0:T(8,128)(2,1)}, u32[]{:S(2)}, u32[]{:S(2)}) async-start(bf16[8,2,2,32,192]{4,3,2,1,0:T(8,128)(2,1)} %bitcast.73), calls=%async_computation.2 | async-start | bytes 1048576 | tf_op jit(solution)/shard_map/all_to_all | solution.py:160
  60.8 7.3 %copy-start.21 = (bf16[2,8,2,16,192]{4,3,2,1,0:T(8,128)(2,1)}, bf16[2,8,2,16,192]{4,3,2,1,0:T(8,128)(2,1)S(1)}, u32[]{:S(2)}) copy-start(bf16[2,8,2,16,192]{4,3,2,1,0:T(8,128)(2,1)S(1)} %collective-permute-done.2.refs_0_) | copy-start | bytes 589828
  65.6 2.5 %copy-start.23 = (bf16[2,8,2,16,192]{4,3,2,1,0:T(8,128)(2,1)}, bf16[2,8,2,16,192]{4,3,2,1,0:T(8,128)(2,1)S(1)}, u32[]{:S(2)}) copy-start(bf16[2,8,2,16,192]{4,3,2,1,0:T(8,128)(2,1)S(1)} %collective-permute-done.3.refs_3_) | copy-start | bytes 589828
  67.7 7.1 %copy-start.9 = (bf16[2,8,2,16,192]{4,3,2,1,0:T(8,128)(2,1)}, bf16[2,8,2,16,192]{4,3,2,1,0:T(8,128)(2,1)S(1)}, u32[]{:S(2)}) copy-start(bf16[2,8,2,16,192]{4,3,2,1,0:T(8,128)(2,1)S(1)} %get-tuple-element.21.refs_2_.refs_6_) | copy-start | bytes 589828
  67.7 7.1 %copy-start.4 = (bf16[8,2,2,32,192]{4,3,2,1,0:T(8,128)(2,1)S(1)}, bf16[8,2,2,32,192]{4,3,2,1,0:T(8,128)(2,1)}, u32[]{:S(2)}) copy-start(bf16[8,2,2,32,192]{4,3,2,1,0:T(8,128)(2,1)} %copy-done.3) | copy-start | bytes 1179652
  67.7 12.5 %collective-permute-start.4 = (bf16[1,8,2,16,192]{4,3,2,1,0:T(8,128)(2,1)}, bf16[1,8,2,16,192]{4,3,2,1,0:T(8,128)(2,1)}, u32[]{:S(2)}, u32[]{:S(2)}) collective-permute-start(bf16[1,8,2,16,192]{4,3,2,1,0:T(8,128)(2,1)} %get-tuple-element.19.refs_3_.refs_7_), channel_id=1, source_target_pairs={{0,8},{8,16},{16,24},{24,0},{1,9},{9,17},{17,25},{25,1},{2,10},{10... | collective-permute-start | bytes 294920 | tf_op jit(solution)/shard_map/ppermute | solution.py:176
  68.1 12.1 %collective-permute-start.5 = (bf16[1,8,2,16,192]{4,3,2,1,0:T(8,128)(2,1)}, bf16[1,8,2,16,192]{4,3,2,1,0:T(8,128)(2,1)}, u32[]{:S(2)}, u32[]{:S(2)}) collective-permute-start(bf16[1,8,2,16,192]{4,3,2,1,0:T(8,128)(2,1)} %get-tuple-element.20.refs_1_.refs_5_), channel_id=1, source_target_pairs={{8,0},{16,8},{24,16},{0,24},{9,1},{17,9},{25,17},{1,25},{10,2},{18... | collective-permute-start | bytes 294920 | tf_op jit(solution)/shard_map/ppermute | solution.py:176
  73.5 1.3 copy-start.18
  73.5 1.3 copy-start.20
  73.5 1.3 copy-start.22
  73.5 1.3 copy-start.24
  76.1 21.6 %all-to-all-start.4 = ((bf16[8,2,2,32,192]{4,3,2,1,0:T(8,128)(2,1)}), bf16[8,2,2,32,192]{4,3,2,1,0:T(8,128)(2,1)}, u32[]{:S(2)}, u32[]{:S(2)}) async-start(bf16[8,2,2,32,192]{4,3,2,1,0:T(8,128)(2,1)} %bitcast.92), calls=%async_computation.4 | async-start | bytes 1048576 | tf_op jit(solution)/shard_map/all_to_all | solution.py:160
  85.8 5.0 %copy-start.13 = (bf16[2,8,2,16,192]{4,3,2,1,0:T(8,128)(2,1)}, bf16[2,8,2,16,192]{4,3,2,1,0:T(8,128)(2,1)S(1)}, u32[]{:S(2)}) copy-start(bf16[2,8,2,16,192]{4,3,2,1,0:T(8,128)(2,1)S(1)} %get-tuple-element.24.refs_2_) | copy-start | bytes 589828
  85.8 11.8 %collective-permute-start.6 = (bf16[1,8,2,16,192]{4,3,2,1,0:T(8,128)(2,1)}, bf16[1,8,2,16,192]{4,3,2,1,0:T(8,128)(2,1)}, u32[]{:S(2)}, u32[]{:S(2)}) collective-permute-start(bf16[1,8,2,16,192]{4,3,2,1,0:T(8,128)(2,1)} %get-tuple-element.22.refs_3_), channel_id=1, source_target_pairs={{0,8},{8,16},{16,24},{24,0},{1,9},{9,17},{17,25},{25,1},{2,10},{10... | collective-permute-start | bytes 294920 | tf_op jit(solution)/shard_map/ppermute | solution.py:176
  85.8 11.8 %collective-permute-start.7 = (bf16[1,8,2,16,192]{4,3,2,1,0:T(8,128)(2,1)}, bf16[1,8,2,16,192]{4,3,2,1,0:T(8,128)(2,1)}, u32[]{:S(2)}, u32[]{:S(2)}) collective-permute-start(bf16[1,8,2,16,192]{4,3,2,1,0:T(8,128)(2,1)} %get-tuple-element.23.refs_1_), channel_id=1, source_target_pairs={{8,0},{16,8},{24,16},{0,24},{9,1},{17,9},{25,17},{1,25},{10,2},{18... | collective-permute-start | bytes 294920 | tf_op jit(solution)/shard_map/ppermute | solution.py:176
  92.9 19.8 %collective-permute-start.19 = (bf16[4,432,192]{1,2,0:T(8,128)(2,1)}, bf16[4,432,192]{1,2,0:T(8,128)(2,1)}, u32[]{:S(2)}, u32[]{:S(2)}) collective-permute-start(bf16[4,432,192]{1,2,0:T(8,128)(2,1)} %copy.44), channel_id=1, source_target_pairs={{0,1},{1,0},{2,3},{3,2},{4,5},{5,4},{6,7},{7,6},{8,9},{9,8},{10,11... | collective-permute-start | bytes 1990664 | tf_op jit(solution)/shard_map/ppermute | solution.py:181
  96.4 1.2 copy-start
  97.6 3.6 %copy-start.1 = (f32[9,192,192]{2,1,0:T(8,128)S(1)}, f32[9,192,192]{2,1,0:T(8,128)}, u32[]{:S(2)}) copy-start(f32[9,192,192]{2,1,0:T(8,128)} %copy-done) | copy-start | bytes 3981316
  101.2 1.5 copy-start.2
  104.9 20.1 %collective-permute-start.8 = (bf16[4,432,192]{1,2,0:T(8,128)(2,1)}, bf16[4,432,192]{1,2,0:T(8,128)(2,1)}, u32[]{:S(2)}, u32[]{:S(2)}) collective-permute-start(bf16[4,432,192]{1,2,0:T(8,128)(2,1)} %copy.35), channel_id=1, source_target_pairs={{0,1},{1,0},{2,3},{3,2},{4,5},{5,4},{6,7},{7,6},{8,9},{9,8},{10,11... | collective-permute-start | bytes 1990664 | tf_op jit(solution)/shard_map/ppermute | solution.py:181
  109.1 2.8 %copy-start.28 = (f32[9,192,192]{2,1,0:T(8,128)S(1)}, f32[9,192,192]{2,1,0:T(8,128)}, u32[]{:S(2)}) copy-start(f32[9,192,192]{2,1,0:T(8,128)} %get-tuple-element.42) | copy-start | bytes 3981316
  118.8 11.5 %collective-permute-start.21 = (bf16[432,192]{1,0:T(8,128)(2,1)}, bf16[432,192]{1,0:T(8,128)(2,1)}, u32[]{:S(2)}, u32[]{:S(2)}) collective-permute-start(bf16[432,192]{1,0:T(8,128)(2,1)} %bitcast.110), channel_id=1, source_target_pairs={{0,4},{2,6},{4,0},{6,2},{1,5},{3,7},{5,1},{7,3},{8,12},{10,14},{12... | collective-permute-start | bytes 497672 | tf_op jit(solution)/shard_map/ppermute | solution.py:181
  120.7 12.8 %collective-permute-start.22 = (bf16[432,192]{1,0:T(8,128)(2,1)}, bf16[432,192]{1,0:T(8,128)(2,1)}, u32[]{:S(2)}, u32[]{:S(2)}) collective-permute-start(bf16[432,192]{1,0:T(8,128)(2,1)} %bitcast.107), channel_id=1, source_target_pairs={{0,6},{2,4},{4,2},{6,0},{1,7},{3,5},{5,3},{7,1},{8,14},{10,12},{12... | collective-permute-start | bytes 497672 | tf_op jit(solution)/shard_map/ppermute | solution.py:181
  122.1 13.1 %collective-permute-start.20 = (bf16[432,192]{1,0:T(8,128)(2,1)}, bf16[432,192]{1,0:T(8,128)(2,1)}, u32[]{:S(2)}, u32[]{:S(2)}) collective-permute-start(bf16[432,192]{1,0:T(8,128)(2,1)} %bitcast.106), channel_id=1, source_target_pairs={{0,2},{2,0},{4,6},{6,4},{1,3},{3,1},{5,7},{7,5},{8,10},{10,8},{12,... | collective-permute-start | bytes 497672 | tf_op jit(solution)/shard_map/ppermute | solution.py:181
  126.5 8.8 %copy-start.29 = (f32[1,432,192]{2,1,0:T(8,128)S(1)}, f32[1,432,192]{2,1,0:T(8,128)}, u32[]{:S(2)}) copy-start(f32[1,432,192]{2,1,0:T(8,128)} %copy.46) | copy-start | bytes 995332
  127.0 10.0 %collective-permute-start.10 = (bf16[432,192]{1,0:T(8,128)(2,1)S(1)}, bf16[432,192]{1,0:T(8,128)(2,1)S(1)}, u32[]{:S(2)}, u32[]{:S(2)}) collective-permute-start(bf16[432,192]{1,0:T(8,128)(2,1)S(1)} %bitcast.112), channel_id=1, source_target_pairs={{0,4},{2,6},{4,0},{6,2},{1,5},{3,7},{5,1},{7,3},{8,12},{10,14},{12... | collective-permute-start | bytes 497672 | tf_op jit(solution)/shard_map/ppermute | solution.py:181
  128.9 13.2 %collective-permute-start.11 = (bf16[432,192]{1,0:T(8,128)(2,1)S(1)}, bf16[432,192]{1,0:T(8,128)(2,1)}, u32[]{:S(2)}, u32[]{:S(2)}) collective-permute-start(bf16[432,192]{1,0:T(8,128)(2,1)S(1)} %bitcast.109), channel_id=1, source_target_pairs={{0,6},{2,4},{4,2},{6,0},{1,7},{3,5},{5,3},{7,1},{8,14},{10,12},{12... | collective-permute-start | bytes 497672 | tf_op jit(solution)/shard_map/ppermute | solution.py:181
  130.4 13.1 %collective-permute-start.9 = (bf16[432,192]{1,0:T(8,128)(2,1)S(1)}, bf16[432,192]{1,0:T(8,128)(2,1)}, u32[]{:S(2)}, u32[]{:S(2)}) collective-permute-start(bf16[432,192]{1,0:T(8,128)(2,1)S(1)} %bitcast.108), channel_id=1, source_target_pairs={{0,2},{2,0},{4,6},{6,4},{1,3},{3,1},{5,7},{7,5},{8,10},{10,8},{12,... | collective-permute-start | bytes 497672 | tf_op jit(solution)/shard_map/ppermute | solution.py:181
  136.5 10.2 %collective-permute-start.25 = (bf16[432,192]{1,0:T(8,128)(2,1)S(1)}, bf16[432,192]{1,0:T(8,128)(2,1)S(1)}, u32[]{:S(2)}, u32[]{:S(2)}) collective-permute-start(bf16[432,192]{1,0:T(8,128)(2,1)S(1)} %fusion.2), channel_id=1, source_target_pairs={{0,24},{8,16},{16,8},{24,0},{1,25},{9,17},{17,9},{25,1},{2,26},{10... | collective-permute-start | bytes 497672 | tf_op jit(solution)/shard_map/ppermute | solution.py:181
  136.6 29.6 %collective-permute-start.24 = (bf16[432,192]{1,0:T(8,128)(2,1)S(1)}, bf16[432,192]{1,0:T(8,128)(2,1)}, u32[]{:S(2)}, u32[]{:S(2)}) collective-permute-start(bf16[432,192]{1,0:T(8,128)(2,1)S(1)} %fusion.2), channel_id=1, source_target_pairs={{0,16},{8,24},{16,0},{24,8},{1,17},{9,25},{17,1},{25,9},{2,18},{10... | collective-permute-start | bytes 497672 | tf_op jit(solution)/shard_map/ppermute | solution.py:181
  136.9 29.3 %collective-permute-start.23 = (bf16[432,192]{1,0:T(8,128)(2,1)S(1)}, bf16[432,192]{1,0:T(8,128)(2,1)S(1)}, u32[]{:S(2)}, u32[]{:S(2)}) collective-permute-start(bf16[432,192]{1,0:T(8,128)(2,1)S(1)} %fusion.2), channel_id=1, source_target_pairs={{0,8},{8,0},{16,24},{24,16},{1,9},{9,1},{17,25},{25,17},{2,10},{10... | collective-permute-start | bytes 497672 | tf_op jit(solution)/shard_map/ppermute | solution.py:181
  144.6 24.6 %collective-permute-start.14 = (bf16[432,192]{1,0:T(8,128)(2,1)S(1)}, bf16[432,192]{1,0:T(8,128)(2,1)S(1)}, u32[]{:S(2)}, u32[]{:S(2)}) collective-permute-start(bf16[432,192]{1,0:T(8,128)(2,1)S(1)} %fusion.5), channel_id=1, source_target_pairs={{0,24},{8,16},{16,8},{24,0},{1,25},{9,17},{17,9},{25,1},{2,26},{10... | collective-permute-start | bytes 497672 | tf_op jit(solution)/shard_map/ppermute | solution.py:181
  144.7 27.6 %collective-permute-start.13 = (bf16[432,192]{1,0:T(8,128)(2,1)S(1)}, bf16[432,192]{1,0:T(8,128)(2,1)S(1)}, u32[]{:S(2)}, u32[]{:S(2)}) collective-permute-start(bf16[432,192]{1,0:T(8,128)(2,1)S(1)} %fusion.5), channel_id=1, source_target_pairs={{0,16},{8,24},{16,0},{24,8},{1,17},{9,25},{17,1},{25,9},{2,18},{10... | collective-permute-start | bytes 497672 | tf_op jit(solution)/shard_map/ppermute | solution.py:181
  146.8 25.5 %collective-permute-start.12 = (bf16[432,192]{1,0:T(8,128)(2,1)S(1)}, bf16[432,192]{1,0:T(8,128)(2,1)S(1)}, u32[]{:S(2)}, u32[]{:S(2)}) collective-permute-start(bf16[432,192]{1,0:T(8,128)(2,1)S(1)} %fusion.5), channel_id=1, source_target_pairs={{0,8},{8,0},{16,24},{24,16},{1,9},{9,1},{17,25},{25,17},{2,10},{10... | collective-permute-start | bytes 497672 | tf_op jit(solution)/shard_map/ppermute | solution.py:181
  167.2 8.7 %collective-permute-start.28 = (bf16[432,192]{1,0:T(8,128)(2,1)S(1)}, bf16[432,192]{1,0:T(8,128)(2,1)S(1)}, u32[]{:S(2)}, u32[]{:S(2)}) collective-permute-start(bf16[432,192]{1,0:T(8,128)(2,1)S(1)} %add_convert_fusion), channel_id=1, source_target_pairs={{0,6},{2,4},{4,2},{6,0},{1,7},{3,5},{5,3},{7,1},{8,14},{10,12},{12... | collective-permute-start | bytes 497672 | tf_op jit(solution)/shard_map/ppermute | solution.py:181
  168.7 10.9 %collective-permute-start.27 = (bf16[432,192]{1,0:T(8,128)(2,1)S(1)}, bf16[432,192]{1,0:T(8,128)(2,1)S(1)}, u32[]{:S(2)}, u32[]{:S(2)}) collective-permute-start(bf16[432,192]{1,0:T(8,128)(2,1)S(1)} %add_convert_fusion), channel_id=1, source_target_pairs={{0,4},{2,6},{4,0},{6,2},{1,5},{3,7},{5,1},{7,3},{8,12},{10,14},{12... | collective-permute-start | bytes 497672 | tf_op jit(solution)/shard_map/ppermute | solution.py:181
  169.2 12.7 %collective-permute-start.26 = (bf16[432,192]{1,0:T(8,128)(2,1)S(1)}, bf16[432,192]{1,0:T(8,128)(2,1)S(1)}, u32[]{:S(2)}, u32[]{:S(2)}) collective-permute-start(bf16[432,192]{1,0:T(8,128)(2,1)S(1)} %add_convert_fusion), channel_id=1, source_target_pairs={{0,2},{2,0},{4,6},{6,4},{1,3},{3,1},{5,7},{7,5},{8,10},{10,8},{12,... | collective-permute-start | bytes 497672 | tf_op jit(solution)/shard_map/ppermute | solution.py:181
  172.4 11.4 %collective-permute-start.17 = (bf16[432,192]{1,0:T(8,128)(2,1)S(1)}, bf16[432,192]{1,0:T(8,128)(2,1)S(1)}, u32[]{:S(2)}, u32[]{:S(2)}) collective-permute-start(bf16[432,192]{1,0:T(8,128)(2,1)S(1)} %add_convert_fusion.1), channel_id=1, source_target_pairs={{0,6},{2,4},{4,2},{6,0},{1,7},{3,5},{5,3},{7,1},{8,14},{10,12},{12... | collective-permute-start | bytes 497672 | tf_op jit(solution)/shard_map/ppermute | solution.py:181
  173.9 11.1 %collective-permute-start.16 = (bf16[432,192]{1,0:T(8,128)(2,1)S(1)}, bf16[432,192]{1,0:T(8,128)(2,1)S(1)}, u32[]{:S(2)}, u32[]{:S(2)}) collective-permute-start(bf16[432,192]{1,0:T(8,128)(2,1)S(1)} %add_convert_fusion.1), channel_id=1, source_target_pairs={{0,4},{2,6},{4,0},{6,2},{1,5},{3,7},{5,1},{7,3},{8,12},{10,14},{12... | collective-permute-start | bytes 497672 | tf_op jit(solution)/shard_map/ppermute | solution.py:181
  175.9 10.1 %collective-permute-start.15 = (bf16[432,192]{1,0:T(8,128)(2,1)S(1)}, bf16[432,192]{1,0:T(8,128)(2,1)S(1)}, u32[]{:S(2)}, u32[]{:S(2)}) collective-permute-start(bf16[432,192]{1,0:T(8,128)(2,1)S(1)} %add_convert_fusion.1), channel_id=1, source_target_pairs={{0,2},{2,0},{4,6},{6,4},{1,3},{3,1},{5,7},{7,5},{8,10},{10,8},{12,... | collective-permute-start | bytes 497672 | tf_op jit(solution)/shard_map/ppermute | solution.py:181
  183.3 5.9 %copy-start.12 = (bf16[2,8,2,16,192]{4,3,2,1,0:T(8,128)(2,1)S(1)}, bf16[2,8,2,16,192]{4,3,2,1,0:T(8,128)(2,1)}, u32[]{:S(2)}) copy-start(bf16[2,8,2,16,192]{4,3,2,1,0:T(8,128)(2,1)} %copy-done.9) | copy-start | bytes 589828
  183.3 5.9 %copy-start.15 = (bf16[2,8,2,16,192]{4,3,2,1,0:T(8,128)(2,1)S(1)}, bf16[2,8,2,16,192]{4,3,2,1,0:T(8,128)(2,1)}, u32[]{:S(2)}) copy-start(bf16[2,8,2,16,192]{4,3,2,1,0:T(8,128)(2,1)} %copy-done.13) | copy-start | bytes 589828
  183.3 5.9 %copy-start.16 = (bf16[9,192,192]{2,1,0:T(8,128)(2,1)S(1)}, bf16[9,192,192]{2,1,0:T(8,128)(2,1)}, u32[]{:S(2)}) copy-start(bf16[9,192,192]{2,1,0:T(8,128)(2,1)} %refs_8_.1) | copy-start | bytes 1990660
  183.3 22.5 %collective-permute-start.29 = (bf16[4,432,192]{1,2,0:T(8,128)(2,1)}, bf16[4,432,192]{1,2,0:T(8,128)(2,1)}, u32[]{:S(2)}, u32[]{:S(2)}) collective-permute-start(bf16[4,432,192]{1,2,0:T(8,128)(2,1)} %copy.50), channel_id=1, source_target_pairs={{0,1},{1,0},{2,3},{3,2},{4,5},{5,4},{6,7},{7,6},{8,9},{9,8},{10,11... | collective-permute-start | bytes 1990664 | tf_op jit(solution)/shard_map/ppermute | solution.py:181
  183.8 2.2 %copy-start.34 = (bf16[432,192]{1,0:T(8,128)(2,1)}, bf16[432,192]{1,0:T(8,128)(2,1)S(1)}, u32[]{:S(2)}) copy-start(bf16[432,192]{1,0:T(8,128)(2,1)S(1)} %collective-permute-done.17) | copy-start | bytes 497668
  189.2 20.6 %collective-permute-start.18 = (bf16[4,432,192]{1,2,0:T(8,128)(2,1)}, bf16[4,432,192]{1,2,0:T(8,128)(2,1)}, u32[]{:S(2)}, u32[]{:S(2)}) collective-permute-start(bf16[4,432,192]{1,2,0:T(8,128)(2,1)} %copy.41), channel_id=1, source_target_pairs={{0,1},{1,0},{2,3},{3,2},{4,5},{5,4},{6,7},{7,6},{8,9},{9,8},{10,11... | collective-permute-start | bytes 1990664 | tf_op jit(solution)/shard_map/ppermute | solution.py:181
  192.7 12.3 %all-to-all-start.3 = ((bf16[8,2,2,32,192]{4,3,2,1,0:T(8,128)(2,1)}), bf16[8,2,2,32,192]{4,3,2,1,0:T(8,128)(2,1)S(1)}, u32[]{:S(2)}, u32[]{:S(2)}) async-start(bf16[8,2,2,32,192]{4,3,2,1,0:T(8,128)(2,1)} %bitcast.15), calls=%async_computation.3 | async-start | bytes 1048576 | tf_op jit(solution)/shard_map/all_to_all | solution.py:168
  (9 other events, 8.9 us)

commit v2 on v1

v2 whole, which is shorter than its diff:
```python
import jax
import jax.numpy as jnp
from jax import lax
from jax.experimental import pallas as pl
from jax.experimental.pallas import tpu as pltpu
from jax.sharding import Mesh
from jax.sharding import PartitionSpec as P


F32 = jnp.float32
BF16 = jnp.bfloat16
STRIDE = 16
TAPS = [(r, c) for r in (-1, 0, 1) for c in (-1, 0, 1)]
PLANE = ("x", "y", "c")
VMEM_LIMIT = 16 * 1024 * 1024


def call(body, outs, scratch, flops, *args):
    specs, arrays, size = [], [], 0
    for arg in args:
        if isinstance(arg, tuple):
            arg, member = arg
            shape = arg.shape[:3] + (None,) + arg.shape[4:]
            specs.append(pl.BlockSpec(shape, lambda step, member=member: (0, 0, 0, member, 0, 0, 0, 0, 0)))
            size += arg.size // arg.shape[3] * arg.dtype.itemsize
        else:
            specs.append(pl.BlockSpec(memory_space=pltpu.VMEM))
            size += arg.size * arg.dtype.itemsize
        arrays.append(arg)
    size += sum(o.size * o.dtype.itemsize for o in outs)
    return pl.pallas_call(
        body,
        grid=(1,),
        out_shape=outs,
        in_specs=specs,
        out_specs=[pl.BlockSpec(memory_space=pltpu.VMEM)] * len(outs),
        scratch_shapes=scratch,
        compiler_params=pltpu.CompilerParams(vmem_limit_bytes=VMEM_LIMIT),
        cost_estimate=pl.CostEstimate(flops=flops, bytes_accessed=size, transcendentals=0),
    )(*arrays)


def class_column(ref, col):
    part = ref[col // 2, :, :, :, :, col % 2] if len(ref.shape) == 8 else ref[:, :, :, :, col]
    return part.reshape((8, 2) + part.shape[-2:])


def class_flat(ref):
    cols = [class_column(ref, col) for col in range(4)]
    chan = cols[0].shape[-1]
    return jnp.concatenate([col.reshape(-1, chan) for col in cols], 0)


def fill(padded, pieces, step):
    rows = padded.shape[1] - 2 * step
    edge = jnp.zeros(padded.shape[:1] + (step,) + padded.shape[2:], BF16)
    padded[:, :step] = edge
    padded[:, step + rows :] = edge
    at = 0
    for ref in pieces:
        if len(ref.shape) > 5:
            for col in range(4 if len(ref.shape) == 8 else 2):
                padded[at, step : step + rows] = class_column(ref, col)
                at += 1
        else:
            padded[at : at + ref.shape[0], step : step + rows] = ref[...]
            at += ref.shape[0]


def window(padded, tap, step):
    r, c = tap
    top, left = step - r * step, step - c * step
    part = padded[left : left + 4, top : top + 8]
    return part.reshape(-1, part.shape[-1])


def pulled(padded, weights, step):
    total = None
    for k, tap in enumerate(TAPS):
        term = lax.dot_general(
            window(padded, tap, step), weights[k], (((1,), (1,)), ((), ())), preferred_element_type=F32
        )
        total = term if total is None else total + term
    return total


def store(refs, value):
    value = value.astype(BF16)
    at = 0
    for ref in refs:
        if len(ref.shape) == 8:
            cols = value.reshape((4, 2, 2, 2, 2) + ref.shape[-2:])
            for col in range(4):
                ref[col // 2, :, :, :, :, col % 2] = cols[col]
        else:
            size = ref.size // ref.shape[-1]
            ref[...] = value[at : at + size].reshape(ref.shape)
            at += size


def flat(refs):
    if len(refs) == 1:
        return class_flat(refs[0])
    return jnp.concatenate([ref[...].reshape(-1, ref.shape[-1]) for ref in refs], 0)


def conv_two(field, act, weights, step, outs):
    n = len(field)

    def body(*refs):
        pieces, act_ref, w_ref = refs[:n], refs[n], refs[n + 1]
        out_refs, padded = refs[n + 2 : -1], refs[-1]
        fill(padded, pieces, step)
        grad = pulled(padded, w_ref, step)
        pre = class_flat(act_ref).astype(F32)
        sigma = jax.nn.sigmoid(pre)
        store(out_refs, grad * sigma * (1.0 + pre * (1.0 - sigma)))

    chan = weights.shape[-1]
    return call(body, outs, [padded_shape(chan, step)], conv_flops(chan), *field, act, weights)


def conv_one(field, base, weights, step, outs):
    n, b = len(field), len(base)

    def body(*refs):
        pieces, base_refs, w_ref = refs[:n], refs[n : n + b], refs[n + b]
        out_refs, padded = refs[n + b + 1 : -1], refs[-1]
        fill(padded, pieces, step)
        grad = pulled(padded, w_ref, step)
        store(out_refs, flat(base_refs).astype(F32) + grad)

    chan = weights.shape[-1]
    return call(body, outs, [padded_shape(chan, step)], conv_flops(chan), *field, *base, weights)


def tap_products(pieces, src_ref, active, step, padded, out_ref):
    fill(padded, pieces, step)
    src = class_flat(src_ref)
    chan = src.shape[-1]
    if active:
        pre = src.astype(F32)
        src = (pre * jax.nn.sigmoid(pre)).astype(BF16)
    turned = src.T
    for k, tap in enumerate(TAPS):
        out_ref[k * chan : (k + 1) * chan] = jnp.dot(
            turned, window(padded, tap, step), preferred_element_type=F32
        )
    used = len(TAPS) * chan
    out_ref[used:] = jnp.zeros((out_ref.shape[0] - used, chan), F32)


def padded_rows(chan):
    return -(-len(TAPS) * chan // 256) * 256


def weight_grad(field, source, step, chan):
    n = len(field)

    def body(*refs):
        tap_products(refs[:n], refs[n], True, step, refs[n + 2], refs[n + 1])

    out = [jax.ShapeDtypeStruct((padded_rows(chan), chan), F32)]
    return call(body, out, [padded_shape(chan, step)], conv_flops(chan), *field, source)[0]


def weight_grad_split(field, source, step, chan, other):
    n = len(field)

    def body(*refs):
        other_ref, keep_ref, give_ref, padded, total = refs[n + 1 :]
        tap_products(refs[:n], refs[n], False, step, padded, total)
        core = lax.axis_index("c")

        @pl.when(core == 0)
        def _():
            keep_ref[...] = other_ref[...]
            give_ref[...] = total[...].astype(BF16)

        @pl.when(core != 0)
        def _():
            keep_ref[...] = total[...]
            give_ref[...] = other_ref[...].astype(BF16)

    shape = (padded_rows(chan), chan)
    outs = [jax.ShapeDtypeStruct(shape, F32), jax.ShapeDtypeStruct(shape, BF16)]
    scratch = [padded_shape(chan, step), pltpu.VMEM(shape, F32)]
    keep, give = call(body, outs, scratch, conv_flops(chan), *field, source, other)
    parts = (4, 4, shape[0] // 16, chan)
    return keep.reshape(parts), xor(give, "c", 1).reshape(parts)


def conv_flops(chan):
    return 2 * len(TAPS) * 1024 * chan * chan


def padded_shape(chan, step):
    return pltpu.VMEM((4 + 2 * step, 8 + 2 * step, 2, STRIDE, chan), BF16)


def coarse(cols, chan):
    return jax.ShapeDtypeStruct((cols, 8, 2, STRIDE, chan), BF16)


def pack_classes(*values):
    height, breadth, chan = values[0].shape
    group = lax.axis_size(PLANE)
    n = len(values)

    def body(*refs):
        out_ref = refs[-1]
        size = STRIDE // group
        for i in range(n):
            for target in range(group):
                for ih in range(height // STRIDE):
                    at = ih * STRIDE + target * size
                    out_ref[target, i, ih] = refs[i][at : at + size].reshape(out_ref.shape[3:])

    shape = (group, n, height // STRIDE, STRIDE // group, breadth // STRIDE, STRIDE, chan)
    return call(body, [jax.ShapeDtypeStruct(shape, BF16)], [], 0, *values)[0]


def swap_classes(packed):
    moved = lax.all_to_all(packed, PLANE, 0, 0)
    return moved.reshape((2, 2, 2) + moved.shape[1:])


def gather_classes(value, height, breadth):
    chan = value.shape[-1]
    group = lax.axis_size(PLANE)
    parts = value.reshape((group,) + value.shape[3:])
    parts = lax.all_to_all(parts, PLANE, 0, 0)
    return parts.transpose(1, 0, 2, 3, 4, 5).reshape(height, breadth, chan)


def ring(left_edge, right_edge):
    count = lax.axis_size("z")
    up = [(i, (i + 1) % count) for i in range(count)]
    down = [(b, a) for a, b in up]
    return lax.ppermute(right_edge, "z", up), lax.ppermute(left_edge, "z", down)


def xor(value, axis, k):
    count = lax.axis_size(axis)
    return lax.ppermute(value, axis, [(i, i ^ k) for i in range(count)])


def quarter():
    return 2 * lax.axis_index("x") + lax.axis_index("y")


def sum_plane(keep, got):
    part = keep.shape[1:]

    def body(keep_ref, got_ref, own_ref, *sent_refs):
        for k in range(4):
            at = quarter() ^ k
            total = keep_ref[at] + got_ref[at].astype(F32)
            if k == 0:
                own_ref[...] = total
            else:
                sent_refs[k - 1][...] = total.astype(BF16)

    outs = [jax.ShapeDtypeStruct(part, F32)] + [jax.ShapeDtypeStruct(part, BF16)] * 3
    own, *sent = call(body, outs, [], 0, keep, got)
    return own, [xor(value, ("x", "y"), k + 1) for k, value in enumerate(sent)]


def sum_ring(own, terms):
    count = lax.axis_size("z")
    part = own.shape
    if count != 4:
        total = own + sum(term.astype(F32) for term in terms)
        k = 1
        while k < count:
            total = total.astype(BF16)
            total = total.astype(F32) + xor(total, "z", k).astype(F32)
            k = 2 * k
        return total.astype(BF16)

    def body(own_ref, *refs):
        term_refs, mine_ref, sent_refs = refs[:3], refs[3], refs[4:]
        for k in range(4):
            at = lax.axis_index("z") ^ k
            total = own_ref[at]
            for ref in term_refs:
                total = total + ref[at].astype(F32)
            if k == 0:
                mine_ref[...] = total
            else:
                sent_refs[k - 1][...] = total.astype(BF16)

    outs = [jax.ShapeDtypeStruct(part[1:], F32)] + [jax.ShapeDtypeStruct(part[1:], BF16)] * 3
    mine, *sent = call(body, outs, [], 0, own, *terms)
    for k, value in enumerate(sent):
        mine = mine + xor(value, "z", k + 1).astype(F32)
    mine = mine.astype(BF16)
    spread = [mine] + [xor(mine, "z", k) for k in (1, 2, 3)]

    def join(*refs):
        for k in range(4):
            refs[4][lax.axis_index("z") ^ k] = refs[k][...]

    return call(join, [jax.ShapeDtypeStruct(part, BF16)], [], 0, *spread)[0]


def spread_weights(part, taps):
    quarters = [part] + [xor(part, ("x", "y"), k) for k in (1, 2, 3)]
    others = [xor(value, "c", 1) for value in quarters]
    chan = part.shape[-1]
    used = taps * chan

    def body(*refs):
        own_refs, other_refs, first_ref, second_ref = refs[:4], refs[4:8], refs[8], refs[9]

        def put(out_ref, part_refs):
            for k, ref in enumerate(part_refs):
                value = ref[...].astype(F32).reshape(-1, chan)
                rows = value.shape[0]
                at = quarter() ^ k

                @pl.when(at < 3)
                def _():
                    out_ref[pl.ds(pl.multiple_of(at * rows, 16), rows)] = value

                @pl.when(at == 3)
                def _():
                    out_ref[3 * rows :] = value[: used - 3 * rows]

        core = lax.axis_index("c")

        @pl.when(core == 0)
        def _():
            put(first_ref, own_refs)
            put(second_ref, other_refs)

        @pl.when(core != 0)
        def _():
            put(first_ref, other_refs)
            put(second_ref, own_refs)

    outs = [jax.ShapeDtypeStruct((used, chan), F32)] * 2
    one, two = call(body, outs, [], 0, *quarters, *others)
    return one.reshape(taps, chan, chan), two.reshape(taps, chan, chan)


def sum_weights(keep, give):
    part = sum_ring(*sum_plane(keep, give))
    return spread_weights(part, len(TAPS))


def local(
    first_block_input,
    first_block_preactivation,
    second_block_input,
    second_block_preactivation,
    output_gradient_final,
    first_block_conv_one,
    first_block_conv_two,
    second_block_conv_one,
    second_block_conv_two,
):
    height, breadth, chan = output_gradient_final.shape
    final = swap_classes(pack_classes(output_gradient_final))
    low, high = ring(final[0, :, :, 0], final[1, :, :, 0])
    act_two = pack_classes(second_block_preactivation)
    late = pack_classes(first_block_preactivation, second_block_input, first_block_input)
    final, act_two = lax.optimization_barrier((final, act_two))
    act_two = swap_classes(act_two)
    final, act_two = (final, 0), (act_two, 0)

    halves = [coarse(2, chan)] * 2
    thirds = [coarse(1, chan), coarse(2, chan), coarse(1, chan)]

    wide = [low, final, high]
    pre = conv_two(wide, act_two, second_block_conv_two, 2, halves)
    late, pre = lax.optimization_barrier((late, pre))
    late = swap_classes(late)
    act_one, entry_two, entry_one = (late, 0), (late, 1), (late, 2)
    low, high = ring(pre[0], pre[1])
    second_two = weight_grad(wide, act_two, 2, chan)
    low, high, second_two = lax.optimization_barrier((low, high, second_two))
    wide = [low, *pre, high]
    mid = conv_one(wide, [final], second_block_conv_one, 2, thirds)
    low, high = ring(mid[0], mid[2])
    keep, got = weight_grad_split(wide, entry_two, 2, chan, second_two)
    low, high, keep = lax.optimization_barrier((low, high, keep))
    second = keep, got
    wide = [low, *mid, high]
    pre = conv_two(wide, act_one, first_block_conv_two, 1, thirds)
    low, high = ring(pre[0], pre[2])
    first_two = weight_grad(wide, act_one, 1, chan)
    low, high, first_two = lax.optimization_barrier((low, high, first_two))
    wide = [low, *pre, high]
    whole = [jax.ShapeDtypeStruct((2, 2, 2, 2, 2, 2, STRIDE, chan), BF16)]
    out = conv_one(wide, mid, first_block_conv_one, 1, whole)[0]
    out, wide[0] = lax.optimization_barrier((out, wide[0]))
    first = weight_grad_split(wide, entry_one, 1, chan, first_two)
    out = gather_classes(out, height, breadth)
    second_two, second_one = sum_weights(*second)
    own, terms = sum_plane(*first)
    out, terms = lax.optimization_barrier((out, terms))
    first_two, first_one = spread_weights(sum_ring(own, terms), len(TAPS))
    return out, first_one, first_two, second_one, second_two


def solution(mesh):
    lon, lat = mesh.shape["lon"], mesh.shape["lat"]
    split = Mesh(mesh.devices.reshape(lon // 2, 2, lat // 2, 2), ("z", "x", "y", "c"))
    grid = P(("y", "c"), ("z", "x"), None)
    return jax.shard_map(
        local,
        mesh=split,
        in_specs=(grid,) * 5 + (P(),) * 4,
        out_specs=(grid, P(), P(), P(), P()),
        check_vma=False,
    )
```

time: 215 us -> 175 us (0.81)
  waiting for transfers between devices: 69.4 us -> 54.1 us
  other arithmetic: 14.7 us -> 0.94 us
  local copies, waits for them, and re-layouts: 36.3 us -> 26.5 us
  starting transfers between devices: 69.1 us -> 62.7 us
  Pallas kernels: 23 us -> 28.4 us
    all_to_all x1, waiting for transfers between devices: 8.68 us -> 0.01 us  [gather_classes(): parts = lax.all_to_all(parts, PLANE, 0, 0)]
    convert_element_type x8 -> x2, other arithmetic: 9.34 us -> 0.94 us  [sum_ring(): mine = mine.astype(BF16)]
    all_to_all x5 -> x3, starting transfers between devices: 20.6 us -> 12.5 us  [swap_classes(): moved = lax.all_to_all(packed, PLANE, 0, 0)]
    unnamed x74 -> x78, local copies, waits for them, and re-layouts: 9.41 us -> 17.4 us
    all_to_all x5 -> x3, waiting for transfers between devices: 15.9 us -> 7.98 us  [swap_classes(): moved = lax.all_to_all(packed, PLANE, 0, 0)]
    dynamic_slice x12 -> x0, local copies, waits for them, and re-layouts: 7.48 us -> none  [the longest x8 4.57 us: sum_weights(): lax.dynamic_index_in_dim(sent, mine ^ k, 0, keepdims=False)]
    pallas_call x10 -> x19, Pallas kernels: 23 us -> 28.4 us  [call(): pl.pallas_call(body, grid=(1,), out_shape=outs, in_specs=specs, out_specs...]
    reshape x7 -> x0, local copies, waits for them, and re-layouts: 5.33 us -> none  [the longest x5 5.29 us: scatter_classes(): value.reshape(2, group, STRIDE // group, breadth, chan)]
  transfers between devices with their start and end apart: 36 -> 46, of which waited for: 20 -> 19; matrix products, arithmetic and copies ran while one was open for 18% -> 6% of each run, Pallas kernels for 10% -> 12%
where the time goes in v2:
time: 175 us; the launch traced here: 174 us
  starting transfers between devices  62.7 us (36%)
  waiting for transfers between devices  54.1 us (31%)
  Pallas kernels  28.4 us (16%)
  local copies, waits for them, and re-layouts  26.5 us (15%)
    ppermute x34, starting transfers between devices, xor(): return lax.ppermute(value, axis, [(i, i ^ k) for i in range(count)])  30.6 us
    ppermute x34, waiting for transfers between devices, xor(): return lax.ppermute(value, axis, [(i, i ^ k) for i in range(count)])  29 us
    pallas_call x19, Pallas kernels, call(): pl.pallas_call(body, grid=(1,), out_shape=outs, in_specs=specs, out_specs...  28.4 us
    unnamed x78, local copies, waits for them, and re-layouts  17.4 us
    all_to_all x3, starting transfers between devices, swap_classes(): moved = lax.all_to_all(packed, PLANE, 0, 0)  12.5 us
    ppermute x4, starting transfers between devices, ring(): lax.ppermute(left_edge, 'z', down)  10.8 us
    ppermute x4, waiting for transfers between devices, ring(): lax.ppermute(left_edge, 'z', down)  9.01 us
    ppermute x4, waiting for transfers between devices, ring(): lax.ppermute(right_edge, 'z', up)  8.06 us
  transfers between devices with their start and end apart: 46, of which 19 were waited for; matrix products, arithmetic and copies ran while one was open for 6% of the time, Pallas kernels for 12%

profile of v2, /device:TPU:0, one launch (start us, length us, event | category | flops | bytes accessed | tf_op | source)
XLA Modules:
  0.0 173.6 jit_solution(3593315537594366447)
XLA Ops:
  0.6 1.0 copy-done.16
  2.5 5.2 %all-to-all-start = ((bf16[8,1,2,2,2,16,192]{6,5,4,3,2,1,0:T(8,128)(2,1)}), bf16[8,1,2,2,2,16,192]{6,5,4,3,2,1,0:T(8,128)(2,1)S(1)}, u32[]{:S(2)}, u32[]{:S(2)}) async-start(bf16[8,1,2,2,2,16,192]{6,5,4,3,2,1,0:T(8,128)(2,1)} %shard_map.129), calls=%async_computation | async-start | bytes 1048576 | tf_op jit(solution)/shard_map/all_to_all | solution.py:224
  8.5 8.0 %all-to-all-done = bf16[8,1,2,2,2,16,192]{6,5,4,3,2,1,0:T(8,128)(2,1)S(1)} async-done(((bf16[8,1,2,2,2,16,192]{6,5,4,3,2,1,0:T(8,128)(2,1)}), bf16[8,1,2,2,2,16,192]{6,5,4,3,2,1,0:T(8,128)(2,1)S(1)}, u32[]{:S(2)}, u32[]{:S(2)}) %all-to-all-start) | async-done | bytes 393248 | tf_op jit(solution)/shard_map/all_to_all | solution.py:224
  16.5 3.5 %all-to-all-start.1 = ((bf16[8,1,2,2,2,16,192]{6,5,4,3,2,1,0:T(8,128)(2,1)}), bf16[8,1,2,2,2,16,192]{6,5,4,3,2,1,0:T(8,128)(2,1)S(1)}, u32[]{:S(2)}, u32[]{:S(2)}) async-start(bf16[8,1,2,2,2,16,192]{6,5,4,3,2,1,0:T(8,128)(2,1)} %shard_map.130), calls=%async_computation.1 | async-start | bytes 1048576 | tf_op jit(solution)/shard_map/all_to_all | solution.py:224
  20.1 1.6 collective-permute-start
  21.7 2.2 %collective-permute-start.1 = (bf16[2,2,2,2,2,16,192]{6,5,4,3,2,1,0:T(8,128)(2,1)S(1)}, bf16[2,2,2,2,2,16,192]{6,5,4,3,2,1,0:T(8,128)(2,1)S(1)}, u32[]{:S(2)}, u32[]{:S(2)}) collective-permute-start(bf16[2,2,2,2,2,16,192]{6,5,4,3,2,1,0:T(8,128)(2,1)S(1)} %bitcast.30), channel_id=1, source_target_pairs={{8,0},{16,8},{24,16},{0,24},{9,1},{17,9},{25,17},{1,25},{10,2},{18... | collective-permute-start | bytes 589832 | tf_op jit(solution)/shard_map/ppermute | solution.py:240
  24.0 1.2 shard_map.128
  25.2 5.9 %collective-permute-done.refs_0_ = bf16[2,2,2,2,2,16,192]{6,5,4,3,2,1,0:T(8,128)(2,1)S(1)} collective-permute-done((bf16[2,2,2,2,2,16,192]{6,5,4,3,2,1,0:T(8,128)(2,1)S(1)}, bf16[2,2,2,2,2,16,192]{6,5,4,3,2,1,0:T(8,128)(2,1)S(1)}, u32[]{:S(2)}, u32[]{:S(2)}) %collective-permute-start) | collective-permute-done | bytes 196640 | tf_op jit(solution)/shard_map/ppermute | solution.py:240
  31.1 4.6 %collective-permute-done.1.refs_2_ = bf16[2,2,2,2,2,16,192]{6,5,4,3,2,1,0:T(8,128)(2,1)S(1)} collective-permute-done((bf16[2,2,2,2,2,16,192]{6,5,4,3,2,1,0:T(8,128)(2,1)S(1)}, bf16[2,2,2,2,2,16,192]{6,5,4,3,2,1,0:T(8,128)(2,1)S(1)}, u32[]{:S(2)}, u32[]{:S(2)}) %collective-permute-start.1) | collective-permute-done | bytes 196640 | tf_op jit(solution)/shard_map/ppermute | solution.py:240
  35.7 1.4 copy-done.37
  37.1 2.2 %shard_map.131 = (bf16[2,8,2,16,192]{4,3,2,1,0:T(8,128)(2,1)}, bf16[2,8,2,16,192]{4,3,2,1,0:T(8,128)(2,1)}) custom-call(bf16[2,2,2,2,2,16,192]{6,5,4,3,2,1,0:T(8,128)(2,1)S(1)} %collective-permute-done.refs_0_, bf16[2,2,2,1,2,2,2,16,192]{8,7,6,5,4,3,2,1,0:T(8,128)(2,1)S(1)} %bitcast.20, ...), custom_call_target="tpu_custom_call" | custom-call | flops 679477248 | bytes 2236416 | tf_op jit(solution)/shard_map/pallas_call | solution.py:31
  39.3 3.9 %all-to-all-start.2 = ((bf16[8,3,2,2,2,16,192]{6,5,4,3,2,1,0:T(8,128)(2,1)}), bf16[8,3,2,2,2,16,192]{6,5,4,3,2,1,0:T(8,128)(2,1)S(1)}, u32[]{:S(2)}, u32[]{:S(2)}) async-start(bf16[8,3,2,2,2,16,192]{6,5,4,3,2,1,0:T(8,128)(2,1)} %shard_map.128), calls=%async_computation.2 | async-start | bytes 3145728 | tf_op jit(solution)/shard_map/all_to_all | solution.py:224
  43.2 1.1 collective-permute-start.2
  44.3 2.7 %collective-permute-start.3 = (bf16[2,8,2,16,192]{4,3,2,1,0:T(8,128)(2,1)}, bf16[2,8,2,16,192]{4,3,2,1,0:T(8,128)(2,1)S(1)}, u32[]{:S(2)}, u32[]{:S(2)}) collective-permute-start(bf16[2,8,2,16,192]{4,3,2,1,0:T(8,128)(2,1)} %get-tuple-element.62.refs_1_), channel_id=1, source_target_pairs={{8,0},{16,8},{24,16},{0,24},{9,1},{17,9},{25,17},{1,25},{10,2},{18... | collective-permute-start | bytes 589832 | tf_op jit(solution)/shard_map/ppermute | solution.py:240
  47.0 1.0 copy-done.1
  48.1 1.0 copy-done.7
  49.1 0.9 copy-done.34
  50.1 0.9 copy-done.36
  51.0 1.3 shard_map.132.refs_5_
  52.3 2.1 %collective-permute-done.2.refs_0_ = bf16[2,8,2,16,192]{4,3,2,1,0:T(8,128)(2,1)S(1)} collective-permute-done((bf16[2,8,2,16,192]{4,3,2,1,0:T(8,128)(2,1)}, bf16[2,8,2,16,192]{4,3,2,1,0:T(8,128)(2,1)S(1)}, u32[]{:S(2)}, u32[]{:S(2)}) %collective-permute-start.2) | collective-permute-done | bytes 196640 | tf_op jit(solution)/shard_map/ppermute | solution.py:240
  54.4 4.2 %collective-permute-done.3.refs_3_ = bf16[2,8,2,16,192]{4,3,2,1,0:T(8,128)(2,1)S(1)} collective-permute-done((bf16[2,8,2,16,192]{4,3,2,1,0:T(8,128)(2,1)}, bf16[2,8,2,16,192]{4,3,2,1,0:T(8,128)(2,1)S(1)}, u32[]{:S(2)}, u32[]{:S(2)}) %collective-permute-start.3) | collective-permute-done | bytes 196640 | tf_op jit(solution)/shard_map/ppermute | solution.py:240
  58.6 3.2 %shard_map.133 = (bf16[1,8,2,16,192]{4,3,2,1,0:T(8,128)(2,1)S(1)}, bf16[2,8,2,16,192]{4,3,2,1,0:T(8,128)(2,1)S(1)}, bf16[1,8,2,16,192]{4,3,2,1,0:T(8,128)(2,1)}) custom-call(bf16[2,8,2,16,192]{4,3,2,1,0:T(8,128)(2,1)S(1)} %collective-permute-done.2.refs_0_, bf16[2,8,2,16,192]{4,3,2,1,0:T(8,128)(2,1)} %get-tuple-element.62.refs_1_, ...), custom_call_target="tpu_custom_call" | custom-call | flops 679477248 | bytes 2236416 | tf_op jit(solution)/shard_map/pallas_call | solution.py:31
  63.3 3.0 %collective-permute-start.5 = (bf16[1,8,2,16,192]{4,3,2,1,0:T(8,128)(2,1)S(1)}, bf16[1,8,2,16,192]{4,3,2,1,0:T(8,128)(2,1)}, u32[]{:S(2)}, u32[]{:S(2)}) collective-permute-start(bf16[1,8,2,16,192]{4,3,2,1,0:T(8,128)(2,1)S(1)} %get-tuple-element.66.refs_1_.refs_5_), channel_id=1, source_target_pairs={{8,0},{16,8},{24,16},{0,24},{9,1},{17,9},{25,17},{1,25},{10,2},{18... | collective-permute-start | bytes 294920 | tf_op jit(solution)/shard_map/ppermute | solution.py:240
  66.3 0.9 copy-done.30
  67.3 0.9 copy-done.32
  68.2 2.5 %shard_map.134 = (f32[1792,192]{1,0:T(8,128)S(1)}, bf16[1792,192]{1,0:T(8,128)(2,1)S(1)}) custom-call(bf16[2,8,2,16,192]{4,3,2,1,0:T(8,128)(2,1)S(1)} %copy-done.30, bf16[2,8,2,16,192]{4,3,2,1,0:T(8,128)(2,1)} %get-tuple-element.62.refs_1_, bf16[2,8,2,16,192]{4,3,2,1,0:T(8,128)(2,1)} %get-tuple-element.61.refs_2_, ...), custom_call_target="tpu_custom_call" | custom-call | flops 679477248 | bytes 4620288 | tf_op jit(solution)/shard_map/pallas_call | solution.py:31
  70.9 3.0 %shard_map.135 = (bf16[1,8,2,16,192]{4,3,2,1,0:T(8,128)(2,1)S(1)}, bf16[2,8,2,16,192]{4,3,2,1,0:T(8,128)(2,1)S(1)}, bf16[1,8,2,16,192]{4,3,2,1,0:T(8,128)(2,1)S(1)}) custom-call(bf16[1,8,2,16,192]{4,3,2,1,0:T(8,128)(2,1)} %collective-permute-done.4.refs_0_, bf16[1,8,2,16,192]{4,3,2,1,0:T(8,128)(2,1)S(1)} %get-tuple-element.66.refs_1_.refs_5_, ...), custom_call_target="tpu_custom_call" | custom-call | flops 679477248 | bytes 2039808 | tf_op jit(solution)/shard_map/pallas_call | solution.py:31
  74.0 1.1 collective-permute-start.6
  75.1 2.8 %collective-permute-start.7 = (bf16[1,8,2,16,192]{4,3,2,1,0:T(8,128)(2,1)S(1)}, bf16[1,8,2,16,192]{4,3,2,1,0:T(8,128)(2,1)S(1)}, u32[]{:S(2)}, u32[]{:S(2)}) collective-permute-start(bf16[1,8,2,16,192]{4,3,2,1,0:T(8,128)(2,1)S(1)} %get-tuple-element.74.refs_1_), channel_id=1, source_target_pairs={{8,0},{16,8},{24,16},{0,24},{9,1},{17,9},{25,17},{1,25},{10,2},{18... | collective-permute-start | bytes 294920 | tf_op jit(solution)/shard_map/ppermute | solution.py:240
  77.9 2.1 %copy.18 = bf16[1792,192]{0,1:T(8,128)(2,1)} copy(bf16[1792,192]{1,0:T(8,128)(2,1)} %copy-done.12) | data formatting | bytes 1376256 | tf_op jit(solution)/shard_map/pallas_call | solution.py:31
  80.0 2.4 %shard_map.136.refs_6_ = f32[1792,192]{1,0:T(8,128)S(1)} custom-call(bf16[1,8,2,16,192]{4,3,2,1,0:T(8,128)(2,1)} %collective-permute-done.4.refs_0_, bf16[1,8,2,16,192]{4,3,2,1,0:T(8,128)(2,1)S(1)} %get-tuple-element.66.refs_1_.refs_5_, bf16[2,8,2,16,192]{4,3,2,1,0:T(8,128)(2,1)S(1)} %copy-done.5, ...), custom_call_target="tpu_custom_call" | custom-call | flops 679477248 | bytes 2359296 | tf_op jit(solution)/shard_map/pallas_call | solution.py:31
  82.6 3.1 %shard_map.137 = bf16[2,2,2,2,2,2,16,192]{7,6,5,4,3,2,1,0:T(8,128)(2,1)} custom-call(bf16[1,8,2,16,192]{4,3,2,1,0:T(8,128)(2,1)S(1)} %collective-permute-done.6.refs_0_, bf16[1,8,2,16,192]{4,3,2,1,0:T(8,128)(2,1)S(1)} %get-tuple-element.74.refs_1_, bf16[2,8,2,16,192]{4,3,2,1,0:T(8,128)(2,1)S(1)} %get-tuple-element.76.refs_2_, ...), custom_call_target="tpu_custom_call" | custom-call | flops 679477248 | bytes 2039808 | tf_op jit(solution)/shard_map/pallas_call | solution.py:31
  87.0 0.9 copy-done.11
  91.5 1.5 shard_map.138
  94.0 2.1 %copy.16 = bf16[1792,192]{0,1:T(8,128)(2,1)} copy(bf16[1792,192]{1,0:T(8,128)(2,1)} %copy-done.13) | data formatting | bytes 1376256 | tf_op jit(solution)/shard_map/pallas_call | solution.py:31
  96.5 1.4 copy.19
  97.9 1.5 copy-done.9
  100.4 1.6 collective-permute-start.26
  102.0 1.5 collective-permute-start.27
  103.8 4.1 %all-to-all-start.3 = ((bf16[8,2,2,2,16,192]{5,4,3,2,1,0:T(8,128)(2,1)}), bf16[8,2,2,2,16,192]{5,4,3,2,1,0:T(8,128)(2,1)}, u32[]{:S(2)}, u32[]{:S(2)}) async-start(bf16[8,2,2,2,16,192]{5,4,3,2,1,0:T(8,128)(2,1)} %bitcast.6), calls=%async_computation.3 | async-start | bytes 1048576 | tf_op jit(solution)/shard_map/all_to_all | solution.py:232
  108.2 2.4 %collective-permute-done.27.refs_1_ = bf16[4,112,192]{2,1,0:T(8,128)(2,1)S(1)} collective-permute-done((bf16[4,112,192]{2,1,0:T(8,128)(2,1)}, bf16[4,112,192]{2,1,0:T(8,128)(2,1)S(1)}, u32[]{:S(2)}, u32[]{:S(2)}) %collective-permute-start.27) | collective-permute-done | bytes 172064 | tf_op jit(solution)/shard_map/ppermute | solution.py:245
  110.7 4.8 %collective-permute-done.28.refs_2_ = bf16[4,112,192]{2,1,0:T(8,128)(2,1)S(1)} collective-permute-done((bf16[4,112,192]{2,1,0:T(8,128)(2,1)}, bf16[4,112,192]{2,1,0:T(8,128)(2,1)S(1)}, u32[]{:S(2)}, u32[]{:S(2)}) %collective-permute-start.28) | collective-permute-done | bytes 172064 | tf_op jit(solution)/shard_map/ppermute | solution.py:245
  115.7 2.2 %collective-permute-start.30 = (bf16[112,192]{1,0:T(8,128)(2,1)S(1)}, bf16[112,192]{1,0:T(8,128)(2,1)}, u32[]{:S(2)}, u32[]{:S(2)}) collective-permute-start(bf16[112,192]{1,0:T(8,128)(2,1)S(1)} %get-tuple-element.105), channel_id=1, source_target_pairs={{0,16},{8,24},{16,0},{24,8},{1,17},{9,25},{17,1},{25,9},{2,18},{10... | collective-permute-start | bytes 129032 | tf_op jit(solution)/shard_map/ppermute | solution.py:245
  117.9 2.2 %collective-permute-start.31 = (bf16[112,192]{1,0:T(8,128)(2,1)S(1)}, bf16[112,192]{1,0:T(8,128)(2,1)}, u32[]{:S(2)}, u32[]{:S(2)}) collective-permute-start(bf16[112,192]{1,0:T(8,128)(2,1)S(1)} %get-tuple-element.106), channel_id=1, source_target_pairs={{0,24},{8,16},{16,8},{24,0},{1,25},{9,17},{17,9},{25,1},{2,26},{10... | collective-permute-start | bytes 129032 | tf_op jit(solution)/shard_map/ppermute | solution.py:245
  120.1 1.4 copy.17
  121.5 0.9 shard_map.139
  122.5 1.6 collective-permute-start.9
  124.1 1.5 collective-permute-start.10
  126.9 1.7 collective-permute-start.34
  128.6 1.9 %copy.15 = bf16[2,8,2,2,16,192]{5,4,3,2,1,0:T(8,128)(2,1)} copy(bf16[2,8,2,2,16,192]{5,4,3,2,0,1:T(8,128)(2,1)} %bitcast.7) | data formatting | bytes 786432 | tf_op jit(solution)/shard_map/transpose | solution.py:233
  130.9 2.3 %collective-permute-start.32 = (bf16[112,192]{1,0:T(8,128)(2,1)S(1)}, bf16[112,192]{1,0:T(8,128)(2,1)S(1)}, u32[]{:S(2)}, u32[]{:S(2)}) collective-permute-start(bf16[112,192]{1,0:T(8,128)(2,1)S(1)} %add_convert_fusion.refs_0_), channel_id=1, source_target_pairs={{0,8},{8,0},{16,24},{24,16},{1,9},{9,1},{17,25},{25,17},{2,10},{10... | collective-permute-start | bytes 129032 | tf_op jit(solution)/shard_map/ppermute | solution.py:245
  133.5 3.1 %collective-permute-start.13 = (bf16[112,192]{1,0:T(8,128)(2,1)S(1)}, bf16[112,192]{1,0:T(8,128)(2,1)S(1)}, u32[]{:S(2)}, u32[]{:S(2)}) collective-permute-start(bf16[112,192]{1,0:T(8,128)(2,1)S(1)} %get-tuple-element.93), channel_id=1, source_target_pairs={{0,16},{8,24},{16,0},{24,8},{1,17},{9,25},{17,1},{25,9},{2,18},{10... | collective-permute-start | bytes 129032 | tf_op jit(solution)/shard_map/ppermute | solution.py:245
  136.6 1.3 collective-permute-start.14
  138.0 2.5 %collective-permute-start.37 = (bf16[4,112,192]{2,1,0:T(8,128)(2,1)S(1)}, bf16[4,112,192]{2,1,0:T(8,128)(2,1)S(1)}, u32[]{:S(2)}, u32[]{:S(2)}) collective-permute-start(bf16[4,112,192]{2,1,0:T(8,128)(2,1)S(1)} %shard_map.145.refs_0_), channel_id=1, source_target_pairs={{0,6},{2,4},{4,2},{6,0},{1,7},{3,5},{5,3},{7,1},{8,14},{10,12},{12... | collective-permute-start | bytes 516104 | tf_op jit(solution)/shard_map/ppermute | solution.py:245
  141.6 1.0 collective-permute-done.14
  142.6 1.6 collective-permute-start.17
  144.2 4.4 %collective-permute-done.17.refs_3_ = bf16[112,192]{1,0:T(8,128)(2,1)S(1)} collective-permute-done((bf16[112,192]{1,0:T(8,128)(2,1)S(1)}, bf16[112,192]{1,0:T(8,128)(2,1)S(1)}, u32[]{:S(2)}, u32[]{:S(2)}) %collective-permute-start.17) | collective-permute-done | bytes 43040 | tf_op jit(solution)/shard_map/ppermute | solution.py:245
  148.6 5.1 %collective-permute-done.16.refs_2_ = bf16[112,192]{1,0:T(8,128)(2,1)S(1)} collective-permute-done((bf16[112,192]{1,0:T(8,128)(2,1)S(1)}, bf16[112,192]{1,0:T(8,128)(2,1)S(1)}, u32[]{:S(2)}, u32[]{:S(2)}) %collective-permute-start.16) | collective-permute-done | bytes 43040 | tf_op jit(solution)/shard_map/ppermute | solution.py:245
  153.8 4.2 %collective-permute-done.15.refs_1_ = bf16[112,192]{1,0:T(8,128)(2,1)S(1)} collective-permute-done((bf16[112,192]{1,0:T(8,128)(2,1)S(1)}, bf16[112,192]{1,0:T(8,128)(2,1)S(1)}, u32[]{:S(2)}, u32[]{:S(2)}) %collective-permute-start.15) | collective-permute-done | bytes 43040 | tf_op jit(solution)/shard_map/ppermute | solution.py:245
  158.0 2.6 %collective-permute-start.20 = (bf16[4,112,192]{2,1,0:T(8,128)(2,1)S(1)}, bf16[4,112,192]{2,1,0:T(8,128)(2,1)S(1)}, u32[]{:S(2)}, u32[]{:S(2)}) collective-permute-start(bf16[4,112,192]{2,1,0:T(8,128)(2,1)S(1)} %shard_map.141.refs_0_), channel_id=1, source_target_pairs={{0,6},{2,4},{4,2},{6,0},{1,7},{3,5},{5,3},{7,1},{8,14},{10,12},{12... | collective-permute-start | bytes 516104 | tf_op jit(solution)/shard_map/ppermute | solution.py:245
  162.1 3.1 %collective-permute-done.20.refs_3_ = bf16[4,112,192]{2,1,0:T(8,128)(2,1)S(1)} collective-permute-done((bf16[4,112,192]{2,1,0:T(8,128)(2,1)S(1)}, bf16[4,112,192]{2,1,0:T(8,128)(2,1)S(1)}, u32[]{:S(2)}, u32[]{:S(2)}) %collective-permute-start.20) | collective-permute-done | bytes 172064 | tf_op jit(solution)/shard_map/ppermute | solution.py:245
  165.2 2.6 %collective-permute-done.19.refs_2_ = bf16[4,112,192]{2,1,0:T(8,128)(2,1)S(1)} collective-permute-done((bf16[4,112,192]{2,1,0:T(8,128)(2,1)S(1)}, bf16[4,112,192]{2,1,0:T(8,128)(2,1)S(1)}, u32[]{:S(2)}, u32[]{:S(2)}) %collective-permute-start.19) | collective-permute-done | bytes 172064 | tf_op jit(solution)/shard_map/ppermute | solution.py:245
  169.3 2.1 %shard_map.146 = (f32[1728,192]{1,0:T(8,128)}, f32[1728,192]{1,0:T(8,128)}) custom-call(bf16[4,112,192]{2,1,0:T(8,128)(2,1)S(1)} %shard_map.145.refs_0_, bf16[4,112,192]{2,1,0:T(8,128)(2,1)S(1)} %collective-permute-done.35.refs_1_, bf16[4,112,192]{2,1,0:T(8,128)(2,1)S(1)} %collective-permute-done.36.refs_2_, ...), custom_call_target="tpu_custom_call" | custom-call | bytes 4030464 | tf_op jit(solution)/shard_map/pallas_call | solution.py:31
  171.4 2.1 %shard_map.142 = (f32[1728,192]{1,0:T(8,128)}, f32[1728,192]{1,0:T(8,128)}) custom-call(bf16[4,112,192]{2,1,0:T(8,128)(2,1)S(1)} %shard_map.141.refs_0_, bf16[4,112,192]{2,1,0:T(8,128)(2,1)S(1)} %collective-permute-done.18.refs_1_, bf16[4,112,192]{2,1,0:T(8,128)(2,1)S(1)} %collective-permute-done.19.refs_2_, ...), custom_call_target="tpu_custom_call" | custom-call | bytes 4030464 | tf_op jit(solution)/shard_map/pallas_call | solution.py:31
  (133 shorter events, 17.8 us)
Async XLA Ops:
  1.7 6.0 %copy-start.17 = (bf16[32,32,192]{2,1,0:T(8,128)(2,1)S(1)}, bf16[32,32,192]{2,1,0:T(8,128)(2,1)}, u32[]{:S(2)}) copy-start(bf16[32,32,192]{2,1,0:T(8,128)(2,1)} %refs_0_.5) | copy-start | bytes 1179652
  2.5 14.0 %all-to-all-start = ((bf16[8,1,2,2,2,16,192]{6,5,4,3,2,1,0:T(8,128)(2,1)}), bf16[8,1,2,2,2,16,192]{6,5,4,3,2,1,0:T(8,128)(2,1)S(1)}, u32[]{:S(2)}, u32[]{:S(2)}) async-start(bf16[8,1,2,2,2,16,192]{6,5,4,3,2,1,0:T(8,128)(2,1)} %shard_map.129), calls=%async_computation | async-start | bytes 1048576 | tf_op jit(solution)/shard_map/all_to_all | solution.py:224
  7.7 16.3 %copy-start.18 = (bf16[32,32,192]{2,1,0:T(8,128)(2,1)S(1)}, bf16[32,32,192]{2,1,0:T(8,128)(2,1)}, u32[]{:S(2)}) copy-start(bf16[32,32,192]{2,1,0:T(8,128)(2,1)} %refs_0_.3) | copy-start | bytes 1179652
  7.7 16.3 %copy-start.19 = (bf16[32,32,192]{2,1,0:T(8,128)(2,1)S(1)}, bf16[32,32,192]{2,1,0:T(8,128)(2,1)}, u32[]{:S(2)}) copy-start(bf16[32,32,192]{2,1,0:T(8,128)(2,1)} %refs_1_.1) | copy-start | bytes 1179652
  7.7 16.2 %copy-start.20 = (bf16[32,32,192]{2,1,0:T(8,128)(2,1)S(1)}, bf16[32,32,192]{2,1,0:T(8,128)(2,1)}, u32[]{:S(2)}) copy-start(bf16[32,32,192]{2,1,0:T(8,128)(2,1)} %refs_2_.1) | copy-start | bytes 1179652
  16.5 19.2 %copy-start = (bf16[8,1,2,2,2,16,192]{6,5,4,3,2,1,0:T(8,128)(2,1)}, bf16[8,1,2,2,2,16,192]{6,5,4,3,2,1,0:T(8,128)(2,1)S(1)}, u32[]{:S(2)}) copy-start(bf16[8,1,2,2,2,16,192]{6,5,4,3,2,1,0:T(8,128)(2,1)S(1)} %all-to-all-done) | copy-start | bytes 1179652
  16.5 19.2 %all-to-all-start.1 = ((bf16[8,1,2,2,2,16,192]{6,5,4,3,2,1,0:T(8,128)(2,1)}), bf16[8,1,2,2,2,16,192]{6,5,4,3,2,1,0:T(8,128)(2,1)S(1)}, u32[]{:S(2)}, u32[]{:S(2)}) async-start(bf16[8,1,2,2,2,16,192]{6,5,4,3,2,1,0:T(8,128)(2,1)} %shard_map.130), calls=%async_computation.1 | async-start | bytes 1048576 | tf_op jit(solution)/shard_map/all_to_all | solution.py:224
  20.1 11.0 %collective-permute-start = (bf16[2,2,2,2,2,16,192]{6,5,4,3,2,1,0:T(8,128)(2,1)S(1)}, bf16[2,2,2,2,2,16,192]{6,5,4,3,2,1,0:T(8,128)(2,1)S(1)}, u32[]{:S(2)}, u32[]{:S(2)}) collective-permute-start(bf16[2,2,2,2,2,16,192]{6,5,4,3,2,1,0:T(8,128)(2,1)S(1)} %bitcast.31), channel_id=1, source_target_pairs={{0,8},{8,16},{16,24},{24,0},{1,9},{9,17},{17,25},{25,1},{2,10},{10... | collective-permute-start | bytes 589832 | tf_op jit(solution)/shard_map/ppermute | solution.py:240
  21.7 14.0 %collective-permute-start.1 = (bf16[2,2,2,2,2,16,192]{6,5,4,3,2,1,0:T(8,128)(2,1)S(1)}, bf16[2,2,2,2,2,16,192]{6,5,4,3,2,1,0:T(8,128)(2,1)S(1)}, u32[]{:S(2)}, u32[]{:S(2)}) collective-permute-start(bf16[2,2,2,2,2,16,192]{6,5,4,3,2,1,0:T(8,128)(2,1)S(1)} %bitcast.30), channel_id=1, source_target_pairs={{8,0},{16,8},{24,16},{0,24},{9,1},{17,9},{25,17},{1,25},{10,2},{18... | collective-permute-start | bytes 589832 | tf_op jit(solution)/shard_map/ppermute | solution.py:240
  31.1 8.3 %copy-start.33 = (bf16[2,2,2,2,2,16,192]{6,5,4,3,2,1,0:T(8,128)(2,1)}, bf16[2,2,2,2,2,16,192]{6,5,4,3,2,1,0:T(8,128)(2,1)S(1)}, u32[]{:S(2)}) copy-start(bf16[2,2,2,2,2,16,192]{6,5,4,3,2,1,0:T(8,128)(2,1)S(1)} %collective-permute-done.refs_0_) | copy-start | bytes 589828
  35.7 3.7 %copy-start.35 = (bf16[2,2,2,2,2,16,192]{6,5,4,3,2,1,0:T(8,128)(2,1)}, bf16[2,2,2,2,2,16,192]{6,5,4,3,2,1,0:T(8,128)(2,1)S(1)}, u32[]{:S(2)}) copy-start(bf16[2,2,2,2,2,16,192]{6,5,4,3,2,1,0:T(8,128)(2,1)S(1)} %collective-permute-done.1.refs_2_) | copy-start | bytes 589828
  35.7 3.7 %copy-start.6 = (bf16[8,1,2,2,2,16,192]{6,5,4,3,2,1,0:T(8,128)(2,1)}, bf16[8,1,2,2,2,16,192]{6,5,4,3,2,1,0:T(8,128)(2,1)S(1)}, u32[]{:S(2)}) copy-start(bf16[8,1,2,2,2,16,192]{6,5,4,3,2,1,0:T(8,128)(2,1)S(1)} %all-to-all-done.1) | copy-start | bytes 1179652
  39.3 27.0 %all-to-all-start.2 = ((bf16[8,3,2,2,2,16,192]{6,5,4,3,2,1,0:T(8,128)(2,1)}), bf16[8,3,2,2,2,16,192]{6,5,4,3,2,1,0:T(8,128)(2,1)S(1)}, u32[]{:S(2)}, u32[]{:S(2)}) async-start(bf16[8,3,2,2,2,16,192]{6,5,4,3,2,1,0:T(8,128)(2,1)} %shard_map.128), calls=%async_computation.2 | async-start | bytes 3145728 | tf_op jit(solution)/shard_map/all_to_all | solution.py:224
  43.2 11.2 %collective-permute-start.2 = (bf16[2,8,2,16,192]{4,3,2,1,0:T(8,128)(2,1)}, bf16[2,8,2,16,192]{4,3,2,1,0:T(8,128)(2,1)S(1)}, u32[]{:S(2)}, u32[]{:S(2)}) collective-permute-start(bf16[2,8,2,16,192]{4,3,2,1,0:T(8,128)(2,1)} %get-tuple-element.61.refs_2_), channel_id=1, source_target_pairs={{0,8},{8,16},{16,24},{24,0},{1,9},{9,17},{17,25},{25,1},{2,10},{10... | collective-permute-start | bytes 589832 | tf_op jit(solution)/shard_map/ppermute | solution.py:240
  44.3 14.3 %collective-permute-start.3 = (bf16[2,8,2,16,192]{4,3,2,1,0:T(8,128)(2,1)}, bf16[2,8,2,16,192]{4,3,2,1,0:T(8,128)(2,1)S(1)}, u32[]{:S(2)}, u32[]{:S(2)}) collective-permute-start(bf16[2,8,2,16,192]{4,3,2,1,0:T(8,128)(2,1)} %get-tuple-element.62.refs_1_), channel_id=1, source_target_pairs={{8,0},{16,8},{24,16},{0,24},{9,1},{17,9},{25,17},{1,25},{10,2},{18... | collective-permute-start | bytes 589832 | tf_op jit(solution)/shard_map/ppermute | solution.py:240
  51.0 7.6 %copy-start.2 = (bf16[8,1,2,2,2,16,192]{6,5,4,3,2,1,0:T(8,128)(2,1)S(1)}, bf16[8,1,2,2,2,16,192]{6,5,4,3,2,1,0:T(8,128)(2,1)}, u32[]{:S(2)}) copy-start(bf16[8,1,2,2,2,16,192]{6,5,4,3,2,1,0:T(8,128)(2,1)} %copy-done) | copy-start | bytes 1179652
  51.0 7.6 %copy-start.38 = (bf16[9,192,192]{2,1,0:T(8,128)(2,1)S(1)}, bf16[9,192,192]{2,1,0:T(8,128)(2,1)}, u32[]{:S(2)}) copy-start(bf16[9,192,192]{2,1,0:T(8,128)(2,1)} %refs_5_.1) | copy-start | bytes 1990660
  54.4 9.0 %copy-start.29 = (bf16[2,8,2,16,192]{4,3,2,1,0:T(8,128)(2,1)}, bf16[2,8,2,16,192]{4,3,2,1,0:T(8,128)(2,1)S(1)}, u32[]{:S(2)}) copy-start(bf16[2,8,2,16,192]{4,3,2,1,0:T(8,128)(2,1)S(1)} %collective-permute-done.2.refs_0_) | copy-start | bytes 589828
  58.6 4.7 %copy-start.31 = (bf16[2,8,2,16,192]{4,3,2,1,0:T(8,128)(2,1)}, bf16[2,8,2,16,192]{4,3,2,1,0:T(8,128)(2,1)S(1)}, u32[]{:S(2)}) copy-start(bf16[2,8,2,16,192]{4,3,2,1,0:T(8,128)(2,1)S(1)} %collective-permute-done.3.refs_3_) | copy-start | bytes 589828
  62.5 8.4 %collective-permute-start.4 = (bf16[1,8,2,16,192]{4,3,2,1,0:T(8,128)(2,1)}, bf16[1,8,2,16,192]{4,3,2,1,0:T(8,128)(2,1)}, u32[]{:S(2)}, u32[]{:S(2)}) collective-permute-start(bf16[1,8,2,16,192]{4,3,2,1,0:T(8,128)(2,1)} %get-tuple-element.65.refs_3_.refs_7_), channel_id=1, source_target_pairs={{0,8},{8,16},{16,24},{24,0},{1,9},{9,17},{17,25},{25,1},{2,10},{10... | collective-permute-start | bytes 294920 | tf_op jit(solution)/shard_map/ppermute | solution.py:240
  63.3 7.6 %collective-permute-start.5 = (bf16[1,8,2,16,192]{4,3,2,1,0:T(8,128)(2,1)S(1)}, bf16[1,8,2,16,192]{4,3,2,1,0:T(8,128)(2,1)}, u32[]{:S(2)}, u32[]{:S(2)}) collective-permute-start(bf16[1,8,2,16,192]{4,3,2,1,0:T(8,128)(2,1)S(1)} %get-tuple-element.66.refs_1_.refs_5_), channel_id=1, source_target_pairs={{8,0},{16,8},{24,16},{0,24},{9,1},{17,9},{25,17},{1,25},{10,2},{18... | collective-permute-start | bytes 294920 | tf_op jit(solution)/shard_map/ppermute | solution.py:240
  70.8 3.2 %copy-start.8 = (f32[1792,192]{1,0:T(8,128)}, f32[1792,192]{1,0:T(8,128)S(1)}, u32[]{:S(2)}) copy-start(f32[1792,192]{1,0:T(8,128)S(1)} %get-tuple-element.69) | copy-start | bytes 4128772
  70.8 3.2 %copy-start.12 = (bf16[1792,192]{1,0:T(8,128)(2,1)}, bf16[1792,192]{1,0:T(8,128)(2,1)S(1)}, u32[]{:S(2)}) copy-start(bf16[1792,192]{1,0:T(8,128)(2,1)S(1)} %get-tuple-element.98) | copy-start | bytes 2064388
  70.9 9.1 %copy-start.5 = (bf16[2,8,2,16,192]{4,3,2,1,0:T(8,128)(2,1)S(1)}, bf16[2,8,2,16,192]{4,3,2,1,0:T(8,128)(2,1)}, u32[]{:S(2)}) copy-start(bf16[2,8,2,16,192]{4,3,2,1,0:T(8,128)(2,1)} %copy-done.3) | copy-start | bytes 589828
  74.0 8.6 %copy-start.10 = (bf16[2,8,2,16,192]{4,3,2,1,0:T(8,128)(2,1)}, bf16[2,8,2,16,192]{4,3,2,1,0:T(8,128)(2,1)S(1)}, u32[]{:S(2)}) copy-start(bf16[2,8,2,16,192]{4,3,2,1,0:T(8,128)(2,1)S(1)} %get-tuple-element.76.refs_2_) | copy-start | bytes 589828
  74.0 8.6 %copy-start.21 = (bf16[1,8,2,16,192]{4,3,2,1,0:T(8,128)(2,1)}, bf16[1,8,2,16,192]{4,3,2,1,0:T(8,128)(2,1)S(1)}, u32[]{:S(2)}) copy-start(bf16[1,8,2,16,192]{4,3,2,1,0:T(8,128)(2,1)S(1)} %get-tuple-element.74.refs_1_) | copy-start | bytes 294916
  74.0 8.6 %copy-start.23 = (bf16[1,8,2,16,192]{4,3,2,1,0:T(8,128)(2,1)}, bf16[1,8,2,16,192]{4,3,2,1,0:T(8,128)(2,1)S(1)}, u32[]{:S(2)}) copy-start(bf16[1,8,2,16,192]{4,3,2,1,0:T(8,128)(2,1)S(1)} %get-tuple-element.73.refs_3_) | copy-start | bytes 294916
  74.0 8.4 %collective-permute-start.6 = (bf16[1,8,2,16,192]{4,3,2,1,0:T(8,128)(2,1)S(1)}, bf16[1,8,2,16,192]{4,3,2,1,0:T(8,128)(2,1)S(1)}, u32[]{:S(2)}, u32[]{:S(2)}) collective-permute-start(bf16[1,8,2,16,192]{4,3,2,1,0:T(8,128)(2,1)S(1)} %get-tuple-element.73.refs_3_), channel_id=1, source_target_pairs={{0,8},{8,16},{16,24},{24,0},{1,9},{9,17},{17,25},{25,1},{2,10},{10... | collective-permute-start | bytes 294920 | tf_op jit(solution)/shard_map/ppermute | solution.py:240
  75.1 7.5 %collective-permute-start.7 = (bf16[1,8,2,16,192]{4,3,2,1,0:T(8,128)(2,1)S(1)}, bf16[1,8,2,16,192]{4,3,2,1,0:T(8,128)(2,1)S(1)}, u32[]{:S(2)}, u32[]{:S(2)}) collective-permute-start(bf16[1,8,2,16,192]{4,3,2,1,0:T(8,128)(2,1)S(1)} %get-tuple-element.74.refs_1_), channel_id=1, source_target_pairs={{8,0},{16,8},{24,16},{0,24},{9,1},{17,9},{25,17},{1,25},{10,2},{18... | collective-permute-start | bytes 294920 | tf_op jit(solution)/shard_map/ppermute | solution.py:240
  80.0 16.5 %collective-permute-start.25 = (bf16[1792,192]{0,1:T(8,128)(2,1)}, bf16[1792,192]{0,1:T(8,128)(2,1)}, u32[]{:S(2)}, u32[]{:S(2)}) collective-permute-start(bf16[1792,192]{0,1:T(8,128)(2,1)} %copy.18), channel_id=1, source_target_pairs={{0,1},{1,0},{2,3},{3,2},{4,5},{5,4},{6,7},{7,6},{8,9},{9,8},{10,11... | collective-permute-start | bytes 2064392 | tf_op jit(solution)/shard_map/ppermute | solution.py:245
  96.2 23.9 %collective-permute-start.8 = (bf16[1792,192]{0,1:T(8,128)(2,1)}, bf16[1792,192]{0,1:T(8,128)(2,1)}, u32[]{:S(2)}, u32[]{:S(2)}) collective-permute-start(bf16[1792,192]{0,1:T(8,128)(2,1)} %copy.16), channel_id=1, source_target_pairs={{0,1},{1,0},{2,3},{3,2},{4,5},{5,4},{6,7},{7,6},{8,9},{9,8},{10,11... | collective-permute-start | bytes 2064392 | tf_op jit(solution)/shard_map/ppermute | solution.py:245
  100.4 7.9 %collective-permute-start.26 = (bf16[4,112,192]{2,1,0:T(8,128)(2,1)}, bf16[4,112,192]{2,1,0:T(8,128)(2,1)S(1)}, u32[]{:S(2)}, u32[]{:S(2)}) collective-permute-start(bf16[4,112,192]{2,1,0:T(8,128)(2,1)} %get-tuple-element.100), channel_id=1, source_target_pairs={{0,2},{2,0},{4,6},{6,4},{1,3},{3,1},{5,7},{7,5},{8,10},{10,8},{12,... | collective-permute-start | bytes 516104 | tf_op jit(solution)/shard_map/ppermute | solution.py:245
  102.0 8.7 %collective-permute-start.27 = (bf16[4,112,192]{2,1,0:T(8,128)(2,1)}, bf16[4,112,192]{2,1,0:T(8,128)(2,1)S(1)}, u32[]{:S(2)}, u32[]{:S(2)}) collective-permute-start(bf16[4,112,192]{2,1,0:T(8,128)(2,1)} %get-tuple-element.101), channel_id=1, source_target_pairs={{0,4},{2,6},{4,0},{6,2},{1,5},{3,7},{5,1},{7,3},{8,12},{10,14},{12... | collective-permute-start | bytes 516104 | tf_op jit(solution)/shard_map/ppermute | solution.py:245
  103.4 12.1 %collective-permute-start.28 = (bf16[4,112,192]{2,1,0:T(8,128)(2,1)}, bf16[4,112,192]{2,1,0:T(8,128)(2,1)S(1)}, u32[]{:S(2)}, u32[]{:S(2)}) collective-permute-start(bf16[4,112,192]{2,1,0:T(8,128)(2,1)} %get-tuple-element.102), channel_id=1, source_target_pairs={{0,6},{2,4},{4,2},{6,0},{1,7},{3,5},{5,3},{7,1},{8,14},{10,12},{12... | collective-permute-start | bytes 516104 | tf_op jit(solution)/shard_map/ppermute | solution.py:245
  103.8 24.7 %all-to-all-start.3 = ((bf16[8,2,2,2,16,192]{5,4,3,2,1,0:T(8,128)(2,1)}), bf16[8,2,2,2,16,192]{5,4,3,2,1,0:T(8,128)(2,1)}, u32[]{:S(2)}, u32[]{:S(2)}) async-start(bf16[8,2,2,2,16,192]{5,4,3,2,1,0:T(8,128)(2,1)} %bitcast.6), calls=%async_computation.3 | async-start | bytes 1048576 | tf_op jit(solution)/shard_map/all_to_all | solution.py:232
  115.6 9.9 %collective-permute-start.29 = (bf16[112,192]{1,0:T(8,128)(2,1)S(1)}, bf16[112,192]{1,0:T(8,128)(2,1)}, u32[]{:S(2)}, u32[]{:S(2)}) collective-permute-start(bf16[112,192]{1,0:T(8,128)(2,1)S(1)} %get-tuple-element.104), channel_id=1, source_target_pairs={{0,8},{8,0},{16,24},{24,16},{1,9},{9,1},{17,25},{25,17},{2,10},{10... | collective-permute-start | bytes 129032 | tf_op jit(solution)/shard_map/ppermute | solution.py:245
  115.7 10.2 %collective-permute-start.30 = (bf16[112,192]{1,0:T(8,128)(2,1)S(1)}, bf16[112,192]{1,0:T(8,128)(2,1)}, u32[]{:S(2)}, u32[]{:S(2)}) collective-permute-start(bf16[112,192]{1,0:T(8,128)(2,1)S(1)} %get-tuple-element.105), channel_id=1, source_target_pairs={{0,16},{8,24},{16,0},{24,8},{1,17},{9,25},{17,1},{25,9},{2,18},{10... | collective-permute-start | bytes 129032 | tf_op jit(solution)/shard_map/ppermute | solution.py:245
  117.9 8.0 %collective-permute-start.31 = (bf16[112,192]{1,0:T(8,128)(2,1)S(1)}, bf16[112,192]{1,0:T(8,128)(2,1)}, u32[]{:S(2)}, u32[]{:S(2)}) collective-permute-start(bf16[112,192]{1,0:T(8,128)(2,1)S(1)} %get-tuple-element.106), channel_id=1, source_target_pairs={{0,24},{8,16},{16,8},{24,0},{1,25},{9,17},{17,9},{25,1},{2,26},{10... | collective-permute-start | bytes 129032 | tf_op jit(solution)/shard_map/ppermute | solution.py:245
  122.5 8.4 %collective-permute-start.9 = (bf16[4,112,192]{2,1,0:T(8,128)(2,1)}, bf16[4,112,192]{2,1,0:T(8,128)(2,1)S(1)}, u32[]{:S(2)}, u32[]{:S(2)}) collective-permute-start(bf16[4,112,192]{2,1,0:T(8,128)(2,1)} %get-tuple-element.83), channel_id=1, source_target_pairs={{0,2},{2,0},{4,6},{6,4},{1,3},{3,1},{5,7},{7,5},{8,10},{10,8},{12,... | collective-permute-start | bytes 516104 | tf_op jit(solution)/shard_map/ppermute | solution.py:245
  124.1 9.1 %collective-permute-start.10 = (bf16[4,112,192]{2,1,0:T(8,128)(2,1)}, bf16[4,112,192]{2,1,0:T(8,128)(2,1)S(1)}, u32[]{:S(2)}, u32[]{:S(2)}) collective-permute-start(bf16[4,112,192]{2,1,0:T(8,128)(2,1)} %get-tuple-element.84), channel_id=1, source_target_pairs={{0,4},{2,6},{4,0},{6,2},{1,5},{3,7},{5,1},{7,3},{8,12},{10,14},{12... | collective-permute-start | bytes 516104 | tf_op jit(solution)/shard_map/ppermute | solution.py:245
  125.6 7.8 %collective-permute-start.11 = (bf16[4,112,192]{2,1,0:T(8,128)(2,1)}, bf16[4,112,192]{2,1,0:T(8,128)(2,1)S(1)}, u32[]{:S(2)}, u32[]{:S(2)}) collective-permute-start(bf16[4,112,192]{2,1,0:T(8,128)(2,1)} %get-tuple-element.85), channel_id=1, source_target_pairs={{0,6},{2,4},{4,2},{6,0},{1,7},{3,5},{5,3},{7,1},{8,14},{10,12},{12... | collective-permute-start | bytes 516104 | tf_op jit(solution)/shard_map/ppermute | solution.py:245
  126.9 9.7 %collective-permute-start.34 = (bf16[112,192]{1,0:T(8,128)(2,1)S(1)}, bf16[112,192]{1,0:T(8,128)(2,1)S(1)}, u32[]{:S(2)}, u32[]{:S(2)}) collective-permute-start(bf16[112,192]{1,0:T(8,128)(2,1)S(1)} %add_convert_fusion.refs_0_), channel_id=1, source_target_pairs={{0,24},{8,16},{16,8},{24,0},{1,25},{9,17},{17,9},{25,1},{2,26},{10... | collective-permute-start | bytes 129032 | tf_op jit(solution)/shard_map/ppermute | solution.py:245
  130.5 7.4 %collective-permute-start.33 = (bf16[112,192]{1,0:T(8,128)(2,1)S(1)}, bf16[112,192]{1,0:T(8,128)(2,1)S(1)}, u32[]{:S(2)}, u32[]{:S(2)}) collective-permute-start(bf16[112,192]{1,0:T(8,128)(2,1)S(1)} %add_convert_fusion.refs_0_), channel_id=1, source_target_pairs={{0,16},{8,24},{16,0},{24,8},{1,17},{9,25},{17,1},{25,9},{2,18},{10... | collective-permute-start | bytes 129032 | tf_op jit(solution)/shard_map/ppermute | solution.py:245
  130.9 7.0 %collective-permute-start.32 = (bf16[112,192]{1,0:T(8,128)(2,1)S(1)}, bf16[112,192]{1,0:T(8,128)(2,1)S(1)}, u32[]{:S(2)}, u32[]{:S(2)}) collective-permute-start(bf16[112,192]{1,0:T(8,128)(2,1)S(1)} %add_convert_fusion.refs_0_), channel_id=1, source_target_pairs={{0,8},{8,0},{16,24},{24,16},{1,9},{9,1},{17,25},{25,17},{2,10},{10... | collective-permute-start | bytes 129032 | tf_op jit(solution)/shard_map/ppermute | solution.py:245
  133.4 7.1 %collective-permute-start.12 = (bf16[112,192]{1,0:T(8,128)(2,1)S(1)}, bf16[112,192]{1,0:T(8,128)(2,1)S(1)}, u32[]{:S(2)}, u32[]{:S(2)}) collective-permute-start(bf16[112,192]{1,0:T(8,128)(2,1)S(1)} %get-tuple-element.92), channel_id=1, source_target_pairs={{0,8},{8,0},{16,24},{24,16},{1,9},{9,1},{17,25},{25,17},{2,10},{10... | collective-permute-start | bytes 129032 | tf_op jit(solution)/shard_map/ppermute | solution.py:245
  133.5 7.6 %collective-permute-start.13 = (bf16[112,192]{1,0:T(8,128)(2,1)S(1)}, bf16[112,192]{1,0:T(8,128)(2,1)S(1)}, u32[]{:S(2)}, u32[]{:S(2)}) collective-permute-start(bf16[112,192]{1,0:T(8,128)(2,1)S(1)} %get-tuple-element.93), channel_id=1, source_target_pairs={{0,16},{8,24},{16,0},{24,8},{1,17},{9,25},{17,1},{25,9},{2,18},{10... | collective-permute-start | bytes 129032 | tf_op jit(solution)/shard_map/ppermute | solution.py:245
  136.6 6.0 %collective-permute-start.14 = (bf16[112,192]{1,0:T(8,128)(2,1)S(1)}, bf16[112,192]{1,0:T(8,128)(2,1)S(1)}, u32[]{:S(2)}, u32[]{:S(2)}) collective-permute-start(bf16[112,192]{1,0:T(8,128)(2,1)S(1)} %get-tuple-element.94), channel_id=1, source_target_pairs={{0,24},{8,16},{16,8},{24,0},{1,25},{9,17},{17,9},{25,1},{2,26},{10... | collective-permute-start | bytes 129032 | tf_op jit(solution)/shard_map/ppermute | solution.py:245
  137.9 22.7 %collective-permute-start.38 = (bf16[4,112,192]{2,1,0:T(8,128)(2,1)S(1)}, bf16[4,112,192]{2,1,0:T(8,128)(2,1)S(1)}, u32[]{:S(2)}, u32[]{:S(2)}) collective-permute-start(bf16[4,112,192]{2,1,0:T(8,128)(2,1)S(1)} %shard_map.145.refs_0_), channel_id=1, source_target_pairs={{0,1},{1,0},{2,3},{3,2},{4,5},{5,4},{6,7},{7,6},{8,9},{9,8},{10,11... | collective-permute-start | bytes 516104 | tf_op jit(solution)/shard_map/ppermute | solution.py:245
  138.0 23.1 %collective-permute-start.37 = (bf16[4,112,192]{2,1,0:T(8,128)(2,1)S(1)}, bf16[4,112,192]{2,1,0:T(8,128)(2,1)S(1)}, u32[]{:S(2)}, u32[]{:S(2)}) collective-permute-start(bf16[4,112,192]{2,1,0:T(8,128)(2,1)S(1)} %shard_map.145.refs_0_), channel_id=1, source_target_pairs={{0,6},{2,4},{4,2},{6,0},{1,7},{3,5},{5,3},{7,1},{8,14},{10,12},{12... | collective-permute-start | bytes 516104 | tf_op jit(solution)/shard_map/ppermute | solution.py:245
  140.5 21.0 %collective-permute-start.36 = (bf16[4,112,192]{2,1,0:T(8,128)(2,1)S(1)}, bf16[4,112,192]{2,1,0:T(8,128)(2,1)S(1)}, u32[]{:S(2)}, u32[]{:S(2)}) collective-permute-start(bf16[4,112,192]{2,1,0:T(8,128)(2,1)S(1)} %shard_map.145.refs_0_), channel_id=1, source_target_pairs={{0,4},{2,6},{4,0},{6,2},{1,5},{3,7},{5,1},{7,3},{8,12},{10,14},{12... | collective-permute-start | bytes 516104 | tf_op jit(solution)/shard_map/ppermute | solution.py:245
  141.1 20.5 %collective-permute-start.35 = (bf16[4,112,192]{2,1,0:T(8,128)(2,1)S(1)}, bf16[4,112,192]{2,1,0:T(8,128)(2,1)S(1)}, u32[]{:S(2)}, u32[]{:S(2)}) collective-permute-start(bf16[4,112,192]{2,1,0:T(8,128)(2,1)S(1)} %shard_map.145.refs_0_), channel_id=1, source_target_pairs={{0,2},{2,0},{4,6},{6,4},{1,3},{3,1},{5,7},{7,5},{8,10},{10,8},{12,... | collective-permute-start | bytes 516104 | tf_op jit(solution)/shard_map/ppermute | solution.py:245
  142.6 6.0 %collective-permute-start.17 = (bf16[112,192]{1,0:T(8,128)(2,1)S(1)}, bf16[112,192]{1,0:T(8,128)(2,1)S(1)}, u32[]{:S(2)}, u32[]{:S(2)}) collective-permute-start(bf16[112,192]{1,0:T(8,128)(2,1)S(1)} %add_convert_fusion.1.refs_0_), channel_id=1, source_target_pairs={{0,24},{8,16},{16,8},{24,0},{1,25},{9,17},{17,9},{25,1},{2,26},{10... | collective-permute-start | bytes 129032 | tf_op jit(solution)/shard_map/ppermute | solution.py:245
  148.6 5.1 %collective-permute-start.16 = (bf16[112,192]{1,0:T(8,128)(2,1)S(1)}, bf16[112,192]{1,0:T(8,128)(2,1)S(1)}, u32[]{:S(2)}, u32[]{:S(2)}) collective-permute-start(bf16[112,192]{1,0:T(8,128)(2,1)S(1)} %add_convert_fusion.1.refs_0_), channel_id=1, source_target_pairs={{0,16},{8,24},{16,0},{24,8},{1,17},{9,25},{17,1},{25,9},{2,18},{10... | collective-permute-start | bytes 129032 | tf_op jit(solution)/shard_map/ppermute | solution.py:245
  153.8 4.2 %collective-permute-start.15 = (bf16[112,192]{1,0:T(8,128)(2,1)S(1)}, bf16[112,192]{1,0:T(8,128)(2,1)S(1)}, u32[]{:S(2)}, u32[]{:S(2)}) collective-permute-start(bf16[112,192]{1,0:T(8,128)(2,1)S(1)} %add_convert_fusion.1.refs_0_), channel_id=1, source_target_pairs={{0,8},{8,0},{16,24},{24,16},{1,9},{9,1},{17,25},{25,17},{2,10},{10... | collective-permute-start | bytes 129032 | tf_op jit(solution)/shard_map/ppermute | solution.py:245
  158.0 7.2 %collective-permute-start.20 = (bf16[4,112,192]{2,1,0:T(8,128)(2,1)S(1)}, bf16[4,112,192]{2,1,0:T(8,128)(2,1)S(1)}, u32[]{:S(2)}, u32[]{:S(2)}) collective-permute-start(bf16[4,112,192]{2,1,0:T(8,128)(2,1)S(1)} %shard_map.141.refs_0_), channel_id=1, source_target_pairs={{0,6},{2,4},{4,2},{6,0},{1,7},{3,5},{5,3},{7,1},{8,14},{10,12},{12... | collective-permute-start | bytes 516104 | tf_op jit(solution)/shard_map/ppermute | solution.py:245
  160.6 7.2 %collective-permute-start.19 = (bf16[4,112,192]{2,1,0:T(8,128)(2,1)S(1)}, bf16[4,112,192]{2,1,0:T(8,128)(2,1)S(1)}, u32[]{:S(2)}, u32[]{:S(2)}) collective-permute-start(bf16[4,112,192]{2,1,0:T(8,128)(2,1)S(1)} %shard_map.141.refs_0_), channel_id=1, source_target_pairs={{0,4},{2,6},{4,0},{6,2},{1,5},{3,7},{5,1},{7,3},{8,12},{10,14},{12... | collective-permute-start | bytes 516104 | tf_op jit(solution)/shard_map/ppermute | solution.py:245
  161.2 6.7 %collective-permute-start.18 = (bf16[4,112,192]{2,1,0:T(8,128)(2,1)S(1)}, bf16[4,112,192]{2,1,0:T(8,128)(2,1)S(1)}, u32[]{:S(2)}, u32[]{:S(2)}) collective-permute-start(bf16[4,112,192]{2,1,0:T(8,128)(2,1)S(1)} %shard_map.141.refs_0_), channel_id=1, source_target_pairs={{0,2},{2,0},{4,6},{6,4},{1,3},{3,1},{5,7},{7,5},{8,10},{10,8},{12,... | collective-permute-start | bytes 516104 | tf_op jit(solution)/shard_map/ppermute | solution.py:245
  161.5 6.8 %collective-permute-start.41 = (bf16[4,112,192]{2,1,0:T(8,128)(2,1)S(1)}, bf16[4,112,192]{2,1,0:T(8,128)(2,1)S(1)}, u32[]{:S(2)}, u32[]{:S(2)}) collective-permute-start(bf16[4,112,192]{2,1,0:T(8,128)(2,1)S(1)} %collective-permute-done.37.refs_3_), channel_id=1, source_target_pairs={{0,1},{1,0},{2,3},{3,2},{4,5},{5,4},{6,7},{7,6},{8,9},{9,8},{10,11... | collective-permute-start | bytes 516104 | tf_op jit(solution)/shard_map/ppermute | solution.py:245
  161.6 6.8 %collective-permute-start.40 = (bf16[4,112,192]{2,1,0:T(8,128)(2,1)S(1)}, bf16[4,112,192]{2,1,0:T(8,128)(2,1)S(1)}, u32[]{:S(2)}, u32[]{:S(2)}) collective-permute-start(bf16[4,112,192]{2,1,0:T(8,128)(2,1)S(1)} %collective-permute-done.36.refs_2_), channel_id=1, source_target_pairs={{0,1},{1,0},{2,3},{3,2},{4,5},{5,4},{6,7},{7,6},{8,9},{9,8},{10,11... | collective-permute-start | bytes 516104 | tf_op jit(solution)/shard_map/ppermute | solution.py:245
  165.2 6.3 %collective-permute-start.21 = (bf16[4,112,192]{2,1,0:T(8,128)(2,1)S(1)}, bf16[4,112,192]{2,1,0:T(8,128)(2,1)S(1)}, u32[]{:S(2)}, u32[]{:S(2)}) collective-permute-start(bf16[4,112,192]{2,1,0:T(8,128)(2,1)S(1)} %shard_map.141.refs_0_), channel_id=1, source_target_pairs={{0,1},{1,0},{2,3},{3,2},{4,5},{5,4},{6,7},{7,6},{8,9},{9,8},{10,11... | collective-permute-start | bytes 516104 | tf_op jit(solution)/shard_map/ppermute | solution.py:245
  167.8 1.5 collective-permute-start.39
  167.8 3.6 %collective-permute-start.24 = (bf16[4,112,192]{2,1,0:T(8,128)(2,1)S(1)}, bf16[4,112,192]{2,1,0:T(8,128)(2,1)S(1)}, u32[]{:S(2)}, u32[]{:S(2)}) collective-permute-start(bf16[4,112,192]{2,1,0:T(8,128)(2,1)S(1)} %collective-permute-done.20.refs_3_), channel_id=1, source_target_pairs={{0,1},{1,0},{2,3},{3,2},{4,5},{5,4},{6,7},{7,6},{8,9},{9,8},{10,11... | collective-permute-start | bytes 516104 | tf_op jit(solution)/shard_map/ppermute | solution.py:245
  168.3 3.1 %collective-permute-start.23 = (bf16[4,112,192]{2,1,0:T(8,128)(2,1)S(1)}, bf16[4,112,192]{2,1,0:T(8,128)(2,1)S(1)}, u32[]{:S(2)}, u32[]{:S(2)}) collective-permute-start(bf16[4,112,192]{2,1,0:T(8,128)(2,1)S(1)} %collective-permute-done.19.refs_2_), channel_id=1, source_target_pairs={{0,1},{1,0},{2,3},{3,2},{4,5},{5,4},{6,7},{7,6},{8,9},{9,8},{10,11... | collective-permute-start | bytes 516104 | tf_op jit(solution)/shard_map/ppermute | solution.py:245
  168.4 3.0 %collective-permute-start.22 = (bf16[4,112,192]{2,1,0:T(8,128)(2,1)S(1)}, bf16[4,112,192]{2,1,0:T(8,128)(2,1)S(1)}, u32[]{:S(2)}, u32[]{:S(2)}) collective-permute-start(bf16[4,112,192]{2,1,0:T(8,128)(2,1)S(1)} %collective-permute-done.18.refs_1_), channel_id=1, source_target_pairs={{0,1},{1,0},{2,3},{3,2},{4,5},{5,4},{6,7},{7,6},{8,9},{9,8},{10,11... | collective-permute-start | bytes 516104 | tf_op jit(solution)/shard_map/ppermute | solution.py:245
  (21 other events, 25.3 us)

commit v3 on v2

--- a/solution.py
+++ b/solution.py
@@ -13,10 +13,12 @@
 TAPS = [(r, c) for r in (-1, 0, 1) for c in (-1, 0, 1)]
 PLANE = ("x", "y", "c")
 VMEM_LIMIT = 16 * 1024 * 1024
-
-
-def call(body, outs, scratch, flops, *args):
-    specs, arrays, size = [], [], 0
+WEIGHT = 20
+
+
+def call(body, outs, scratch, flops, *args, after=()):
+    specs = [pl.BlockSpec(memory_space=pl.ANY)] * len(after)
+    arrays, size = list(after), 0
     for arg in args:
         if isinstance(arg, tuple):
             arg, member = arg
@@ -29,14 +31,14 @@
         arrays.append(arg)
     size += sum(o.size * o.dtype.itemsize for o in outs)
     return pl.pallas_call(
-        body,
+        lambda *refs: body(*refs[len(after) :]),
         grid=(1,),
         out_shape=outs,
         in_specs=specs,
         out_specs=[pl.BlockSpec(memory_space=pltpu.VMEM)] * len(outs),
         scratch_shapes=scratch,
         compiler_params=pltpu.CompilerParams(vmem_limit_bytes=VMEM_LIMIT),
-        cost_estimate=pl.CostEstimate(flops=flops, bytes_accessed=size, transcendentals=0),
+        cost_estimate=pl.CostEstimate(flops=WEIGHT * flops, bytes_accessed=size, transcendentals=0),
     )(*arrays)
 
 
@@ -104,7 +106,7 @@
     return jnp.concatenate([ref[...].reshape(-1, ref.shape[-1]) for ref in refs], 0)
 
 
-def conv_two(field, act, weights, step, outs):
+def conv_two(field, act, weights, step, outs, after=()):
     n = len(field)
 
     def body(*refs):
@@ -117,10 +119,12 @@
         store(out_refs, grad * sigma * (1.0 + pre * (1.0 - sigma)))
 
     chan = weights.shape[-1]
-    return call(body, outs, [padded_shape(chan, step)], conv_flops(chan), *field, act, weights)
-
-
-def conv_one(field, base, weights, step, outs):
+    outs = outs + [padded_shape(chan, step)]
+    *parts, wide = call(body, outs, [], conv_flops(chan), *field, act, weights, after=after)
+    return parts, wide
+
+
+def conv_one(field, base, weights, step, outs, after=()):
     n, b = len(field), len(base)
 
     def body(*refs):
@@ -131,11 +135,12 @@
         store(out_refs, flat(base_refs).astype(F32) + grad)
 
     chan = weights.shape[-1]
-    return call(body, outs, [padded_shape(chan, step)], conv_flops(chan), *field, *base, weights)
-
-
-def tap_products(pieces, src_ref, active, step, padded, out_ref):
-    fill(padded, pieces, step)
+    outs = outs + [padded_shape(chan, step)]
+    *parts, wide = call(body, outs, [], conv_flops(chan), *field, *base, weights, after=after)
+    return parts, wide
+
+
+def tap_products(padded, src_ref, active, step, out_ref):
     src = class_flat(src_ref)
     chan = src.shape[-1]
     if active:
@@ -154,40 +159,41 @@
     return -(-len(TAPS) * chan // 256) * 256
 
 
-def weight_grad(field, source, step, chan):
-    n = len(field)
-
-    def body(*refs):
-        tap_products(refs[:n], refs[n], True, step, refs[n + 2], refs[n + 1])
+def weight_grad(wide, source, step, chan, after=()):
+    def body(wide_ref, src_ref, out_ref):
+        tap_products(wide_ref, src_ref, True, step, out_ref)
 
     out = [jax.ShapeDtypeStruct((padded_rows(chan), chan), F32)]
-    return call(body, out, [padded_shape(chan, step)], conv_flops(chan), *field, source)[0]
-
-
-def weight_grad_split(field, source, step, chan, other):
-    n = len(field)
-
-    def body(*refs):
-        other_ref, keep_ref, give_ref, padded, total = refs[n + 1 :]
-        tap_products(refs[:n], refs[n], False, step, padded, total)
+    return call(body, out, [], conv_flops(chan), wide, source, after=after)[0]
+
+
+def weight_grad_split(wide, source, step, chan, other, after=()):
+    rows = padded_rows(chan)
+    part = (4, rows // 16, chan)
+
+    def body(wide_ref, src_ref, other_ref, keep_ref, *refs):
+        give_refs, total = refs[:4], refs[4]
+        tap_products(wide_ref, src_ref, False, step, total)
         core = lax.axis_index("c")
+
+        def split(kept, given):
+            keep_ref[...] = kept[...].reshape(keep_ref.shape)
+            for k, ref in enumerate(give_refs):
+                at = pl.multiple_of((quarter() ^ k) * (rows // 4), 16)
+                ref[...] = given[pl.ds(at, rows // 4)].astype(BF16).reshape(part)
 
         @pl.when(core == 0)
         def _():
-            keep_ref[...] = other_ref[...]
-            give_ref[...] = total[...].astype(BF16)
+            split(other_ref, total)
 
         @pl.when(core != 0)
         def _():
-            keep_ref[...] = total[...]
-            give_ref[...] = other_ref[...].astype(BF16)
-
-    shape = (padded_rows(chan), chan)
-    outs = [jax.ShapeDtypeStruct(shape, F32), jax.ShapeDtypeStruct(shape, BF16)]
-    scratch = [padded_shape(chan, step), pltpu.VMEM(shape, F32)]
-    keep, give = call(body, outs, scratch, conv_flops(chan), *field, source, other)
-    parts = (4, 4, shape[0] // 16, chan)
-    return keep.reshape(parts), xor(give, "c", 1).reshape(parts)
+            split(total, other_ref)
+
+    outs = [jax.ShapeDtypeStruct((4,) + part, F32)] + [jax.ShapeDtypeStruct(part, BF16)] * 4
+    scratch = [pltpu.VMEM((rows, chan), F32)]
+    keep, *give = call(body, outs, scratch, conv_flops(chan), wide, source, other, after=after)
+    return keep, [xor(value, "c", 1) for value in give]
 
 
 def conv_flops(chan):
@@ -195,14 +201,14 @@
 
 
 def padded_shape(chan, step):
-    return pltpu.VMEM((4 + 2 * step, 8 + 2 * step, 2, STRIDE, chan), BF16)
+    return jax.ShapeDtypeStruct((4 + 2 * step, 8 + 2 * step, 2, STRIDE, chan), BF16)
 
 
 def coarse(cols, chan):
     return jax.ShapeDtypeStruct((cols, 8, 2, STRIDE, chan), BF16)
 
 
-def pack_classes(*values):
+def pack_classes(*values, after=()):
     height, breadth, chan = values[0].shape
     group = lax.axis_size(PLANE)
     n = len(values)
@@ -217,7 +223,7 @@
                     out_ref[target, i, ih] = refs[i][at : at + size].reshape(out_ref.shape[3:])
 
     shape = (group, n, height // STRIDE, STRIDE // group, breadth // STRIDE, STRIDE, chan)
-    return call(body, [jax.ShapeDtypeStruct(shape, BF16)], [], 0, *values)[0]
+    return call(body, [jax.ShapeDtypeStruct(shape, BF16)], [], 0, *values, after=after)[0]
 
 
 def swap_classes(packed):
@@ -249,24 +255,25 @@
     return 2 * lax.axis_index("x") + lax.axis_index("y")
 
 
-def sum_plane(keep, got):
+def sum_plane(keep, got, after=()):
     part = keep.shape[1:]
 
-    def body(keep_ref, got_ref, own_ref, *sent_refs):
+    def body(keep_ref, *refs):
+        got_refs, own_ref, sent_refs = refs[:4], refs[4], refs[5:]
         for k in range(4):
-            at = quarter() ^ k
-            total = keep_ref[at] + got_ref[at].astype(F32)
+            total = keep_ref[quarter() ^ k] + got_refs[k][...].astype(F32)
             if k == 0:
                 own_ref[...] = total
             else:
                 sent_refs[k - 1][...] = total.astype(BF16)
 
     outs = [jax.ShapeDtypeStruct(part, F32)] + [jax.ShapeDtypeStruct(part, BF16)] * 3
-    own, *sent = call(body, outs, [], 0, keep, got)
-    return own, [xor(value, ("x", "y"), k + 1) for k, value in enumerate(sent)]
-
-
-def sum_ring(own, terms):
+    own, *sent = call(body, outs, [], 0, keep, *got, after=after)
+    return own, sent
+
+
+def sum_ring(own, sent, after=()):
+    terms = [xor(value, ("x", "y"), k + 1) for k, value in enumerate(sent)]
     count = lax.axis_size("z")
     part = own.shape
     if count != 4:
@@ -291,7 +298,7 @@
                 sent_refs[k - 1][...] = total.astype(BF16)
 
     outs = [jax.ShapeDtypeStruct(part[1:], F32)] + [jax.ShapeDtypeStruct(part[1:], BF16)] * 3
-    mine, *sent = call(body, outs, [], 0, own, *terms)
+    mine, *sent = call(body, outs, [], 0, own, *terms, after=after)
     for k, value in enumerate(sent):
         mine = mine + xor(value, "z", k + 1).astype(F32)
     mine = mine.astype(BF16)
@@ -342,11 +349,6 @@
     outs = [jax.ShapeDtypeStruct((used, chan), F32)] * 2
     one, two = call(body, outs, [], 0, *quarters, *others)
     return one.reshape(taps, chan, chan), two.reshape(taps, chan, chan)
-
-
-def sum_weights(keep, give):
-    part = sum_ring(*sum_plane(keep, give))
-    return spread_weights(part, len(TAPS))
 
 
 def local(
@@ -363,44 +365,37 @@
     height, breadth, chan = output_gradient_final.shape
     final = swap_classes(pack_classes(output_gradient_final))
     low, high = ring(final[0, :, :, 0], final[1, :, :, 0])
-    act_two = pack_classes(second_block_preactivation)
-    late = pack_classes(first_block_preactivation, second_block_input, first_block_input)
-    final, act_two = lax.optimization_barrier((final, act_two))
-    act_two = swap_classes(act_two)
-    final, act_two = (final, 0), (act_two, 0)
+    act_two = (swap_classes(pack_classes(second_block_preactivation, after=[final])), 0)
+    final = (final, 0)
 
     halves = [coarse(2, chan)] * 2
     thirds = [coarse(1, chan), coarse(2, chan), coarse(1, chan)]
 
-    wide = [low, final, high]
-    pre = conv_two(wide, act_two, second_block_conv_two, 2, halves)
-    late, pre = lax.optimization_barrier((late, pre))
+    pre, wide = conv_two([low, final, high], act_two, second_block_conv_two, 2, halves)
+    late = pack_classes(first_block_preactivation, second_block_input, first_block_input, after=[low, high])
     late = swap_classes(late)
     act_one, entry_two, entry_one = (late, 0), (late, 1), (late, 2)
     low, high = ring(pre[0], pre[1])
     second_two = weight_grad(wide, act_two, 2, chan)
-    low, high, second_two = lax.optimization_barrier((low, high, second_two))
-    wide = [low, *pre, high]
-    mid = conv_one(wide, [final], second_block_conv_one, 2, thirds)
+    field = [low, *pre, high]
+    mid, wide = conv_one(field, [final], second_block_conv_one, 2, thirds, after=[second_two])
     low, high = ring(mid[0], mid[2])
     keep, got = weight_grad_split(wide, entry_two, 2, chan, second_two)
-    low, high, keep = lax.optimization_barrier((low, high, keep))
-    second = keep, got
-    wide = [low, *mid, high]
-    pre = conv_two(wide, act_one, first_block_conv_two, 1, thirds)
+    field = [low, *mid, high]
+    pre, wide = conv_two(field, act_one, first_block_conv_two, 1, thirds, after=[keep])
     low, high = ring(pre[0], pre[2])
     first_two = weight_grad(wide, act_one, 1, chan)
-    low, high, first_two = lax.optimization_barrier((low, high, first_two))
-    wide = [low, *pre, high]
+    own, sent = sum_plane(keep, got, after=[first_two])
     whole = [jax.ShapeDtypeStruct((2, 2, 2, 2, 2, 2, STRIDE, chan), BF16)]
-    out = conv_one(wide, mid, first_block_conv_one, 1, whole)[0]
-    out, wide[0] = lax.optimization_barrier((out, wide[0]))
-    first = weight_grad_split(wide, entry_one, 1, chan, first_two)
+    field = [low, *pre, high]
+    (out,), wide = conv_one(field, mid, first_block_conv_one, 1, whole, after=[own])
+    keep, got = weight_grad_split(wide, entry_one, 1, chan, first_two)
     out = gather_classes(out, height, breadth)
-    second_two, second_one = sum_weights(*second)
-    own, terms = sum_plane(*first)
-    out, terms = lax.optimization_barrier((out, terms))
-    first_two, first_one = spread_weights(sum_ring(own, terms), len(TAPS))
+    part = sum_ring(own, sent, after=[keep])
+    own, sent = sum_plane(keep, got)
+    second_two, second_one = spread_weights(part, len(TAPS))
+    part = sum_ring(own, sent, after=[out])
+    first_two, first_one = spread_weights(part, len(TAPS))
     return out, first_one, first_two, second_one, second_two
 
 

time: 175 us -> 156 us (0.89)
  local copies, waits for them, and re-layouts: 26.5 us -> 12.5 us
  blocking collectives: 0 us -> 13.9 us
  Pallas kernels: 28.4 us -> 21.2 us
  waiting for transfers between devices: 54.1 us -> 47.5 us
  starting transfers between devices: 62.7 us -> 58.7 us
    all_to_all x0 -> x1, blocking collectives: none -> 13.9 us  [swap_classes(): moved = lax.all_to_all(packed, PLANE, 0, 0)]
    all_to_all x3 -> x2, waiting for transfers between devices: 7.98 us -> 0.01 us  [swap_classes(): moved = lax.all_to_all(packed, PLANE, 0, 0)]
    pallas_call x19, Pallas kernels: 28.4 us -> 21.2 us  [call(): pl.pallas_call(lambda *refs: body(*refs[len(after):]), grid=(1,), out_sha...]
    unnamed x78 -> x42, local copies, waits for them, and re-layouts: 17.4 us -> 11.4 us
    all_to_all x3 -> x2, starting transfers between devices: 12.5 us -> 7.34 us  [swap_classes(): moved = lax.all_to_all(packed, PLANE, 0, 0)]
    ppermute x4, waiting for transfers between devices: 8.06 us -> 13 us  [ring(): lax.ppermute(right_edge, 'z', up)]
    pallas_call x2 -> x0, local copies, waits for them, and re-layouts: 4.28 us -> none  [call(): pl.pallas_call(body, grid=(1,), out_shape=outs, in_specs=specs, out_specs...]
    ppermute x34 -> x40, waiting for transfers between devices: 29 us -> 25.6 us  [xor(): return lax.ppermute(value, axis, [(i, i ^ k) for i in range(count)])]
  transfers between devices with their start and end apart: 46 -> 51, of which waited for: 19 -> 15; matrix products, arithmetic and copies ran while one was open for 6% -> 1% of each run, Pallas kernels for 12% -> 12%
where the time goes in v3:
time: 156 us; the launch traced here: 155 us
  starting transfers between devices  58.7 us (38%)
  waiting for transfers between devices  47.5 us (30%)
  Pallas kernels  21.2 us (14%)
  blocking collectives  13.9 us (9%)
  local copies, waits for them, and re-layouts  12.5 us (8%)
    ppermute x40, starting transfers between devices, xor(): return lax.ppermute(value, axis, [(i, i ^ k) for i in range(count)])  31.6 us
    ppermute x40, waiting for transfers between devices, xor(): return lax.ppermute(value, axis, [(i, i ^ k) for i in range(count)])  25.6 us
    pallas_call x19, Pallas kernels, call(): pl.pallas_call(lambda *refs: body(*refs[len(after):]), grid=(1,), out_sha...  21.2 us
    all_to_all x1, blocking collectives, swap_classes(): moved = lax.all_to_all(packed, PLANE, 0, 0)  13.9 us
    ppermute x4, waiting for transfers between devices, ring(): lax.ppermute(right_edge, 'z', up)  13 us
    unnamed x42, local copies, waits for them, and re-layouts  11.4 us
    ppermute x4, starting transfers between devices, ring(): lax.ppermute(left_edge, 'z', down)  11.3 us
    ppermute x4, waiting for transfers between devices, ring(): lax.ppermute(left_edge, 'z', down)  8.84 us
  transfers between devices with their start and end apart: 51, of which 15 were waited for; matrix products, arithmetic and copies ran while one was open for 1% of the time, Pallas kernels for 12%

profile of v3, /device:TPU:0, one launch (start us, length us, event | category | flops | bytes accessed | tf_op | source)
XLA Modules:
  0.0 154.9 jit_solution(18082262781050524361)
XLA Ops:
  0.7 1.1 copy-done.5
  1.8 13.9 %all_to_all.20 = bf16[8,1,2,2,2,16,192]{6,5,4,3,2,1,0:T(8,128)(2,1)S(1)} all-to-all(bf16[8,1,2,2,2,16,192]{6,5,4,3,2,1,0:T(8,128)(2,1)S(1)} %shard_map.128), channel_id=1, replica_groups=mesh['z'=4,'x'=2,'y'=2,'c'=2] {'x','y','c'}, dimensions={0} | all-to-all | bytes 786432 | tf_op jit(solution)/shard_map/all_to_all | solution.py:230
  15.7 0.8 shard_map.129
  16.5 3.5 %all-to-all-start.1 = ((bf16[8,1,2,2,2,16,192]{6,5,4,3,2,1,0:T(8,128)(2,1)}), bf16[8,1,2,2,2,16,192]{6,5,4,3,2,1,0:T(8,128)(2,1)S(1)}, u32[]{:S(2)}, u32[]{:S(2)}) async-start(bf16[8,1,2,2,2,16,192]{6,5,4,3,2,1,0:T(8,128)(2,1)} %shard_map.129), calls=%async_computation.1 | async-start | bytes 1048576 | tf_op jit(solution)/shard_map/all_to_all | solution.py:230
  20.0 1.6 %collective-permute-start = (bf16[2,2,2,2,2,16,192]{6,5,4,3,2,1,0:T(8,128)(2,1)S(1)}, bf16[2,2,2,2,2,16,192]{6,5,4,3,2,1,0:T(8,128)(2,1)S(1)}, u32[]{:S(2)}, u32[]{:S(2)}) collective-permute-start(bf16[2,2,2,2,2,16,192]{6,5,4,3,2,1,0:T(8,128)(2,1)S(1)} %bitcast.25), channel_id=1, source_target_pairs={{0,8},{8,16},{16,24},{24,0},{1,9},{9,17},{17,25},{25,1},{2,10},{10... | collective-permute-start | bytes 589832 | tf_op jit(solution)/shard_map/ppermute | solution.py:246
  21.7 2.2 %collective-permute-start.1 = (bf16[2,2,2,2,2,16,192]{6,5,4,3,2,1,0:T(8,128)(2,1)S(1)}, bf16[2,2,2,2,2,16,192]{6,5,4,3,2,1,0:T(8,128)(2,1)S(1)}, u32[]{:S(2)}, u32[]{:S(2)}) collective-permute-start(bf16[2,2,2,2,2,16,192]{6,5,4,3,2,1,0:T(8,128)(2,1)S(1)} %bitcast.24), channel_id=1, source_target_pairs={{8,0},{16,8},{24,16},{0,24},{9,1},{17,9},{25,17},{1,25},{10,2},{18... | collective-permute-start | bytes 589832 | tf_op jit(solution)/shard_map/ppermute | solution.py:246
  23.9 7.1 %collective-permute-done.refs_0_ = bf16[2,2,2,2,2,16,192]{6,5,4,3,2,1,0:T(8,128)(2,1)S(1)} collective-permute-done((bf16[2,2,2,2,2,16,192]{6,5,4,3,2,1,0:T(8,128)(2,1)S(1)}, bf16[2,2,2,2,2,16,192]{6,5,4,3,2,1,0:T(8,128)(2,1)S(1)}, u32[]{:S(2)}, u32[]{:S(2)}) %collective-permute-start) | collective-permute-done | bytes 196640 | tf_op jit(solution)/shard_map/ppermute | solution.py:246
  31.0 4.6 %collective-permute-done.1.refs_2_.refs_1_ = bf16[2,2,2,2,2,16,192]{6,5,4,3,2,1,0:T(8,128)(2,1)S(1)} collective-permute-done((bf16[2,2,2,2,2,16,192]{6,5,4,3,2,1,0:T(8,128)(2,1)S(1)}, bf16[2,2,2,2,2,16,192]{6,5,4,3,2,1,0:T(8,128)(2,1)S(1)}, u32[]{:S(2)}, u32[]{:S(2)}) %collective-permute-start.1) | collective-permute-done | bytes 196640 | tf_op jit(solution)/shard_map/ppermute | solution.py:246
  35.7 1.2 shard_map.133
  36.9 3.8 %all-to-all-start.2 = ((bf16[8,3,2,2,2,16,192]{6,5,4,3,2,1,0:T(8,128)(2,1)}), bf16[8,3,2,2,2,16,192]{6,5,4,3,2,1,0:T(8,128)(2,1)S(1)}, u32[]{:S(2)}, u32[]{:S(2)}) async-start(bf16[8,3,2,2,2,16,192]{6,5,4,3,2,1,0:T(8,128)(2,1)} %shard_map.133), calls=%async_computation.2 | async-start | bytes 3145728 | tf_op jit(solution)/shard_map/all_to_all | solution.py:230
  40.8 1.2 copy-done.13
  41.9 1.5 shard_map.130
  43.4 1.2 collective-permute-start.2
  44.6 2.7 %collective-permute-start.3 = (bf16[2,8,2,16,192]{4,3,2,1,0:T(8,128)(2,1)S(1)}, bf16[2,8,2,16,192]{4,3,2,1,0:T(8,128)(2,1)S(1)}, u32[]{:S(2)}, u32[]{:S(2)}) collective-permute-start(bf16[2,8,2,16,192]{4,3,2,1,0:T(8,128)(2,1)S(1)} %get-tuple-element.50.refs_2_), channel_id=1, source_target_pairs={{8,0},{16,8},{24,16},{0,24},{9,1},{17,9},{25,17},{1,25},{10,2},{18... | collective-permute-start | bytes 589832 | tf_op jit(solution)/shard_map/ppermute | solution.py:246
  47.3 1.2 shard_map.131.refs_0_.refs_2_
  48.5 5.9 %collective-permute-done.2.refs_1_ = bf16[2,8,2,16,192]{4,3,2,1,0:T(8,128)(2,1)S(1)} collective-permute-done((bf16[2,8,2,16,192]{4,3,2,1,0:T(8,128)(2,1)S(1)}, bf16[2,8,2,16,192]{4,3,2,1,0:T(8,128)(2,1)S(1)}, u32[]{:S(2)}, u32[]{:S(2)}) %collective-permute-start.2) | collective-permute-done | bytes 196640 | tf_op jit(solution)/shard_map/ppermute | solution.py:246
  54.4 4.2 %collective-permute-done.3.refs_4_ = bf16[2,8,2,16,192]{4,3,2,1,0:T(8,128)(2,1)S(1)} collective-permute-done((bf16[2,8,2,16,192]{4,3,2,1,0:T(8,128)(2,1)S(1)}, bf16[2,8,2,16,192]{4,3,2,1,0:T(8,128)(2,1)S(1)}, u32[]{:S(2)}, u32[]{:S(2)}) %collective-permute-start.3) | collective-permute-done | bytes 196640 | tf_op jit(solution)/shard_map/ppermute | solution.py:246
  58.7 1.4 shard_map.132
  60.1 1.1 copy-done.19
  61.2 0.7 collective-permute-start.4
  62.0 3.1 %collective-permute-start.5 = (bf16[1,8,2,16,192]{4,3,2,1,0:T(8,128)(2,1)S(1)}, bf16[1,8,2,16,192]{4,3,2,1,0:T(8,128)(2,1)S(1)}, u32[]{:S(2)}, u32[]{:S(2)}) collective-permute-start(bf16[1,8,2,16,192]{4,3,2,1,0:T(8,128)(2,1)S(1)} %get-tuple-element.54.refs_2_.refs_6_), channel_id=1, source_target_pairs={{8,0},{16,8},{24,16},{0,24},{9,1},{17,9},{25,17},{1,25},{10,2},{18... | collective-permute-start | bytes 294920 | tf_op jit(solution)/shard_map/ppermute | solution.py:246
  65.1 1.5 copy-done.18
  66.6 1.4 copy-done.20
  68.0 1.3 shard_map.134
  70.4 1.5 shard_map.135
  72.6 3.2 %collective-permute-start.11 = (bf16[1,8,2,16,192]{4,3,2,1,0:T(8,128)(2,1)S(1)}, bf16[1,8,2,16,192]{4,3,2,1,0:T(8,128)(2,1)S(1)}, u32[]{:S(2)}, u32[]{:S(2)}) collective-permute-start(bf16[1,8,2,16,192]{4,3,2,1,0:T(8,128)(2,1)S(1)} %get-tuple-element.63.refs_2_), channel_id=1, source_target_pairs={{8,0},{16,8},{24,16},{0,24},{9,1},{17,9},{25,17},{1,25},{10,2},{18... | collective-permute-start | bytes 294920 | tf_op jit(solution)/shard_map/ppermute | solution.py:246
  75.8 1.2 shard_map.136.refs_0_.refs_2_
  77.1 0.8 shard_map.137
  77.9 1.7 %collective-permute-start.32 = (bf16[4,112,192]{2,1,0:T(8,128)(2,1)S(1)}, bf16[4,112,192]{2,1,0:T(8,128)(2,1)S(1)}, u32[]{:S(2)}, u32[]{:S(2)}) collective-permute-start(bf16[4,112,192]{2,1,0:T(8,128)(2,1)S(1)} %get-tuple-element.82), channel_id=1, source_target_pairs={{0,2},{2,0},{4,6},{6,4},{1,3},{3,1},{5,7},{7,5},{8,10},{10,8},{12,... | collective-permute-start | bytes 516104 | tf_op jit(solution)/shard_map/ppermute | solution.py:251
  79.6 1.5 collective-permute-start.33
  81.4 1.4 shard_map.138
  82.9 0.8 copy-done.6
  83.6 2.3 %shard_map.139 = (f32[4,4,112,192]{3,2,1,0:T(8,128)S(1)}, bf16[4,112,192]{2,1,0:T(8,128)(2,1)}, bf16[4,112,192]{2,1,0:T(8,128)(2,1)}, bf16[4,112,192]{2,1,0:T(8,128)(2,1)}, bf16[4,112,192]{2,1,0:T(8,128)(2,1)}) custom-call(bf16[6,10,2,16,192]{4,3,2,1,0:T(8,128)(2,1)S(1)} %get-tuple-element.66.refs_0_, ...), custom_call_target="tpu_custom_call" | custom-call | flops 13589544960 | bytes 4571136 | tf_op jit(solution)/shard_map/pallas_call | solution.py:33
  87.1 1.0 collective-permute-done.33.refs_3_
  88.8 4.3 %all-to-all-start.3 = ((bf16[8,2,2,2,16,192]{5,4,3,2,1,0:T(8,128)(2,1)}), bf16[8,2,2,2,16,192]{5,4,3,2,1,0:T(8,128)(2,1)}, u32[]{:S(2)}, u32[]{:S(2)}) async-start(bf16[8,2,2,2,16,192]{5,4,3,2,1,0:T(8,128)(2,1)} %bitcast.21), calls=%async_computation.3 | async-start | bytes 1048576 | tf_op jit(solution)/shard_map/all_to_all | solution.py:238
  93.2 1.0 copy-done.8
  94.2 0.9 copy-done.10
  95.1 0.9 copy-done.12
  96.1 1.0 shard_map.144
  97.2 1.5 collective-permute-start.36
  98.7 2.9 %collective-permute-start.37 = (bf16[112,192]{1,0:T(8,128)(2,1)S(1)}, bf16[112,192]{1,0:T(8,128)(2,1)S(1)}, u32[]{:S(2)}, u32[]{:S(2)}) collective-permute-start(bf16[112,192]{1,0:T(8,128)(2,1)S(1)} %get-tuple-element.88), channel_id=1, source_target_pairs={{0,24},{8,16},{16,8},{24,0},{1,25},{9,17},{17,9},{25,1},{2,26},{10... | collective-permute-start | bytes 129032 | tf_op jit(solution)/shard_map/ppermute | solution.py:251
  101.6 0.9 shard_map.140
  102.5 1.7 %collective-permute-start.16 = (bf16[4,112,192]{2,1,0:T(8,128)(2,1)}, bf16[4,112,192]{2,1,0:T(8,128)(2,1)S(1)}, u32[]{:S(2)}, u32[]{:S(2)}) collective-permute-start(bf16[4,112,192]{2,1,0:T(8,128)(2,1)} %get-tuple-element.73), channel_id=1, source_target_pairs={{0,2},{2,0},{4,6},{6,4},{1,3},{3,1},{5,7},{7,5},{8,10},{10,8},{12,... | collective-permute-start | bytes 516104 | tf_op jit(solution)/shard_map/ppermute | solution.py:251
  104.2 1.5 collective-permute-start.17
  106.1 1.6 %collective-permute-start.40 = (bf16[112,192]{1,0:T(8,128)(2,1)S(1)}, bf16[112,192]{1,0:T(8,128)(2,1)S(1)}, u32[]{:S(2)}, u32[]{:S(2)}) collective-permute-start(bf16[112,192]{1,0:T(8,128)(2,1)S(1)} %add_convert_fusion.refs_0_), channel_id=1, source_target_pairs={{0,24},{8,16},{16,8},{24,0},{1,25},{9,17},{17,9},{25,1},{2,26},{10... | collective-permute-start | bytes 129032 | tf_op jit(solution)/shard_map/ppermute | solution.py:251
  108.3 1.1 copy.15
  109.4 1.0 collective-permute-done.16.refs_2_
  110.4 1.3 collective-permute-start.38
  111.7 1.3 collective-permute-done.17.refs_3_
  113.0 3.0 %collective-permute-done.18.refs_4_ = bf16[4,112,192]{2,1,0:T(8,128)(2,1)S(1)} collective-permute-done((bf16[4,112,192]{2,1,0:T(8,128)(2,1)}, bf16[4,112,192]{2,1,0:T(8,128)(2,1)S(1)}, u32[]{:S(2)}, u32[]{:S(2)}) %collective-permute-start.18) | collective-permute-done | bytes 172064 | tf_op jit(solution)/shard_map/ppermute | solution.py:251
  116.1 1.2 collective-permute-start.20
  117.4 3.2 %collective-permute-start.21 = (bf16[112,192]{1,0:T(8,128)(2,1)S(1)}, bf16[112,192]{1,0:T(8,128)(2,1)S(1)}, u32[]{:S(2)}, u32[]{:S(2)}) collective-permute-start(bf16[112,192]{1,0:T(8,128)(2,1)S(1)} %get-tuple-element.79), channel_id=1, source_target_pairs={{0,24},{8,16},{16,8},{24,0},{1,25},{9,17},{17,9},{25,1},{2,26},{10... | collective-permute-start | bytes 129032 | tf_op jit(solution)/shard_map/ppermute | solution.py:251
  120.6 2.4 %collective-permute-start.43 = (bf16[4,112,192]{2,1,0:T(8,128)(2,1)S(1)}, bf16[4,112,192]{2,1,0:T(8,128)(2,1)S(1)}, u32[]{:S(2)}, u32[]{:S(2)}) collective-permute-start(bf16[4,112,192]{2,1,0:T(8,128)(2,1)S(1)} %shard_map.145.refs_0_), channel_id=1, source_target_pairs={{0,6},{2,4},{4,2},{6,0},{1,7},{3,5},{5,3},{7,1},{8,14},{10,12},{12... | collective-permute-start | bytes 516104 | tf_op jit(solution)/shard_map/ppermute | solution.py:251
  123.6 0.9 collective-permute-start.41
  124.5 2.1 %collective-permute-start.24 = (bf16[112,192]{1,0:T(8,128)(2,1)S(1)}, bf16[112,192]{1,0:T(8,128)(2,1)S(1)}, u32[]{:S(2)}, u32[]{:S(2)}) collective-permute-start(bf16[112,192]{1,0:T(8,128)(2,1)S(1)} %add_convert_fusion.1.refs_0_), channel_id=1, source_target_pairs={{0,24},{8,16},{16,8},{24,0},{1,25},{9,17},{17,9},{25,1},{2,26},{10... | collective-permute-start | bytes 129032 | tf_op jit(solution)/shard_map/ppermute | solution.py:251
  126.6 4.1 %collective-permute-done.24.refs_3_ = bf16[112,192]{1,0:T(8,128)(2,1)S(1)} collective-permute-done((bf16[112,192]{1,0:T(8,128)(2,1)S(1)}, bf16[112,192]{1,0:T(8,128)(2,1)S(1)}, u32[]{:S(2)}, u32[]{:S(2)}) %collective-permute-start.24) | collective-permute-done | bytes 43040 | tf_op jit(solution)/shard_map/ppermute | solution.py:251
  130.7 5.1 %collective-permute-done.23.refs_2_ = bf16[112,192]{1,0:T(8,128)(2,1)S(1)} collective-permute-done((bf16[112,192]{1,0:T(8,128)(2,1)S(1)}, bf16[112,192]{1,0:T(8,128)(2,1)S(1)}, u32[]{:S(2)}, u32[]{:S(2)}) %collective-permute-start.23) | collective-permute-done | bytes 43040 | tf_op jit(solution)/shard_map/ppermute | solution.py:251
  135.9 4.2 %collective-permute-done.22.refs_1_ = bf16[112,192]{1,0:T(8,128)(2,1)S(1)} collective-permute-done((bf16[112,192]{1,0:T(8,128)(2,1)S(1)}, bf16[112,192]{1,0:T(8,128)(2,1)S(1)}, u32[]{:S(2)}, u32[]{:S(2)}) %collective-permute-start.22) | collective-permute-done | bytes 43040 | tf_op jit(solution)/shard_map/ppermute | solution.py:251
  140.1 1.9 %collective-permute-start.27 = (bf16[4,112,192]{2,1,0:T(8,128)(2,1)S(1)}, bf16[4,112,192]{2,1,0:T(8,128)(2,1)S(1)}, u32[]{:S(2)}, u32[]{:S(2)}) collective-permute-start(bf16[4,112,192]{2,1,0:T(8,128)(2,1)S(1)} %shard_map.142.refs_0_), channel_id=1, source_target_pairs={{0,6},{2,4},{4,2},{6,0},{1,7},{3,5},{5,3},{7,1},{8,14},{10,12},{12... | collective-permute-start | bytes 516104 | tf_op jit(solution)/shard_map/ppermute | solution.py:251
  142.5 1.1 collective-permute-start.25
  144.1 3.2 %collective-permute-done.27.refs_3_ = bf16[4,112,192]{2,1,0:T(8,128)(2,1)S(1)} collective-permute-done((bf16[4,112,192]{2,1,0:T(8,128)(2,1)S(1)}, bf16[4,112,192]{2,1,0:T(8,128)(2,1)S(1)}, u32[]{:S(2)}, u32[]{:S(2)}) %collective-permute-start.27) | collective-permute-done | bytes 172064 | tf_op jit(solution)/shard_map/ppermute | solution.py:251
  147.3 1.8 %collective-permute-done.26.refs_2_ = bf16[4,112,192]{2,1,0:T(8,128)(2,1)S(1)} collective-permute-done((bf16[4,112,192]{2,1,0:T(8,128)(2,1)S(1)}, bf16[4,112,192]{2,1,0:T(8,128)(2,1)S(1)}, u32[]{:S(2)}, u32[]{:S(2)}) %collective-permute-start.26) | collective-permute-done | bytes 172064 | tf_op jit(solution)/shard_map/ppermute | solution.py:251
  150.6 2.1 %shard_map.146 = (f32[1728,192]{1,0:T(8,128)}, f32[1728,192]{1,0:T(8,128)}) custom-call(bf16[4,112,192]{2,1,0:T(8,128)(2,1)S(1)} %shard_map.145.refs_0_, bf16[4,112,192]{2,1,0:T(8,128)(2,1)S(1)} %collective-permute-done.41.refs_1_, bf16[4,112,192]{2,1,0:T(8,128)(2,1)S(1)} %collective-permute-done.42.refs_2_, ...), custom_call_target="tpu_custom_call" | custom-call | bytes 4030464 | tf_op jit(solution)/shard_map/pallas_call | solution.py:33
  152.8 2.1 %shard_map.143 = (f32[1728,192]{1,0:T(8,128)}, f32[1728,192]{1,0:T(8,128)}) custom-call(bf16[4,112,192]{2,1,0:T(8,128)(2,1)S(1)} %shard_map.142.refs_0_, bf16[4,112,192]{2,1,0:T(8,128)(2,1)S(1)} %collective-permute-done.25.refs_1_, bf16[4,112,192]{2,1,0:T(8,128)(2,1)S(1)} %collective-permute-done.26.refs_2_, ...), custom_call_target="tpu_custom_call" | custom-call | bytes 4030464 | tf_op jit(solution)/shard_map/pallas_call | solution.py:33
  (104 shorter events, 8.6 us)
Async XLA Ops:
  0.6 15.0 %copy-start.1 = (bf16[32,32,192]{2,1,0:T(8,128)(2,1)S(1)}, bf16[32,32,192]{2,1,0:T(8,128)(2,1)}, u32[]{:S(2)}) copy-start(bf16[32,32,192]{2,1,0:T(8,128)(2,1)} %refs_1_.1) | copy-start | bytes 1179652
  15.7 20.0 %copy-start.2 = (bf16[32,32,192]{2,1,0:T(8,128)(2,1)S(1)}, bf16[32,32,192]{2,1,0:T(8,128)(2,1)}, u32[]{:S(2)}) copy-start(bf16[32,32,192]{2,1,0:T(8,128)(2,1)} %refs_2_.1) | copy-start | bytes 1179652
  15.7 20.0 %copy-start.3 = (bf16[32,32,192]{2,1,0:T(8,128)(2,1)S(1)}, bf16[32,32,192]{2,1,0:T(8,128)(2,1)}, u32[]{:S(2)}) copy-start(bf16[32,32,192]{2,1,0:T(8,128)(2,1)} %refs_3_.1) | copy-start | bytes 1179652
  15.7 20.0 %copy-start.4 = (bf16[32,32,192]{2,1,0:T(8,128)(2,1)S(1)}, bf16[32,32,192]{2,1,0:T(8,128)(2,1)}, u32[]{:S(2)}) copy-start(bf16[32,32,192]{2,1,0:T(8,128)(2,1)} %refs_4_.3) | copy-start | bytes 1179652
  16.5 20.4 %all-to-all-start.1 = ((bf16[8,1,2,2,2,16,192]{6,5,4,3,2,1,0:T(8,128)(2,1)}), bf16[8,1,2,2,2,16,192]{6,5,4,3,2,1,0:T(8,128)(2,1)S(1)}, u32[]{:S(2)}, u32[]{:S(2)}) async-start(bf16[8,1,2,2,2,16,192]{6,5,4,3,2,1,0:T(8,128)(2,1)} %shard_map.129), calls=%async_computation.1 | async-start | bytes 1048576 | tf_op jit(solution)/shard_map/all_to_all | solution.py:230
  20.0 11.0 %collective-permute-start = (bf16[2,2,2,2,2,16,192]{6,5,4,3,2,1,0:T(8,128)(2,1)S(1)}, bf16[2,2,2,2,2,16,192]{6,5,4,3,2,1,0:T(8,128)(2,1)S(1)}, u32[]{:S(2)}, u32[]{:S(2)}) collective-permute-start(bf16[2,2,2,2,2,16,192]{6,5,4,3,2,1,0:T(8,128)(2,1)S(1)} %bitcast.25), channel_id=1, source_target_pairs={{0,8},{8,16},{16,24},{24,0},{1,9},{9,17},{17,25},{25,1},{2,10},{10... | collective-permute-start | bytes 589832 | tf_op jit(solution)/shard_map/ppermute | solution.py:246
  21.7 14.0 %collective-permute-start.1 = (bf16[2,2,2,2,2,16,192]{6,5,4,3,2,1,0:T(8,128)(2,1)S(1)}, bf16[2,2,2,2,2,16,192]{6,5,4,3,2,1,0:T(8,128)(2,1)S(1)}, u32[]{:S(2)}, u32[]{:S(2)}) collective-permute-start(bf16[2,2,2,2,2,16,192]{6,5,4,3,2,1,0:T(8,128)(2,1)S(1)} %bitcast.24), channel_id=1, source_target_pairs={{8,0},{16,8},{24,16},{0,24},{9,1},{17,9},{25,17},{1,25},{10,2},{18... | collective-permute-start | bytes 589832 | tf_op jit(solution)/shard_map/ppermute | solution.py:246
  36.9 28.2 %all-to-all-start.2 = ((bf16[8,3,2,2,2,16,192]{6,5,4,3,2,1,0:T(8,128)(2,1)}), bf16[8,3,2,2,2,16,192]{6,5,4,3,2,1,0:T(8,128)(2,1)S(1)}, u32[]{:S(2)}, u32[]{:S(2)}) async-start(bf16[8,3,2,2,2,16,192]{6,5,4,3,2,1,0:T(8,128)(2,1)} %shard_map.133), calls=%async_computation.2 | async-start | bytes 3145728 | tf_op jit(solution)/shard_map/all_to_all | solution.py:230
  40.8 1.2 copy-start.13
  43.4 11.0 %collective-permute-start.2 = (bf16[2,8,2,16,192]{4,3,2,1,0:T(8,128)(2,1)S(1)}, bf16[2,8,2,16,192]{4,3,2,1,0:T(8,128)(2,1)S(1)}, u32[]{:S(2)}, u32[]{:S(2)}) collective-permute-start(bf16[2,8,2,16,192]{4,3,2,1,0:T(8,128)(2,1)S(1)} %get-tuple-element.49.refs_3_), channel_id=1, source_target_pairs={{0,8},{8,16},{16,24},{24,0},{1,9},{9,17},{17,25},{25,1},{2,10},{10... | collective-permute-start | bytes 589832 | tf_op jit(solution)/shard_map/ppermute | solution.py:246
  44.6 14.1 %collective-permute-start.3 = (bf16[2,8,2,16,192]{4,3,2,1,0:T(8,128)(2,1)S(1)}, bf16[2,8,2,16,192]{4,3,2,1,0:T(8,128)(2,1)S(1)}, u32[]{:S(2)}, u32[]{:S(2)}) collective-permute-start(bf16[2,8,2,16,192]{4,3,2,1,0:T(8,128)(2,1)S(1)} %get-tuple-element.50.refs_2_), channel_id=1, source_target_pairs={{8,0},{16,8},{24,16},{0,24},{9,1},{17,9},{25,17},{1,25},{10,2},{18... | collective-permute-start | bytes 589832 | tf_op jit(solution)/shard_map/ppermute | solution.py:246
  47.3 11.4 %copy-start.14 = (bf16[9,192,192]{2,1,0:T(8,128)(2,1)S(1)}, bf16[9,192,192]{2,1,0:T(8,128)(2,1)}, u32[]{:S(2)}) copy-start(bf16[9,192,192]{2,1,0:T(8,128)(2,1)} %refs_6_.1) | copy-start | bytes 1990660
  48.5 11.6 %copy-start.17 = (f32[1792,192]{1,0:T(8,128)}, f32[1792,192]{1,0:T(8,128)S(1)}, u32[]{:S(2)}) copy-start(f32[1792,192]{1,0:T(8,128)S(1)} %shard_map.131.refs_0_.refs_2_) | copy-start | bytes 4128772
  61.2 8.8 %collective-permute-start.4 = (bf16[1,8,2,16,192]{4,3,2,1,0:T(8,128)(2,1)S(1)}, bf16[1,8,2,16,192]{4,3,2,1,0:T(8,128)(2,1)S(1)}, u32[]{:S(2)}, u32[]{:S(2)}) collective-permute-start(bf16[1,8,2,16,192]{4,3,2,1,0:T(8,128)(2,1)S(1)} %get-tuple-element.53.refs_4_.refs_8_), channel_id=1, source_target_pairs={{0,8},{8,16},{16,24},{24,0},{1,9},{9,17},{17,25},{25,1},{2,10},{10... | collective-permute-start | bytes 294920 | tf_op jit(solution)/shard_map/ppermute | solution.py:246
  62.0 8.4 %collective-permute-start.5 = (bf16[1,8,2,16,192]{4,3,2,1,0:T(8,128)(2,1)S(1)}, bf16[1,8,2,16,192]{4,3,2,1,0:T(8,128)(2,1)S(1)}, u32[]{:S(2)}, u32[]{:S(2)}) collective-permute-start(bf16[1,8,2,16,192]{4,3,2,1,0:T(8,128)(2,1)S(1)} %get-tuple-element.54.refs_2_.refs_6_), channel_id=1, source_target_pairs={{8,0},{16,8},{24,16},{0,24},{9,1},{17,9},{25,17},{1,25},{10,2},{18... | collective-permute-start | bytes 294920 | tf_op jit(solution)/shard_map/ppermute | solution.py:246
  65.1 1.5 copy-start.18
  66.6 1.4 copy-start.20
  68.0 2.5 %copy-start.15 = (bf16[9,192,192]{2,1,0:T(8,128)(2,1)S(1)}, bf16[9,192,192]{2,1,0:T(8,128)(2,1)}, u32[]{:S(2)}) copy-start(bf16[9,192,192]{2,1,0:T(8,128)(2,1)} %refs_7_.1) | copy-start | bytes 1990660
  69.3 3.2 %collective-permute-start.6 = (bf16[4,112,192]{2,1,0:T(8,128)(2,1)S(1)}, bf16[4,112,192]{2,1,0:T(8,128)(2,1)S(1)}, u32[]{:S(2)}, u32[]{:S(2)}) collective-permute-start(bf16[4,112,192]{2,1,0:T(8,128)(2,1)S(1)} %get-tuple-element.57), channel_id=1, source_target_pairs={{0,1},{1,0},{2,3},{3,2},{4,5},{5,4},{6,7},{7,6},{8,9},{9,8},{10,11... | collective-permute-start | bytes 516104 | tf_op jit(solution)/shard_map/ppermute | solution.py:251
  69.4 7.6 %collective-permute-start.7 = (bf16[4,112,192]{2,1,0:T(8,128)(2,1)S(1)}, bf16[4,112,192]{2,1,0:T(8,128)(2,1)S(1)}, u32[]{:S(2)}, u32[]{:S(2)}) collective-permute-start(bf16[4,112,192]{2,1,0:T(8,128)(2,1)S(1)} %get-tuple-element.58), channel_id=1, source_target_pairs={{0,1},{1,0},{2,3},{3,2},{4,5},{5,4},{6,7},{7,6},{8,9},{9,8},{10,11... | collective-permute-start | bytes 516104 | tf_op jit(solution)/shard_map/ppermute | solution.py:251
  69.9 7.1 %collective-permute-start.8 = (bf16[4,112,192]{2,1,0:T(8,128)(2,1)S(1)}, bf16[4,112,192]{2,1,0:T(8,128)(2,1)S(1)}, u32[]{:S(2)}, u32[]{:S(2)}) collective-permute-start(bf16[4,112,192]{2,1,0:T(8,128)(2,1)S(1)} %get-tuple-element.59), channel_id=1, source_target_pairs={{0,1},{1,0},{2,3},{3,2},{4,5},{5,4},{6,7},{7,6},{8,9},{9,8},{10,11... | collective-permute-start | bytes 516104 | tf_op jit(solution)/shard_map/ppermute | solution.py:251
  70.0 7.1 %collective-permute-start.9 = (bf16[4,112,192]{2,1,0:T(8,128)(2,1)S(1)}, bf16[4,112,192]{2,1,0:T(8,128)(2,1)S(1)}, u32[]{:S(2)}, u32[]{:S(2)}) collective-permute-start(bf16[4,112,192]{2,1,0:T(8,128)(2,1)S(1)} %get-tuple-element.60), channel_id=1, source_target_pairs={{0,1},{1,0},{2,3},{3,2},{4,5},{5,4},{6,7},{7,6},{8,9},{9,8},{10,11... | collective-permute-start | bytes 516104 | tf_op jit(solution)/shard_map/ppermute | solution.py:251
  71.9 9.5 %collective-permute-start.10 = (bf16[1,8,2,16,192]{4,3,2,1,0:T(8,128)(2,1)S(1)}, bf16[1,8,2,16,192]{4,3,2,1,0:T(8,128)(2,1)S(1)}, u32[]{:S(2)}, u32[]{:S(2)}) collective-permute-start(bf16[1,8,2,16,192]{4,3,2,1,0:T(8,128)(2,1)S(1)} %get-tuple-element.62.refs_4_), channel_id=1, source_target_pairs={{0,8},{8,16},{16,24},{24,0},{1,9},{9,17},{17,25},{25,1},{2,10},{10... | collective-permute-start | bytes 294920 | tf_op jit(solution)/shard_map/ppermute | solution.py:246
  72.6 8.8 %collective-permute-start.11 = (bf16[1,8,2,16,192]{4,3,2,1,0:T(8,128)(2,1)S(1)}, bf16[1,8,2,16,192]{4,3,2,1,0:T(8,128)(2,1)S(1)}, u32[]{:S(2)}, u32[]{:S(2)}) collective-permute-start(bf16[1,8,2,16,192]{4,3,2,1,0:T(8,128)(2,1)S(1)} %get-tuple-element.63.refs_2_), channel_id=1, source_target_pairs={{8,0},{16,8},{24,16},{0,24},{9,1},{17,9},{25,17},{1,25},{10,2},{18... | collective-permute-start | bytes 294920 | tf_op jit(solution)/shard_map/ppermute | solution.py:246
  77.0 4.4 %copy-start.16 = (bf16[9,192,192]{2,1,0:T(8,128)(2,1)S(1)}, bf16[9,192,192]{2,1,0:T(8,128)(2,1)}, u32[]{:S(2)}) copy-start(bf16[9,192,192]{2,1,0:T(8,128)(2,1)} %refs_9_.1) | copy-start | bytes 1990660
  77.9 4.9 %copy-start.7 = (f32[4,112,192]{2,1,0:T(8,128)}, f32[4,112,192]{2,1,0:T(8,128)S(1)}, u32[]{:S(2)}) copy-start(f32[4,112,192]{2,1,0:T(8,128)S(1)} %get-tuple-element.61.refs_0_.refs_1_) | copy-start | bytes 1032196
  77.9 8.5 %collective-permute-start.32 = (bf16[4,112,192]{2,1,0:T(8,128)(2,1)S(1)}, bf16[4,112,192]{2,1,0:T(8,128)(2,1)S(1)}, u32[]{:S(2)}, u32[]{:S(2)}) collective-permute-start(bf16[4,112,192]{2,1,0:T(8,128)(2,1)S(1)} %get-tuple-element.82), channel_id=1, source_target_pairs={{0,2},{2,0},{4,6},{6,4},{1,3},{3,1},{5,7},{7,5},{8,10},{10,8},{12,... | collective-permute-start | bytes 516104 | tf_op jit(solution)/shard_map/ppermute | solution.py:251
  79.6 8.5 %collective-permute-start.33 = (bf16[4,112,192]{2,1,0:T(8,128)(2,1)S(1)}, bf16[4,112,192]{2,1,0:T(8,128)(2,1)S(1)}, u32[]{:S(2)}, u32[]{:S(2)}) collective-permute-start(bf16[4,112,192]{2,1,0:T(8,128)(2,1)S(1)} %get-tuple-element.83), channel_id=1, source_target_pairs={{0,4},{2,6},{4,0},{6,2},{1,5},{3,7},{5,1},{7,3},{8,12},{10,14},{12... | collective-permute-start | bytes 516104 | tf_op jit(solution)/shard_map/ppermute | solution.py:251
  81.0 12.1 %collective-permute-start.34 = (bf16[4,112,192]{2,1,0:T(8,128)(2,1)}, bf16[4,112,192]{2,1,0:T(8,128)(2,1)}, u32[]{:S(2)}, u32[]{:S(2)}) collective-permute-start(bf16[4,112,192]{2,1,0:T(8,128)(2,1)} %get-tuple-element.84), channel_id=1, source_target_pairs={{0,6},{2,4},{4,2},{6,0},{1,7},{3,5},{5,3},{7,1},{8,14},{10,12},{12... | collective-permute-start | bytes 516104 | tf_op jit(solution)/shard_map/ppermute | solution.py:251
  85.9 11.3 %collective-permute-start.12 = (bf16[4,112,192]{2,1,0:T(8,128)(2,1)}, bf16[4,112,192]{2,1,0:T(8,128)(2,1)S(1)}, u32[]{:S(2)}, u32[]{:S(2)}) collective-permute-start(bf16[4,112,192]{2,1,0:T(8,128)(2,1)} %get-tuple-element.68), channel_id=1, source_target_pairs={{0,1},{1,0},{2,3},{3,2},{4,5},{5,4},{6,7},{7,6},{8,9},{9,8},{10,11... | collective-permute-start | bytes 516104 | tf_op jit(solution)/shard_map/ppermute | solution.py:251
  85.9 12.8 %collective-permute-start.13 = (bf16[4,112,192]{2,1,0:T(8,128)(2,1)}, bf16[4,112,192]{2,1,0:T(8,128)(2,1)S(1)}, u32[]{:S(2)}, u32[]{:S(2)}) collective-permute-start(bf16[4,112,192]{2,1,0:T(8,128)(2,1)} %get-tuple-element.69), channel_id=1, source_target_pairs={{0,1},{1,0},{2,3},{3,2},{4,5},{5,4},{6,7},{7,6},{8,9},{9,8},{10,11... | collective-permute-start | bytes 516104 | tf_op jit(solution)/shard_map/ppermute | solution.py:251
  87.1 14.4 %collective-permute-start.14 = (bf16[4,112,192]{2,1,0:T(8,128)(2,1)}, bf16[4,112,192]{2,1,0:T(8,128)(2,1)S(1)}, u32[]{:S(2)}, u32[]{:S(2)}) collective-permute-start(bf16[4,112,192]{2,1,0:T(8,128)(2,1)} %get-tuple-element.70), channel_id=1, source_target_pairs={{0,1},{1,0},{2,3},{3,2},{4,5},{5,4},{6,7},{7,6},{8,9},{9,8},{10,11... | collective-permute-start | bytes 516104 | tf_op jit(solution)/shard_map/ppermute | solution.py:251
  88.8 12.8 %collective-permute-start.15 = (bf16[4,112,192]{2,1,0:T(8,128)(2,1)}, bf16[4,112,192]{2,1,0:T(8,128)(2,1)S(1)}, u32[]{:S(2)}, u32[]{:S(2)}) collective-permute-start(bf16[4,112,192]{2,1,0:T(8,128)(2,1)} %get-tuple-element.71), channel_id=1, source_target_pairs={{0,1},{1,0},{2,3},{3,2},{4,5},{5,4},{6,7},{7,6},{8,9},{9,8},{10,11... | collective-permute-start | bytes 516104 | tf_op jit(solution)/shard_map/ppermute | solution.py:251
  88.8 19.4 %all-to-all-start.3 = ((bf16[8,2,2,2,16,192]{5,4,3,2,1,0:T(8,128)(2,1)}), bf16[8,2,2,2,16,192]{5,4,3,2,1,0:T(8,128)(2,1)}, u32[]{:S(2)}, u32[]{:S(2)}) async-start(bf16[8,2,2,2,16,192]{5,4,3,2,1,0:T(8,128)(2,1)} %bitcast.21), calls=%async_computation.3 | async-start | bytes 1048576 | tf_op jit(solution)/shard_map/all_to_all | solution.py:238
  97.1 8.6 %collective-permute-start.35 = (bf16[112,192]{1,0:T(8,128)(2,1)S(1)}, bf16[112,192]{1,0:T(8,128)(2,1)S(1)}, u32[]{:S(2)}, u32[]{:S(2)}) collective-permute-start(bf16[112,192]{1,0:T(8,128)(2,1)S(1)} %get-tuple-element.86), channel_id=1, source_target_pairs={{0,8},{8,0},{16,24},{24,16},{1,9},{9,1},{17,25},{25,17},{2,10},{10... | collective-permute-start | bytes 129032 | tf_op jit(solution)/shard_map/ppermute | solution.py:251
  97.2 8.8 %collective-permute-start.36 = (bf16[112,192]{1,0:T(8,128)(2,1)S(1)}, bf16[112,192]{1,0:T(8,128)(2,1)S(1)}, u32[]{:S(2)}, u32[]{:S(2)}) collective-permute-start(bf16[112,192]{1,0:T(8,128)(2,1)S(1)} %get-tuple-element.87), channel_id=1, source_target_pairs={{0,16},{8,24},{16,0},{24,8},{1,17},{9,25},{17,1},{25,9},{2,18},{10... | collective-permute-start | bytes 129032 | tf_op jit(solution)/shard_map/ppermute | solution.py:251
  98.7 7.3 %collective-permute-start.37 = (bf16[112,192]{1,0:T(8,128)(2,1)S(1)}, bf16[112,192]{1,0:T(8,128)(2,1)S(1)}, u32[]{:S(2)}, u32[]{:S(2)}) collective-permute-start(bf16[112,192]{1,0:T(8,128)(2,1)S(1)} %get-tuple-element.88), channel_id=1, source_target_pairs={{0,24},{8,16},{16,8},{24,0},{1,25},{9,17},{17,9},{25,1},{2,26},{10... | collective-permute-start | bytes 129032 | tf_op jit(solution)/shard_map/ppermute | solution.py:251
  102.5 7.8 %collective-permute-start.16 = (bf16[4,112,192]{2,1,0:T(8,128)(2,1)}, bf16[4,112,192]{2,1,0:T(8,128)(2,1)S(1)}, u32[]{:S(2)}, u32[]{:S(2)}) collective-permute-start(bf16[4,112,192]{2,1,0:T(8,128)(2,1)} %get-tuple-element.73), channel_id=1, source_target_pairs={{0,2},{2,0},{4,6},{6,4},{1,3},{3,1},{5,7},{7,5},{8,10},{10,8},{12,... | collective-permute-start | bytes 516104 | tf_op jit(solution)/shard_map/ppermute | solution.py:251
  104.2 8.8 %collective-permute-start.17 = (bf16[4,112,192]{2,1,0:T(8,128)(2,1)}, bf16[4,112,192]{2,1,0:T(8,128)(2,1)S(1)}, u32[]{:S(2)}, u32[]{:S(2)}) collective-permute-start(bf16[4,112,192]{2,1,0:T(8,128)(2,1)} %get-tuple-element.74), channel_id=1, source_target_pairs={{0,4},{2,6},{4,0},{6,2},{1,5},{3,7},{5,1},{7,3},{8,12},{10,14},{12... | collective-permute-start | bytes 516104 | tf_op jit(solution)/shard_map/ppermute | solution.py:251
  105.7 10.2 %collective-permute-start.18 = (bf16[4,112,192]{2,1,0:T(8,128)(2,1)}, bf16[4,112,192]{2,1,0:T(8,128)(2,1)S(1)}, u32[]{:S(2)}, u32[]{:S(2)}) collective-permute-start(bf16[4,112,192]{2,1,0:T(8,128)(2,1)} %get-tuple-element.75), channel_id=1, source_target_pairs={{0,6},{2,4},{4,2},{6,0},{1,7},{3,5},{5,3},{7,1},{8,14},{10,12},{12... | collective-permute-start | bytes 516104 | tf_op jit(solution)/shard_map/ppermute | solution.py:251
  106.1 11.3 %collective-permute-start.40 = (bf16[112,192]{1,0:T(8,128)(2,1)S(1)}, bf16[112,192]{1,0:T(8,128)(2,1)S(1)}, u32[]{:S(2)}, u32[]{:S(2)}) collective-permute-start(bf16[112,192]{1,0:T(8,128)(2,1)S(1)} %add_convert_fusion.refs_0_), channel_id=1, source_target_pairs={{0,24},{8,16},{16,8},{24,0},{1,25},{9,17},{17,9},{25,1},{2,26},{10... | collective-permute-start | bytes 129032 | tf_op jit(solution)/shard_map/ppermute | solution.py:251
  107.7 12.8 %collective-permute-start.39 = (bf16[112,192]{1,0:T(8,128)(2,1)S(1)}, bf16[112,192]{1,0:T(8,128)(2,1)S(1)}, u32[]{:S(2)}, u32[]{:S(2)}) collective-permute-start(bf16[112,192]{1,0:T(8,128)(2,1)S(1)} %add_convert_fusion.refs_0_), channel_id=1, source_target_pairs={{0,16},{8,24},{16,0},{24,8},{1,17},{9,25},{17,1},{25,9},{2,18},{10... | collective-permute-start | bytes 129032 | tf_op jit(solution)/shard_map/ppermute | solution.py:251
  109.3 43.4 %copy-start = (bf16[2,8,2,2,16,192]{5,4,3,2,1,0:T(8,128)(2,1)}, bf16[2,8,2,2,16,192]{5,4,3,2,1,0:T(8,128)(2,1)S(1)}, u32[]{:S(2)}) copy-start(bf16[2,8,2,2,16,192]{5,4,3,2,1,0:T(8,128)(2,1)S(1)} %copy.15) | copy-start | bytes 1179652
  110.4 10.2 %collective-permute-start.38 = (bf16[112,192]{1,0:T(8,128)(2,1)S(1)}, bf16[112,192]{1,0:T(8,128)(2,1)S(1)}, u32[]{:S(2)}, u32[]{:S(2)}) collective-permute-start(bf16[112,192]{1,0:T(8,128)(2,1)S(1)} %add_convert_fusion.refs_0_), channel_id=1, source_target_pairs={{0,8},{8,0},{16,24},{24,16},{1,9},{9,1},{17,25},{25,17},{2,10},{10... | collective-permute-start | bytes 129032 | tf_op jit(solution)/shard_map/ppermute | solution.py:251
  116.1 7.0 %collective-permute-start.19 = (bf16[112,192]{1,0:T(8,128)(2,1)S(1)}, bf16[112,192]{1,0:T(8,128)(2,1)S(1)}, u32[]{:S(2)}, u32[]{:S(2)}) collective-permute-start(bf16[112,192]{1,0:T(8,128)(2,1)S(1)} %get-tuple-element.77), channel_id=1, source_target_pairs={{0,8},{8,0},{16,24},{24,16},{1,9},{9,1},{17,25},{25,17},{2,10},{10... | collective-permute-start | bytes 129032 | tf_op jit(solution)/shard_map/ppermute | solution.py:251
  116.1 7.4 %collective-permute-start.20 = (bf16[112,192]{1,0:T(8,128)(2,1)S(1)}, bf16[112,192]{1,0:T(8,128)(2,1)S(1)}, u32[]{:S(2)}, u32[]{:S(2)}) collective-permute-start(bf16[112,192]{1,0:T(8,128)(2,1)S(1)} %get-tuple-element.78), channel_id=1, source_target_pairs={{0,16},{8,24},{16,0},{24,8},{1,17},{9,25},{17,1},{25,9},{2,18},{10... | collective-permute-start | bytes 129032 | tf_op jit(solution)/shard_map/ppermute | solution.py:251
  117.4 7.1 %collective-permute-start.21 = (bf16[112,192]{1,0:T(8,128)(2,1)S(1)}, bf16[112,192]{1,0:T(8,128)(2,1)S(1)}, u32[]{:S(2)}, u32[]{:S(2)}) collective-permute-start(bf16[112,192]{1,0:T(8,128)(2,1)S(1)} %get-tuple-element.79), channel_id=1, source_target_pairs={{0,24},{8,16},{16,8},{24,0},{1,25},{9,17},{17,9},{25,1},{2,26},{10... | collective-permute-start | bytes 129032 | tf_op jit(solution)/shard_map/ppermute | solution.py:251
  120.6 21.4 %collective-permute-start.44 = (bf16[4,112,192]{2,1,0:T(8,128)(2,1)S(1)}, bf16[4,112,192]{2,1,0:T(8,128)(2,1)S(1)}, u32[]{:S(2)}, u32[]{:S(2)}) collective-permute-start(bf16[4,112,192]{2,1,0:T(8,128)(2,1)S(1)} %shard_map.145.refs_0_), channel_id=1, source_target_pairs={{0,1},{1,0},{2,3},{3,2},{4,5},{5,4},{6,7},{7,6},{8,9},{9,8},{10,11... | collective-permute-start | bytes 516104 | tf_op jit(solution)/shard_map/ppermute | solution.py:251
  120.6 21.9 %collective-permute-start.43 = (bf16[4,112,192]{2,1,0:T(8,128)(2,1)S(1)}, bf16[4,112,192]{2,1,0:T(8,128)(2,1)S(1)}, u32[]{:S(2)}, u32[]{:S(2)}) collective-permute-start(bf16[4,112,192]{2,1,0:T(8,128)(2,1)S(1)} %shard_map.145.refs_0_), channel_id=1, source_target_pairs={{0,6},{2,4},{4,2},{6,0},{1,7},{3,5},{5,3},{7,1},{8,14},{10,12},{12... | collective-permute-start | bytes 516104 | tf_op jit(solution)/shard_map/ppermute | solution.py:251
  123.0 20.6 %collective-permute-start.42 = (bf16[4,112,192]{2,1,0:T(8,128)(2,1)S(1)}, bf16[4,112,192]{2,1,0:T(8,128)(2,1)S(1)}, u32[]{:S(2)}, u32[]{:S(2)}) collective-permute-start(bf16[4,112,192]{2,1,0:T(8,128)(2,1)S(1)} %shard_map.145.refs_0_), channel_id=1, source_target_pairs={{0,4},{2,6},{4,0},{6,2},{1,5},{3,7},{5,1},{7,3},{8,12},{10,14},{12... | collective-permute-start | bytes 516104 | tf_op jit(solution)/shard_map/ppermute | solution.py:251
  123.6 20.1 %collective-permute-start.41 = (bf16[4,112,192]{2,1,0:T(8,128)(2,1)S(1)}, bf16[4,112,192]{2,1,0:T(8,128)(2,1)S(1)}, u32[]{:S(2)}, u32[]{:S(2)}) collective-permute-start(bf16[4,112,192]{2,1,0:T(8,128)(2,1)S(1)} %shard_map.145.refs_0_), channel_id=1, source_target_pairs={{0,2},{2,0},{4,6},{6,4},{1,3},{3,1},{5,7},{7,5},{8,10},{10,8},{12,... | collective-permute-start | bytes 516104 | tf_op jit(solution)/shard_map/ppermute | solution.py:251
  124.5 6.3 %collective-permute-start.24 = (bf16[112,192]{1,0:T(8,128)(2,1)S(1)}, bf16[112,192]{1,0:T(8,128)(2,1)S(1)}, u32[]{:S(2)}, u32[]{:S(2)}) collective-permute-start(bf16[112,192]{1,0:T(8,128)(2,1)S(1)} %add_convert_fusion.1.refs_0_), channel_id=1, source_target_pairs={{0,24},{8,16},{16,8},{24,0},{1,25},{9,17},{17,9},{25,1},{2,26},{10... | collective-permute-start | bytes 129032 | tf_op jit(solution)/shard_map/ppermute | solution.py:251
  130.7 5.1 %collective-permute-start.23 = (bf16[112,192]{1,0:T(8,128)(2,1)S(1)}, bf16[112,192]{1,0:T(8,128)(2,1)S(1)}, u32[]{:S(2)}, u32[]{:S(2)}) collective-permute-start(bf16[112,192]{1,0:T(8,128)(2,1)S(1)} %add_convert_fusion.1.refs_0_), channel_id=1, source_target_pairs={{0,16},{8,24},{16,0},{24,8},{1,17},{9,25},{17,1},{25,9},{2,18},{10... | collective-permute-start | bytes 129032 | tf_op jit(solution)/shard_map/ppermute | solution.py:251
  135.9 4.2 %collective-permute-start.22 = (bf16[112,192]{1,0:T(8,128)(2,1)S(1)}, bf16[112,192]{1,0:T(8,128)(2,1)S(1)}, u32[]{:S(2)}, u32[]{:S(2)}) collective-permute-start(bf16[112,192]{1,0:T(8,128)(2,1)S(1)} %add_convert_fusion.1.refs_0_), channel_id=1, source_target_pairs={{0,8},{8,0},{16,24},{24,16},{1,9},{9,1},{17,25},{25,17},{2,10},{10... | collective-permute-start | bytes 129032 | tf_op jit(solution)/shard_map/ppermute | solution.py:251
  140.1 7.2 %collective-permute-start.27 = (bf16[4,112,192]{2,1,0:T(8,128)(2,1)S(1)}, bf16[4,112,192]{2,1,0:T(8,128)(2,1)S(1)}, u32[]{:S(2)}, u32[]{:S(2)}) collective-permute-start(bf16[4,112,192]{2,1,0:T(8,128)(2,1)S(1)} %shard_map.142.refs_0_), channel_id=1, source_target_pairs={{0,6},{2,4},{4,2},{6,0},{1,7},{3,5},{5,3},{7,1},{8,14},{10,12},{12... | collective-permute-start | bytes 516104 | tf_op jit(solution)/shard_map/ppermute | solution.py:251
  142.0 7.2 %collective-permute-start.26 = (bf16[4,112,192]{2,1,0:T(8,128)(2,1)S(1)}, bf16[4,112,192]{2,1,0:T(8,128)(2,1)S(1)}, u32[]{:S(2)}, u32[]{:S(2)}) collective-permute-start(bf16[4,112,192]{2,1,0:T(8,128)(2,1)S(1)} %shard_map.142.refs_0_), channel_id=1, source_target_pairs={{0,4},{2,6},{4,0},{6,2},{1,5},{3,7},{5,1},{7,3},{8,12},{10,14},{12... | collective-permute-start | bytes 516104 | tf_op jit(solution)/shard_map/ppermute | solution.py:251
  142.5 7.1 %collective-permute-start.25 = (bf16[4,112,192]{2,1,0:T(8,128)(2,1)S(1)}, bf16[4,112,192]{2,1,0:T(8,128)(2,1)S(1)}, u32[]{:S(2)}, u32[]{:S(2)}) collective-permute-start(bf16[4,112,192]{2,1,0:T(8,128)(2,1)S(1)} %shard_map.142.refs_0_), channel_id=1, source_target_pairs={{0,2},{2,0},{4,6},{6,4},{1,3},{3,1},{5,7},{7,5},{8,10},{10,8},{12,... | collective-permute-start | bytes 516104 | tf_op jit(solution)/shard_map/ppermute | solution.py:251
  143.6 6.0 %collective-permute-start.47 = (bf16[4,112,192]{2,1,0:T(8,128)(2,1)S(1)}, bf16[4,112,192]{2,1,0:T(8,128)(2,1)S(1)}, u32[]{:S(2)}, u32[]{:S(2)}) collective-permute-start(bf16[4,112,192]{2,1,0:T(8,128)(2,1)S(1)} %collective-permute-done.43.refs_3_), channel_id=1, source_target_pairs={{0,1},{1,0},{2,3},{3,2},{4,5},{5,4},{6,7},{7,6},{8,9},{9,8},{10,11... | collective-permute-start | bytes 516104 | tf_op jit(solution)/shard_map/ppermute | solution.py:251
  143.6 6.5 %collective-permute-start.46 = (bf16[4,112,192]{2,1,0:T(8,128)(2,1)S(1)}, bf16[4,112,192]{2,1,0:T(8,128)(2,1)S(1)}, u32[]{:S(2)}, u32[]{:S(2)}) collective-permute-start(bf16[4,112,192]{2,1,0:T(8,128)(2,1)S(1)} %collective-permute-done.42.refs_2_), channel_id=1, source_target_pairs={{0,1},{1,0},{2,3},{3,2},{4,5},{5,4},{6,7},{7,6},{8,9},{9,8},{10,11... | collective-permute-start | bytes 516104 | tf_op jit(solution)/shard_map/ppermute | solution.py:251
  147.3 5.5 %collective-permute-start.28 = (bf16[4,112,192]{2,1,0:T(8,128)(2,1)S(1)}, bf16[4,112,192]{2,1,0:T(8,128)(2,1)S(1)}, u32[]{:S(2)}, u32[]{:S(2)}) collective-permute-start(bf16[4,112,192]{2,1,0:T(8,128)(2,1)S(1)} %shard_map.142.refs_0_), channel_id=1, source_target_pairs={{0,1},{1,0},{2,3},{3,2},{4,5},{5,4},{6,7},{7,6},{8,9},{9,8},{10,11... | collective-permute-start | bytes 516104 | tf_op jit(solution)/shard_map/ppermute | solution.py:251
  149.2 1.5 collective-permute-start.45
  149.7 3.1 %collective-permute-start.31 = (bf16[4,112,192]{2,1,0:T(8,128)(2,1)S(1)}, bf16[4,112,192]{2,1,0:T(8,128)(2,1)S(1)}, u32[]{:S(2)}, u32[]{:S(2)}) collective-permute-start(bf16[4,112,192]{2,1,0:T(8,128)(2,1)S(1)} %collective-permute-done.27.refs_3_), channel_id=1, source_target_pairs={{0,1},{1,0},{2,3},{3,2},{4,5},{5,4},{6,7},{7,6},{8,9},{9,8},{10,11... | collective-permute-start | bytes 516104 | tf_op jit(solution)/shard_map/ppermute | solution.py:251
  149.7 3.1 %collective-permute-start.30 = (bf16[4,112,192]{2,1,0:T(8,128)(2,1)S(1)}, bf16[4,112,192]{2,1,0:T(8,128)(2,1)S(1)}, u32[]{:S(2)}, u32[]{:S(2)}) collective-permute-start(bf16[4,112,192]{2,1,0:T(8,128)(2,1)S(1)} %collective-permute-done.26.refs_2_), channel_id=1, source_target_pairs={{0,1},{1,0},{2,3},{3,2},{4,5},{5,4},{6,7},{7,6},{8,9},{9,8},{10,11... | collective-permute-start | bytes 516104 | tf_op jit(solution)/shard_map/ppermute | solution.py:251
  150.2 2.6 %collective-permute-start.29 = (bf16[4,112,192]{2,1,0:T(8,128)(2,1)S(1)}, bf16[4,112,192]{2,1,0:T(8,128)(2,1)S(1)}, u32[]{:S(2)}, u32[]{:S(2)}) collective-permute-start(bf16[4,112,192]{2,1,0:T(8,128)(2,1)S(1)} %collective-permute-done.25.refs_1_), channel_id=1, source_target_pairs={{0,1},{1,0},{2,3},{3,2},{4,5},{5,4},{6,7},{7,6},{8,9},{9,8},{10,11... | collective-permute-start | bytes 516104 | tf_op jit(solution)/shard_map/ppermute | solution.py:251
  (8 other events, 7.3 us)

commit v4 on v3

--- a/solution.py
+++ b/solution.py
@@ -13,7 +13,6 @@
 TAPS = [(r, c) for r in (-1, 0, 1) for c in (-1, 0, 1)]
 PLANE = ("x", "y", "c")
 VMEM_LIMIT = 16 * 1024 * 1024
-WEIGHT = 20
 
 
 def call(body, outs, scratch, flops, *args, after=()):
@@ -38,7 +37,7 @@
         out_specs=[pl.BlockSpec(memory_space=pltpu.VMEM)] * len(outs),
         scratch_shapes=scratch,
         compiler_params=pltpu.CompilerParams(vmem_limit_bytes=VMEM_LIMIT),
-        cost_estimate=pl.CostEstimate(flops=WEIGHT * flops, bytes_accessed=size, transcendentals=0),
+        cost_estimate=pl.CostEstimate(flops=flops, bytes_accessed=size, transcendentals=0),
     )(*arrays)
 
 
@@ -120,7 +119,7 @@
 
     chan = weights.shape[-1]
     outs = outs + [padded_shape(chan, step)]
-    *parts, wide = call(body, outs, [], conv_flops(chan), *field, act, weights, after=after)
+    *parts, wide = call(body, outs, [], conv_flops(chan, step), *field, act, weights, after=after)
     return parts, wide
 
 
@@ -129,15 +128,17 @@
 
     def body(*refs):
         pieces, base_refs, w_ref = refs[:n], refs[n : n + b], refs[n + b]
-        out_refs, padded = refs[n + b + 1 : -1], refs[-1]
-        fill(padded, pieces, step)
+        out_refs, padded = refs[n + b + 1 :], pieces[0]
+        if n > 1:
+            out_refs, padded = out_refs[:-1], out_refs[-1]
+            fill(padded, pieces, step)
         grad = pulled(padded, w_ref, step)
         store(out_refs, flat(base_refs).astype(F32) + grad)
 
     chan = weights.shape[-1]
-    outs = outs + [padded_shape(chan, step)]
-    *parts, wide = call(body, outs, [], conv_flops(chan), *field, *base, weights, after=after)
-    return parts, wide
+    outs = outs + [padded_shape(chan, step)] * (n > 1)
+    parts = call(body, outs, [], conv_flops(chan, step), *field, *base, weights, after=after)
+    return parts[: len(parts) - (n > 1)], parts[-1]
 
 
 def tap_products(padded, src_ref, active, step, out_ref):
@@ -151,36 +152,41 @@
         out_ref[k * chan : (k + 1) * chan] = jnp.dot(
             turned, window(padded, tap, step), preferred_element_type=F32
         )
-    used = len(TAPS) * chan
-    out_ref[used:] = jnp.zeros((out_ref.shape[0] - used, chan), F32)
-
-
-def padded_rows(chan):
-    return -(-len(TAPS) * chan // 256) * 256
+
+
+def tap_rows(chan):
+    return len(TAPS) * chan
 
 
 def weight_grad(wide, source, step, chan, after=()):
     def body(wide_ref, src_ref, out_ref):
         tap_products(wide_ref, src_ref, True, step, out_ref)
 
-    out = [jax.ShapeDtypeStruct((padded_rows(chan), chan), F32)]
-    return call(body, out, [], conv_flops(chan), wide, source, after=after)[0]
-
-
-def weight_grad_split(wide, source, step, chan, other, after=()):
-    rows = padded_rows(chan)
-    part = (4, rows // 16, chan)
-
-    def body(wide_ref, src_ref, other_ref, keep_ref, *refs):
-        give_refs, total = refs[:4], refs[4]
+    out = [jax.ShapeDtypeStruct((tap_rows(chan), chan), F32)]
+    return call(body, out, [], conv_flops(chan, step), wide, source, after=after)[0]
+
+
+def weight_grad_split(field, source, step, chan, other, after=()):
+    n = len(field)
+
+    rows = tap_rows(chan)
+    shape = (rows // 16, 16, chan)
+
+    part = (2, rows // 64, 16, chan)
+
+    def body(*refs):
+        src_ref, other_ref, keep_ref, *give_refs = refs[n : n + 5]
+        wide_ref, total = refs[n + 5 if n > 1 else 0], refs[-1]
+        if n > 1:
+            fill(wide_ref, refs[:n], step)
         tap_products(wide_ref, src_ref, False, step, total)
         core = lax.axis_index("c")
 
         def split(kept, given):
-            keep_ref[...] = kept[...].reshape(keep_ref.shape)
-            for k, ref in enumerate(give_refs):
+            keep_ref[...] = kept[...].reshape(shape)
+            for k in range(4):
                 at = pl.multiple_of((quarter() ^ k) * (rows // 4), 16)
-                ref[...] = given[pl.ds(at, rows // 4)].astype(BF16).reshape(part)
+                give_refs[k // 2][k % 2] = given[pl.ds(at, rows // 4)].astype(BF16).reshape(part[1:])
 
         @pl.when(core == 0)
         def _():
@@ -190,14 +196,16 @@
         def _():
             split(total, other_ref)
 
-    outs = [jax.ShapeDtypeStruct((4,) + part, F32)] + [jax.ShapeDtypeStruct(part, BF16)] * 4
+    outs = [jax.ShapeDtypeStruct(shape, F32)] + [jax.ShapeDtypeStruct(part, BF16)] * 2
+    if n > 1:
+        outs.append(padded_shape(chan, step))
     scratch = [pltpu.VMEM((rows, chan), F32)]
-    keep, *give = call(body, outs, scratch, conv_flops(chan), wide, source, other, after=after)
-    return keep, [xor(value, "c", 1) for value in give]
-
-
-def conv_flops(chan):
-    return 2 * len(TAPS) * 1024 * chan * chan
+    keep, one, two, *wide = call(body, outs, scratch, conv_flops(chan, step), *field, source, other, after=after)
+    return keep, [xor(one, "c", 1), xor(two, "c", 1)], wide
+
+
+def conv_flops(chan, step):
+    return (20 if step == 1 else 20) * 2 * len(TAPS) * 1024 * chan * chan
 
 
 def padded_shape(chan, step):
@@ -256,12 +264,14 @@
 
 
 def sum_plane(keep, got, after=()):
-    part = keep.shape[1:]
+    tiles = keep.shape[0] // 4
+    part = (tiles,) + keep.shape[1:]
 
     def body(keep_ref, *refs):
-        got_refs, own_ref, sent_refs = refs[:4], refs[4], refs[5:]
+        got_refs, own_ref, sent_refs = refs[:2], refs[2], refs[3:]
         for k in range(4):
-            total = keep_ref[quarter() ^ k] + got_refs[k][...].astype(F32)
+            at = pl.ds((quarter() ^ k) * tiles, tiles)
+            total = keep_ref[at] + got_refs[k // 2][k % 2].astype(F32)
             if k == 0:
                 own_ref[...] = total
             else:
@@ -272,67 +282,80 @@
     return own, sent
 
 
-def sum_ring(own, sent, after=()):
-    terms = [xor(value, ("x", "y"), k + 1) for k, value in enumerate(sent)]
-    count = lax.axis_size("z")
-    part = own.shape
-    if count != 4:
-        total = own + sum(term.astype(F32) for term in terms)
-        k = 1
-        while k < count:
-            total = total.astype(BF16)
-            total = total.astype(F32) + xor(total, "z", k).astype(F32)
-            k = 2 * k
-        return total.astype(BF16)
-
-    def body(own_ref, *refs):
-        term_refs, mine_ref, sent_refs = refs[:3], refs[3], refs[4:]
+def sum_plane_swap(keep, got, after=()):
+    tiles = keep.shape[0] // 4
+    part = (4, tiles) + keep.shape[1:]
+
+    def body(keep_ref, *refs):
         for k in range(4):
-            at = lax.axis_index("z") ^ k
-            total = own_ref[at]
-            for ref in term_refs:
-                total = total + ref[at].astype(F32)
-            if k == 0:
-                mine_ref[...] = total
-            else:
-                sent_refs[k - 1][...] = total.astype(BF16)
-
-    outs = [jax.ShapeDtypeStruct(part[1:], F32)] + [jax.ShapeDtypeStruct(part[1:], BF16)] * 3
-    mine, *sent = call(body, outs, [], 0, own, *terms, after=after)
-    for k, value in enumerate(sent):
-        mine = mine + xor(value, "z", k + 1).astype(F32)
-    mine = mine.astype(BF16)
-    spread = [mine] + [xor(mine, "z", k) for k in (1, 2, 3)]
-
-    def join(*refs):
-        for k in range(4):
-            refs[4][lax.axis_index("z") ^ k] = refs[k][...]
-
-    return call(join, [jax.ShapeDtypeStruct(part, BF16)], [], 0, *spread)[0]
-
-
-def spread_weights(part, taps):
+            at = quarter() ^ k
+            total = keep_ref[pl.ds(at * tiles, tiles)] + refs[k // 2][k % 2].astype(F32)
+            refs[2][at] = total.astype(BF16)
+
+    own = call(body, [jax.ShapeDtypeStruct(part, BF16)], [], 0, keep, *got, after=after)[0]
+    return own, lax.all_to_all(own, ("x", "y"), 0, 0)
+
+
+def add_parts(parts, after=()):
+    def body(parts_ref, out_ref):
+        total = parts_ref[0].astype(F32)
+        for k in range(1, parts_ref.shape[0]):
+            total = total + parts_ref[k].astype(F32)
+        out_ref[...] = total.astype(BF16)
+
+    return call(body, [jax.ShapeDtypeStruct(parts.shape[1:], BF16)], [], 0, parts, after=after)[0]
+
+
+def add(*terms, after=()):
+    def body(*refs):
+        total = refs[0][...].astype(F32)
+        for ref in refs[1:-1]:
+            total = total + ref[...].astype(F32)
+        refs[-1][...] = total.astype(BF16)
+
+    return call(body, [jax.ShapeDtypeStruct(terms[0].shape, BF16)], [], 0, *terms, after=after)[0]
+
+
+def plane_terms(sent):
+    return [xor(value, ("x", "y"), k + 1) for k, value in enumerate(sent)]
+
+
+def sum_far(part, after=()):
+    k = 2
+    while k < lax.axis_size("z"):
+        part = add(part, xor(part, "z", k), after=after)
+        k = 2 * k
+    return part
+
+
+def join(*parts, after=()):
+    def body(*refs):
+        for k, ref in enumerate(refs[:-1]):
+            refs[-1][k] = ref[...]
+
+    out = [jax.ShapeDtypeStruct((len(parts),) + parts[0].shape, BF16)]
+    return call(body, out, [], 0, *parts, after=after)[0]
+
+
+def spread_weights(part, taps, gate=None, after=()):
     quarters = [part] + [xor(part, ("x", "y"), k) for k in (1, 2, 3)]
-    others = [xor(value, "c", 1) for value in quarters]
+    if gate is None:
+        others = [xor(value, "c", 1) for value in quarters]
+    else:
+        others = [xor(join(*quarters[:2], after=[gate]), "c", 1), xor(join(*quarters[2:], after=[gate]), "c", 1)]
     chan = part.shape[-1]
-    used = taps * chan
-
-    def body(*refs):
-        own_refs, other_refs, first_ref, second_ref = refs[:4], refs[4:8], refs[8], refs[9]
+
+    def body(*refs):
+        own_refs, other_refs, first_ref, second_ref = refs[:4], refs[4:-2], refs[-2], refs[-1]
+        if len(other_refs) == 2:
+            other_refs = [ref.at[k] for ref in other_refs for k in range(2)]
 
         def put(out_ref, part_refs):
             for k, ref in enumerate(part_refs):
                 value = ref[...].astype(F32).reshape(-1, chan)
                 rows = value.shape[0]
-                at = quarter() ^ k
-
-                @pl.when(at < 3)
-                def _():
-                    out_ref[pl.ds(pl.multiple_of(at * rows, 16), rows)] = value
-
-                @pl.when(at == 3)
-                def _():
-                    out_ref[3 * rows :] = value[: used - 3 * rows]
+                at = (quarter() ^ k) * rows
+                out_ref[pl.ds(pl.multiple_of(at, 16), rows)] = value
 
         core = lax.axis_index("c")
 
@@ -346,8 +369,8 @@
             put(first_ref, other_refs)
             put(second_ref, own_refs)
 
-    outs = [jax.ShapeDtypeStruct((used, chan), F32)] * 2
-    one, two = call(body, outs, [], 0, *quarters, *others)
+    outs = [jax.ShapeDtypeStruct((taps * chan, chan), F32)] * 2
+    one, two = call(body, outs, [], 0, *quarters, *others, after=after)
     return one.reshape(taps, chan, chan), two.reshape(taps, chan, chan)
 
 
@@ -371,31 +394,37 @@
     halves = [coarse(2, chan)] * 2
     thirds = [coarse(1, chan), coarse(2, chan), coarse(1, chan)]
 
-    pre, wide = conv_two([low, final, high], act_two, second_block_conv_two, 2, halves)
-    late = pack_classes(first_block_preactivation, second_block_input, first_block_input, after=[low, high])
-    late = swap_classes(late)
+    late = [first_block_preactivation, second_block_input, first_block_input]
+    packed = pack_classes(*late, after=[act_two[0]])
+    late = swap_classes(packed)
     act_one, entry_two, entry_one = (late, 0), (late, 1), (late, 2)
+    field = [low, final, high]
+    pre, wide = conv_two(field, act_two, second_block_conv_two, 2, halves, after=[packed])
     low, high = ring(pre[0], pre[1])
     second_two = weight_grad(wide, act_two, 2, chan)
     field = [low, *pre, high]
     mid, wide = conv_one(field, [final], second_block_conv_one, 2, thirds, after=[second_two])
     low, high = ring(mid[0], mid[2])
-    keep, got = weight_grad_split(wide, entry_two, 2, chan, second_two)
+    keep, got, _ = weight_grad_split([wide], entry_two, 2, chan, second_two)
     field = [low, *mid, high]
     pre, wide = conv_two(field, act_one, first_block_conv_two, 1, thirds, after=[keep])
     low, high = ring(pre[0], pre[2])
-    first_two = weight_grad(wide, act_one, 1, chan)
-    own, sent = sum_plane(keep, got, after=[first_two])
+    own, parts = sum_plane_swap(keep, got)
+    first_two = weight_grad(wide, act_one, 1, chan, after=[own])
+    field = [low, *pre, high]
     whole = [jax.ShapeDtypeStruct((2, 2, 2, 2, 2, 2, STRIDE, chan), BF16)]
-    field = [low, *pre, high]
-    (out,), wide = conv_one(field, mid, first_block_conv_one, 1, whole, after=[own])
-    keep, got = weight_grad_split(wide, entry_one, 1, chan, first_two)
+    keep, got, wide = weight_grad_split(field, entry_one, 1, chan, first_two)
+    part = add_parts(parts)
+    own_b, sent_b = sum_plane(keep, got, after=[part])
+    part = add(part, xor(part, "z", 1), after=[own_b])
+    part_b = add(own_b, *plane_terms(sent_b), after=[part])
+    (out,), _ = conv_one(wide, mid, first_block_conv_one, 1, whole, after=[part_b])
     out = gather_classes(out, height, breadth)
-    part = sum_ring(own, sent, after=[keep])
-    own, sent = sum_plane(keep, got)
-    second_two, second_one = spread_weights(part, len(TAPS))
-    part = sum_ring(own, sent, after=[out])
-    first_two, first_one = spread_weights(part, len(TAPS))
+    part = sum_far(part, after=[part_b])
+    part_b = add(part_b, xor(part_b, "z", 1), after=[part])
+    second_two, second_one = spread_weights(part, len(TAPS), gate=part_b)
+    part_b = sum_far(part_b, after=[second_two, out])
+    first_two, first_one = spread_weights(part_b, len(TAPS))
     return out, first_one, first_two, second_one, second_two
 
 

time: 156 us -> 150 us (0.962)
  starting transfers between devices: 58.7 us -> 47.1 us
  waiting for transfers between devices: 47.5 us -> 51.8 us
    ppermute x40 -> x23, starting transfers between devices: 31.6 us -> 16.6 us  [xor(): return lax.ppermute(value, axis, [(i, i ^ k) for i in range(count)])]
    ppermute x4, waiting for transfers between devices: 13 us -> 6.01 us  [ring(): lax.ppermute(right_edge, 'z', up)]
    all_to_all x1, waiting for transfers between devices: 0.01 us -> 5.7 us  [gather_classes(): parts = lax.all_to_all(parts, PLANE, 0, 0)]
    all_to_all x2, waiting for transfers between devices: 0.01 us -> 4.11 us  [swap_classes(): moved = lax.all_to_all(packed, PLANE, 0, 0)]
    all_to_all x0 -> x1, starting transfers between devices: none -> 3.84 us  [sum_plane_swap(): return (own, lax.all_to_all(own, ('x', 'y'), 0, 0))]
    all_to_all x0 -> x1, waiting for transfers between devices: none -> 3.8 us  [sum_plane_swap(): return (own, lax.all_to_all(own, ('x', 'y'), 0, 0))]
    ppermute x4, waiting for transfers between devices: 8.84 us -> 6.6 us  [ring(): lax.ppermute(left_edge, 'z', down)]
    pallas_call x19 -> x23, Pallas kernels: 21.2 us -> 21.8 us  [call(): pl.pallas_call(lambda *refs: body(*refs[len(after):]), grid=(1,), out_sha...]
  transfers between devices with their start and end apart: 51 -> 35, of which waited for: 15 -> 18; matrix products, arithmetic and copies ran while one was open for 1% -> 1% of each run, Pallas kernels for 12% -> 13%
where the time goes in v4:
time: 150 us; the launch traced here: 149 us
  waiting for transfers between devices  51.8 us (35%)
  starting transfers between devices  47.1 us (31%)
  Pallas kernels  21.8 us (15%)
  blocking collectives  13.9 us (9%)
  local copies, waits for them, and re-layouts  13.6 us (9%)
    ppermute x23, waiting for transfers between devices, xor(): return lax.ppermute(value, axis, [(i, i ^ k) for i in range(count)])  25.5 us
    pallas_call x23, Pallas kernels, call(): pl.pallas_call(lambda *refs: body(*refs[len(after):]), grid=(1,), out_sha...  21.8 us
    ppermute x23, starting transfers between devices, xor(): return lax.ppermute(value, axis, [(i, i ^ k) for i in range(count)])  16.6 us
    all_to_all x1, blocking collectives, swap_classes(): moved = lax.all_to_all(packed, PLANE, 0, 0)  13.9 us
    ppermute x4, starting transfers between devices, ring(): lax.ppermute(left_edge, 'z', down)  12.3 us
    unnamed x54, local copies, waits for them, and re-layouts  11.7 us
    all_to_all x2, starting transfers between devices, swap_classes(): moved = lax.all_to_all(packed, PLANE, 0, 0)  7.21 us
    ppermute x4, waiting for transfers between devices, ring(): lax.ppermute(left_edge, 'z', down)  6.6 us
  transfers between devices with their start and end apart: 35, of which 18 were waited for; matrix products, arithmetic and copies ran while one was open for 1% of the time, Pallas kernels for 13%

profile of v4, /device:TPU:0, one launch (start us, length us, event | category | flops | bytes accessed | tf_op | source)
XLA Modules:
  0.0 149.2 jit_solution(13457848418740920984)
XLA Ops:
  0.7 1.1 copy-done.8
  1.8 13.9 %all_to_all.25 = bf16[8,1,2,2,2,16,192]{6,5,4,3,2,1,0:T(8,128)(2,1)S(1)} all-to-all(bf16[8,1,2,2,2,16,192]{6,5,4,3,2,1,0:T(8,128)(2,1)S(1)} %shard_map.128), channel_id=1, replica_groups=mesh['z'=4,'x'=2,'y'=2,'c'=2] {'x','y','c'}, dimensions={0} | all-to-all | bytes 786432 | tf_op jit(solution)/shard_map/all_to_all | solution.py:238
  15.7 0.8 shard_map.129
  16.5 3.5 %all-to-all-start.1 = ((bf16[8,1,2,2,2,16,192]{6,5,4,3,2,1,0:T(8,128)(2,1)}), bf16[8,1,2,2,2,16,192]{6,5,4,3,2,1,0:T(8,128)(2,1)S(1)}, u32[]{:S(2)}, u32[]{:S(2)}) async-start(bf16[8,1,2,2,2,16,192]{6,5,4,3,2,1,0:T(8,128)(2,1)} %shard_map.129), calls=%async_computation.1 | async-start | bytes 1048576 | tf_op jit(solution)/shard_map/all_to_all | solution.py:238
  20.0 0.8 fusion
  20.8 1.6 %collective-permute-start = (bf16[2,2,2,2,2,16,192]{6,5,4,3,2,1,0:T(8,128)(2,1)}, bf16[2,2,2,2,2,16,192]{6,5,4,3,2,1,0:T(8,128)(2,1)}, u32[]{:S(2)}, u32[]{:S(2)}) collective-permute-start(bf16[2,2,2,2,2,16,192]{6,5,4,3,2,1,0:T(8,128)(2,1)} %bitcast.2), channel_id=1, source_target_pairs={{0,8},{8,16},{16,24},{24,0},{1,9},{9,17},{17,25},{25,1},{2,10},{10... | collective-permute-start | bytes 589832 | tf_op jit(solution)/shard_map/ppermute | solution.py:254
  22.4 2.2 %collective-permute-start.1 = (bf16[2,2,2,2,2,16,192]{6,5,4,3,2,1,0:T(8,128)(2,1)}, bf16[2,2,2,2,2,16,192]{6,5,4,3,2,1,0:T(8,128)(2,1)}, u32[]{:S(2)}, u32[]{:S(2)}) collective-permute-start(bf16[2,2,2,2,2,16,192]{6,5,4,3,2,1,0:T(8,128)(2,1)} %bitcast.3), channel_id=1, source_target_pairs={{8,0},{16,8},{24,16},{0,24},{9,1},{17,9},{25,17},{1,25},{10,2},{18... | collective-permute-start | bytes 589832 | tf_op jit(solution)/shard_map/ppermute | solution.py:254
  24.7 4.1 %all-to-all-done.1 = bf16[8,1,2,2,2,16,192]{6,5,4,3,2,1,0:T(8,128)(2,1)S(1)} async-done(((bf16[8,1,2,2,2,16,192]{6,5,4,3,2,1,0:T(8,128)(2,1)}), bf16[8,1,2,2,2,16,192]{6,5,4,3,2,1,0:T(8,128)(2,1)S(1)}, u32[]{:S(2)}, u32[]{:S(2)}) %all-to-all-start.1) | async-done | bytes 393248 | tf_op jit(solution)/shard_map/all_to_all | solution.py:238
  28.8 1.2 shard_map.130.refs_0_
  30.0 3.7 %all-to-all-start.2 = ((bf16[8,3,2,2,2,16,192]{6,5,4,3,2,1,0:T(8,128)(2,1)}), bf16[8,3,2,2,2,16,192]{6,5,4,3,2,1,0:T(8,128)(2,1)S(1)}, u32[]{:S(2)}, u32[]{:S(2)}) async-start(bf16[8,3,2,2,2,16,192]{6,5,4,3,2,1,0:T(8,128)(2,1)} %shard_map.130.refs_0_), calls=%async_computation.2 | async-start | bytes 3145728 | tf_op jit(solution)/shard_map/all_to_all | solution.py:238
  33.8 2.9 %collective-permute-done.1.refs_3_ = bf16[2,2,2,2,2,16,192]{6,5,4,3,2,1,0:T(8,128)(2,1)} collective-permute-done((bf16[2,2,2,2,2,16,192]{6,5,4,3,2,1,0:T(8,128)(2,1)}, bf16[2,2,2,2,2,16,192]{6,5,4,3,2,1,0:T(8,128)(2,1)}, u32[]{:S(2)}, u32[]{:S(2)}) %collective-permute-start.1) | collective-permute-done | bytes 196640 | tf_op jit(solution)/shard_map/ppermute | solution.py:254
  36.7 2.5 %shard_map.131 = (bf16[2,8,2,16,192]{4,3,2,1,0:T(8,128)(2,1)S(1)}, bf16[2,8,2,16,192]{4,3,2,1,0:T(8,128)(2,1)S(1)}, bf16[8,12,2,16,192]{4,3,2,1,0:T(8,128)(2,1)S(1)}) custom-call(bf16[8,3,2,2,2,16,192]{6,5,4,3,2,1,0:T(8,128)(2,1)} %shard_map.130.refs_0_, bf16[2,2,2,2,2,16,192]{6,5,4,3,2,1,0:T(8,128)(2,1)} %collective-permute-done.refs_1_, ...), custom_call_target="tpu_custom_call" | custom-call | flops 13589544960 | bytes 3416064 | tf_op jit(solution)/shard_map/pallas_call | solution.py:32
  39.2 1.2 collective-permute-start.2
  40.4 2.7 %collective-permute-start.3 = (bf16[2,8,2,16,192]{4,3,2,1,0:T(8,128)(2,1)S(1)}, bf16[2,8,2,16,192]{4,3,2,1,0:T(8,128)(2,1)S(1)}, u32[]{:S(2)}, u32[]{:S(2)}) collective-permute-start(bf16[2,8,2,16,192]{4,3,2,1,0:T(8,128)(2,1)S(1)} %get-tuple-element.33.refs_2_), channel_id=1, source_target_pairs={{8,0},{16,8},{24,16},{0,24},{9,1},{17,9},{25,17},{1,25},{10,2},{18... | collective-permute-start | bytes 589832 | tf_op jit(solution)/shard_map/ppermute | solution.py:254
  43.1 1.2 shard_map.132.refs_0_.refs_2_
  44.3 6.0 %collective-permute-done.2.refs_1_ = bf16[2,8,2,16,192]{4,3,2,1,0:T(8,128)(2,1)S(1)} collective-permute-done((bf16[2,8,2,16,192]{4,3,2,1,0:T(8,128)(2,1)S(1)}, bf16[2,8,2,16,192]{4,3,2,1,0:T(8,128)(2,1)S(1)}, u32[]{:S(2)}, u32[]{:S(2)}) %collective-permute-start.2) | collective-permute-done | bytes 196640 | tf_op jit(solution)/shard_map/ppermute | solution.py:254
  50.3 3.6 %collective-permute-done.3.refs_4_ = bf16[2,8,2,16,192]{4,3,2,1,0:T(8,128)(2,1)S(1)} collective-permute-done((bf16[2,8,2,16,192]{4,3,2,1,0:T(8,128)(2,1)S(1)}, bf16[2,8,2,16,192]{4,3,2,1,0:T(8,128)(2,1)S(1)}, u32[]{:S(2)}, u32[]{:S(2)}) %collective-permute-start.3) | collective-permute-done | bytes 196640 | tf_op jit(solution)/shard_map/ppermute | solution.py:254
  54.0 1.4 shard_map.133
  55.4 1.1 copy-done.19
  56.6 0.3 collective-permute-start.6
  56.9 3.5 %collective-permute-start.7 = (bf16[1,8,2,16,192]{4,3,2,1,0:T(8,128)(2,1)S(1)}, bf16[1,8,2,16,192]{4,3,2,1,0:T(8,128)(2,1)S(1)}, u32[]{:S(2)}, u32[]{:S(2)}) collective-permute-start(bf16[1,8,2,16,192]{4,3,2,1,0:T(8,128)(2,1)S(1)} %get-tuple-element.39.refs_2_), channel_id=1, source_target_pairs={{8,0},{16,8},{24,16},{0,24},{9,1},{17,9},{25,17},{1,25},{10,2},{18... | collective-permute-start | bytes 294920 | tf_op jit(solution)/shard_map/ppermute | solution.py:254
  60.4 2.0 %copy-done.18 = f32[1728,192]{1,0:T(8,128)S(1)} copy-done((f32[1728,192]{1,0:T(8,128)S(1)}, f32[1728,192]{1,0:T(8,128)}, u32[]{:S(2)}) %copy-start.18) | copy-done | bytes 1327128
  62.4 1.4 copy-done.20
  63.9 1.3 shard_map.134
  65.3 0.5 collective-permute-start.5
  65.8 1.5 %shard_map.137 = (bf16[1,8,2,16,192]{4,3,2,1,0:T(8,128)(2,1)S(1)}, bf16[2,8,2,16,192]{4,3,2,1,0:T(8,128)(2,1)S(1)}, bf16[1,8,2,16,192]{4,3,2,1,0:T(8,128)(2,1)S(1)}, bf16[6,10,2,16,192]{4,3,2,1,0:T(8,128)(2,1)S(1)}) custom-call(f32[108,16,192]{2,1,0:T(8,128)S(1)} %get-tuple-element.35.refs_0_, ...), custom_call_target="tpu_custom_call" | custom-call | flops 13589544960 | bytes 2777088 | tf_op jit(solution)/shard_map/pallas_call | solution.py:32
  67.3 0.9 copy-done.21
  68.3 3.8 %collective-permute-start.9 = (bf16[1,8,2,16,192]{4,3,2,1,0:T(8,128)(2,1)S(1)}, bf16[1,8,2,16,192]{4,3,2,1,0:T(8,128)(2,1)S(1)}, u32[]{:S(2)}, u32[]{:S(2)}) collective-permute-start(bf16[1,8,2,16,192]{4,3,2,1,0:T(8,128)(2,1)S(1)} %get-tuple-element.42.refs_1_), channel_id=1, source_target_pairs={{8,0},{16,8},{24,16},{0,24},{9,1},{17,9},{25,17},{1,25},{10,2},{18... | collective-permute-start | bytes 294920 | tf_op jit(solution)/shard_map/ppermute | solution.py:254
  72.1 1.1 shard_map.135.refs_0_
  73.2 3.8 %all-to-all-start.3 = ((bf16[4,27,16,192]{3,2,1,0:T(8,128)(2,1)}), bf16[4,27,16,192]{3,2,1,0:T(8,128)(2,1)S(1)}, u32[]{:S(2)}, u32[]{:S(2)}) async-start(bf16[4,27,16,192]{3,2,1,0:T(8,128)(2,1)} %shard_map.135.refs_0_), calls=%async_computation.3 | async-start | bytes 1769472 | tf_op jit(solution)/shard_map/all_to_all | solution.py:296
  77.0 1.2 copy-done.22
  78.2 1.2 shard_map.138.refs_6_
  79.5 1.4 copy-done.3
  80.9 2.5 %shard_map.139 = (f32[108,16,192]{2,1,0:T(8,128)S(1)}, bf16[2,27,16,192]{3,2,1,0:T(8,128)(2,1)}, bf16[2,27,16,192]{3,2,1,0:T(8,128)(2,1)}, bf16[6,10,2,16,192]{4,3,2,1,0:T(8,128)(2,1)S(1)}) custom-call(bf16[1,8,2,16,192]{4,3,2,1,0:T(8,128)(2,1)S(1)} %collective-permute-done.8.refs_0_, bf16[1,8,2,16,192]{4,3,2,1,0:T(8,128)(2,1)S(1)} %get-tuple-element.42.refs_1_, ...), custom_call_target="tpu_custom_call" | custom-call | flops 13589544960 | bytes 5038080 | tf_op jit(solution)/shard_map/pallas_call | solution.py:32
  83.3 0.9 copy-done.23
  84.3 0.5 collective-permute-start.11
  84.8 3.8 %all-to-all-done.3.refs_0_ = bf16[4,27,16,192]{3,2,1,0:T(8,128)(2,1)S(1)} async-done(((bf16[4,27,16,192]{3,2,1,0:T(8,128)(2,1)}), bf16[4,27,16,192]{3,2,1,0:T(8,128)(2,1)S(1)}, u32[]{:S(2)}, u32[]{:S(2)}) %all-to-all-start.3) | async-done | bytes 663584 | tf_op jit(solution)/shard_map/all_to_all | solution.py:296
  89.0 1.5 %collective-permute-start.13 = (bf16[27,16,192]{2,1,0:T(8,128)(2,1)S(1)}, bf16[27,16,192]{2,1,0:T(8,128)(2,1)S(1)}, u32[]{:S(2)}, u32[]{:S(2)}) collective-permute-start(bf16[27,16,192]{2,1,0:T(8,128)(2,1)S(1)} %get-tuple-element.49), channel_id=1, source_target_pairs={{0,2},{2,0},{4,6},{6,4},{1,3},{3,1},{5,7},{7,5},{8,10},{10,8},{12,... | collective-permute-start | bytes 497672 | tf_op jit(solution)/shard_map/ppermute | solution.py:259
  90.5 0.6 collective-permute-start.14
  91.0 1.5 collective-permute-start.15
  92.5 2.6 %collective-permute-done.12.refs_2_ = bf16[27,16,192]{2,1,0:T(8,128)(2,1)S(1)} collective-permute-done((bf16[27,16,192]{2,1,0:T(8,128)(2,1)S(1)}, bf16[27,16,192]{2,1,0:T(8,128)(2,1)S(1)}, u32[]{:S(2)}, u32[]{:S(2)}) %collective-permute-start.12) | collective-permute-done | bytes 165920 | tf_op jit(solution)/shard_map/ppermute | solution.py:259
  95.4 3.3 %collective-permute-done.14.refs_3_ = bf16[27,16,192]{2,1,0:T(8,128)(2,1)S(1)} collective-permute-done((bf16[27,16,192]{2,1,0:T(8,128)(2,1)S(1)}, bf16[27,16,192]{2,1,0:T(8,128)(2,1)S(1)}, u32[]{:S(2)}, u32[]{:S(2)}) %collective-permute-start.14) | collective-permute-done | bytes 165920 | tf_op jit(solution)/shard_map/ppermute | solution.py:259
  98.7 3.3 %collective-permute-done.15.refs_4_ = bf16[27,16,192]{2,1,0:T(8,128)(2,1)S(1)} collective-permute-done((bf16[27,16,192]{2,1,0:T(8,128)(2,1)S(1)}, bf16[27,16,192]{2,1,0:T(8,128)(2,1)S(1)}, u32[]{:S(2)}, u32[]{:S(2)}) %collective-permute-start.15) | collective-permute-done | bytes 165920 | tf_op jit(solution)/shard_map/ppermute | solution.py:259
  102.1 1.8 %collective-permute-start.20 = (bf16[27,16,192]{2,1,0:T(8,128)(2,1)S(1)}, bf16[27,16,192]{2,1,0:T(8,128)(2,1)S(1)}, u32[]{:S(2)}, u32[]{:S(2)}) collective-permute-start(bf16[27,16,192]{2,1,0:T(8,128)(2,1)S(1)} %shard_map.142.refs_0_.refs_1_), channel_id=1, source_target_pairs={{0,8},{8,0},{16,24},{24,16},{1,9},{9,1},{17,25},{25,17},{2,10},{10... | collective-permute-start | bytes 497672 | tf_op jit(solution)/shard_map/ppermute | solution.py:259
  103.9 2.6 %collective-permute-done.16.refs_2_ = bf16[27,16,192]{2,1,0:T(8,128)(2,1)S(1)} collective-permute-done((bf16[27,16,192]{2,1,0:T(8,128)(2,1)S(1)}, bf16[27,16,192]{2,1,0:T(8,128)(2,1)S(1)}, u32[]{:S(2)}, u32[]{:S(2)}) %collective-permute-start.16) | collective-permute-done | bytes 165920 | tf_op jit(solution)/shard_map/ppermute | solution.py:259
  106.5 2.9 %collective-permute-start.19 = (bf16[27,16,192]{2,1,0:T(8,128)(2,1)S(1)}, bf16[27,16,192]{2,1,0:T(8,128)(2,1)S(1)}, u32[]{:S(2)}, u32[]{:S(2)}) collective-permute-start(bf16[27,16,192]{2,1,0:T(8,128)(2,1)S(1)} %shard_map.144.refs_0_.refs_1_), channel_id=1, source_target_pairs={{0,6},{2,4},{4,2},{6,0},{1,7},{3,5},{5,3},{7,1},{8,14},{10,12},{12... | collective-permute-start | bytes 497672 | tf_op jit(solution)/shard_map/ppermute | solution.py:259
  109.4 0.7 collective-permute-start.18
  110.1 1.4 collective-permute-start.17
  111.5 2.2 %shard_map.143 = bf16[2,2,2,2,2,2,16,192]{7,6,5,4,3,2,1,0:T(8,128)(2,1)} custom-call(bf16[27,16,192]{2,1,0:T(8,128)(2,1)S(1)} %shard_map.142.refs_0_.refs_1_, bf16[6,10,2,16,192]{4,3,2,1,0:T(8,128)(2,1)S(1)} %copy-done.24, bf16[1,8,2,16,192]{4,3,2,1,0:T(8,128)(2,1)S(1)} %copy-done.14, bf16[2,8,2,16,192]{4,3,2,1,0:T(8,128)(2,1)S(1)} %copy-done.26, ...), custom_call_target="tpu_custom_call" | custom-call | flops 13589544960 | bytes 2187264 | tf_op jit(solution)/shard_map/pallas_call | solution.py:32
  113.8 4.2 %all-to-all-start.4 = ((bf16[8,2,2,2,16,192]{5,4,3,2,1,0:T(8,128)(2,1)}), bf16[8,2,2,2,16,192]{5,4,3,2,1,0:T(8,128)(2,1)}, u32[]{:S(2)}, u32[]{:S(2)}) async-start(bf16[8,2,2,2,16,192]{5,4,3,2,1,0:T(8,128)(2,1)} %bitcast.5), calls=%async_computation.4 | async-start | bytes 1048576 | tf_op jit(solution)/shard_map/all_to_all | solution.py:246
  118.0 2.3 %collective-permute-done.18.refs_1_.refs_2_ = bf16[27,16,192]{2,1,0:T(8,128)(2,1)S(1)} collective-permute-done((bf16[27,16,192]{2,1,0:T(8,128)(2,1)S(1)}, bf16[27,16,192]{2,1,0:T(8,128)(2,1)S(1)}, u32[]{:S(2)}, u32[]{:S(2)}) %collective-permute-start.18) | collective-permute-done | bytes 165920 | tf_op jit(solution)/shard_map/ppermute | solution.py:259
  120.5 0.6 collective-permute-start.21
  121.1 5.7 %all-to-all-done.4 = bf16[8,2,2,2,16,192]{5,4,3,2,1,0:T(8,128)(2,1)} async-done(((bf16[8,2,2,2,16,192]{5,4,3,2,1,0:T(8,128)(2,1)}), bf16[8,2,2,2,16,192]{5,4,3,2,1,0:T(8,128)(2,1)}, u32[]{:S(2)}, u32[]{:S(2)}) %all-to-all-start.4) | async-done | bytes 393248 | tf_op jit(solution)/shard_map/all_to_all | solution.py:246
  126.8 1.1 copy.15
  127.9 2.0 %shard_map.148 = (f32[1728,192]{1,0:T(8,128)}, f32[1728,192]{1,0:T(8,128)}) custom-call(bf16[27,16,192]{2,1,0:T(8,128)(2,1)S(1)} %shard_map.144.refs_0_.refs_1_, bf16[27,16,192]{2,1,0:T(8,128)(2,1)S(1)} %collective-permute-done.17.refs_2_.refs_1_, bf16[27,16,192]{2,1,0:T(8,128)(2,1)S(1)} %collective-permute-done.18.refs_1_.refs_2_, ...), custom_call_target="tpu_custom_call" | custom-call | bytes 3981312 | tf_op jit(solution)/shard_map/pallas_call | solution.py:32
  129.9 0.9 collective-permute-done.23.refs_3_
  130.9 1.5 copy-done.1
  132.4 2.7 %collective-permute-start.26 = (bf16[27,16,192]{2,1,0:T(8,128)(2,1)S(1)}, bf16[27,16,192]{2,1,0:T(8,128)(2,1)S(1)}, u32[]{:S(2)}, u32[]{:S(2)}) collective-permute-start(bf16[27,16,192]{2,1,0:T(8,128)(2,1)S(1)} %shard_map.149.refs_0_), channel_id=1, source_target_pairs={{0,6},{2,4},{4,2},{6,0},{1,7},{3,5},{5,3},{7,1},{8,14},{10,12},{12... | collective-permute-start | bytes 497672 | tf_op jit(solution)/shard_map/ppermute | solution.py:259
  135.2 1.2 collective-permute-start.24
  136.4 5.3 %collective-permute-done.26.refs_3_ = bf16[27,16,192]{2,1,0:T(8,128)(2,1)S(1)} collective-permute-done((bf16[27,16,192]{2,1,0:T(8,128)(2,1)S(1)}, bf16[27,16,192]{2,1,0:T(8,128)(2,1)S(1)}, u32[]{:S(2)}, u32[]{:S(2)}) %collective-permute-start.26) | collective-permute-done | bytes 165920 | tf_op jit(solution)/shard_map/ppermute | solution.py:259
  141.7 3.7 %collective-permute-done.25.refs_2_ = bf16[27,16,192]{2,1,0:T(8,128)(2,1)S(1)} collective-permute-done((bf16[27,16,192]{2,1,0:T(8,128)(2,1)S(1)}, bf16[27,16,192]{2,1,0:T(8,128)(2,1)S(1)}, u32[]{:S(2)}, u32[]{:S(2)}) %collective-permute-start.25) | collective-permute-done | bytes 165920 | tf_op jit(solution)/shard_map/ppermute | solution.py:259
  145.5 0.4 collective-permute-start.28
  145.9 1.0 collective-permute-done.29.refs_6_
  147.2 2.0 %shard_map.150 = (f32[1728,192]{1,0:T(8,128)}, f32[1728,192]{1,0:T(8,128)}) custom-call(bf16[27,16,192]{2,1,0:T(8,128)(2,1)S(1)} %shard_map.149.refs_0_, bf16[27,16,192]{2,1,0:T(8,128)(2,1)S(1)} %collective-permute-done.24.refs_1_, bf16[27,16,192]{2,1,0:T(8,128)(2,1)S(1)} %collective-permute-done.25.refs_2_, ...), custom_call_target="tpu_custom_call" | custom-call | bytes 3981312 | tf_op jit(solution)/shard_map/pallas_call | solution.py:32
  (86 shorter events, 1.7 us)
Async XLA Ops:
  0.6 15.0 %copy-start.4 = (bf16[32,32,192]{2,1,0:T(8,128)(2,1)S(1)}, bf16[32,32,192]{2,1,0:T(8,128)(2,1)}, u32[]{:S(2)}) copy-start(bf16[32,32,192]{2,1,0:T(8,128)(2,1)} %refs_1_.2) | copy-start | bytes 1179652
  0.6 1.1 copy-start.8
  15.7 13.1 %copy-start.5 = (bf16[32,32,192]{2,1,0:T(8,128)(2,1)S(1)}, bf16[32,32,192]{2,1,0:T(8,128)(2,1)}, u32[]{:S(2)}) copy-start(bf16[32,32,192]{2,1,0:T(8,128)(2,1)} %refs_1_.3) | copy-start | bytes 1179652
  15.7 13.1 %copy-start.6 = (bf16[32,32,192]{2,1,0:T(8,128)(2,1)S(1)}, bf16[32,32,192]{2,1,0:T(8,128)(2,1)}, u32[]{:S(2)}) copy-start(bf16[32,32,192]{2,1,0:T(8,128)(2,1)} %refs_2_.1) | copy-start | bytes 1179652
  15.7 13.1 %copy-start.7 = (bf16[32,32,192]{2,1,0:T(8,128)(2,1)S(1)}, bf16[32,32,192]{2,1,0:T(8,128)(2,1)}, u32[]{:S(2)}) copy-start(bf16[32,32,192]{2,1,0:T(8,128)(2,1)} %refs_3_.1) | copy-start | bytes 1179652
  16.5 12.3 %all-to-all-start.1 = ((bf16[8,1,2,2,2,16,192]{6,5,4,3,2,1,0:T(8,128)(2,1)}), bf16[8,1,2,2,2,16,192]{6,5,4,3,2,1,0:T(8,128)(2,1)S(1)}, u32[]{:S(2)}, u32[]{:S(2)}) async-start(bf16[8,1,2,2,2,16,192]{6,5,4,3,2,1,0:T(8,128)(2,1)} %shard_map.129), calls=%async_computation.1 | async-start | bytes 1048576 | tf_op jit(solution)/shard_map/all_to_all | solution.py:238
  20.8 12.9 %collective-permute-start = (bf16[2,2,2,2,2,16,192]{6,5,4,3,2,1,0:T(8,128)(2,1)}, bf16[2,2,2,2,2,16,192]{6,5,4,3,2,1,0:T(8,128)(2,1)}, u32[]{:S(2)}, u32[]{:S(2)}) collective-permute-start(bf16[2,2,2,2,2,16,192]{6,5,4,3,2,1,0:T(8,128)(2,1)} %bitcast.2), channel_id=1, source_target_pairs={{0,8},{8,16},{16,24},{24,0},{1,9},{9,17},{17,25},{25,1},{2,10},{10... | collective-permute-start | bytes 589832 | tf_op jit(solution)/shard_map/ppermute | solution.py:254
  22.4 14.3 %collective-permute-start.1 = (bf16[2,2,2,2,2,16,192]{6,5,4,3,2,1,0:T(8,128)(2,1)}, bf16[2,2,2,2,2,16,192]{6,5,4,3,2,1,0:T(8,128)(2,1)}, u32[]{:S(2)}, u32[]{:S(2)}) collective-permute-start(bf16[2,2,2,2,2,16,192]{6,5,4,3,2,1,0:T(8,128)(2,1)} %bitcast.3), channel_id=1, source_target_pairs={{8,0},{16,8},{24,16},{0,24},{9,1},{17,9},{25,17},{1,25},{10,2},{18... | collective-permute-start | bytes 589832 | tf_op jit(solution)/shard_map/ppermute | solution.py:254
  30.0 6.7 %copy-start.9 = (bf16[9,192,192]{2,1,0:T(8,128)(2,1)S(1)}, bf16[9,192,192]{2,1,0:T(8,128)(2,1)}, u32[]{:S(2)}) copy-start(bf16[9,192,192]{2,1,0:T(8,128)(2,1)} %refs_5_.2) | copy-start | bytes 1990660
  30.0 30.4 %all-to-all-start.2 = ((bf16[8,3,2,2,2,16,192]{6,5,4,3,2,1,0:T(8,128)(2,1)}), bf16[8,3,2,2,2,16,192]{6,5,4,3,2,1,0:T(8,128)(2,1)S(1)}, u32[]{:S(2)}, u32[]{:S(2)}) async-start(bf16[8,3,2,2,2,16,192]{6,5,4,3,2,1,0:T(8,128)(2,1)} %shard_map.130.refs_0_), calls=%async_computation.2 | async-start | bytes 3145728 | tf_op jit(solution)/shard_map/all_to_all | solution.py:238
  39.2 11.1 %collective-permute-start.2 = (bf16[2,8,2,16,192]{4,3,2,1,0:T(8,128)(2,1)S(1)}, bf16[2,8,2,16,192]{4,3,2,1,0:T(8,128)(2,1)S(1)}, u32[]{:S(2)}, u32[]{:S(2)}) collective-permute-start(bf16[2,8,2,16,192]{4,3,2,1,0:T(8,128)(2,1)S(1)} %get-tuple-element.32.refs_3_), channel_id=1, source_target_pairs={{0,8},{8,16},{16,24},{24,0},{1,9},{9,17},{17,25},{25,1},{2,10},{10... | collective-permute-start | bytes 589832 | tf_op jit(solution)/shard_map/ppermute | solution.py:254
  40.4 13.6 %collective-permute-start.3 = (bf16[2,8,2,16,192]{4,3,2,1,0:T(8,128)(2,1)S(1)}, bf16[2,8,2,16,192]{4,3,2,1,0:T(8,128)(2,1)S(1)}, u32[]{:S(2)}, u32[]{:S(2)}) collective-permute-start(bf16[2,8,2,16,192]{4,3,2,1,0:T(8,128)(2,1)S(1)} %get-tuple-element.33.refs_2_), channel_id=1, source_target_pairs={{8,0},{16,8},{24,16},{0,24},{9,1},{17,9},{25,17},{1,25},{10,2},{18... | collective-permute-start | bytes 589832 | tf_op jit(solution)/shard_map/ppermute | solution.py:254
  43.1 10.9 %copy-start.10 = (bf16[9,192,192]{2,1,0:T(8,128)(2,1)S(1)}, bf16[9,192,192]{2,1,0:T(8,128)(2,1)}, u32[]{:S(2)}) copy-start(bf16[9,192,192]{2,1,0:T(8,128)(2,1)} %refs_6_.1) | copy-start | bytes 1990660
  44.3 11.1 %copy-start.17 = (f32[1728,192]{1,0:T(8,128)}, f32[1728,192]{1,0:T(8,128)S(1)}, u32[]{:S(2)}) copy-start(f32[1728,192]{1,0:T(8,128)S(1)} %shard_map.132.refs_0_.refs_2_) | copy-start | bytes 3981316
  55.4 1.1 copy-start.19
  56.6 9.2 %copy-start.13 = (bf16[1,8,2,16,192]{4,3,2,1,0:T(8,128)(2,1)}, bf16[1,8,2,16,192]{4,3,2,1,0:T(8,128)(2,1)S(1)}, u32[]{:S(2)}) copy-start(bf16[1,8,2,16,192]{4,3,2,1,0:T(8,128)(2,1)S(1)} %get-tuple-element.39.refs_2_) | copy-start | bytes 294916
  56.6 9.2 %copy-start.15 = (bf16[1,8,2,16,192]{4,3,2,1,0:T(8,128)(2,1)}, bf16[1,8,2,16,192]{4,3,2,1,0:T(8,128)(2,1)S(1)}, u32[]{:S(2)}) copy-start(bf16[1,8,2,16,192]{4,3,2,1,0:T(8,128)(2,1)S(1)} %get-tuple-element.38.refs_4_) | copy-start | bytes 294916
  56.6 9.2 %copy-start.25 = (bf16[2,8,2,16,192]{4,3,2,1,0:T(8,128)(2,1)}, bf16[2,8,2,16,192]{4,3,2,1,0:T(8,128)(2,1)S(1)}, u32[]{:S(2)}) copy-start(bf16[2,8,2,16,192]{4,3,2,1,0:T(8,128)(2,1)S(1)} %get-tuple-element.40.refs_3_) | copy-start | bytes 589828
  56.6 9.2 %collective-permute-start.6 = (bf16[1,8,2,16,192]{4,3,2,1,0:T(8,128)(2,1)S(1)}, bf16[1,8,2,16,192]{4,3,2,1,0:T(8,128)(2,1)S(1)}, u32[]{:S(2)}, u32[]{:S(2)}) collective-permute-start(bf16[1,8,2,16,192]{4,3,2,1,0:T(8,128)(2,1)S(1)} %get-tuple-element.38.refs_4_), channel_id=1, source_target_pairs={{0,8},{8,16},{16,24},{24,0},{1,9},{9,17},{17,25},{25,1},{2,10},{10... | collective-permute-start | bytes 294920 | tf_op jit(solution)/shard_map/ppermute | solution.py:254
  56.9 8.9 %collective-permute-start.7 = (bf16[1,8,2,16,192]{4,3,2,1,0:T(8,128)(2,1)S(1)}, bf16[1,8,2,16,192]{4,3,2,1,0:T(8,128)(2,1)S(1)}, u32[]{:S(2)}, u32[]{:S(2)}) collective-permute-start(bf16[1,8,2,16,192]{4,3,2,1,0:T(8,128)(2,1)S(1)} %get-tuple-element.39.refs_2_), channel_id=1, source_target_pairs={{8,0},{16,8},{24,16},{0,24},{9,1},{17,9},{25,17},{1,25},{10,2},{18... | collective-permute-start | bytes 294920 | tf_op jit(solution)/shard_map/ppermute | solution.py:254
  60.4 16.6 %copy-start.2 = (bf16[8,3,2,2,2,16,192]{6,5,4,3,2,1,0:T(8,128)(2,1)}, bf16[8,3,2,2,2,16,192]{6,5,4,3,2,1,0:T(8,128)(2,1)S(1)}, u32[]{:S(2)}) copy-start(bf16[8,3,2,2,2,16,192]{6,5,4,3,2,1,0:T(8,128)(2,1)S(1)} %all-to-all-done.2) | copy-start | bytes 3538948
  60.4 2.0 %copy-start.18 = (f32[1728,192]{1,0:T(8,128)S(1)}, f32[1728,192]{1,0:T(8,128)}, u32[]{:S(2)}) copy-start(f32[1728,192]{1,0:T(8,128)} %copy-done.17) | copy-start | bytes 3981316
  62.4 1.4 copy-start.20
  63.9 2.0 %copy-start.11 = (bf16[9,192,192]{2,1,0:T(8,128)(2,1)S(1)}, bf16[9,192,192]{2,1,0:T(8,128)(2,1)}, u32[]{:S(2)}) copy-start(bf16[9,192,192]{2,1,0:T(8,128)(2,1)} %refs_7_.1) | copy-start | bytes 1990660
  65.2 6.9 %collective-permute-start.4 = (bf16[2,27,16,192]{3,2,1,0:T(8,128)(2,1)S(1)}, bf16[2,27,16,192]{3,2,1,0:T(8,128)(2,1)S(1)}, u32[]{:S(2)}, u32[]{:S(2)}) collective-permute-start(bf16[2,27,16,192]{3,2,1,0:T(8,128)(2,1)S(1)} %get-tuple-element.36), channel_id=1, source_target_pairs={{0,1},{1,0},{2,3},{3,2},{4,5},{5,4},{6,7},{7,6},{8,9},{9,8},{10,11... | collective-permute-start | bytes 995336 | tf_op jit(solution)/shard_map/ppermute | solution.py:259
  65.3 6.8 %collective-permute-start.5 = (bf16[2,27,16,192]{3,2,1,0:T(8,128)(2,1)S(1)}, bf16[2,27,16,192]{3,2,1,0:T(8,128)(2,1)S(1)}, u32[]{:S(2)}, u32[]{:S(2)}) collective-permute-start(bf16[2,27,16,192]{3,2,1,0:T(8,128)(2,1)S(1)} %get-tuple-element.37), channel_id=1, source_target_pairs={{0,1},{1,0},{2,3},{3,2},{4,5},{5,4},{6,7},{7,6},{8,9},{9,8},{10,11... | collective-permute-start | bytes 995336 | tf_op jit(solution)/shard_map/ppermute | solution.py:259
  67.3 0.9 copy-start.21
  68.3 11.2 %collective-permute-start.8 = (bf16[1,8,2,16,192]{4,3,2,1,0:T(8,128)(2,1)S(1)}, bf16[1,8,2,16,192]{4,3,2,1,0:T(8,128)(2,1)S(1)}, u32[]{:S(2)}, u32[]{:S(2)}) collective-permute-start(bf16[1,8,2,16,192]{4,3,2,1,0:T(8,128)(2,1)S(1)} %get-tuple-element.41.refs_3_), channel_id=1, source_target_pairs={{0,8},{8,16},{16,24},{24,0},{1,9},{9,17},{17,25},{25,1},{2,10},{10... | collective-permute-start | bytes 294920 | tf_op jit(solution)/shard_map/ppermute | solution.py:254
  68.3 11.2 %collective-permute-start.9 = (bf16[1,8,2,16,192]{4,3,2,1,0:T(8,128)(2,1)S(1)}, bf16[1,8,2,16,192]{4,3,2,1,0:T(8,128)(2,1)S(1)}, u32[]{:S(2)}, u32[]{:S(2)}) collective-permute-start(bf16[1,8,2,16,192]{4,3,2,1,0:T(8,128)(2,1)S(1)} %get-tuple-element.42.refs_1_), channel_id=1, source_target_pairs={{8,0},{16,8},{24,16},{0,24},{9,1},{17,9},{25,17},{1,25},{10,2},{18... | collective-permute-start | bytes 294920 | tf_op jit(solution)/shard_map/ppermute | solution.py:254
  73.2 15.4 %all-to-all-start.3 = ((bf16[4,27,16,192]{3,2,1,0:T(8,128)(2,1)}), bf16[4,27,16,192]{3,2,1,0:T(8,128)(2,1)S(1)}, u32[]{:S(2)}, u32[]{:S(2)}) async-start(bf16[4,27,16,192]{3,2,1,0:T(8,128)(2,1)} %shard_map.135.refs_0_), calls=%async_computation.3 | async-start | bytes 1769472 | tf_op jit(solution)/shard_map/all_to_all | solution.py:296
  77.0 1.2 copy-start.22
  79.5 1.4 copy-start.3
  83.3 0.9 copy-start.23
  84.3 4.5 %collective-permute-start.10 = (bf16[2,27,16,192]{3,2,1,0:T(8,128)(2,1)}, bf16[2,27,16,192]{3,2,1,0:T(8,128)(2,1)S(1)}, u32[]{:S(2)}, u32[]{:S(2)}) collective-permute-start(bf16[2,27,16,192]{3,2,1,0:T(8,128)(2,1)} %get-tuple-element.46), channel_id=1, source_target_pairs={{0,1},{1,0},{2,3},{3,2},{4,5},{5,4},{6,7},{7,6},{8,9},{9,8},{10,11... | collective-permute-start | bytes 995336 | tf_op jit(solution)/shard_map/ppermute | solution.py:259
  84.3 4.5 %collective-permute-start.11 = (bf16[2,27,16,192]{3,2,1,0:T(8,128)(2,1)}, bf16[2,27,16,192]{3,2,1,0:T(8,128)(2,1)S(1)}, u32[]{:S(2)}, u32[]{:S(2)}) collective-permute-start(bf16[2,27,16,192]{3,2,1,0:T(8,128)(2,1)} %get-tuple-element.47), channel_id=1, source_target_pairs={{0,1},{1,0},{2,3},{3,2},{4,5},{5,4},{6,7},{7,6},{8,9},{9,8},{10,11... | collective-permute-start | bytes 995336 | tf_op jit(solution)/shard_map/ppermute | solution.py:259
  88.7 6.4 %collective-permute-start.12 = (bf16[27,16,192]{2,1,0:T(8,128)(2,1)S(1)}, bf16[27,16,192]{2,1,0:T(8,128)(2,1)S(1)}, u32[]{:S(2)}, u32[]{:S(2)}) collective-permute-start(bf16[27,16,192]{2,1,0:T(8,128)(2,1)S(1)} %shard_map.136.refs_0_.refs_1_), channel_id=1, source_target_pairs={{0,8},{8,0},{16,24},{24,16},{1,9},{9,1},{17,25},{25,17},{2,10},{10... | collective-permute-start | bytes 497672 | tf_op jit(solution)/shard_map/ppermute | solution.py:259
  89.0 6.4 %collective-permute-start.13 = (bf16[27,16,192]{2,1,0:T(8,128)(2,1)S(1)}, bf16[27,16,192]{2,1,0:T(8,128)(2,1)S(1)}, u32[]{:S(2)}, u32[]{:S(2)}) collective-permute-start(bf16[27,16,192]{2,1,0:T(8,128)(2,1)S(1)} %get-tuple-element.49), channel_id=1, source_target_pairs={{0,2},{2,0},{4,6},{6,4},{1,3},{3,1},{5,7},{7,5},{8,10},{10,8},{12,... | collective-permute-start | bytes 497672 | tf_op jit(solution)/shard_map/ppermute | solution.py:259
  90.5 8.2 %collective-permute-start.14 = (bf16[27,16,192]{2,1,0:T(8,128)(2,1)S(1)}, bf16[27,16,192]{2,1,0:T(8,128)(2,1)S(1)}, u32[]{:S(2)}, u32[]{:S(2)}) collective-permute-start(bf16[27,16,192]{2,1,0:T(8,128)(2,1)S(1)} %get-tuple-element.50), channel_id=1, source_target_pairs={{0,4},{2,6},{4,0},{6,2},{1,5},{3,7},{5,1},{7,3},{8,12},{10,14},{12... | collective-permute-start | bytes 497672 | tf_op jit(solution)/shard_map/ppermute | solution.py:259
  91.0 10.9 %collective-permute-start.15 = (bf16[27,16,192]{2,1,0:T(8,128)(2,1)S(1)}, bf16[27,16,192]{2,1,0:T(8,128)(2,1)S(1)}, u32[]{:S(2)}, u32[]{:S(2)}) collective-permute-start(bf16[27,16,192]{2,1,0:T(8,128)(2,1)S(1)} %get-tuple-element.51), channel_id=1, source_target_pairs={{0,6},{2,4},{4,2},{6,0},{1,7},{3,5},{5,3},{7,1},{8,14},{10,12},{12... | collective-permute-start | bytes 497672 | tf_op jit(solution)/shard_map/ppermute | solution.py:259
  95.1 16.4 %copy-start.12 = (bf16[9,192,192]{2,1,0:T(8,128)(2,1)S(1)}, bf16[9,192,192]{2,1,0:T(8,128)(2,1)}, u32[]{:S(2)}) copy-start(bf16[9,192,192]{2,1,0:T(8,128)(2,1)} %refs_5_.3) | copy-start | bytes 1990660
  95.1 16.4 %copy-start.14 = (bf16[1,8,2,16,192]{4,3,2,1,0:T(8,128)(2,1)S(1)}, bf16[1,8,2,16,192]{4,3,2,1,0:T(8,128)(2,1)}, u32[]{:S(2)}) copy-start(bf16[1,8,2,16,192]{4,3,2,1,0:T(8,128)(2,1)} %copy-done.13) | copy-start | bytes 294916
  95.1 16.4 %copy-start.16 = (bf16[1,8,2,16,192]{4,3,2,1,0:T(8,128)(2,1)S(1)}, bf16[1,8,2,16,192]{4,3,2,1,0:T(8,128)(2,1)}, u32[]{:S(2)}) copy-start(bf16[1,8,2,16,192]{4,3,2,1,0:T(8,128)(2,1)} %copy-done.15) | copy-start | bytes 294916
  95.1 16.4 %copy-start.24 = (bf16[6,10,2,16,192]{4,3,2,1,0:T(8,128)(2,1)S(1)}, bf16[6,10,2,16,192]{4,3,2,1,0:T(8,128)(2,1)}, u32[]{:S(2)}) copy-start(bf16[6,10,2,16,192]{4,3,2,1,0:T(8,128)(2,1)} %copy-done.23) | copy-start | bytes 2211844
  95.1 16.4 %copy-start.26 = (bf16[2,8,2,16,192]{4,3,2,1,0:T(8,128)(2,1)S(1)}, bf16[2,8,2,16,192]{4,3,2,1,0:T(8,128)(2,1)}, u32[]{:S(2)}) copy-start(bf16[2,8,2,16,192]{4,3,2,1,0:T(8,128)(2,1)} %copy-done.25) | copy-start | bytes 589828
  95.2 11.2 %collective-permute-start.16 = (bf16[27,16,192]{2,1,0:T(8,128)(2,1)S(1)}, bf16[27,16,192]{2,1,0:T(8,128)(2,1)S(1)}, u32[]{:S(2)}, u32[]{:S(2)}) collective-permute-start(bf16[27,16,192]{2,1,0:T(8,128)(2,1)S(1)} %shard_map.141.refs_0_.refs_1_), channel_id=1, source_target_pairs={{0,16},{8,24},{16,0},{24,8},{1,17},{9,25},{17,1},{25,9},{2,18},{10... | collective-permute-start | bytes 497672 | tf_op jit(solution)/shard_map/ppermute | solution.py:259
  102.1 15.9 %collective-permute-start.20 = (bf16[27,16,192]{2,1,0:T(8,128)(2,1)S(1)}, bf16[27,16,192]{2,1,0:T(8,128)(2,1)S(1)}, u32[]{:S(2)}, u32[]{:S(2)}) collective-permute-start(bf16[27,16,192]{2,1,0:T(8,128)(2,1)S(1)} %shard_map.142.refs_0_.refs_1_), channel_id=1, source_target_pairs={{0,8},{8,0},{16,24},{24,16},{1,9},{9,1},{17,25},{25,17},{2,10},{10... | collective-permute-start | bytes 497672 | tf_op jit(solution)/shard_map/ppermute | solution.py:259
  106.5 11.5 %collective-permute-start.19 = (bf16[27,16,192]{2,1,0:T(8,128)(2,1)S(1)}, bf16[27,16,192]{2,1,0:T(8,128)(2,1)S(1)}, u32[]{:S(2)}, u32[]{:S(2)}) collective-permute-start(bf16[27,16,192]{2,1,0:T(8,128)(2,1)S(1)} %shard_map.144.refs_0_.refs_1_), channel_id=1, source_target_pairs={{0,6},{2,4},{4,2},{6,0},{1,7},{3,5},{5,3},{7,1},{8,14},{10,12},{12... | collective-permute-start | bytes 497672 | tf_op jit(solution)/shard_map/ppermute | solution.py:259
  109.4 10.9 %collective-permute-start.18 = (bf16[27,16,192]{2,1,0:T(8,128)(2,1)S(1)}, bf16[27,16,192]{2,1,0:T(8,128)(2,1)S(1)}, u32[]{:S(2)}, u32[]{:S(2)}) collective-permute-start(bf16[27,16,192]{2,1,0:T(8,128)(2,1)S(1)} %shard_map.144.refs_0_.refs_1_), channel_id=1, source_target_pairs={{0,4},{2,6},{4,0},{6,2},{1,5},{3,7},{5,1},{7,3},{8,12},{10,14},{12... | collective-permute-start | bytes 497672 | tf_op jit(solution)/shard_map/ppermute | solution.py:259
  110.1 10.3 %collective-permute-start.17 = (bf16[27,16,192]{2,1,0:T(8,128)(2,1)S(1)}, bf16[27,16,192]{2,1,0:T(8,128)(2,1)S(1)}, u32[]{:S(2)}, u32[]{:S(2)}) collective-permute-start(bf16[27,16,192]{2,1,0:T(8,128)(2,1)S(1)} %shard_map.144.refs_0_.refs_1_), channel_id=1, source_target_pairs={{0,2},{2,0},{4,6},{6,4},{1,3},{3,1},{5,7},{7,5},{8,10},{10,8},{12,... | collective-permute-start | bytes 497672 | tf_op jit(solution)/shard_map/ppermute | solution.py:259
  113.8 13.0 %all-to-all-start.4 = ((bf16[8,2,2,2,16,192]{5,4,3,2,1,0:T(8,128)(2,1)}), bf16[8,2,2,2,16,192]{5,4,3,2,1,0:T(8,128)(2,1)}, u32[]{:S(2)}, u32[]{:S(2)}) async-start(bf16[8,2,2,2,16,192]{5,4,3,2,1,0:T(8,128)(2,1)} %bitcast.5), calls=%async_computation.4 | async-start | bytes 1048576 | tf_op jit(solution)/shard_map/all_to_all | solution.py:246
  120.4 7.5 %collective-permute-start.22 = (bf16[2,27,16,192]{3,2,1,0:T(8,128)(2,1)S(1)}, bf16[2,27,16,192]{3,2,1,0:T(8,128)(2,1)S(1)}, u32[]{:S(2)}, u32[]{:S(2)}) collective-permute-start(bf16[2,27,16,192]{3,2,1,0:T(8,128)(2,1)S(1)} %shard_map.147), channel_id=1, source_target_pairs={{0,1},{1,0},{2,3},{3,2},{4,5},{5,4},{6,7},{7,6},{8,9},{9,8},{10,11... | collective-permute-start | bytes 995336 | tf_op jit(solution)/shard_map/ppermute | solution.py:259
  120.5 7.4 %collective-permute-start.21 = (bf16[2,27,16,192]{3,2,1,0:T(8,128)(2,1)S(1)}, bf16[2,27,16,192]{3,2,1,0:T(8,128)(2,1)S(1)}, u32[]{:S(2)}, u32[]{:S(2)}) collective-permute-start(bf16[2,27,16,192]{3,2,1,0:T(8,128)(2,1)S(1)} %shard_map.146), channel_id=1, source_target_pairs={{0,1},{1,0},{2,3},{3,2},{4,5},{5,4},{6,7},{7,6},{8,9},{9,8},{10,11... | collective-permute-start | bytes 995336 | tf_op jit(solution)/shard_map/ppermute | solution.py:259
  121.1 9.8 %collective-permute-start.23 = (bf16[27,16,192]{2,1,0:T(8,128)(2,1)S(1)}, bf16[27,16,192]{2,1,0:T(8,128)(2,1)S(1)}, u32[]{:S(2)}, u32[]{:S(2)}) collective-permute-start(bf16[27,16,192]{2,1,0:T(8,128)(2,1)S(1)} %shard_map.145.refs_0_.refs_2_), channel_id=1, source_target_pairs={{0,16},{8,24},{16,0},{24,8},{1,17},{9,25},{17,1},{25,9},{2,18},{10... | collective-permute-start | bytes 497672 | tf_op jit(solution)/shard_map/ppermute | solution.py:259
  127.8 4.6 %copy-start = (bf16[2,8,2,2,16,192]{5,4,3,2,1,0:T(8,128)(2,1)}, bf16[2,8,2,2,16,192]{5,4,3,2,1,0:T(8,128)(2,1)S(1)}, u32[]{:S(2)}) copy-start(bf16[2,8,2,2,16,192]{5,4,3,2,1,0:T(8,128)(2,1)S(1)} %copy.15) | copy-start | bytes 1179652
  130.9 1.5 copy-start.1
  132.4 9.3 %collective-permute-start.26 = (bf16[27,16,192]{2,1,0:T(8,128)(2,1)S(1)}, bf16[27,16,192]{2,1,0:T(8,128)(2,1)S(1)}, u32[]{:S(2)}, u32[]{:S(2)}) collective-permute-start(bf16[27,16,192]{2,1,0:T(8,128)(2,1)S(1)} %shard_map.149.refs_0_), channel_id=1, source_target_pairs={{0,6},{2,4},{4,2},{6,0},{1,7},{3,5},{5,3},{7,1},{8,14},{10,12},{12... | collective-permute-start | bytes 497672 | tf_op jit(solution)/shard_map/ppermute | solution.py:259
  135.2 10.2 %collective-permute-start.25 = (bf16[27,16,192]{2,1,0:T(8,128)(2,1)S(1)}, bf16[27,16,192]{2,1,0:T(8,128)(2,1)S(1)}, u32[]{:S(2)}, u32[]{:S(2)}) collective-permute-start(bf16[27,16,192]{2,1,0:T(8,128)(2,1)S(1)} %shard_map.149.refs_0_), channel_id=1, source_target_pairs={{0,4},{2,6},{4,0},{6,2},{1,5},{3,7},{5,1},{7,3},{8,12},{10,14},{12... | collective-permute-start | bytes 497672 | tf_op jit(solution)/shard_map/ppermute | solution.py:259
  135.2 10.3 %collective-permute-start.24 = (bf16[27,16,192]{2,1,0:T(8,128)(2,1)S(1)}, bf16[27,16,192]{2,1,0:T(8,128)(2,1)S(1)}, u32[]{:S(2)}, u32[]{:S(2)}) collective-permute-start(bf16[27,16,192]{2,1,0:T(8,128)(2,1)S(1)} %shard_map.149.refs_0_), channel_id=1, source_target_pairs={{0,2},{2,0},{4,6},{6,4},{1,3},{3,1},{5,7},{7,5},{8,10},{10,8},{12,... | collective-permute-start | bytes 497672 | tf_op jit(solution)/shard_map/ppermute | solution.py:259
  136.4 9.5 %collective-permute-start.27 = (bf16[27,16,192]{2,1,0:T(8,128)(2,1)S(1)}, bf16[27,16,192]{2,1,0:T(8,128)(2,1)S(1)}, u32[]{:S(2)}, u32[]{:S(2)}) collective-permute-start(bf16[27,16,192]{2,1,0:T(8,128)(2,1)S(1)} %shard_map.149.refs_0_), channel_id=1, source_target_pairs={{0,1},{1,0},{2,3},{3,2},{4,5},{5,4},{6,7},{7,6},{8,9},{9,8},{10,11... | collective-permute-start | bytes 497672 | tf_op jit(solution)/shard_map/ppermute | solution.py:259
  141.7 4.2 %collective-permute-start.30 = (bf16[27,16,192]{2,1,0:T(8,128)(2,1)S(1)}, bf16[27,16,192]{2,1,0:T(8,128)(2,1)S(1)}, u32[]{:S(2)}, u32[]{:S(2)}) collective-permute-start(bf16[27,16,192]{2,1,0:T(8,128)(2,1)S(1)} %collective-permute-done.26.refs_3_), channel_id=1, source_target_pairs={{0,1},{1,0},{2,3},{3,2},{4,5},{5,4},{6,7},{7,6},{8,9},{9,8},{10,11... | collective-permute-start | bytes 497672 | tf_op jit(solution)/shard_map/ppermute | solution.py:259
  145.4 1.5 collective-permute-start.29
  145.5 1.6 %collective-permute-start.28 = (bf16[27,16,192]{2,1,0:T(8,128)(2,1)S(1)}, bf16[27,16,192]{2,1,0:T(8,128)(2,1)S(1)}, u32[]{:S(2)}, u32[]{:S(2)}) collective-permute-start(bf16[27,16,192]{2,1,0:T(8,128)(2,1)S(1)} %collective-permute-done.24.refs_1_), channel_id=1, source_target_pairs={{0,1},{1,0},{2,3},{3,2},{4,5},{5,4},{6,7},{7,6},{8,9},{9,8},{10,11... | collective-permute-start | bytes 497672 | tf_op jit(solution)/shard_map/ppermute | solution.py:259

commit v5 on v4

--- a/solution.py
+++ b/solution.py
@@ -37,7 +37,7 @@
         out_specs=[pl.BlockSpec(memory_space=pltpu.VMEM)] * len(outs),
         scratch_shapes=scratch,
         compiler_params=pltpu.CompilerParams(vmem_limit_bytes=VMEM_LIMIT),
-        cost_estimate=pl.CostEstimate(flops=flops, bytes_accessed=size, transcendentals=0),
+        cost_estimate=pl.CostEstimate(flops=flops, bytes_accessed=size if flops else 0, transcendentals=0),
     )(*arrays)
 
 
@@ -388,14 +388,15 @@
     height, breadth, chan = output_gradient_final.shape
     final = swap_classes(pack_classes(output_gradient_final))
     low, high = ring(final[0, :, :, 0], final[1, :, :, 0])
-    act_two = (swap_classes(pack_classes(second_block_preactivation, after=[final])), 0)
+    packed = pack_classes(second_block_preactivation, after=[final])
+    act_two = (swap_classes(packed), 0)
     final = (final, 0)
 
     halves = [coarse(2, chan)] * 2
     thirds = [coarse(1, chan), coarse(2, chan), coarse(1, chan)]
 
     late = [first_block_preactivation, second_block_input, first_block_input]
-    packed = pack_classes(*late, after=[act_two[0]])
+    packed = pack_classes(*late, after=[packed])
     late = swap_classes(packed)
     act_one, entry_two, entry_one = (late, 0), (late, 1), (late, 2)
     field = [low, final, high]
@@ -417,14 +418,14 @@
     part = add_parts(parts)
     own_b, sent_b = sum_plane(keep, got, after=[part])
     part = add(part, xor(part, "z", 1), after=[own_b])
-    part_b = add(own_b, *plane_terms(sent_b), after=[part])
-    (out,), _ = conv_one(wide, mid, first_block_conv_one, 1, whole, after=[part_b])
+    (out,), _ = conv_one(wide, mid, first_block_conv_one, 1, whole, after=[part])
+    part_b = add(own_b, *plane_terms(sent_b), after=[part, out])
     out = gather_classes(out, height, breadth)
     part = sum_far(part, after=[part_b])
     part_b = add(part_b, xor(part_b, "z", 1), after=[part])
     second_two, second_one = spread_weights(part, len(TAPS), gate=part_b)
-    part_b = sum_far(part_b, after=[second_two, out])
-    first_two, first_one = spread_weights(part_b, len(TAPS))
+    part_b = sum_far(part_b, after=[out])
+    first_two, first_one = spread_weights(part_b, len(TAPS), after=[second_two])
     return out, first_one, first_two, second_one, second_two
 
 

time: 150 us -> 144 us (0.960)
  waiting for transfers between devices: 51.8 us -> 44.9 us
    all_to_all x1, waiting for transfers between devices: 5.7 us -> 0.01 us  [gather_classes(): parts = lax.all_to_all(parts, PLANE, 0, 0)]
    ppermute x23, starting transfers between devices: 16.6 us -> 18.3 us  [xor(): return lax.ppermute(value, axis, [(i, i ^ k) for i in range(count)])]
  transfers between devices with their start and end apart: 35 -> 35, of which waited for: 18 -> 13; matrix products, arithmetic and copies ran while one was open for 1% -> 1% of each run, Pallas kernels for 13% -> 13%
where the time goes in v5:
time: 144 us; the launch traced here: 143 us
  starting transfers between devices  48.3 us (34%)
  waiting for transfers between devices  44.9 us (31%)
  Pallas kernels  21.5 us (15%)
  blocking collectives  13.9 us (10%)
  local copies, waits for them, and re-layouts  13.8 us (10%)
    ppermute x23, waiting for transfers between devices, xor(): return lax.ppermute(value, axis, [(i, i ^ k) for i in range(count)])  24.4 us
    pallas_call x23, Pallas kernels, call(): pl.pallas_call(lambda *refs: body(*refs[len(after):]), grid=(1,), out_sha...  21.5 us
    ppermute x23, starting transfers between devices, xor(): return lax.ppermute(value, axis, [(i, i ^ k) for i in range(count)])  18.3 us
    all_to_all x1, blocking collectives, swap_classes(): moved = lax.all_to_all(packed, PLANE, 0, 0)  13.9 us
    unnamed x54, local copies, waits for them, and re-layouts  12.9 us
    ppermute x4, starting transfers between devices, ring(): lax.ppermute(left_edge, 'z', down)  12.3 us
    ppermute x4, waiting for transfers between devices, ring(): lax.ppermute(left_edge, 'z', down)  7.88 us
    all_to_all x2, starting transfers between devices, swap_classes(): moved = lax.all_to_all(packed, PLANE, 0, 0)  7.08 us
  transfers between devices with their start and end apart: 35, of which 13 were waited for; matrix products, arithmetic and copies ran while one was open for 1% of the time, Pallas kernels for 13%

profile of v5, /device:TPU:0, one launch (start us, length us, event | category | flops | bytes accessed | tf_op | source)
XLA Modules:
  0.0 143.3 jit_solution(16861930861700343959)
XLA Ops:
  0.7 1.1 copy-done.8
  1.8 13.9 %all_to_all.25 = bf16[8,1,2,2,2,16,192]{6,5,4,3,2,1,0:T(8,128)(2,1)S(1)} all-to-all(bf16[8,1,2,2,2,16,192]{6,5,4,3,2,1,0:T(8,128)(2,1)S(1)} %shard_map.128), channel_id=1, replica_groups=mesh['z'=4,'x'=2,'y'=2,'c'=2] {'x','y','c'}, dimensions={0} | all-to-all | bytes 786432 | tf_op jit(solution)/shard_map/all_to_all | solution.py:238
  15.7 0.8 shard_map.129.refs_0_
  16.5 3.5 %all-to-all-start.1 = ((bf16[8,1,2,2,2,16,192]{6,5,4,3,2,1,0:T(8,128)(2,1)}), bf16[8,1,2,2,2,16,192]{6,5,4,3,2,1,0:T(8,128)(2,1)S(1)}, u32[]{:S(2)}, u32[]{:S(2)}) async-start(bf16[8,1,2,2,2,16,192]{6,5,4,3,2,1,0:T(8,128)(2,1)} %shard_map.129.refs_0_), calls=%async_computation.1 | async-start | bytes 1048576 | tf_op jit(solution)/shard_map/all_to_all | solution.py:238
  20.0 0.8 fusion
  20.8 1.6 %collective-permute-start = (bf16[2,2,2,2,2,16,192]{6,5,4,3,2,1,0:T(8,128)(2,1)}, bf16[2,2,2,2,2,16,192]{6,5,4,3,2,1,0:T(8,128)(2,1)S(1)}, u32[]{:S(2)}, u32[]{:S(2)}) collective-permute-start(bf16[2,2,2,2,2,16,192]{6,5,4,3,2,1,0:T(8,128)(2,1)} %bitcast.1), channel_id=1, source_target_pairs={{0,8},{8,16},{16,24},{24,0},{1,9},{9,17},{17,25},{25,1},{2,10},{10... | collective-permute-start | bytes 589832 | tf_op jit(solution)/shard_map/ppermute | solution.py:254
  22.4 2.2 %collective-permute-start.1 = (bf16[2,2,2,2,2,16,192]{6,5,4,3,2,1,0:T(8,128)(2,1)}, bf16[2,2,2,2,2,16,192]{6,5,4,3,2,1,0:T(8,128)(2,1)S(1)}, u32[]{:S(2)}, u32[]{:S(2)}) collective-permute-start(bf16[2,2,2,2,2,16,192]{6,5,4,3,2,1,0:T(8,128)(2,1)} %bitcast.2), channel_id=1, source_target_pairs={{8,0},{16,8},{24,16},{0,24},{9,1},{17,9},{25,17},{1,25},{10,2},{18... | collective-permute-start | bytes 589832 | tf_op jit(solution)/shard_map/ppermute | solution.py:254
  24.7 1.2 shard_map.130.refs_0_
  25.9 2.9 %all-to-all-done.1 = bf16[8,1,2,2,2,16,192]{6,5,4,3,2,1,0:T(8,128)(2,1)S(1)} async-done(((bf16[8,1,2,2,2,16,192]{6,5,4,3,2,1,0:T(8,128)(2,1)}), bf16[8,1,2,2,2,16,192]{6,5,4,3,2,1,0:T(8,128)(2,1)S(1)}, u32[]{:S(2)}, u32[]{:S(2)}) %all-to-all-start.1) | async-done | bytes 393248 | tf_op jit(solution)/shard_map/all_to_all | solution.py:238
  28.8 3.6 %all-to-all-start.2 = ((bf16[8,3,2,2,2,16,192]{6,5,4,3,2,1,0:T(8,128)(2,1)}), bf16[8,3,2,2,2,16,192]{6,5,4,3,2,1,0:T(8,128)(2,1)S(1)}, u32[]{:S(2)}, u32[]{:S(2)}) async-start(bf16[8,3,2,2,2,16,192]{6,5,4,3,2,1,0:T(8,128)(2,1)} %shard_map.130.refs_0_), calls=%async_computation.2 | async-start | bytes 3145728 | tf_op jit(solution)/shard_map/all_to_all | solution.py:238
  32.4 4.2 %collective-permute-done.1.refs_3_ = bf16[2,2,2,2,2,16,192]{6,5,4,3,2,1,0:T(8,128)(2,1)S(1)} collective-permute-done((bf16[2,2,2,2,2,16,192]{6,5,4,3,2,1,0:T(8,128)(2,1)}, bf16[2,2,2,2,2,16,192]{6,5,4,3,2,1,0:T(8,128)(2,1)S(1)}, u32[]{:S(2)}, u32[]{:S(2)}) %collective-permute-start.1) | collective-permute-done | bytes 196640 | tf_op jit(solution)/shard_map/ppermute | solution.py:254
  36.6 1.2 copy-done.9
  37.8 1.5 %shard_map.131 = (bf16[2,8,2,16,192]{4,3,2,1,0:T(8,128)(2,1)S(1)}, bf16[2,8,2,16,192]{4,3,2,1,0:T(8,128)(2,1)S(1)}, bf16[8,12,2,16,192]{4,3,2,1,0:T(8,128)(2,1)S(1)}) custom-call(bf16[8,3,2,2,2,16,192]{6,5,4,3,2,1,0:T(8,128)(2,1)} %shard_map.130.refs_0_, bf16[2,2,2,2,2,16,192]{6,5,4,3,2,1,0:T(8,128)(2,1)S(1)} %collective-permute-done.refs_1_, ...), custom_call_target="tpu_custom_call" | custom-call | flops 13589544960 | bytes 3416064 | tf_op jit(solution)/shard_map/pallas_call | solution.py:32
  39.3 1.2 collective-permute-start.2
  40.4 2.7 %collective-permute-start.3 = (bf16[2,8,2,16,192]{4,3,2,1,0:T(8,128)(2,1)S(1)}, bf16[2,8,2,16,192]{4,3,2,1,0:T(8,128)(2,1)S(1)}, u32[]{:S(2)}, u32[]{:S(2)}) collective-permute-start(bf16[2,8,2,16,192]{4,3,2,1,0:T(8,128)(2,1)S(1)} %get-tuple-element.33.refs_2_), channel_id=1, source_target_pairs={{8,0},{16,8},{24,16},{0,24},{9,1},{17,9},{25,17},{1,25},{10,2},{18... | collective-permute-start | bytes 589832 | tf_op jit(solution)/shard_map/ppermute | solution.py:254
  43.1 1.2 shard_map.132.refs_0_.refs_2_
  44.4 6.0 %collective-permute-done.2.refs_1_ = bf16[2,8,2,16,192]{4,3,2,1,0:T(8,128)(2,1)S(1)} collective-permute-done((bf16[2,8,2,16,192]{4,3,2,1,0:T(8,128)(2,1)S(1)}, bf16[2,8,2,16,192]{4,3,2,1,0:T(8,128)(2,1)S(1)}, u32[]{:S(2)}, u32[]{:S(2)}) %collective-permute-start.2) | collective-permute-done | bytes 196640 | tf_op jit(solution)/shard_map/ppermute | solution.py:254
  50.4 3.6 %collective-permute-done.3.refs_4_ = bf16[2,8,2,16,192]{4,3,2,1,0:T(8,128)(2,1)S(1)} collective-permute-done((bf16[2,8,2,16,192]{4,3,2,1,0:T(8,128)(2,1)S(1)}, bf16[2,8,2,16,192]{4,3,2,1,0:T(8,128)(2,1)S(1)}, u32[]{:S(2)}, u32[]{:S(2)}) %collective-permute-start.3) | collective-permute-done | bytes 196640 | tf_op jit(solution)/shard_map/ppermute | solution.py:254
  54.0 1.4 shard_map.133
  55.5 1.1 copy-done.19
  56.6 0.3 collective-permute-start.6
  56.9 3.5 %collective-permute-start.7 = (bf16[1,8,2,16,192]{4,3,2,1,0:T(8,128)(2,1)S(1)}, bf16[1,8,2,16,192]{4,3,2,1,0:T(8,128)(2,1)S(1)}, u32[]{:S(2)}, u32[]{:S(2)}) collective-permute-start(bf16[1,8,2,16,192]{4,3,2,1,0:T(8,128)(2,1)S(1)} %get-tuple-element.39.refs_2_), channel_id=1, source_target_pairs={{8,0},{16,8},{24,16},{0,24},{9,1},{17,9},{25,17},{1,25},{10,2},{18... | collective-permute-start | bytes 294920 | tf_op jit(solution)/shard_map/ppermute | solution.py:254
  60.4 2.0 %copy-done.18 = f32[1728,192]{1,0:T(8,128)S(1)} copy-done((f32[1728,192]{1,0:T(8,128)S(1)}, f32[1728,192]{1,0:T(8,128)}, u32[]{:S(2)}) %copy-start.18) | copy-done | bytes 1327128
  62.5 1.4 copy-done.20
  63.9 1.3 shard_map.134
  65.3 0.5 collective-permute-start.5
  65.8 1.5 %shard_map.137 = (bf16[1,8,2,16,192]{4,3,2,1,0:T(8,128)(2,1)S(1)}, bf16[2,8,2,16,192]{4,3,2,1,0:T(8,128)(2,1)S(1)}, bf16[1,8,2,16,192]{4,3,2,1,0:T(8,128)(2,1)S(1)}, bf16[6,10,2,16,192]{4,3,2,1,0:T(8,128)(2,1)S(1)}) custom-call(f32[108,16,192]{2,1,0:T(8,128)S(1)} %get-tuple-element.35.refs_0_, ...), custom_call_target="tpu_custom_call" | custom-call | flops 13589544960 | bytes 2777088 | tf_op jit(solution)/shard_map/pallas_call | solution.py:32
  67.4 0.9 copy-done.21
  68.3 3.8 %collective-permute-start.9 = (bf16[1,8,2,16,192]{4,3,2,1,0:T(8,128)(2,1)S(1)}, bf16[1,8,2,16,192]{4,3,2,1,0:T(8,128)(2,1)S(1)}, u32[]{:S(2)}, u32[]{:S(2)}) collective-permute-start(bf16[1,8,2,16,192]{4,3,2,1,0:T(8,128)(2,1)S(1)} %get-tuple-element.42.refs_1_), channel_id=1, source_target_pairs={{8,0},{16,8},{24,16},{0,24},{9,1},{17,9},{25,17},{1,25},{10,2},{18... | collective-permute-start | bytes 294920 | tf_op jit(solution)/shard_map/ppermute | solution.py:254
  72.1 1.1 shard_map.135.refs_0_
  73.2 3.8 %all-to-all-start.3 = ((bf16[4,27,16,192]{3,2,1,0:T(8,128)(2,1)}), bf16[4,27,16,192]{3,2,1,0:T(8,128)(2,1)S(1)}, u32[]{:S(2)}, u32[]{:S(2)}) async-start(bf16[4,27,16,192]{3,2,1,0:T(8,128)(2,1)} %shard_map.135.refs_0_), calls=%async_computation.3 | async-start | bytes 1769472 | tf_op jit(solution)/shard_map/all_to_all | solution.py:296
  77.1 1.2 copy-done.22
  78.3 1.2 shard_map.138.refs_6_
  79.5 1.4 copy-done.3
  80.9 2.5 %shard_map.139 = (f32[108,16,192]{2,1,0:T(8,128)S(1)}, bf16[2,27,16,192]{3,2,1,0:T(8,128)(2,1)}, bf16[2,27,16,192]{3,2,1,0:T(8,128)(2,1)}, bf16[6,10,2,16,192]{4,3,2,1,0:T(8,128)(2,1)S(1)}) custom-call(bf16[1,8,2,16,192]{4,3,2,1,0:T(8,128)(2,1)S(1)} %collective-permute-done.8.refs_0_, bf16[1,8,2,16,192]{4,3,2,1,0:T(8,128)(2,1)S(1)} %get-tuple-element.42.refs_1_, ...), custom_call_target="tpu_custom_call" | custom-call | flops 13589544960 | bytes 5038080 | tf_op jit(solution)/shard_map/pallas_call | solution.py:32
  83.4 0.9 copy-done.23
  84.3 0.5 collective-permute-start.11
  84.8 3.8 %all-to-all-done.3.refs_0_ = bf16[4,27,16,192]{3,2,1,0:T(8,128)(2,1)S(1)} async-done(((bf16[4,27,16,192]{3,2,1,0:T(8,128)(2,1)}), bf16[4,27,16,192]{3,2,1,0:T(8,128)(2,1)S(1)}, u32[]{:S(2)}, u32[]{:S(2)}) %all-to-all-start.3) | async-done | bytes 663584 | tf_op jit(solution)/shard_map/all_to_all | solution.py:296
  88.9 0.9 shard_map.140
  89.8 1.5 %collective-permute-start.13 = (bf16[27,16,192]{2,1,0:T(8,128)(2,1)}, bf16[27,16,192]{2,1,0:T(8,128)(2,1)S(1)}, u32[]{:S(2)}, u32[]{:S(2)}) collective-permute-start(bf16[27,16,192]{2,1,0:T(8,128)(2,1)} %get-tuple-element.50), channel_id=1, source_target_pairs={{0,2},{2,0},{4,6},{6,4},{1,3},{3,1},{5,7},{7,5},{8,10},{10,8},{12,... | collective-permute-start | bytes 497672 | tf_op jit(solution)/shard_map/ppermute | solution.py:259
  91.3 0.6 collective-permute-start.14
  91.8 1.5 %collective-permute-start.15 = (bf16[27,16,192]{2,1,0:T(8,128)(2,1)}, bf16[27,16,192]{2,1,0:T(8,128)(2,1)S(1)}, u32[]{:S(2)}, u32[]{:S(2)}) collective-permute-start(bf16[27,16,192]{2,1,0:T(8,128)(2,1)} %get-tuple-element.52), channel_id=1, source_target_pairs={{0,6},{2,4},{4,2},{6,0},{1,7},{3,5},{5,3},{7,1},{8,14},{10,12},{12... | collective-permute-start | bytes 497672 | tf_op jit(solution)/shard_map/ppermute | solution.py:259
  93.3 1.8 %collective-permute-done.12.refs_2_ = bf16[27,16,192]{2,1,0:T(8,128)(2,1)S(1)} collective-permute-done((bf16[27,16,192]{2,1,0:T(8,128)(2,1)S(1)}, bf16[27,16,192]{2,1,0:T(8,128)(2,1)S(1)}, u32[]{:S(2)}, u32[]{:S(2)}) %collective-permute-start.12) | collective-permute-done | bytes 165920 | tf_op jit(solution)/shard_map/ppermute | solution.py:259
  95.3 2.2 %shard_map.142.refs_1_ = bf16[2,2,2,2,2,2,16,192]{7,6,5,4,3,2,1,0:T(8,128)(2,1)} custom-call(bf16[27,16,192]{2,1,0:T(8,128)(2,1)S(1)} %shard_map.141.refs_0_.refs_1_, bf16[6,10,2,16,192]{4,3,2,1,0:T(8,128)(2,1)S(1)} %copy-done.24, bf16[1,8,2,16,192]{4,3,2,1,0:T(8,128)(2,1)S(1)} %copy-done.14, bf16[2,8,2,16,192]{4,3,2,1,0:T(8,128)(2,1)S(1)} %copy-done.26, ...), custom_call_target="tpu_custom_call" | custom-call | flops 13589544960 | bytes 2187264 | tf_op jit(solution)/shard_map/pallas_call | solution.py:32
  97.5 3.7 %all-to-all-start.4 = ((bf16[8,2,2,2,16,192]{5,4,3,2,1,0:T(8,128)(2,1)}), bf16[8,2,2,2,16,192]{5,4,3,2,1,0:T(8,128)(2,1)S(1)}, u32[]{:S(2)}, u32[]{:S(2)}) async-start(bf16[8,2,2,2,16,192]{5,4,3,2,1,0:T(8,128)(2,1)} %bitcast.5), calls=%async_computation.4 | async-start | bytes 1048576 | tf_op jit(solution)/shard_map/all_to_all | solution.py:246
  101.2 1.7 %collective-permute-done.15.refs_5_ = bf16[27,16,192]{2,1,0:T(8,128)(2,1)S(1)} collective-permute-done((bf16[27,16,192]{2,1,0:T(8,128)(2,1)}, bf16[27,16,192]{2,1,0:T(8,128)(2,1)S(1)}, u32[]{:S(2)}, u32[]{:S(2)}) %collective-permute-start.15) | collective-permute-done | bytes 165920 | tf_op jit(solution)/shard_map/ppermute | solution.py:259
  103.1 1.8 %collective-permute-start.20 = (bf16[27,16,192]{2,1,0:T(8,128)(2,1)S(1)}, bf16[27,16,192]{2,1,0:T(8,128)(2,1)S(1)}, u32[]{:S(2)}, u32[]{:S(2)}) collective-permute-start(bf16[27,16,192]{2,1,0:T(8,128)(2,1)S(1)} %shard_map.143.refs_0_.refs_1_), channel_id=1, source_target_pairs={{0,8},{8,0},{16,24},{24,16},{1,9},{9,1},{17,25},{25,17},{2,10},{10... | collective-permute-start | bytes 497672 | tf_op jit(solution)/shard_map/ppermute | solution.py:259
  104.9 1.6 %collective-permute-done.16.refs_2_ = bf16[27,16,192]{2,1,0:T(8,128)(2,1)S(1)} collective-permute-done((bf16[27,16,192]{2,1,0:T(8,128)(2,1)S(1)}, bf16[27,16,192]{2,1,0:T(8,128)(2,1)S(1)}, u32[]{:S(2)}, u32[]{:S(2)}) %collective-permute-start.16) | collective-permute-done | bytes 165920 | tf_op jit(solution)/shard_map/ppermute | solution.py:259
  106.5 2.9 %collective-permute-start.19 = (bf16[27,16,192]{2,1,0:T(8,128)(2,1)S(1)}, bf16[27,16,192]{2,1,0:T(8,128)(2,1)S(1)}, u32[]{:S(2)}, u32[]{:S(2)}) collective-permute-start(bf16[27,16,192]{2,1,0:T(8,128)(2,1)S(1)} %shard_map.144.refs_0_.refs_1_), channel_id=1, source_target_pairs={{0,6},{2,4},{4,2},{6,0},{1,7},{3,5},{5,3},{7,1},{8,14},{10,12},{12... | collective-permute-start | bytes 497672 | tf_op jit(solution)/shard_map/ppermute | solution.py:259
  109.4 0.7 collective-permute-start.18
  110.1 1.4 collective-permute-start.17
  111.6 0.7 collective-permute-start.23
  112.3 4.0 %collective-permute-done.19.refs_2_.refs_3_ = bf16[27,16,192]{2,1,0:T(8,128)(2,1)S(1)} collective-permute-done((bf16[27,16,192]{2,1,0:T(8,128)(2,1)S(1)}, bf16[27,16,192]{2,1,0:T(8,128)(2,1)S(1)}, u32[]{:S(2)}, u32[]{:S(2)}) %collective-permute-start.19) | collective-permute-done | bytes 165920 | tf_op jit(solution)/shard_map/ppermute | solution.py:259
  116.2 4.1 %collective-permute-done.18.refs_1_.refs_2_ = bf16[27,16,192]{2,1,0:T(8,128)(2,1)S(1)} collective-permute-done((bf16[27,16,192]{2,1,0:T(8,128)(2,1)S(1)}, bf16[27,16,192]{2,1,0:T(8,128)(2,1)S(1)}, u32[]{:S(2)}, u32[]{:S(2)}) %collective-permute-start.18) | collective-permute-done | bytes 165920 | tf_op jit(solution)/shard_map/ppermute | solution.py:259
  120.6 2.2 %collective-permute-done.23.refs_2_ = bf16[27,16,192]{2,1,0:T(8,128)(2,1)S(1)} collective-permute-done((bf16[27,16,192]{2,1,0:T(8,128)(2,1)S(1)}, bf16[27,16,192]{2,1,0:T(8,128)(2,1)S(1)}, u32[]{:S(2)}, u32[]{:S(2)}) %collective-permute-start.23) | collective-permute-done | bytes 165920 | tf_op jit(solution)/shard_map/ppermute | solution.py:259
  122.8 3.3 %collective-permute-start.26 = (bf16[27,16,192]{2,1,0:T(8,128)(2,1)S(1)}, bf16[27,16,192]{2,1,0:T(8,128)(2,1)S(1)}, u32[]{:S(2)}, u32[]{:S(2)}) collective-permute-start(bf16[27,16,192]{2,1,0:T(8,128)(2,1)S(1)} %shard_map.149.refs_1_), channel_id=1, source_target_pairs={{0,6},{2,4},{4,2},{6,0},{1,7},{3,5},{5,3},{7,1},{8,14},{10,12},{12... | collective-permute-start | bytes 497672 | tf_op jit(solution)/shard_map/ppermute | solution.py:259
  126.1 0.8 collective-permute-start.25
  126.9 1.3 collective-permute-start.24
  128.3 4.1 %collective-permute-done.26.refs_4_ = bf16[27,16,192]{2,1,0:T(8,128)(2,1)S(1)} collective-permute-done((bf16[27,16,192]{2,1,0:T(8,128)(2,1)S(1)}, bf16[27,16,192]{2,1,0:T(8,128)(2,1)S(1)}, u32[]{:S(2)}, u32[]{:S(2)}) %collective-permute-start.26) | collective-permute-done | bytes 165920 | tf_op jit(solution)/shard_map/ppermute | solution.py:259
  132.4 4.8 %collective-permute-done.25.refs_3_ = bf16[27,16,192]{2,1,0:T(8,128)(2,1)S(1)} collective-permute-done((bf16[27,16,192]{2,1,0:T(8,128)(2,1)S(1)}, bf16[27,16,192]{2,1,0:T(8,128)(2,1)S(1)}, u32[]{:S(2)}, u32[]{:S(2)}) %collective-permute-start.25) | collective-permute-done | bytes 165920 | tf_op jit(solution)/shard_map/ppermute | solution.py:259
  137.2 0.5 collective-permute-start.29
  137.8 2.0 %shard_map.148 = (f32[1728,192]{1,0:T(8,128)}, f32[1728,192]{1,0:T(8,128)}) custom-call(bf16[27,16,192]{2,1,0:T(8,128)(2,1)S(1)} %shard_map.144.refs_0_.refs_1_, bf16[27,16,192]{2,1,0:T(8,128)(2,1)S(1)} %collective-permute-done.17.refs_2_.refs_1_, bf16[27,16,192]{2,1,0:T(8,128)(2,1)S(1)} %collective-permute-done.18.refs_1_.refs_2_, ...), custom_call_target="tpu_custom_call" | custom-call | tf_op jit(solution)/shard_map/pallas_call | solution.py:32
  139.8 1.5 %copy-done.1 = f32[1728,192]{1,0:T(8,128)S(1)} copy-done((f32[1728,192]{1,0:T(8,128)S(1)}, f32[1728,192]{1,0:T(8,128)}, u32[]{:S(2)}) %copy-start.1) | copy-done | bytes 1327128
  141.3 2.0 %shard_map.150 = (f32[1728,192]{1,0:T(8,128)}, f32[1728,192]{1,0:T(8,128)}) custom-call(f32[9,192,192]{2,1,0:T(8,128)S(1)} %bitcast.18, bf16[27,16,192]{2,1,0:T(8,128)(2,1)S(1)} %shard_map.149.refs_1_, bf16[27,16,192]{2,1,0:T(8,128)(2,1)S(1)} %collective-permute-done.24.refs_2_, bf16[27,16,192]{2,1,0:T(8,128)(2,1)S(1)} %collective-permute-done.25.refs_3_, ...), custom_call_target="tpu_custom_call" | custom-call | tf_op jit(solution)/shard_map/pallas_call | solution.py:32
  (86 shorter events, 1.1 us)
Async XLA Ops:
  0.6 15.0 %copy-start.4 = (bf16[32,32,192]{2,1,0:T(8,128)(2,1)S(1)}, bf16[32,32,192]{2,1,0:T(8,128)(2,1)}, u32[]{:S(2)}) copy-start(bf16[32,32,192]{2,1,0:T(8,128)(2,1)} %refs_1_.2) | copy-start | bytes 1179652
  0.6 1.1 copy-start.8
  15.7 9.0 %copy-start.5 = (bf16[32,32,192]{2,1,0:T(8,128)(2,1)S(1)}, bf16[32,32,192]{2,1,0:T(8,128)(2,1)}, u32[]{:S(2)}) copy-start(bf16[32,32,192]{2,1,0:T(8,128)(2,1)} %refs_1_.3) | copy-start | bytes 1179652
  15.7 9.0 %copy-start.6 = (bf16[32,32,192]{2,1,0:T(8,128)(2,1)S(1)}, bf16[32,32,192]{2,1,0:T(8,128)(2,1)}, u32[]{:S(2)}) copy-start(bf16[32,32,192]{2,1,0:T(8,128)(2,1)} %refs_2_.1) | copy-start | bytes 1179652
  15.7 9.0 %copy-start.7 = (bf16[32,32,192]{2,1,0:T(8,128)(2,1)S(1)}, bf16[32,32,192]{2,1,0:T(8,128)(2,1)}, u32[]{:S(2)}) copy-start(bf16[32,32,192]{2,1,0:T(8,128)(2,1)} %refs_3_.1) | copy-start | bytes 1179652
  16.5 12.3 %all-to-all-start.1 = ((bf16[8,1,2,2,2,16,192]{6,5,4,3,2,1,0:T(8,128)(2,1)}), bf16[8,1,2,2,2,16,192]{6,5,4,3,2,1,0:T(8,128)(2,1)S(1)}, u32[]{:S(2)}, u32[]{:S(2)}) async-start(bf16[8,1,2,2,2,16,192]{6,5,4,3,2,1,0:T(8,128)(2,1)} %shard_map.129.refs_0_), calls=%async_computation.1 | async-start | bytes 1048576 | tf_op jit(solution)/shard_map/all_to_all | solution.py:238
  20.8 11.5 %collective-permute-start = (bf16[2,2,2,2,2,16,192]{6,5,4,3,2,1,0:T(8,128)(2,1)}, bf16[2,2,2,2,2,16,192]{6,5,4,3,2,1,0:T(8,128)(2,1)S(1)}, u32[]{:S(2)}, u32[]{:S(2)}) collective-permute-start(bf16[2,2,2,2,2,16,192]{6,5,4,3,2,1,0:T(8,128)(2,1)} %bitcast.1), channel_id=1, source_target_pairs={{0,8},{8,16},{16,24},{24,0},{1,9},{9,17},{17,25},{25,1},{2,10},{10... | collective-permute-start | bytes 589832 | tf_op jit(solution)/shard_map/ppermute | solution.py:254
  22.4 14.2 %collective-permute-start.1 = (bf16[2,2,2,2,2,16,192]{6,5,4,3,2,1,0:T(8,128)(2,1)}, bf16[2,2,2,2,2,16,192]{6,5,4,3,2,1,0:T(8,128)(2,1)S(1)}, u32[]{:S(2)}, u32[]{:S(2)}) collective-permute-start(bf16[2,2,2,2,2,16,192]{6,5,4,3,2,1,0:T(8,128)(2,1)} %bitcast.2), channel_id=1, source_target_pairs={{8,0},{16,8},{24,16},{0,24},{9,1},{17,9},{25,17},{1,25},{10,2},{18... | collective-permute-start | bytes 589832 | tf_op jit(solution)/shard_map/ppermute | solution.py:254
  28.8 31.7 %all-to-all-start.2 = ((bf16[8,3,2,2,2,16,192]{6,5,4,3,2,1,0:T(8,128)(2,1)}), bf16[8,3,2,2,2,16,192]{6,5,4,3,2,1,0:T(8,128)(2,1)S(1)}, u32[]{:S(2)}, u32[]{:S(2)}) async-start(bf16[8,3,2,2,2,16,192]{6,5,4,3,2,1,0:T(8,128)(2,1)} %shard_map.130.refs_0_), calls=%async_computation.2 | async-start | bytes 3145728 | tf_op jit(solution)/shard_map/all_to_all | solution.py:238
  36.6 1.2 copy-start.9
  39.3 11.1 %collective-permute-start.2 = (bf16[2,8,2,16,192]{4,3,2,1,0:T(8,128)(2,1)S(1)}, bf16[2,8,2,16,192]{4,3,2,1,0:T(8,128)(2,1)S(1)}, u32[]{:S(2)}, u32[]{:S(2)}) collective-permute-start(bf16[2,8,2,16,192]{4,3,2,1,0:T(8,128)(2,1)S(1)} %get-tuple-element.32.refs_3_), channel_id=1, source_target_pairs={{0,8},{8,16},{16,24},{24,0},{1,9},{9,17},{17,25},{25,1},{2,10},{10... | collective-permute-start | bytes 589832 | tf_op jit(solution)/shard_map/ppermute | solution.py:254
  40.4 13.6 %collective-permute-start.3 = (bf16[2,8,2,16,192]{4,3,2,1,0:T(8,128)(2,1)S(1)}, bf16[2,8,2,16,192]{4,3,2,1,0:T(8,128)(2,1)S(1)}, u32[]{:S(2)}, u32[]{:S(2)}) collective-permute-start(bf16[2,8,2,16,192]{4,3,2,1,0:T(8,128)(2,1)S(1)} %get-tuple-element.33.refs_2_), channel_id=1, source_target_pairs={{8,0},{16,8},{24,16},{0,24},{9,1},{17,9},{25,17},{1,25},{10,2},{18... | collective-permute-start | bytes 589832 | tf_op jit(solution)/shard_map/ppermute | solution.py:254
  43.1 10.9 %copy-start.10 = (bf16[9,192,192]{2,1,0:T(8,128)(2,1)S(1)}, bf16[9,192,192]{2,1,0:T(8,128)(2,1)}, u32[]{:S(2)}) copy-start(bf16[9,192,192]{2,1,0:T(8,128)(2,1)} %refs_6_.1) | copy-start | bytes 1990660
  44.4 11.1 %copy-start.17 = (f32[1728,192]{1,0:T(8,128)}, f32[1728,192]{1,0:T(8,128)S(1)}, u32[]{:S(2)}) copy-start(f32[1728,192]{1,0:T(8,128)S(1)} %shard_map.132.refs_0_.refs_2_) | copy-start | bytes 3981316
  55.4 1.1 copy-start.19
  56.6 9.2 %copy-start.13 = (bf16[1,8,2,16,192]{4,3,2,1,0:T(8,128)(2,1)}, bf16[1,8,2,16,192]{4,3,2,1,0:T(8,128)(2,1)S(1)}, u32[]{:S(2)}) copy-start(bf16[1,8,2,16,192]{4,3,2,1,0:T(8,128)(2,1)S(1)} %get-tuple-element.39.refs_2_) | copy-start | bytes 294916
  56.6 9.2 %copy-start.15 = (bf16[1,8,2,16,192]{4,3,2,1,0:T(8,128)(2,1)}, bf16[1,8,2,16,192]{4,3,2,1,0:T(8,128)(2,1)S(1)}, u32[]{:S(2)}) copy-start(bf16[1,8,2,16,192]{4,3,2,1,0:T(8,128)(2,1)S(1)} %get-tuple-element.38.refs_4_) | copy-start | bytes 294916
  56.6 9.2 %copy-start.25 = (bf16[2,8,2,16,192]{4,3,2,1,0:T(8,128)(2,1)}, bf16[2,8,2,16,192]{4,3,2,1,0:T(8,128)(2,1)S(1)}, u32[]{:S(2)}) copy-start(bf16[2,8,2,16,192]{4,3,2,1,0:T(8,128)(2,1)S(1)} %get-tuple-element.40.refs_3_) | copy-start | bytes 589828
  56.6 9.2 %collective-permute-start.6 = (bf16[1,8,2,16,192]{4,3,2,1,0:T(8,128)(2,1)S(1)}, bf16[1,8,2,16,192]{4,3,2,1,0:T(8,128)(2,1)S(1)}, u32[]{:S(2)}, u32[]{:S(2)}) collective-permute-start(bf16[1,8,2,16,192]{4,3,2,1,0:T(8,128)(2,1)S(1)} %get-tuple-element.38.refs_4_), channel_id=1, source_target_pairs={{0,8},{8,16},{16,24},{24,0},{1,9},{9,17},{17,25},{25,1},{2,10},{10... | collective-permute-start | bytes 294920 | tf_op jit(solution)/shard_map/ppermute | solution.py:254
  56.9 8.9 %collective-permute-start.7 = (bf16[1,8,2,16,192]{4,3,2,1,0:T(8,128)(2,1)S(1)}, bf16[1,8,2,16,192]{4,3,2,1,0:T(8,128)(2,1)S(1)}, u32[]{:S(2)}, u32[]{:S(2)}) collective-permute-start(bf16[1,8,2,16,192]{4,3,2,1,0:T(8,128)(2,1)S(1)} %get-tuple-element.39.refs_2_), channel_id=1, source_target_pairs={{8,0},{16,8},{24,16},{0,24},{9,1},{17,9},{25,17},{1,25},{10,2},{18... | collective-permute-start | bytes 294920 | tf_op jit(solution)/shard_map/ppermute | solution.py:254
  60.4 16.6 %copy-start.2 = (bf16[8,3,2,2,2,16,192]{6,5,4,3,2,1,0:T(8,128)(2,1)}, bf16[8,3,2,2,2,16,192]{6,5,4,3,2,1,0:T(8,128)(2,1)S(1)}, u32[]{:S(2)}) copy-start(bf16[8,3,2,2,2,16,192]{6,5,4,3,2,1,0:T(8,128)(2,1)S(1)} %all-to-all-done.2) | copy-start | bytes 3538948
  60.4 2.0 %copy-start.18 = (f32[1728,192]{1,0:T(8,128)S(1)}, f32[1728,192]{1,0:T(8,128)}, u32[]{:S(2)}) copy-start(f32[1728,192]{1,0:T(8,128)} %copy-done.17) | copy-start | bytes 3981316
  62.5 1.4 copy-start.20
  63.9 2.0 %copy-start.11 = (bf16[9,192,192]{2,1,0:T(8,128)(2,1)S(1)}, bf16[9,192,192]{2,1,0:T(8,128)(2,1)}, u32[]{:S(2)}) copy-start(bf16[9,192,192]{2,1,0:T(8,128)(2,1)} %refs_7_.1) | copy-start | bytes 1990660
  65.2 6.9 %collective-permute-start.4 = (bf16[2,27,16,192]{3,2,1,0:T(8,128)(2,1)S(1)}, bf16[2,27,16,192]{3,2,1,0:T(8,128)(2,1)S(1)}, u32[]{:S(2)}, u32[]{:S(2)}) collective-permute-start(bf16[2,27,16,192]{3,2,1,0:T(8,128)(2,1)S(1)} %get-tuple-element.36), channel_id=1, source_target_pairs={{0,1},{1,0},{2,3},{3,2},{4,5},{5,4},{6,7},{7,6},{8,9},{9,8},{10,11... | collective-permute-start | bytes 995336 | tf_op jit(solution)/shard_map/ppermute | solution.py:259
  65.3 6.8 %collective-permute-start.5 = (bf16[2,27,16,192]{3,2,1,0:T(8,128)(2,1)S(1)}, bf16[2,27,16,192]{3,2,1,0:T(8,128)(2,1)S(1)}, u32[]{:S(2)}, u32[]{:S(2)}) collective-permute-start(bf16[2,27,16,192]{3,2,1,0:T(8,128)(2,1)S(1)} %get-tuple-element.37), channel_id=1, source_target_pairs={{0,1},{1,0},{2,3},{3,2},{4,5},{5,4},{6,7},{7,6},{8,9},{9,8},{10,11... | collective-permute-start | bytes 995336 | tf_op jit(solution)/shard_map/ppermute | solution.py:259
  67.4 0.9 copy-start.21
  68.3 11.2 %collective-permute-start.8 = (bf16[1,8,2,16,192]{4,3,2,1,0:T(8,128)(2,1)S(1)}, bf16[1,8,2,16,192]{4,3,2,1,0:T(8,128)(2,1)S(1)}, u32[]{:S(2)}, u32[]{:S(2)}) collective-permute-start(bf16[1,8,2,16,192]{4,3,2,1,0:T(8,128)(2,1)S(1)} %get-tuple-element.41.refs_3_), channel_id=1, source_target_pairs={{0,8},{8,16},{16,24},{24,0},{1,9},{9,17},{17,25},{25,1},{2,10},{10... | collective-permute-start | bytes 294920 | tf_op jit(solution)/shard_map/ppermute | solution.py:254
  68.3 11.2 %collective-permute-start.9 = (bf16[1,8,2,16,192]{4,3,2,1,0:T(8,128)(2,1)S(1)}, bf16[1,8,2,16,192]{4,3,2,1,0:T(8,128)(2,1)S(1)}, u32[]{:S(2)}, u32[]{:S(2)}) collective-permute-start(bf16[1,8,2,16,192]{4,3,2,1,0:T(8,128)(2,1)S(1)} %get-tuple-element.42.refs_1_), channel_id=1, source_target_pairs={{8,0},{16,8},{24,16},{0,24},{9,1},{17,9},{25,17},{1,25},{10,2},{18... | collective-permute-start | bytes 294920 | tf_op jit(solution)/shard_map/ppermute | solution.py:254
  73.2 15.4 %all-to-all-start.3 = ((bf16[4,27,16,192]{3,2,1,0:T(8,128)(2,1)}), bf16[4,27,16,192]{3,2,1,0:T(8,128)(2,1)S(1)}, u32[]{:S(2)}, u32[]{:S(2)}) async-start(bf16[4,27,16,192]{3,2,1,0:T(8,128)(2,1)} %shard_map.135.refs_0_), calls=%async_computation.3 | async-start | bytes 1769472 | tf_op jit(solution)/shard_map/all_to_all | solution.py:296
  77.1 1.2 copy-start.22
  79.5 1.4 copy-start.3
  83.4 0.9 copy-start.23
  84.3 4.5 %collective-permute-start.10 = (bf16[2,27,16,192]{3,2,1,0:T(8,128)(2,1)}, bf16[2,27,16,192]{3,2,1,0:T(8,128)(2,1)S(1)}, u32[]{:S(2)}, u32[]{:S(2)}) collective-permute-start(bf16[2,27,16,192]{3,2,1,0:T(8,128)(2,1)} %get-tuple-element.46), channel_id=1, source_target_pairs={{0,1},{1,0},{2,3},{3,2},{4,5},{5,4},{6,7},{7,6},{8,9},{9,8},{10,11... | collective-permute-start | bytes 995336 | tf_op jit(solution)/shard_map/ppermute | solution.py:259
  84.3 4.5 %collective-permute-start.11 = (bf16[2,27,16,192]{3,2,1,0:T(8,128)(2,1)}, bf16[2,27,16,192]{3,2,1,0:T(8,128)(2,1)S(1)}, u32[]{:S(2)}, u32[]{:S(2)}) collective-permute-start(bf16[2,27,16,192]{3,2,1,0:T(8,128)(2,1)} %get-tuple-element.47), channel_id=1, source_target_pairs={{0,1},{1,0},{2,3},{3,2},{4,5},{5,4},{6,7},{7,6},{8,9},{9,8},{10,11... | collective-permute-start | bytes 995336 | tf_op jit(solution)/shard_map/ppermute | solution.py:259
  88.7 6.4 %collective-permute-start.12 = (bf16[27,16,192]{2,1,0:T(8,128)(2,1)S(1)}, bf16[27,16,192]{2,1,0:T(8,128)(2,1)S(1)}, u32[]{:S(2)}, u32[]{:S(2)}) collective-permute-start(bf16[27,16,192]{2,1,0:T(8,128)(2,1)S(1)} %shard_map.136.refs_0_.refs_1_), channel_id=1, source_target_pairs={{0,8},{8,0},{16,24},{24,16},{1,9},{9,1},{17,25},{25,17},{2,10},{10... | collective-permute-start | bytes 497672 | tf_op jit(solution)/shard_map/ppermute | solution.py:259
  88.8 6.4 %copy-start.12 = (bf16[9,192,192]{2,1,0:T(8,128)(2,1)S(1)}, bf16[9,192,192]{2,1,0:T(8,128)(2,1)}, u32[]{:S(2)}) copy-start(bf16[9,192,192]{2,1,0:T(8,128)(2,1)} %refs_5_.3) | copy-start | bytes 1990660
  88.8 6.4 %copy-start.14 = (bf16[1,8,2,16,192]{4,3,2,1,0:T(8,128)(2,1)S(1)}, bf16[1,8,2,16,192]{4,3,2,1,0:T(8,128)(2,1)}, u32[]{:S(2)}) copy-start(bf16[1,8,2,16,192]{4,3,2,1,0:T(8,128)(2,1)} %copy-done.13) | copy-start | bytes 294916
  88.9 6.4 %copy-start.16 = (bf16[1,8,2,16,192]{4,3,2,1,0:T(8,128)(2,1)S(1)}, bf16[1,8,2,16,192]{4,3,2,1,0:T(8,128)(2,1)}, u32[]{:S(2)}) copy-start(bf16[1,8,2,16,192]{4,3,2,1,0:T(8,128)(2,1)} %copy-done.15) | copy-start | bytes 294916
  88.9 6.4 %copy-start.24 = (bf16[6,10,2,16,192]{4,3,2,1,0:T(8,128)(2,1)S(1)}, bf16[6,10,2,16,192]{4,3,2,1,0:T(8,128)(2,1)}, u32[]{:S(2)}) copy-start(bf16[6,10,2,16,192]{4,3,2,1,0:T(8,128)(2,1)} %copy-done.23) | copy-start | bytes 2211844
  88.9 6.4 %copy-start.26 = (bf16[2,8,2,16,192]{4,3,2,1,0:T(8,128)(2,1)S(1)}, bf16[2,8,2,16,192]{4,3,2,1,0:T(8,128)(2,1)}, u32[]{:S(2)}) copy-start(bf16[2,8,2,16,192]{4,3,2,1,0:T(8,128)(2,1)} %copy-done.25) | copy-start | bytes 589828
  89.8 11.4 %collective-permute-start.13 = (bf16[27,16,192]{2,1,0:T(8,128)(2,1)}, bf16[27,16,192]{2,1,0:T(8,128)(2,1)S(1)}, u32[]{:S(2)}, u32[]{:S(2)}) collective-permute-start(bf16[27,16,192]{2,1,0:T(8,128)(2,1)} %get-tuple-element.50), channel_id=1, source_target_pairs={{0,2},{2,0},{4,6},{6,4},{1,3},{3,1},{5,7},{7,5},{8,10},{10,8},{12,... | collective-permute-start | bytes 497672 | tf_op jit(solution)/shard_map/ppermute | solution.py:259
  91.3 9.9 %collective-permute-start.14 = (bf16[27,16,192]{2,1,0:T(8,128)(2,1)}, bf16[27,16,192]{2,1,0:T(8,128)(2,1)S(1)}, u32[]{:S(2)}, u32[]{:S(2)}) collective-permute-start(bf16[27,16,192]{2,1,0:T(8,128)(2,1)} %get-tuple-element.51), channel_id=1, source_target_pairs={{0,4},{2,6},{4,0},{6,2},{1,5},{3,7},{5,1},{7,3},{8,12},{10,14},{12... | collective-permute-start | bytes 497672 | tf_op jit(solution)/shard_map/ppermute | solution.py:259
  91.8 11.1 %collective-permute-start.15 = (bf16[27,16,192]{2,1,0:T(8,128)(2,1)}, bf16[27,16,192]{2,1,0:T(8,128)(2,1)S(1)}, u32[]{:S(2)}, u32[]{:S(2)}) collective-permute-start(bf16[27,16,192]{2,1,0:T(8,128)(2,1)} %get-tuple-element.52), channel_id=1, source_target_pairs={{0,6},{2,4},{4,2},{6,0},{1,7},{3,5},{5,3},{7,1},{8,14},{10,12},{12... | collective-permute-start | bytes 497672 | tf_op jit(solution)/shard_map/ppermute | solution.py:259
  95.2 11.2 %collective-permute-start.16 = (bf16[27,16,192]{2,1,0:T(8,128)(2,1)S(1)}, bf16[27,16,192]{2,1,0:T(8,128)(2,1)S(1)}, u32[]{:S(2)}, u32[]{:S(2)}) collective-permute-start(bf16[27,16,192]{2,1,0:T(8,128)(2,1)S(1)} %shard_map.141.refs_0_.refs_1_), channel_id=1, source_target_pairs={{0,16},{8,24},{16,0},{24,8},{1,17},{9,25},{17,1},{25,9},{2,18},{10... | collective-permute-start | bytes 497672 | tf_op jit(solution)/shard_map/ppermute | solution.py:259
  97.5 23.0 %all-to-all-start.4 = ((bf16[8,2,2,2,16,192]{5,4,3,2,1,0:T(8,128)(2,1)}), bf16[8,2,2,2,16,192]{5,4,3,2,1,0:T(8,128)(2,1)S(1)}, u32[]{:S(2)}, u32[]{:S(2)}) async-start(bf16[8,2,2,2,16,192]{5,4,3,2,1,0:T(8,128)(2,1)} %bitcast.5), calls=%async_computation.4 | async-start | bytes 1048576 | tf_op jit(solution)/shard_map/all_to_all | solution.py:246
  103.1 8.4 %collective-permute-start.20 = (bf16[27,16,192]{2,1,0:T(8,128)(2,1)S(1)}, bf16[27,16,192]{2,1,0:T(8,128)(2,1)S(1)}, u32[]{:S(2)}, u32[]{:S(2)}) collective-permute-start(bf16[27,16,192]{2,1,0:T(8,128)(2,1)S(1)} %shard_map.143.refs_0_.refs_1_), channel_id=1, source_target_pairs={{0,8},{8,0},{16,24},{24,16},{1,9},{9,1},{17,25},{25,17},{2,10},{10... | collective-permute-start | bytes 497672 | tf_op jit(solution)/shard_map/ppermute | solution.py:259
  106.5 9.8 %collective-permute-start.19 = (bf16[27,16,192]{2,1,0:T(8,128)(2,1)S(1)}, bf16[27,16,192]{2,1,0:T(8,128)(2,1)S(1)}, u32[]{:S(2)}, u32[]{:S(2)}) collective-permute-start(bf16[27,16,192]{2,1,0:T(8,128)(2,1)S(1)} %shard_map.144.refs_0_.refs_1_), channel_id=1, source_target_pairs={{0,6},{2,4},{4,2},{6,0},{1,7},{3,5},{5,3},{7,1},{8,14},{10,12},{12... | collective-permute-start | bytes 497672 | tf_op jit(solution)/shard_map/ppermute | solution.py:259
  109.4 10.9 %collective-permute-start.18 = (bf16[27,16,192]{2,1,0:T(8,128)(2,1)S(1)}, bf16[27,16,192]{2,1,0:T(8,128)(2,1)S(1)}, u32[]{:S(2)}, u32[]{:S(2)}) collective-permute-start(bf16[27,16,192]{2,1,0:T(8,128)(2,1)S(1)} %shard_map.144.refs_0_.refs_1_), channel_id=1, source_target_pairs={{0,4},{2,6},{4,0},{6,2},{1,5},{3,7},{5,1},{7,3},{8,12},{10,14},{12... | collective-permute-start | bytes 497672 | tf_op jit(solution)/shard_map/ppermute | solution.py:259
  110.1 10.3 %collective-permute-start.17 = (bf16[27,16,192]{2,1,0:T(8,128)(2,1)S(1)}, bf16[27,16,192]{2,1,0:T(8,128)(2,1)S(1)}, u32[]{:S(2)}, u32[]{:S(2)}) collective-permute-start(bf16[27,16,192]{2,1,0:T(8,128)(2,1)S(1)} %shard_map.144.refs_0_.refs_1_), channel_id=1, source_target_pairs={{0,2},{2,0},{4,6},{6,4},{1,3},{3,1},{5,7},{7,5},{8,10},{10,8},{12,... | collective-permute-start | bytes 497672 | tf_op jit(solution)/shard_map/ppermute | solution.py:259
  111.6 11.2 %collective-permute-start.23 = (bf16[27,16,192]{2,1,0:T(8,128)(2,1)S(1)}, bf16[27,16,192]{2,1,0:T(8,128)(2,1)S(1)}, u32[]{:S(2)}, u32[]{:S(2)}) collective-permute-start(bf16[27,16,192]{2,1,0:T(8,128)(2,1)S(1)} %shard_map.145.refs_0_.refs_1_), channel_id=1, source_target_pairs={{0,16},{8,24},{16,0},{24,8},{1,17},{9,25},{17,1},{25,9},{2,18},{10... | collective-permute-start | bytes 497672 | tf_op jit(solution)/shard_map/ppermute | solution.py:259
  120.4 17.3 %collective-permute-start.22 = (bf16[2,27,16,192]{3,2,1,0:T(8,128)(2,1)S(1)}, bf16[2,27,16,192]{3,2,1,0:T(8,128)(2,1)S(1)}, u32[]{:S(2)}, u32[]{:S(2)}) collective-permute-start(bf16[2,27,16,192]{3,2,1,0:T(8,128)(2,1)S(1)} %shard_map.147), channel_id=1, source_target_pairs={{0,1},{1,0},{2,3},{3,2},{4,5},{5,4},{6,7},{7,6},{8,9},{9,8},{10,11... | collective-permute-start | bytes 995336 | tf_op jit(solution)/shard_map/ppermute | solution.py:259
  120.6 22.8 %copy-start = (bf16[2,8,2,2,16,192]{5,4,3,2,1,0:T(8,128)(2,1)}, bf16[2,8,2,2,16,192]{5,4,3,2,1,0:T(8,128)(2,1)S(1)}, u32[]{:S(2)}) copy-start(bf16[2,8,2,2,16,192]{5,4,3,2,1,0:T(8,128)(2,1)S(1)} %copy.15) | copy-start | bytes 1179652
  122.8 9.5 %collective-permute-start.26 = (bf16[27,16,192]{2,1,0:T(8,128)(2,1)S(1)}, bf16[27,16,192]{2,1,0:T(8,128)(2,1)S(1)}, u32[]{:S(2)}, u32[]{:S(2)}) collective-permute-start(bf16[27,16,192]{2,1,0:T(8,128)(2,1)S(1)} %shard_map.149.refs_1_), channel_id=1, source_target_pairs={{0,6},{2,4},{4,2},{6,0},{1,7},{3,5},{5,3},{7,1},{8,14},{10,12},{12... | collective-permute-start | bytes 497672 | tf_op jit(solution)/shard_map/ppermute | solution.py:259
  126.1 11.6 %collective-permute-start.21 = (bf16[2,27,16,192]{3,2,1,0:T(8,128)(2,1)S(1)}, bf16[2,27,16,192]{3,2,1,0:T(8,128)(2,1)S(1)}, u32[]{:S(2)}, u32[]{:S(2)}) collective-permute-start(bf16[2,27,16,192]{3,2,1,0:T(8,128)(2,1)S(1)} %shard_map.146), channel_id=1, source_target_pairs={{0,1},{1,0},{2,3},{3,2},{4,5},{5,4},{6,7},{7,6},{8,9},{9,8},{10,11... | collective-permute-start | bytes 995336 | tf_op jit(solution)/shard_map/ppermute | solution.py:259
  126.1 11.0 %collective-permute-start.25 = (bf16[27,16,192]{2,1,0:T(8,128)(2,1)S(1)}, bf16[27,16,192]{2,1,0:T(8,128)(2,1)S(1)}, u32[]{:S(2)}, u32[]{:S(2)}) collective-permute-start(bf16[27,16,192]{2,1,0:T(8,128)(2,1)S(1)} %shard_map.149.refs_1_), channel_id=1, source_target_pairs={{0,4},{2,6},{4,0},{6,2},{1,5},{3,7},{5,1},{7,3},{8,12},{10,14},{12... | collective-permute-start | bytes 497672 | tf_op jit(solution)/shard_map/ppermute | solution.py:259
  126.9 10.2 %collective-permute-start.24 = (bf16[27,16,192]{2,1,0:T(8,128)(2,1)S(1)}, bf16[27,16,192]{2,1,0:T(8,128)(2,1)S(1)}, u32[]{:S(2)}, u32[]{:S(2)}) collective-permute-start(bf16[27,16,192]{2,1,0:T(8,128)(2,1)S(1)} %shard_map.149.refs_1_), channel_id=1, source_target_pairs={{0,2},{2,0},{4,6},{6,4},{1,3},{3,1},{5,7},{7,5},{8,10},{10,8},{12,... | collective-permute-start | bytes 497672 | tf_op jit(solution)/shard_map/ppermute | solution.py:259
  132.4 7.4 %collective-permute-start.27 = (bf16[27,16,192]{2,1,0:T(8,128)(2,1)S(1)}, bf16[27,16,192]{2,1,0:T(8,128)(2,1)S(1)}, u32[]{:S(2)}, u32[]{:S(2)}) collective-permute-start(bf16[27,16,192]{2,1,0:T(8,128)(2,1)S(1)} %shard_map.149.refs_1_), channel_id=1, source_target_pairs={{0,1},{1,0},{2,3},{3,2},{4,5},{5,4},{6,7},{7,6},{8,9},{9,8},{10,11... | collective-permute-start | bytes 497672 | tf_op jit(solution)/shard_map/ppermute | solution.py:259
  137.2 2.6 %collective-permute-start.30 = (bf16[27,16,192]{2,1,0:T(8,128)(2,1)S(1)}, bf16[27,16,192]{2,1,0:T(8,128)(2,1)S(1)}, u32[]{:S(2)}, u32[]{:S(2)}) collective-permute-start(bf16[27,16,192]{2,1,0:T(8,128)(2,1)S(1)} %collective-permute-done.26.refs_4_), channel_id=1, source_target_pairs={{0,1},{1,0},{2,3},{3,2},{4,5},{5,4},{6,7},{7,6},{8,9},{9,8},{10,11... | collective-permute-start | bytes 497672 | tf_op jit(solution)/shard_map/ppermute | solution.py:259
  137.2 2.6 %collective-permute-start.29 = (bf16[27,16,192]{2,1,0:T(8,128)(2,1)S(1)}, bf16[27,16,192]{2,1,0:T(8,128)(2,1)S(1)}, u32[]{:S(2)}, u32[]{:S(2)}) collective-permute-start(bf16[27,16,192]{2,1,0:T(8,128)(2,1)S(1)} %collective-permute-done.25.refs_3_), channel_id=1, source_target_pairs={{0,1},{1,0},{2,3},{3,2},{4,5},{5,4},{6,7},{7,6},{8,9},{9,8},{10,11... | collective-permute-start | bytes 497672 | tf_op jit(solution)/shard_map/ppermute | solution.py:259
  137.7 2.1 %collective-permute-start.28 = (bf16[27,16,192]{2,1,0:T(8,128)(2,1)S(1)}, bf16[27,16,192]{2,1,0:T(8,128)(2,1)S(1)}, u32[]{:S(2)}, u32[]{:S(2)}) collective-permute-start(bf16[27,16,192]{2,1,0:T(8,128)(2,1)S(1)} %collective-permute-done.24.refs_2_), channel_id=1, source_target_pairs={{0,1},{1,0},{2,3},{3,2},{4,5},{5,4},{6,7},{7,6},{8,9},{9,8},{10,11... | collective-permute-start | bytes 497672 | tf_op jit(solution)/shard_map/ppermute | solution.py:259
  139.8 1.5 %copy-start.1 = (f32[1728,192]{1,0:T(8,128)S(1)}, f32[1728,192]{1,0:T(8,128)}, u32[]{:S(2)}) copy-start(f32[1728,192]{1,0:T(8,128)} %get-tuple-element.53) | copy-start | bytes 3981316

commit v6 on v5

--- a/solution.py
+++ b/solution.py
@@ -1,3 +1,5 @@
+import collections
+
 import jax
 import jax.numpy as jnp
 from jax import lax
@@ -13,29 +15,63 @@
 TAPS = [(r, c) for r in (-1, 0, 1) for c in (-1, 0, 1)]
 PLANE = ("x", "y", "c")
 VMEM_LIMIT = 16 * 1024 * 1024
-
-
-def call(body, outs, scratch, flops, *args, after=()):
+WEIGHT = 20
+
+
+Far = collections.namedtuple("Far", "array member")
+Arriving = collections.namedtuple("Arriving", "copy buffer")
+
+
+def arrived(ref):
+    if isinstance(ref, Arriving):
+        ref.copy.wait()
+        return ref.buffer
+    return ref
+
+
+def call(body, outs, scratch, flops, *args, after=(), far=0):
     specs = [pl.BlockSpec(memory_space=pl.ANY)] * len(after)
     arrays, size = list(after), 0
+    buffers = []
     for arg in args:
-        if isinstance(arg, tuple):
+        if isinstance(arg, Far):
+            member = arg.member
+            arg = arg.array
+            shape = arg.shape if member is None else arg.shape[:3] + arg.shape[4:]
+            buffers += [pltpu.VMEM(shape, arg.dtype), pltpu.SemaphoreType.DMA]
+            specs.append(pl.BlockSpec(memory_space=pltpu.HBM))
+            arg = pltpu.with_memory_space_constraint(arg, pltpu.HBM)
+        elif isinstance(arg, tuple):
             arg, member = arg
             shape = arg.shape[:3] + (None,) + arg.shape[4:]
             specs.append(pl.BlockSpec(shape, lambda step, member=member: (0, 0, 0, member, 0, 0, 0, 0, 0)))
-            size += arg.size // arg.shape[3] * arg.dtype.itemsize
         else:
             specs.append(pl.BlockSpec(memory_space=pltpu.VMEM))
-            size += arg.size * arg.dtype.itemsize
+        size += arg.size * arg.dtype.itemsize
         arrays.append(arg)
     size += sum(o.size * o.dtype.itemsize for o in outs)
+
+    def run(*refs):
+        refs = list(refs[len(after) :])
+        own = len(refs) - len(buffers)
+        slot = own
+        for i, arg in enumerate(args):
+            if isinstance(arg, Far):
+                source = refs[i] if arg.member is None else refs[i].at[:, :, :, arg.member]
+                copy = pltpu.make_async_copy(source, refs[slot], refs[slot + 1])
+                copy.start()
+                refs[i] = Arriving(copy, refs[slot])
+                slot += 2
+        body(*refs[:own])
+
+    near = len(outs) - far
     return pl.pallas_call(
-        lambda *refs: body(*refs[len(after) :]),
+        run,
         grid=(1,),
-        out_shape=outs,
+        out_shape=outs[:near] + [pltpu.HBM(o.shape, o.dtype) for o in outs[near:]],
         in_specs=specs,
-        out_specs=[pl.BlockSpec(memory_space=pltpu.VMEM)] * len(outs),
-        scratch_shapes=scratch,
+        out_specs=[pl.BlockSpec(memory_space=pltpu.VMEM)] * near + [pl.BlockSpec(memory_space=pltpu.HBM)] * far,
+        scratch_shapes=list(scratch) + buffers,
         compiler_params=pltpu.CompilerParams(vmem_limit_bytes=VMEM_LIMIT),
         cost_estimate=pl.CostEstimate(flops=flops, bytes_accessed=size if flops else 0, transcendentals=0),
     )(*arrays)
@@ -110,44 +146,59 @@
 
     def body(*refs):
         pieces, act_ref, w_ref = refs[:n], refs[n], refs[n + 1]
-        out_refs, padded = refs[n + 2 : -1], refs[-1]
+        out_refs, wide_ref, padded, sem = refs[n + 2 : -3], refs[-3], refs[-2], refs[-1]
         fill(padded, pieces, step)
+        copy = pltpu.make_async_copy(padded, wide_ref, sem)
+        copy.start()
         grad = pulled(padded, w_ref, step)
-        pre = class_flat(act_ref).astype(F32)
+        pre = class_flat(arrived(act_ref)).astype(F32)
         sigma = jax.nn.sigmoid(pre)
         store(out_refs, grad * sigma * (1.0 + pre * (1.0 - sigma)))
+        copy.wait()
 
     chan = weights.shape[-1]
-    outs = outs + [padded_shape(chan, step)]
-    *parts, wide = call(body, outs, [], conv_flops(chan, step), *field, act, weights, after=after)
+    wide = padded_shape(chan, step)
+    scratch = [pltpu.VMEM(wide.shape, BF16), pltpu.SemaphoreType.DMA]
+    outs = outs + [wide]
+    *parts, wide = call(body, outs, scratch, conv_flops(chan), *field, act, weights, after=after, far=1)
     return parts, wide
 
 
-def conv_one(field, base, weights, step, outs, after=()):
+def conv_one(field, base, weights, step, outs, after=(), emit=True):
     n, b = len(field), len(base)
 
     def body(*refs):
         pieces, base_refs, w_ref = refs[:n], refs[n : n + b], refs[n + b]
-        out_refs, padded = refs[n + b + 1 :], pieces[0]
-        if n > 1:
-            out_refs, padded = out_refs[:-1], out_refs[-1]
-            fill(padded, pieces, step)
+        out_refs, wide_ref, padded, sem = refs[n + b + 1 : -3], refs[-3], refs[-2], refs[-1]
+        if not emit:
+            out_refs = refs[n + b + 1 : -2]
+        fill(padded, pieces, step)
+        copy = pltpu.make_async_copy(padded, wide_ref, sem) if emit else None
+        if emit:
+            copy.start()
         grad = pulled(padded, w_ref, step)
         store(out_refs, flat(base_refs).astype(F32) + grad)
+        if emit:
+            copy.wait()
 
     chan = weights.shape[-1]
-    outs = outs + [padded_shape(chan, step)] * (n > 1)
-    parts = call(body, outs, [], conv_flops(chan, step), *field, *base, weights, after=after)
-    return parts[: len(parts) - (n > 1)], parts[-1]
-
-
-def tap_products(padded, src_ref, active, step, out_ref):
-    src = class_flat(src_ref)
+    wide = padded_shape(chan, step)
+    scratch = [pltpu.VMEM(wide.shape, BF16), pltpu.SemaphoreType.DMA]
+    outs = outs + [wide] * emit
+    args = (*field, *base, weights)
+    flops = conv_flops(chan) if emit else 0
+    parts = call(body, outs, scratch, flops, *args, after=after, far=int(emit))
+    return parts[: len(parts) - emit], parts[-1]
+
+
+def tap_products(wide_ref, src_ref, active, step, out_ref):
+    src = class_flat(arrived(src_ref))
     chan = src.shape[-1]
     if active:
         pre = src.astype(F32)
         src = (pre * jax.nn.sigmoid(pre)).astype(BF16)
     turned = src.T
+    padded = arrived(wide_ref)
     for k, tap in enumerate(TAPS):
         out_ref[k * chan : (k + 1) * chan] = jnp.dot(
             turned, window(padded, tap, step), preferred_element_type=F32
@@ -159,27 +210,31 @@
 
 
 def weight_grad(wide, source, step, chan, after=()):
-    def body(wide_ref, src_ref, out_ref):
-        tap_products(wide_ref, src_ref, True, step, out_ref)
-
-    out = [jax.ShapeDtypeStruct((tap_rows(chan), chan), F32)]
-    return call(body, out, [], conv_flops(chan, step), wide, source, after=after)[0]
+    def body(wide_ref, src_ref, out_ref, total, sem):
+        tap_products(wide_ref, src_ref, True, step, total)
+        copy = pltpu.make_async_copy(total, out_ref, sem)
+        copy.start()
+        copy.wait()
+
+    shape = (tap_rows(chan), chan)
+    out = [jax.ShapeDtypeStruct(shape, F32)]
+    scratch = [pltpu.VMEM(shape, F32), pltpu.SemaphoreType.DMA]
+    return call(body, out, scratch, conv_flops(chan), Far(wide, None), source, after=after, far=1)[0]
 
 
 def weight_grad_split(field, source, step, chan, other, after=()):
     n = len(field)
-
     rows = tap_rows(chan)
     shape = (rows // 16, 16, chan)
-
     part = (2, rows // 64, 16, chan)
 
     def body(*refs):
         src_ref, other_ref, keep_ref, *give_refs = refs[n : n + 5]
-        wide_ref, total = refs[n + 5 if n > 1 else 0], refs[-1]
+        padded, total = refs[-2:]
         if n > 1:
-            fill(wide_ref, refs[:n], step)
-        tap_products(wide_ref, src_ref, False, step, total)
+            fill(padded, refs[:n], step)
+        tap_products(padded if n > 1 else refs[0], src_ref, False, step, total)
+        other_ref = arrived(other_ref)
         core = lax.axis_index("c")
 
         def split(kept, given):
@@ -197,15 +252,16 @@
             split(total, other_ref)
 
     outs = [jax.ShapeDtypeStruct(shape, F32)] + [jax.ShapeDtypeStruct(part, BF16)] * 2
-    if n > 1:
-        outs.append(padded_shape(chan, step))
-    scratch = [pltpu.VMEM((rows, chan), F32)]
-    keep, one, two, *wide = call(body, outs, scratch, conv_flops(chan, step), *field, source, other, after=after)
-    return keep, [xor(one, "c", 1), xor(two, "c", 1)], wide
-
-
-def conv_flops(chan, step):
-    return (20 if step == 1 else 20) * 2 * len(TAPS) * 1024 * chan * chan
+    scratch = [pltpu.VMEM(padded_shape(chan, step).shape, BF16), pltpu.VMEM((rows, chan), F32)]
+    if n == 1:
+        field = [Far(field[0], None)]
+    args = (*field, source, Far(other, None))
+    keep, one, two = call(body, outs, scratch, conv_flops(chan), *args, after=after)
+    return keep, [xor(one, "c", 1), xor(two, "c", 1)]
+
+
+def conv_flops(chan):
+    return WEIGHT * 2 * len(TAPS) * 1024 * chan * chan
 
 
 def padded_shape(chan, step):
@@ -337,18 +393,19 @@
     return call(body, out, [], 0, *parts, after=after)[0]
 
 
-def spread_weights(part, taps, gate=None, after=()):
+def spread_weights(part, taps, gate, split):
     quarters = [part] + [xor(part, ("x", "y"), k) for k in (1, 2, 3)]
-    if gate is None:
-        others = [xor(value, "c", 1) for value in quarters]
+    others = [xor(join(*quarters[:2], after=[gate]), "c", 1)]
+    if split:
+        others += [xor(value, "c", 1) for value in quarters[2:]]
     else:
-        others = [xor(join(*quarters[:2], after=[gate]), "c", 1), xor(join(*quarters[2:], after=[gate]), "c", 1)]
+        others.append(xor(join(*quarters[2:], after=[gate]), "c", 1))
     chan = part.shape[-1]
 
     def body(*refs):
         own_refs, other_refs, first_ref, second_ref = refs[:4], refs[4:-2], refs[-2], refs[-1]
-        if len(other_refs) == 2:
-            other_refs = [ref.at[k] for ref in other_refs for k in range(2)]
+        pairs = 1 if split else 2
+        other_refs = [ref.at[k] for ref in other_refs[:pairs] for k in range(2)] + list(other_refs[pairs:])
 
         def put(out_ref, part_refs):
             for k, ref in enumerate(part_refs):
@@ -369,9 +426,13 @@
             put(first_ref, other_refs)
             put(second_ref, own_refs)
 
-    outs = [jax.ShapeDtypeStruct((taps * chan, chan), F32)] * 2
-    one, two = call(body, outs, [], 0, *quarters, *others, after=after)
-    return one.reshape(taps, chan, chan), two.reshape(taps, chan, chan)
+    def marked(*refs):
+        body(*refs[:-1])
+        refs[-1][...] = jnp.zeros(refs[-1].shape, F32)
+
+    outs = [jax.ShapeDtypeStruct((taps * chan, chan), F32)] * 2 + [jax.ShapeDtypeStruct((8, 128), F32)]
+    one, two, mark = call(marked, outs, [], 0, *quarters, *others)
+    return mark, one.reshape(taps, chan, chan), two.reshape(taps, chan, chan)
 
 
 def local(
@@ -398,7 +459,7 @@
     late = [first_block_preactivation, second_block_input, first_block_input]
     packed = pack_classes(*late, after=[packed])
     late = swap_classes(packed)
-    act_one, entry_two, entry_one = (late, 0), (late, 1), (late, 2)
+    act_one, entry_two, entry_one = Far(late, 0), Far(late, 1), Far(late, 2)
     field = [low, final, high]
     pre, wide = conv_two(field, act_two, second_block_conv_two, 2, halves, after=[packed])
     low, high = ring(pre[0], pre[1])
@@ -406,7 +467,7 @@
     field = [low, *pre, high]
     mid, wide = conv_one(field, [final], second_block_conv_one, 2, thirds, after=[second_two])
     low, high = ring(mid[0], mid[2])
-    keep, got, _ = weight_grad_split([wide], entry_two, 2, chan, second_two)
+    keep, got = weight_grad_split([wide], entry_two, 2, chan, second_two)
     field = [low, *mid, high]
     pre, wide = conv_two(field, act_one, first_block_conv_two, 1, thirds, after=[keep])
     low, high = ring(pre[0], pre[2])
@@ -414,18 +475,18 @@
     first_two = weight_grad(wide, act_one, 1, chan, after=[own])
     field = [low, *pre, high]
     whole = [jax.ShapeDtypeStruct((2, 2, 2, 2, 2, 2, STRIDE, chan), BF16)]
-    keep, got, wide = weight_grad_split(field, entry_one, 1, chan, first_two)
+    keep, got = weight_grad_split(field, entry_one, 1, chan, first_two)
     part = add_parts(parts)
     own_b, sent_b = sum_plane(keep, got, after=[part])
     part = add(part, xor(part, "z", 1), after=[own_b])
-    (out,), _ = conv_one(wide, mid, first_block_conv_one, 1, whole, after=[part])
+    (out,), _ = conv_one(field, mid, first_block_conv_one, 1, whole, after=[part], emit=False)
     part_b = add(own_b, *plane_terms(sent_b), after=[part, out])
     out = gather_classes(out, height, breadth)
     part = sum_far(part, after=[part_b])
     part_b = add(part_b, xor(part_b, "z", 1), after=[part])
-    second_two, second_one = spread_weights(part, len(TAPS), gate=part_b)
+    mark, second_two, second_one = spread_weights(part, len(TAPS), part_b, False)
     part_b = sum_far(part_b, after=[out])
-    first_two, first_one = spread_weights(part_b, len(TAPS), after=[second_two])
+    _, first_two, first_one = spread_weights(part_b, len(TAPS), mark, True)
     return out, first_one, first_two, second_one, second_two
 
 

time: 144 us -> 140 us (0.972)
  Pallas kernels: 21.5 us -> 31.1 us
  local copies, waits for them, and re-layouts: 13.8 us -> 4.51 us
  waiting for transfers between devices: 44.9 us -> 38.2 us
  starting transfers between devices: 48.3 us -> 50.4 us
    unnamed x54, local copies, waits for them, and re-layouts: 12.9 us -> 2.68 us
    pallas_call x23 -> x24, Pallas kernels: 21.5 us -> 31.1 us  [call(): pl.pallas_call(run, grid=(1,), out_shape=outs[:near] + [pltpu.HBM(o.shape...]
    ppermute x23 -> x22, waiting for transfers between devices: 24.4 us -> 21.2 us  [xor(): return lax.ppermute(value, axis, [(i, i ^ k) for i in range(count)])]
    ppermute x4, waiting for transfers between devices: 6 us -> 4.11 us  [ring(): lax.ppermute(right_edge, 'z', up)]
    ppermute x23 -> x22, starting transfers between devices: 18.3 us -> 19.1 us  [xor(): return lax.ppermute(value, axis, [(i, i ^ k) for i in range(count)])]
  transfers between devices with their start and end apart: 35 -> 34, of which waited for: 13 -> 17; matrix products, arithmetic and copies ran while one was open for 1% -> 1% of each run, Pallas kernels for 13% -> 20%
where the time goes in v6:
time: 140 us; the launch traced here: 139 us
  starting transfers between devices  50.4 us (36%)
  waiting for transfers between devices  38.2 us (27%)
  Pallas kernels  31.1 us (22%)
  blocking collectives  13.9 us (10%)
  local copies, waits for them, and re-layouts  4.51 us (3%)
    pallas_call x24, Pallas kernels, call(): pl.pallas_call(run, grid=(1,), out_shape=outs[:near] + [pltpu.HBM(o.shape...  31.1 us
    ppermute x22, waiting for transfers between devices, xor(): return lax.ppermute(value, axis, [(i, i ^ k) for i in range(count)])  21.2 us
    ppermute x22, starting transfers between devices, xor(): return lax.ppermute(value, axis, [(i, i ^ k) for i in range(count)])  19.1 us
    all_to_all x1, blocking collectives, swap_classes(): moved = lax.all_to_all(packed, PLANE, 0, 0)  13.9 us
    ppermute x4, starting transfers between devices, ring(): lax.ppermute(left_edge, 'z', down)  11.3 us
    all_to_all x2, starting transfers between devices, swap_classes(): moved = lax.all_to_all(packed, PLANE, 0, 0)  7.79 us
    ppermute x4, waiting for transfers between devices, ring(): lax.ppermute(left_edge, 'z', down)  7.16 us
    all_to_all x1, starting transfers between devices, gather_classes(): parts = lax.all_to_all(parts, PLANE, 0, 0)  4.16 us
  transfers between devices with their start and end apart: 34, of which 17 were waited for; matrix products, arithmetic and copies ran while one was open for 1% of the time, Pallas kernels for 20%

profile of v6, /device:TPU:0, one launch (start us, length us, event | category | flops | bytes accessed | tf_op | source)
XLA Modules:
  0.0 139.3 jit_solution(5365363982384970676)
XLA Ops:
  0.7 1.1 copy-done.6
  1.8 13.9 %all_to_all.25 = bf16[8,1,2,2,2,16,192]{6,5,4,3,2,1,0:T(8,128)(2,1)S(1)} all-to-all(bf16[8,1,2,2,2,16,192]{6,5,4,3,2,1,0:T(8,128)(2,1)S(1)} %shard_map.128), channel_id=1, replica_groups=mesh['z'=4,'x'=2,'y'=2,'c'=2] {'x','y','c'}, dimensions={0} | all-to-all | bytes 786432 | tf_op jit(solution)/shard_map/all_to_all | solution.py:294
  15.7 0.8 shard_map.129.refs_0_
  16.5 3.5 %all-to-all-start.1 = ((bf16[8,1,2,2,2,16,192]{6,5,4,3,2,1,0:T(8,128)(2,1)}), bf16[8,1,2,2,2,16,192]{6,5,4,3,2,1,0:T(8,128)(2,1)S(1)}, u32[]{:S(2)}, u32[]{:S(2)}) async-start(bf16[8,1,2,2,2,16,192]{6,5,4,3,2,1,0:T(8,128)(2,1)} %shard_map.129.refs_0_), calls=%async_computation.1 | async-start | bytes 1048576 | tf_op jit(solution)/shard_map/all_to_all | solution.py:294
  20.0 0.8 fusion
  20.7 1.6 %collective-permute-start = (bf16[2,2,2,2,2,16,192]{6,5,4,3,2,1,0:T(8,128)(2,1)}, bf16[2,2,2,2,2,16,192]{6,5,4,3,2,1,0:T(8,128)(2,1)S(1)}, u32[]{:S(2)}, u32[]{:S(2)}) collective-permute-start(bf16[2,2,2,2,2,16,192]{6,5,4,3,2,1,0:T(8,128)(2,1)} %bitcast.1), channel_id=1, source_target_pairs={{0,8},{8,16},{16,24},{24,0},{1,9},{9,17},{17,25},{25,1},{2,10},{10... | collective-permute-start | bytes 589832 | tf_op jit(solution)/shard_map/ppermute | solution.py:310
  22.3 2.2 %collective-permute-start.1 = (bf16[2,2,2,2,2,16,192]{6,5,4,3,2,1,0:T(8,128)(2,1)S(1)}, bf16[2,2,2,2,2,16,192]{6,5,4,3,2,1,0:T(8,128)(2,1)S(1)}, u32[]{:S(2)}, u32[]{:S(2)}) collective-permute-start(bf16[2,2,2,2,2,16,192]{6,5,4,3,2,1,0:T(8,128)(2,1)S(1)} %bitcast.19), channel_id=1, source_target_pairs={{8,0},{16,8},{24,16},{0,24},{9,1},{17,9},{25,17},{1,25},{10,2},{18... | collective-permute-start | bytes 589832 | tf_op jit(solution)/shard_map/ppermute | solution.py:310
  24.6 1.2 shard_map.130.refs_0_
  25.8 2.9 %all-to-all-done.1 = bf16[8,1,2,2,2,16,192]{6,5,4,3,2,1,0:T(8,128)(2,1)S(1)} async-done(((bf16[8,1,2,2,2,16,192]{6,5,4,3,2,1,0:T(8,128)(2,1)}), bf16[8,1,2,2,2,16,192]{6,5,4,3,2,1,0:T(8,128)(2,1)S(1)}, u32[]{:S(2)}, u32[]{:S(2)}) %all-to-all-start.1) | async-done | bytes 393248 | tf_op jit(solution)/shard_map/all_to_all | solution.py:294
  28.8 4.3 %all-to-all-start.2 = ((bf16[8,3,2,2,2,16,192]{6,5,4,3,2,1,0:T(8,128)(2,1)}), bf16[8,3,2,2,2,16,192]{6,5,4,3,2,1,0:T(8,128)(2,1)}, u32[]{:S(2)}, u32[]{:S(2)}) async-start(bf16[8,3,2,2,2,16,192]{6,5,4,3,2,1,0:T(8,128)(2,1)} %shard_map.130.refs_0_), calls=%async_computation.2 | async-start | bytes 3145728 | tf_op jit(solution)/shard_map/all_to_all | solution.py:294
  33.1 3.2 %collective-permute-done.1.refs_3_ = bf16[2,2,2,2,2,16,192]{6,5,4,3,2,1,0:T(8,128)(2,1)S(1)} collective-permute-done((bf16[2,2,2,2,2,16,192]{6,5,4,3,2,1,0:T(8,128)(2,1)S(1)}, bf16[2,2,2,2,2,16,192]{6,5,4,3,2,1,0:T(8,128)(2,1)S(1)}, u32[]{:S(2)}, u32[]{:S(2)}) %collective-permute-start.1) | collective-permute-done | bytes 196640 | tf_op jit(solution)/shard_map/ppermute | solution.py:310
  36.3 1.8 %shard_map.131 = (bf16[2,8,2,16,192]{4,3,2,1,0:T(8,128)(2,1)S(1)}, bf16[2,8,2,16,192]{4,3,2,1,0:T(8,128)(2,1)S(1)}, bf16[8,12,2,16,192]{4,3,2,1,0:T(8,128)(2,1)}) custom-call(bf16[8,3,2,2,2,16,192]{6,5,4,3,2,1,0:T(8,128)(2,1)} %shard_map.130.refs_0_, bf16[2,2,2,2,2,16,192]{6,5,4,3,2,1,0:T(8,128)(2,1)S(1)} %collective-permute-done.refs_1_, ...), custom_call_target="tpu_custom_call" | custom-call | flops 13589544960 | bytes 3416064 | tf_op jit(solution)/shard_map/pallas_call | solution.py:68
  38.1 1.4 collective-permute-start.2
  39.4 2.5 %collective-permute-start.3 = (bf16[2,8,2,16,192]{4,3,2,1,0:T(8,128)(2,1)S(1)}, bf16[2,8,2,16,192]{4,3,2,1,0:T(8,128)(2,1)S(1)}, u32[]{:S(2)}, u32[]{:S(2)}) collective-permute-start(bf16[2,8,2,16,192]{4,3,2,1,0:T(8,128)(2,1)S(1)} %get-tuple-element.33.refs_2_), channel_id=1, source_target_pairs={{8,0},{16,8},{24,16},{0,24},{9,1},{17,9},{25,17},{1,25},{10,2},{18... | collective-permute-start | bytes 589832 | tf_op jit(solution)/shard_map/ppermute | solution.py:310
  42.0 3.8 %shard_map.132.refs_0_.refs_2_ = f32[1728,192]{1,0:T(8,128)} custom-call(bf16[8,12,2,16,192]{4,3,2,1,0:T(8,128)(2,1)} %get-tuple-element.31.refs_0_, bf16[2,2,2,1,2,2,2,16,192]{8,7,6,5,4,3,2,1,0:T(8,128)(2,1)S(1)} %bitcast.18), custom_call_target="tpu_custom_call" | custom-call | flops 13589544960 | bytes 2899968 | tf_op jit(solution)/shard_map/pallas_call | solution.py:68
  45.8 3.4 %collective-permute-done.2.refs_1_ = bf16[2,8,2,16,192]{4,3,2,1,0:T(8,128)(2,1)S(1)} collective-permute-done((bf16[2,8,2,16,192]{4,3,2,1,0:T(8,128)(2,1)S(1)}, bf16[2,8,2,16,192]{4,3,2,1,0:T(8,128)(2,1)S(1)}, u32[]{:S(2)}, u32[]{:S(2)}) %collective-permute-start.2) | collective-permute-done | bytes 196640 | tf_op jit(solution)/shard_map/ppermute | solution.py:310
  49.2 3.9 %collective-permute-done.3.refs_4_ = bf16[2,8,2,16,192]{4,3,2,1,0:T(8,128)(2,1)S(1)} collective-permute-done((bf16[2,8,2,16,192]{4,3,2,1,0:T(8,128)(2,1)S(1)}, bf16[2,8,2,16,192]{4,3,2,1,0:T(8,128)(2,1)S(1)}, u32[]{:S(2)}, u32[]{:S(2)}) %collective-permute-start.3) | collective-permute-done | bytes 196640 | tf_op jit(solution)/shard_map/ppermute | solution.py:310
  53.0 1.5 %copy-done.26 = f32[1728,192]{1,0:T(8,128)S(1)} copy-done((f32[1728,192]{1,0:T(8,128)S(1)}, f32[1728,192]{1,0:T(8,128)}, u32[]{:S(2)}) %copy-start.26) | copy-done | bytes 1327128
  54.5 1.8 %shard_map.133 = (bf16[1,8,2,16,192]{4,3,2,1,0:T(8,128)(2,1)S(1)}, bf16[2,8,2,16,192]{4,3,2,1,0:T(8,128)(2,1)S(1)}, bf16[1,8,2,16,192]{4,3,2,1,0:T(8,128)(2,1)S(1)}, bf16[8,12,2,16,192]{4,3,2,1,0:T(8,128)(2,1)}) custom-call(f32[1728,192]{1,0:T(8,128)S(1)} %copy-done.26, bf16[2,8,2,16,192]{4,3,2,1,0:T(8,128)(2,1)S(1)} %collective-permute-done.2.refs_1_, ...), custom_call_target="tpu_custom_call" | custom-call | flops 13589544960 | bytes 3416064 | tf_op jit(solution)/shard_map/pallas_call | solution.py:68
  56.3 0.4 collective-permute-start.6
  56.7 3.5 %collective-permute-start.7 = (bf16[1,8,2,16,192]{4,3,2,1,0:T(8,128)(2,1)S(1)}, bf16[1,8,2,16,192]{4,3,2,1,0:T(8,128)(2,1)S(1)}, u32[]{:S(2)}, u32[]{:S(2)}) collective-permute-start(bf16[1,8,2,16,192]{4,3,2,1,0:T(8,128)(2,1)S(1)} %get-tuple-element.39.refs_2_.refs_6_), channel_id=1, source_target_pairs={{8,0},{16,8},{24,16},{0,24},{9,1},{17,9},{25,17},{1,25},{10,2},{18... | collective-permute-start | bytes 294920 | tf_op jit(solution)/shard_map/ppermute | solution.py:310
  60.2 3.1 %shard_map.134 = (f32[108,16,192]{2,1,0:T(8,128)S(1)}, bf16[2,27,16,192]{3,2,1,0:T(8,128)(2,1)S(1)}, bf16[2,27,16,192]{3,2,1,0:T(8,128)(2,1)S(1)}) custom-call(bf16[8,12,2,16,192]{4,3,2,1,0:T(8,128)(2,1)} %get-tuple-element.34.refs_0_, bf16[2,2,2,3,2,2,2,16,192]{8,7,6,5,4,3,2,1,0:T(8,128)(2,1)} %bitcast.4.refs_1_.refs_6_.refs_2_.refs_5_, ...), custom_call_target="tpu_custom_call" | custom-call | flops 13589544960 | bytes 5677056 | tf_op jit(solution)/shard_map/pallas_call | solution.py:68
  63.4 0.5 collective-permute-start.5
  63.9 0.7 collective-permute-done.6.refs_1_
  64.7 2.3 %shard_map.137 = (bf16[1,8,2,16,192]{4,3,2,1,0:T(8,128)(2,1)S(1)}, bf16[2,8,2,16,192]{4,3,2,1,0:T(8,128)(2,1)S(1)}, bf16[1,8,2,16,192]{4,3,2,1,0:T(8,128)(2,1)S(1)}, bf16[6,10,2,16,192]{4,3,2,1,0:T(8,128)(2,1)}) custom-call(f32[108,16,192]{2,1,0:T(8,128)S(1)} %get-tuple-element.35.refs_0_, bf16[1,8,2,16,192]{4,3,2,1,0:T(8,128)(2,1)S(1)} %collective-permute-done.6.refs_1_, ...), custom_call_target="tpu_custom_call" | custom-call | flops 13589544960 | bytes 3563520 | tf_op jit(solution)/shard_map/pallas_call | solution.py:68
  67.0 0.8 collective-permute-start.8
  67.8 3.1 %collective-permute-start.9 = (bf16[1,8,2,16,192]{4,3,2,1,0:T(8,128)(2,1)S(1)}, bf16[1,8,2,16,192]{4,3,2,1,0:T(8,128)(2,1)S(1)}, u32[]{:S(2)}, u32[]{:S(2)}) collective-permute-start(bf16[1,8,2,16,192]{4,3,2,1,0:T(8,128)(2,1)S(1)} %get-tuple-element.42.refs_1_.refs_2_), channel_id=1, source_target_pairs={{8,0},{16,8},{24,16},{0,24},{9,1},{17,9},{25,17},{1,25},{10,2},{18... | collective-permute-start | bytes 294920 | tf_op jit(solution)/shard_map/ppermute | solution.py:310
  70.9 1.1 shard_map.135.refs_0_
  72.0 3.9 %all-to-all-start.3 = ((bf16[4,27,16,192]{3,2,1,0:T(8,128)(2,1)}), bf16[4,27,16,192]{3,2,1,0:T(8,128)(2,1)S(1)}, u32[]{:S(2)}, u32[]{:S(2)}) async-start(bf16[4,27,16,192]{3,2,1,0:T(8,128)(2,1)} %shard_map.135.refs_0_), calls=%async_computation.3 | async-start | bytes 1769472 | tf_op jit(solution)/shard_map/all_to_all | solution.py:352
  75.9 3.9 %shard_map.138.refs_6_ = f32[1728,192]{1,0:T(8,128)} custom-call(bf16[4,27,16,192]{3,2,1,0:T(8,128)(2,1)} %shard_map.135.refs_0_, bf16[6,10,2,16,192]{4,3,2,1,0:T(8,128)(2,1)} %get-tuple-element.44.refs_1_, bf16[2,2,2,3,2,2,2,16,192]{8,7,6,5,4,3,2,1,0:T(8,128)(2,1)} %bitcast.4.refs_1_.refs_6_.refs_2_.refs_5_), custom_call_target="tpu_custom_call" | custom-call | flops 13589544960 | bytes 3244032 | tf_op jit(solution)/shard_map/pallas_call | solution.py:68
  79.8 3.6 %shard_map.139 = (f32[108,16,192]{2,1,0:T(8,128)S(1)}, bf16[2,27,16,192]{3,2,1,0:T(8,128)(2,1)}, bf16[2,27,16,192]{3,2,1,0:T(8,128)(2,1)}) custom-call(bf16[1,8,2,16,192]{4,3,2,1,0:T(8,128)(2,1)S(1)} %collective-permute-done.8.refs_0_.refs_1_, bf16[1,8,2,16,192]{4,3,2,1,0:T(8,128)(2,1)S(1)} %get-tuple-element.42.refs_1_.refs_2_, ...), custom_call_target="tpu_custom_call" | custom-call | flops 13589544960 | bytes 5087232 | tf_op jit(solution)/shard_map/pallas_call | solution.py:68
  83.5 0.5 collective-permute-start.11
  84.0 2.8 %all-to-all-done.3.refs_0_ = bf16[4,27,16,192]{3,2,1,0:T(8,128)(2,1)S(1)} async-done(((bf16[4,27,16,192]{3,2,1,0:T(8,128)(2,1)}), bf16[4,27,16,192]{3,2,1,0:T(8,128)(2,1)S(1)}, u32[]{:S(2)}, u32[]{:S(2)}) %all-to-all-start.3) | async-done | bytes 663584 | tf_op jit(solution)/shard_map/all_to_all | solution.py:352
  86.7 0.1 shard_map.136.refs_0_.refs_1_
  87.0 0.9 shard_map.140
  88.0 1.5 %collective-permute-start.13 = (bf16[27,16,192]{2,1,0:T(8,128)(2,1)}, bf16[27,16,192]{2,1,0:T(8,128)(2,1)S(1)}, u32[]{:S(2)}, u32[]{:S(2)}) collective-permute-start(bf16[27,16,192]{2,1,0:T(8,128)(2,1)} %get-tuple-element.49), channel_id=1, source_target_pairs={{0,2},{2,0},{4,6},{6,4},{1,3},{3,1},{5,7},{7,5},{8,10},{10,8},{12,... | collective-permute-start | bytes 497672 | tf_op jit(solution)/shard_map/ppermute | solution.py:315
  89.4 1.1 collective-permute-start.14
  90.6 0.9 collective-permute-start.15
  91.5 1.8 %collective-permute-done.12.refs_2_ = bf16[27,16,192]{2,1,0:T(8,128)(2,1)S(1)} collective-permute-done((bf16[27,16,192]{2,1,0:T(8,128)(2,1)S(1)}, bf16[27,16,192]{2,1,0:T(8,128)(2,1)S(1)}, u32[]{:S(2)}, u32[]{:S(2)}) %collective-permute-start.12) | collective-permute-done | bytes 165920 | tf_op jit(solution)/shard_map/ppermute | solution.py:315
  93.3 0.4 collective-permute-start.16
  93.7 2.2 %shard_map.142.refs_1_ = bf16[2,2,2,2,2,2,16,192]{7,6,5,4,3,2,1,0:T(8,128)(2,1)} custom-call(bf16[27,16,192]{2,1,0:T(8,128)(2,1)S(1)} %shard_map.141.refs_0_.refs_1_, bf16[1,8,2,16,192]{4,3,2,1,0:T(8,128)(2,1)S(1)} %copy-done.20, bf16[1,8,2,16,192]{4,3,2,1,0:T(8,128)(2,1)S(1)} %copy-done.16, bf16[2,8,2,16,192]{4,3,2,1,0:T(8,128)(2,1)S(1)} %copy-done.10, ...), custom_call_target="tpu_custom_call" | custom-call | tf_op jit(solution)/shard_map/pallas_call | solution.py:68
  96.0 4.2 %all-to-all-start.4 = ((bf16[8,2,2,2,16,192]{5,4,3,2,1,0:T(8,128)(2,1)}), bf16[8,2,2,2,16,192]{5,4,3,2,1,0:T(8,128)(2,1)}, u32[]{:S(2)}, u32[]{:S(2)}) async-start(bf16[8,2,2,2,16,192]{5,4,3,2,1,0:T(8,128)(2,1)} %bitcast.5), calls=%async_computation.4 | async-start | bytes 1048576 | tf_op jit(solution)/shard_map/all_to_all | solution.py:302
  100.1 1.0 collective-permute-done.15.refs_5_
  101.1 0.1 shard_map.143.refs_0_.refs_1_
  101.2 1.8 %collective-permute-start.17 = (bf16[27,16,192]{2,1,0:T(8,128)(2,1)S(1)}, bf16[27,16,192]{2,1,0:T(8,128)(2,1)S(1)}, u32[]{:S(2)}, u32[]{:S(2)}) collective-permute-start(bf16[27,16,192]{2,1,0:T(8,128)(2,1)S(1)} %shard_map.143.refs_0_.refs_1_), channel_id=1, source_target_pairs={{0,8},{8,0},{16,24},{24,16},{1,9},{9,1},{17,25},{25,17},{2,10},{10... | collective-permute-start | bytes 497672 | tf_op jit(solution)/shard_map/ppermute | solution.py:315
  103.0 1.5 %collective-permute-done.16.refs_2_ = bf16[27,16,192]{2,1,0:T(8,128)(2,1)S(1)} collective-permute-done((bf16[27,16,192]{2,1,0:T(8,128)(2,1)S(1)}, bf16[27,16,192]{2,1,0:T(8,128)(2,1)S(1)}, u32[]{:S(2)}, u32[]{:S(2)}) %collective-permute-start.16) | collective-permute-done | bytes 165920 | tf_op jit(solution)/shard_map/ppermute | solution.py:315
  104.6 2.9 %collective-permute-start.24 = (bf16[27,16,192]{2,1,0:T(8,128)(2,1)S(1)}, bf16[27,16,192]{2,1,0:T(8,128)(2,1)S(1)}, u32[]{:S(2)}, u32[]{:S(2)}) collective-permute-start(bf16[27,16,192]{2,1,0:T(8,128)(2,1)S(1)} %shard_map.144.refs_0_.refs_1_), channel_id=1, source_target_pairs={{0,6},{2,4},{4,2},{6,0},{1,7},{3,5},{5,3},{7,1},{8,14},{10,12},{12... | collective-permute-start | bytes 497672 | tf_op jit(solution)/shard_map/ppermute | solution.py:315
  107.5 0.7 collective-permute-start.23
  108.3 1.4 collective-permute-start.22
  109.7 1.1 collective-permute-start.18
  110.8 4.2 %collective-permute-done.24.refs_2_.refs_3_ = bf16[27,16,192]{2,1,0:T(8,128)(2,1)S(1)} collective-permute-done((bf16[27,16,192]{2,1,0:T(8,128)(2,1)S(1)}, bf16[27,16,192]{2,1,0:T(8,128)(2,1)S(1)}, u32[]{:S(2)}, u32[]{:S(2)}) %collective-permute-start.24) | collective-permute-done | bytes 165920 | tf_op jit(solution)/shard_map/ppermute | solution.py:315
  115.0 3.5 %collective-permute-done.23.refs_1_.refs_2_ = bf16[27,16,192]{2,1,0:T(8,128)(2,1)S(1)} collective-permute-done((bf16[27,16,192]{2,1,0:T(8,128)(2,1)S(1)}, bf16[27,16,192]{2,1,0:T(8,128)(2,1)S(1)}, u32[]{:S(2)}, u32[]{:S(2)}) %collective-permute-start.23) | collective-permute-done | bytes 165920 | tf_op jit(solution)/shard_map/ppermute | solution.py:315
  118.7 0.6 collective-permute-done.22.refs_2_.refs_1_
  119.3 0.1 collective-permute-start.25
  119.4 1.1 copy.15
  120.5 0.4 collective-permute-done.18.refs_2_
  120.9 1.2 collective-permute-start.19
  122.1 4.3 %collective-permute-start.21 = (bf16[27,16,192]{2,1,0:T(8,128)(2,1)S(1)}, bf16[27,16,192]{2,1,0:T(8,128)(2,1)S(1)}, u32[]{:S(2)}, u32[]{:S(2)}) collective-permute-start(bf16[27,16,192]{2,1,0:T(8,128)(2,1)S(1)} %shard_map.146.refs_1_.refs_0_), channel_id=1, source_target_pairs={{0,6},{2,4},{4,2},{6,0},{1,7},{3,5},{5,3},{7,1},{8,14},{10,12},{12... | collective-permute-start | bytes 497672 | tf_op jit(solution)/shard_map/ppermute | solution.py:315
  126.4 2.0 %shard_map.149 = (f32[1728,192]{1,0:T(8,128)}, f32[1728,192]{1,0:T(8,128)}, f32[8,128]{1,0:T(8,128)S(1)}) custom-call(bf16[27,16,192]{2,1,0:T(8,128)(2,1)S(1)} %shard_map.144.refs_0_.refs_1_, bf16[27,16,192]{2,1,0:T(8,128)(2,1)S(1)} %collective-permute-done.22.refs_2_.refs_1_, bf16[27,16,192]{2,1,0:T(8,128)(2,1)S(1)} %collective-permute-done.23.refs_1_.refs_2_, ...), custom_call_target="tpu_custom_call" | custom-call | tf_op jit(solution)/shard_map/pallas_call | solution.py:68
  128.4 4.7 %collective-permute-done.19.refs_2_.refs_1_ = bf16[27,16,192]{2,1,0:T(8,128)(2,1)S(1)} collective-permute-done((bf16[27,16,192]{2,1,0:T(8,128)(2,1)S(1)}, bf16[27,16,192]{2,1,0:T(8,128)(2,1)S(1)}, u32[]{:S(2)}, u32[]{:S(2)}) %collective-permute-start.19) | collective-permute-done | bytes 165920 | tf_op jit(solution)/shard_map/ppermute | solution.py:315
  133.3 0.5 collective-permute-start.29
  133.8 2.0 %collective-permute-done.20.refs_2_ = bf16[27,16,192]{2,1,0:T(8,128)(2,1)S(1)} collective-permute-done((bf16[27,16,192]{2,1,0:T(8,128)(2,1)S(1)}, bf16[27,16,192]{2,1,0:T(8,128)(2,1)S(1)}, u32[]{:S(2)}, u32[]{:S(2)}) %collective-permute-start.20) | collective-permute-done | bytes 165920 | tf_op jit(solution)/shard_map/ppermute | solution.py:315
  135.8 1.5 %collective-permute-done.28.refs_5_ = bf16[27,16,192]{2,1,0:T(8,128)(2,1)S(1)} collective-permute-done((bf16[27,16,192]{2,1,0:T(8,128)(2,1)S(1)}, bf16[27,16,192]{2,1,0:T(8,128)(2,1)S(1)}, u32[]{:S(2)}, u32[]{:S(2)}) %collective-permute-start.28) | collective-permute-done | bytes 165920 | tf_op jit(solution)/shard_map/ppermute | solution.py:315
  137.2 2.0 %shard_map.151 = (f32[1728,192]{1,0:T(8,128)}, f32[1728,192]{1,0:T(8,128)}, f32[8,128]{1,0:T(8,128)}) custom-call(bf16[27,16,192]{2,1,0:T(8,128)(2,1)S(1)} %shard_map.146.refs_1_.refs_0_, bf16[27,16,192]{2,1,0:T(8,128)(2,1)S(1)} %collective-permute-done.19.refs_2_.refs_1_, bf16[27,16,192]{2,1,0:T(8,128)(2,1)S(1)} %collective-permute-done.20.refs_2_, ...), custom_call_target="tpu_custom_call" | custom-call | tf_op jit(solution)/shard_map/pallas_call | solution.py:68
  (85 shorter events, 0.9 us)
Async XLA Ops:
  0.6 15.0 %copy-start.2 = (bf16[32,32,192]{2,1,0:T(8,128)(2,1)S(1)}, bf16[32,32,192]{2,1,0:T(8,128)(2,1)}, u32[]{:S(2)}) copy-start(bf16[32,32,192]{2,1,0:T(8,128)(2,1)} %refs_1_.2) | copy-start | bytes 1179652
  0.6 1.1 copy-start.6
  15.7 8.9 %copy-start.3 = (bf16[32,32,192]{2,1,0:T(8,128)(2,1)S(1)}, bf16[32,32,192]{2,1,0:T(8,128)(2,1)}, u32[]{:S(2)}) copy-start(bf16[32,32,192]{2,1,0:T(8,128)(2,1)} %refs_1_.3) | copy-start | bytes 1179652
  15.7 8.9 %copy-start.4 = (bf16[32,32,192]{2,1,0:T(8,128)(2,1)S(1)}, bf16[32,32,192]{2,1,0:T(8,128)(2,1)}, u32[]{:S(2)}) copy-start(bf16[32,32,192]{2,1,0:T(8,128)(2,1)} %refs_2_.1) | copy-start | bytes 1179652
  15.7 8.9 %copy-start.5 = (bf16[32,32,192]{2,1,0:T(8,128)(2,1)S(1)}, bf16[32,32,192]{2,1,0:T(8,128)(2,1)}, u32[]{:S(2)}) copy-start(bf16[32,32,192]{2,1,0:T(8,128)(2,1)} %refs_3_.1) | copy-start | bytes 1179652
  16.5 12.3 %all-to-all-start.1 = ((bf16[8,1,2,2,2,16,192]{6,5,4,3,2,1,0:T(8,128)(2,1)}), bf16[8,1,2,2,2,16,192]{6,5,4,3,2,1,0:T(8,128)(2,1)S(1)}, u32[]{:S(2)}, u32[]{:S(2)}) async-start(bf16[8,1,2,2,2,16,192]{6,5,4,3,2,1,0:T(8,128)(2,1)} %shard_map.129.refs_0_), calls=%async_computation.1 | async-start | bytes 1048576 | tf_op jit(solution)/shard_map/all_to_all | solution.py:294
  20.7 12.3 %collective-permute-start = (bf16[2,2,2,2,2,16,192]{6,5,4,3,2,1,0:T(8,128)(2,1)}, bf16[2,2,2,2,2,16,192]{6,5,4,3,2,1,0:T(8,128)(2,1)S(1)}, u32[]{:S(2)}, u32[]{:S(2)}) collective-permute-start(bf16[2,2,2,2,2,16,192]{6,5,4,3,2,1,0:T(8,128)(2,1)} %bitcast.1), channel_id=1, source_target_pairs={{0,8},{8,16},{16,24},{24,0},{1,9},{9,17},{17,25},{25,1},{2,10},{10... | collective-permute-start | bytes 589832 | tf_op jit(solution)/shard_map/ppermute | solution.py:310
  22.3 14.0 %collective-permute-start.1 = (bf16[2,2,2,2,2,16,192]{6,5,4,3,2,1,0:T(8,128)(2,1)S(1)}, bf16[2,2,2,2,2,16,192]{6,5,4,3,2,1,0:T(8,128)(2,1)S(1)}, u32[]{:S(2)}, u32[]{:S(2)}) collective-permute-start(bf16[2,2,2,2,2,16,192]{6,5,4,3,2,1,0:T(8,128)(2,1)S(1)} %bitcast.19), channel_id=1, source_target_pairs={{8,0},{16,8},{24,16},{0,24},{9,1},{17,9},{25,17},{1,25},{10,2},{18... | collective-permute-start | bytes 589832 | tf_op jit(solution)/shard_map/ppermute | solution.py:310
  25.8 10.5 %copy-start.23 = (bf16[9,192,192]{2,1,0:T(8,128)(2,1)S(1)}, bf16[9,192,192]{2,1,0:T(8,128)(2,1)}, u32[]{:S(2)}) copy-start(bf16[9,192,192]{2,1,0:T(8,128)(2,1)} %refs_5_.1) | copy-start | bytes 1990660
  28.8 31.4 %all-to-all-start.2 = ((bf16[8,3,2,2,2,16,192]{6,5,4,3,2,1,0:T(8,128)(2,1)}), bf16[8,3,2,2,2,16,192]{6,5,4,3,2,1,0:T(8,128)(2,1)}, u32[]{:S(2)}, u32[]{:S(2)}) async-start(bf16[8,3,2,2,2,16,192]{6,5,4,3,2,1,0:T(8,128)(2,1)} %shard_map.130.refs_0_), calls=%async_computation.2 | async-start | bytes 3145728 | tf_op jit(solution)/shard_map/all_to_all | solution.py:294
  38.1 11.1 %collective-permute-start.2 = (bf16[2,8,2,16,192]{4,3,2,1,0:T(8,128)(2,1)S(1)}, bf16[2,8,2,16,192]{4,3,2,1,0:T(8,128)(2,1)S(1)}, u32[]{:S(2)}, u32[]{:S(2)}) collective-permute-start(bf16[2,8,2,16,192]{4,3,2,1,0:T(8,128)(2,1)S(1)} %get-tuple-element.32.refs_3_), channel_id=1, source_target_pairs={{0,8},{8,16},{16,24},{24,0},{1,9},{9,17},{17,25},{25,1},{2,10},{10... | collective-permute-start | bytes 589832 | tf_op jit(solution)/shard_map/ppermute | solution.py:310
  39.4 13.6 %collective-permute-start.3 = (bf16[2,8,2,16,192]{4,3,2,1,0:T(8,128)(2,1)S(1)}, bf16[2,8,2,16,192]{4,3,2,1,0:T(8,128)(2,1)S(1)}, u32[]{:S(2)}, u32[]{:S(2)}) collective-permute-start(bf16[2,8,2,16,192]{4,3,2,1,0:T(8,128)(2,1)S(1)} %get-tuple-element.33.refs_2_), channel_id=1, source_target_pairs={{8,0},{16,8},{24,16},{0,24},{9,1},{17,9},{25,17},{1,25},{10,2},{18... | collective-permute-start | bytes 589832 | tf_op jit(solution)/shard_map/ppermute | solution.py:310
  42.0 11.1 %copy-start.24 = (bf16[9,192,192]{2,1,0:T(8,128)(2,1)S(1)}, bf16[9,192,192]{2,1,0:T(8,128)(2,1)}, u32[]{:S(2)}) copy-start(bf16[9,192,192]{2,1,0:T(8,128)(2,1)} %refs_6_.1) | copy-start | bytes 1990660
  53.0 1.5 %copy-start.26 = (f32[1728,192]{1,0:T(8,128)S(1)}, f32[1728,192]{1,0:T(8,128)}, u32[]{:S(2)}) copy-start(f32[1728,192]{1,0:T(8,128)} %shard_map.132.refs_0_.refs_2_) | copy-start | bytes 3981316
  56.3 8.4 %copy-start.7 = (bf16[2,8,2,16,192]{4,3,2,1,0:T(8,128)(2,1)}, bf16[2,8,2,16,192]{4,3,2,1,0:T(8,128)(2,1)S(1)}, u32[]{:S(2)}) copy-start(bf16[2,8,2,16,192]{4,3,2,1,0:T(8,128)(2,1)S(1)} %get-tuple-element.40.refs_3_.refs_7_) | copy-start | bytes 589828
  56.3 8.4 %copy-start.11 = (bf16[1,8,2,16,192]{4,3,2,1,0:T(8,128)(2,1)}, bf16[1,8,2,16,192]{4,3,2,1,0:T(8,128)(2,1)S(1)}, u32[]{:S(2)}) copy-start(bf16[1,8,2,16,192]{4,3,2,1,0:T(8,128)(2,1)S(1)} %get-tuple-element.39.refs_2_.refs_6_) | copy-start | bytes 294916
  56.3 8.4 %copy-start.13 = (bf16[1,8,2,16,192]{4,3,2,1,0:T(8,128)(2,1)}, bf16[1,8,2,16,192]{4,3,2,1,0:T(8,128)(2,1)S(1)}, u32[]{:S(2)}) copy-start(bf16[1,8,2,16,192]{4,3,2,1,0:T(8,128)(2,1)S(1)} %get-tuple-element.38.refs_4_.refs_8_) | copy-start | bytes 294916
  56.3 8.3 %collective-permute-start.6 = (bf16[1,8,2,16,192]{4,3,2,1,0:T(8,128)(2,1)S(1)}, bf16[1,8,2,16,192]{4,3,2,1,0:T(8,128)(2,1)S(1)}, u32[]{:S(2)}, u32[]{:S(2)}) collective-permute-start(bf16[1,8,2,16,192]{4,3,2,1,0:T(8,128)(2,1)S(1)} %get-tuple-element.38.refs_4_.refs_8_), channel_id=1, source_target_pairs={{0,8},{8,16},{16,24},{24,0},{1,9},{9,17},{17,25},{25,1},{2,10},{10... | collective-permute-start | bytes 294920 | tf_op jit(solution)/shard_map/ppermute | solution.py:310
  56.7 7.9 %collective-permute-start.7 = (bf16[1,8,2,16,192]{4,3,2,1,0:T(8,128)(2,1)S(1)}, bf16[1,8,2,16,192]{4,3,2,1,0:T(8,128)(2,1)S(1)}, u32[]{:S(2)}, u32[]{:S(2)}) collective-permute-start(bf16[1,8,2,16,192]{4,3,2,1,0:T(8,128)(2,1)S(1)} %get-tuple-element.39.refs_2_.refs_6_), channel_id=1, source_target_pairs={{8,0},{16,8},{24,16},{0,24},{9,1},{17,9},{25,17},{1,25},{10,2},{18... | collective-permute-start | bytes 294920 | tf_op jit(solution)/shard_map/ppermute | solution.py:310
  60.2 4.5 %copy-start.25 = (bf16[9,192,192]{2,1,0:T(8,128)(2,1)S(1)}, bf16[9,192,192]{2,1,0:T(8,128)(2,1)}, u32[]{:S(2)}) copy-start(bf16[9,192,192]{2,1,0:T(8,128)(2,1)} %refs_7_.1) | copy-start | bytes 1990660
  63.3 7.6 %collective-permute-start.4 = (bf16[2,27,16,192]{3,2,1,0:T(8,128)(2,1)S(1)}, bf16[2,27,16,192]{3,2,1,0:T(8,128)(2,1)S(1)}, u32[]{:S(2)}, u32[]{:S(2)}) collective-permute-start(bf16[2,27,16,192]{3,2,1,0:T(8,128)(2,1)S(1)} %get-tuple-element.36), channel_id=1, source_target_pairs={{0,1},{1,0},{2,3},{3,2},{4,5},{5,4},{6,7},{7,6},{8,9},{9,8},{10,11... | collective-permute-start | bytes 995336 | tf_op jit(solution)/shard_map/ppermute | solution.py:315
  63.4 7.5 %collective-permute-start.5 = (bf16[2,27,16,192]{3,2,1,0:T(8,128)(2,1)S(1)}, bf16[2,27,16,192]{3,2,1,0:T(8,128)(2,1)S(1)}, u32[]{:S(2)}, u32[]{:S(2)}) collective-permute-start(bf16[2,27,16,192]{3,2,1,0:T(8,128)(2,1)S(1)} %get-tuple-element.37), channel_id=1, source_target_pairs={{0,1},{1,0},{2,3},{3,2},{4,5},{5,4},{6,7},{7,6},{8,9},{9,8},{10,11... | collective-permute-start | bytes 995336 | tf_op jit(solution)/shard_map/ppermute | solution.py:315
  67.0 12.8 %copy-start.9 = (bf16[2,8,2,16,192]{4,3,2,1,0:T(8,128)(2,1)}, bf16[2,8,2,16,192]{4,3,2,1,0:T(8,128)(2,1)S(1)}, u32[]{:S(2)}) copy-start(bf16[2,8,2,16,192]{4,3,2,1,0:T(8,128)(2,1)S(1)} %get-tuple-element.43.refs_2_.refs_3_) | copy-start | bytes 589828
  67.0 12.8 %copy-start.15 = (bf16[1,8,2,16,192]{4,3,2,1,0:T(8,128)(2,1)}, bf16[1,8,2,16,192]{4,3,2,1,0:T(8,128)(2,1)S(1)}, u32[]{:S(2)}) copy-start(bf16[1,8,2,16,192]{4,3,2,1,0:T(8,128)(2,1)S(1)} %get-tuple-element.42.refs_1_.refs_2_) | copy-start | bytes 294916
  67.0 12.8 %copy-start.17 = (bf16[1,8,2,16,192]{4,3,2,1,0:T(8,128)(2,1)}, bf16[1,8,2,16,192]{4,3,2,1,0:T(8,128)(2,1)S(1)}, u32[]{:S(2)}) copy-start(bf16[1,8,2,16,192]{4,3,2,1,0:T(8,128)(2,1)S(1)} %get-tuple-element.41.refs_3_.refs_4_) | copy-start | bytes 294916
  67.0 12.7 %collective-permute-start.8 = (bf16[1,8,2,16,192]{4,3,2,1,0:T(8,128)(2,1)S(1)}, bf16[1,8,2,16,192]{4,3,2,1,0:T(8,128)(2,1)S(1)}, u32[]{:S(2)}, u32[]{:S(2)}) collective-permute-start(bf16[1,8,2,16,192]{4,3,2,1,0:T(8,128)(2,1)S(1)} %get-tuple-element.41.refs_3_.refs_4_), channel_id=1, source_target_pairs={{0,8},{8,16},{16,24},{24,0},{1,9},{9,17},{17,25},{25,1},{2,10},{10... | collective-permute-start | bytes 294920 | tf_op jit(solution)/shard_map/ppermute | solution.py:310
  67.8 11.9 %collective-permute-start.9 = (bf16[1,8,2,16,192]{4,3,2,1,0:T(8,128)(2,1)S(1)}, bf16[1,8,2,16,192]{4,3,2,1,0:T(8,128)(2,1)S(1)}, u32[]{:S(2)}, u32[]{:S(2)}) collective-permute-start(bf16[1,8,2,16,192]{4,3,2,1,0:T(8,128)(2,1)S(1)} %get-tuple-element.42.refs_1_.refs_2_), channel_id=1, source_target_pairs={{8,0},{16,8},{24,16},{0,24},{9,1},{17,9},{25,17},{1,25},{10,2},{18... | collective-permute-start | bytes 294920 | tf_op jit(solution)/shard_map/ppermute | solution.py:310
  72.0 14.8 %all-to-all-start.3 = ((bf16[4,27,16,192]{3,2,1,0:T(8,128)(2,1)}), bf16[4,27,16,192]{3,2,1,0:T(8,128)(2,1)S(1)}, u32[]{:S(2)}, u32[]{:S(2)}) async-start(bf16[4,27,16,192]{3,2,1,0:T(8,128)(2,1)} %shard_map.135.refs_0_), calls=%async_computation.3 | async-start | bytes 1769472 | tf_op jit(solution)/shard_map/all_to_all | solution.py:352
  79.7 3.6 %copy-start.19 = (bf16[1,8,2,16,192]{4,3,2,1,0:T(8,128)(2,1)}, bf16[1,8,2,16,192]{4,3,2,1,0:T(8,128)(2,1)S(1)}, u32[]{:S(2)}) copy-start(bf16[1,8,2,16,192]{4,3,2,1,0:T(8,128)(2,1)S(1)} %collective-permute-done.8.refs_0_.refs_1_) | copy-start | bytes 294916
  79.8 3.6 %copy-start.21 = (bf16[1,8,2,16,192]{4,3,2,1,0:T(8,128)(2,1)}, bf16[1,8,2,16,192]{4,3,2,1,0:T(8,128)(2,1)S(1)}, u32[]{:S(2)}) copy-start(bf16[1,8,2,16,192]{4,3,2,1,0:T(8,128)(2,1)S(1)} %collective-permute-done.9.refs_4_.refs_5_) | copy-start | bytes 294916
  83.4 3.5 %collective-permute-start.10 = (bf16[2,27,16,192]{3,2,1,0:T(8,128)(2,1)}, bf16[2,27,16,192]{3,2,1,0:T(8,128)(2,1)S(1)}, u32[]{:S(2)}, u32[]{:S(2)}) collective-permute-start(bf16[2,27,16,192]{3,2,1,0:T(8,128)(2,1)} %get-tuple-element.46), channel_id=1, source_target_pairs={{0,1},{1,0},{2,3},{3,2},{4,5},{5,4},{6,7},{7,6},{8,9},{9,8},{10,11... | collective-permute-start | bytes 995336 | tf_op jit(solution)/shard_map/ppermute | solution.py:315
  83.5 3.5 %collective-permute-start.11 = (bf16[2,27,16,192]{3,2,1,0:T(8,128)(2,1)}, bf16[2,27,16,192]{3,2,1,0:T(8,128)(2,1)S(1)}, u32[]{:S(2)}, u32[]{:S(2)}) collective-permute-start(bf16[2,27,16,192]{3,2,1,0:T(8,128)(2,1)} %get-tuple-element.47), channel_id=1, source_target_pairs={{0,1},{1,0},{2,3},{3,2},{4,5},{5,4},{6,7},{7,6},{8,9},{9,8},{10,11... | collective-permute-start | bytes 995336 | tf_op jit(solution)/shard_map/ppermute | solution.py:315
  86.8 6.4 %collective-permute-start.12 = (bf16[27,16,192]{2,1,0:T(8,128)(2,1)S(1)}, bf16[27,16,192]{2,1,0:T(8,128)(2,1)S(1)}, u32[]{:S(2)}, u32[]{:S(2)}) collective-permute-start(bf16[27,16,192]{2,1,0:T(8,128)(2,1)S(1)} %shard_map.136.refs_0_.refs_1_), channel_id=1, source_target_pairs={{0,8},{8,0},{16,24},{24,16},{1,9},{9,1},{17,25},{25,17},{2,10},{10... | collective-permute-start | bytes 497672 | tf_op jit(solution)/shard_map/ppermute | solution.py:315
  86.9 6.7 %copy-start.1 = (bf16[9,192,192]{2,1,0:T(8,128)(2,1)S(1)}, bf16[9,192,192]{2,1,0:T(8,128)(2,1)}, u32[]{:S(2)}) copy-start(bf16[9,192,192]{2,1,0:T(8,128)(2,1)} %refs_9_.1) | copy-start | bytes 1990660
  87.0 6.7 %copy-start.8 = (bf16[2,8,2,16,192]{4,3,2,1,0:T(8,128)(2,1)S(1)}, bf16[2,8,2,16,192]{4,3,2,1,0:T(8,128)(2,1)}, u32[]{:S(2)}) copy-start(bf16[2,8,2,16,192]{4,3,2,1,0:T(8,128)(2,1)} %copy-done.7) | copy-start | bytes 589828
  87.0 6.7 %copy-start.10 = (bf16[2,8,2,16,192]{4,3,2,1,0:T(8,128)(2,1)S(1)}, bf16[2,8,2,16,192]{4,3,2,1,0:T(8,128)(2,1)}, u32[]{:S(2)}) copy-start(bf16[2,8,2,16,192]{4,3,2,1,0:T(8,128)(2,1)} %copy-done.9) | copy-start | bytes 589828
  87.0 6.7 %copy-start.12 = (bf16[1,8,2,16,192]{4,3,2,1,0:T(8,128)(2,1)S(1)}, bf16[1,8,2,16,192]{4,3,2,1,0:T(8,128)(2,1)}, u32[]{:S(2)}) copy-start(bf16[1,8,2,16,192]{4,3,2,1,0:T(8,128)(2,1)} %copy-done.11) | copy-start | bytes 294916
  87.0 6.7 %copy-start.14 = (bf16[1,8,2,16,192]{4,3,2,1,0:T(8,128)(2,1)S(1)}, bf16[1,8,2,16,192]{4,3,2,1,0:T(8,128)(2,1)}, u32[]{:S(2)}) copy-start(bf16[1,8,2,16,192]{4,3,2,1,0:T(8,128)(2,1)} %copy-done.13) | copy-start | bytes 294916
  87.0 6.7 %copy-start.16 = (bf16[1,8,2,16,192]{4,3,2,1,0:T(8,128)(2,1)S(1)}, bf16[1,8,2,16,192]{4,3,2,1,0:T(8,128)(2,1)}, u32[]{:S(2)}) copy-start(bf16[1,8,2,16,192]{4,3,2,1,0:T(8,128)(2,1)} %copy-done.15) | copy-start | bytes 294916
  87.0 6.7 %copy-start.18 = (bf16[1,8,2,16,192]{4,3,2,1,0:T(8,128)(2,1)S(1)}, bf16[1,8,2,16,192]{4,3,2,1,0:T(8,128)(2,1)}, u32[]{:S(2)}) copy-start(bf16[1,8,2,16,192]{4,3,2,1,0:T(8,128)(2,1)} %copy-done.17) | copy-start | bytes 294916
  87.0 6.7 %copy-start.20 = (bf16[1,8,2,16,192]{4,3,2,1,0:T(8,128)(2,1)S(1)}, bf16[1,8,2,16,192]{4,3,2,1,0:T(8,128)(2,1)}, u32[]{:S(2)}) copy-start(bf16[1,8,2,16,192]{4,3,2,1,0:T(8,128)(2,1)} %copy-done.19) | copy-start | bytes 294916
  87.0 6.7 %copy-start.22 = (bf16[1,8,2,16,192]{4,3,2,1,0:T(8,128)(2,1)S(1)}, bf16[1,8,2,16,192]{4,3,2,1,0:T(8,128)(2,1)}, u32[]{:S(2)}) copy-start(bf16[1,8,2,16,192]{4,3,2,1,0:T(8,128)(2,1)} %copy-done.21) | copy-start | bytes 294916
  88.0 12.2 %collective-permute-start.13 = (bf16[27,16,192]{2,1,0:T(8,128)(2,1)}, bf16[27,16,192]{2,1,0:T(8,128)(2,1)S(1)}, u32[]{:S(2)}, u32[]{:S(2)}) collective-permute-start(bf16[27,16,192]{2,1,0:T(8,128)(2,1)} %get-tuple-element.49), channel_id=1, source_target_pairs={{0,2},{2,0},{4,6},{6,4},{1,3},{3,1},{5,7},{7,5},{8,10},{10,8},{12,... | collective-permute-start | bytes 497672 | tf_op jit(solution)/shard_map/ppermute | solution.py:315
  89.4 10.7 %collective-permute-start.14 = (bf16[27,16,192]{2,1,0:T(8,128)(2,1)}, bf16[27,16,192]{2,1,0:T(8,128)(2,1)S(1)}, u32[]{:S(2)}, u32[]{:S(2)}) collective-permute-start(bf16[27,16,192]{2,1,0:T(8,128)(2,1)} %get-tuple-element.50), channel_id=1, source_target_pairs={{0,4},{2,6},{4,0},{6,2},{1,5},{3,7},{5,1},{7,3},{8,12},{10,14},{12... | collective-permute-start | bytes 497672 | tf_op jit(solution)/shard_map/ppermute | solution.py:315
  90.6 10.6 %collective-permute-start.15 = (bf16[27,16,192]{2,1,0:T(8,128)(2,1)}, bf16[27,16,192]{2,1,0:T(8,128)(2,1)S(1)}, u32[]{:S(2)}, u32[]{:S(2)}) collective-permute-start(bf16[27,16,192]{2,1,0:T(8,128)(2,1)} %get-tuple-element.51), channel_id=1, source_target_pairs={{0,6},{2,4},{4,2},{6,0},{1,7},{3,5},{5,3},{7,1},{8,14},{10,12},{12... | collective-permute-start | bytes 497672 | tf_op jit(solution)/shard_map/ppermute | solution.py:315
  93.3 11.2 %collective-permute-start.16 = (bf16[27,16,192]{2,1,0:T(8,128)(2,1)S(1)}, bf16[27,16,192]{2,1,0:T(8,128)(2,1)S(1)}, u32[]{:S(2)}, u32[]{:S(2)}) collective-permute-start(bf16[27,16,192]{2,1,0:T(8,128)(2,1)S(1)} %shard_map.141.refs_0_.refs_1_), channel_id=1, source_target_pairs={{0,16},{8,24},{16,0},{24,8},{1,17},{9,25},{17,1},{25,9},{2,18},{10... | collective-permute-start | bytes 497672 | tf_op jit(solution)/shard_map/ppermute | solution.py:315
  96.0 23.4 %all-to-all-start.4 = ((bf16[8,2,2,2,16,192]{5,4,3,2,1,0:T(8,128)(2,1)}), bf16[8,2,2,2,16,192]{5,4,3,2,1,0:T(8,128)(2,1)}, u32[]{:S(2)}, u32[]{:S(2)}) async-start(bf16[8,2,2,2,16,192]{5,4,3,2,1,0:T(8,128)(2,1)} %bitcast.5), calls=%async_computation.4 | async-start | bytes 1048576 | tf_op jit(solution)/shard_map/all_to_all | solution.py:302
  101.2 8.4 %collective-permute-start.17 = (bf16[27,16,192]{2,1,0:T(8,128)(2,1)S(1)}, bf16[27,16,192]{2,1,0:T(8,128)(2,1)S(1)}, u32[]{:S(2)}, u32[]{:S(2)}) collective-permute-start(bf16[27,16,192]{2,1,0:T(8,128)(2,1)S(1)} %shard_map.143.refs_0_.refs_1_), channel_id=1, source_target_pairs={{0,8},{8,0},{16,24},{24,16},{1,9},{9,1},{17,25},{25,17},{2,10},{10... | collective-permute-start | bytes 497672 | tf_op jit(solution)/shard_map/ppermute | solution.py:315
  104.6 10.4 %collective-permute-start.24 = (bf16[27,16,192]{2,1,0:T(8,128)(2,1)S(1)}, bf16[27,16,192]{2,1,0:T(8,128)(2,1)S(1)}, u32[]{:S(2)}, u32[]{:S(2)}) collective-permute-start(bf16[27,16,192]{2,1,0:T(8,128)(2,1)S(1)} %shard_map.144.refs_0_.refs_1_), channel_id=1, source_target_pairs={{0,6},{2,4},{4,2},{6,0},{1,7},{3,5},{5,3},{7,1},{8,14},{10,12},{12... | collective-permute-start | bytes 497672 | tf_op jit(solution)/shard_map/ppermute | solution.py:315
  107.5 11.1 %collective-permute-start.23 = (bf16[27,16,192]{2,1,0:T(8,128)(2,1)S(1)}, bf16[27,16,192]{2,1,0:T(8,128)(2,1)S(1)}, u32[]{:S(2)}, u32[]{:S(2)}) collective-permute-start(bf16[27,16,192]{2,1,0:T(8,128)(2,1)S(1)} %shard_map.144.refs_0_.refs_1_), channel_id=1, source_target_pairs={{0,4},{2,6},{4,0},{6,2},{1,5},{3,7},{5,1},{7,3},{8,12},{10,14},{12... | collective-permute-start | bytes 497672 | tf_op jit(solution)/shard_map/ppermute | solution.py:315
  108.3 11.0 %collective-permute-start.22 = (bf16[27,16,192]{2,1,0:T(8,128)(2,1)S(1)}, bf16[27,16,192]{2,1,0:T(8,128)(2,1)S(1)}, u32[]{:S(2)}, u32[]{:S(2)}) collective-permute-start(bf16[27,16,192]{2,1,0:T(8,128)(2,1)S(1)} %shard_map.144.refs_0_.refs_1_), channel_id=1, source_target_pairs={{0,2},{2,0},{4,6},{6,4},{1,3},{3,1},{5,7},{7,5},{8,10},{10,8},{12,... | collective-permute-start | bytes 497672 | tf_op jit(solution)/shard_map/ppermute | solution.py:315
  109.7 11.2 %collective-permute-start.18 = (bf16[27,16,192]{2,1,0:T(8,128)(2,1)S(1)}, bf16[27,16,192]{2,1,0:T(8,128)(2,1)S(1)}, u32[]{:S(2)}, u32[]{:S(2)}) collective-permute-start(bf16[27,16,192]{2,1,0:T(8,128)(2,1)S(1)} %shard_map.145.refs_1_.refs_0_), channel_id=1, source_target_pairs={{0,16},{8,24},{16,0},{24,8},{1,17},{9,25},{17,1},{25,9},{2,18},{10... | collective-permute-start | bytes 497672 | tf_op jit(solution)/shard_map/ppermute | solution.py:315
  118.6 7.8 %collective-permute-start.26 = (bf16[2,27,16,192]{3,2,1,0:T(8,128)(2,1)S(1)}, bf16[2,27,16,192]{3,2,1,0:T(8,128)(2,1)S(1)}, u32[]{:S(2)}, u32[]{:S(2)}) collective-permute-start(bf16[2,27,16,192]{3,2,1,0:T(8,128)(2,1)S(1)} %shard_map.148), channel_id=1, source_target_pairs={{0,1},{1,0},{2,3},{3,2},{4,5},{5,4},{6,7},{7,6},{8,9},{9,8},{10,11... | collective-permute-start | bytes 995336 | tf_op jit(solution)/shard_map/ppermute | solution.py:315
  119.3 7.1 %collective-permute-start.25 = (bf16[2,27,16,192]{3,2,1,0:T(8,128)(2,1)S(1)}, bf16[2,27,16,192]{3,2,1,0:T(8,128)(2,1)S(1)}, u32[]{:S(2)}, u32[]{:S(2)}) collective-permute-start(bf16[2,27,16,192]{3,2,1,0:T(8,128)(2,1)S(1)} %shard_map.147), channel_id=1, source_target_pairs={{0,1},{1,0},{2,3},{3,2},{4,5},{5,4},{6,7},{7,6},{8,9},{9,8},{10,11... | collective-permute-start | bytes 995336 | tf_op jit(solution)/shard_map/ppermute | solution.py:315
  120.5 12.7 %copy-start = (bf16[2,8,2,2,16,192]{5,4,3,2,1,0:T(8,128)(2,1)}, bf16[2,8,2,2,16,192]{5,4,3,2,1,0:T(8,128)(2,1)S(1)}, u32[]{:S(2)}) copy-start(bf16[2,8,2,2,16,192]{5,4,3,2,1,0:T(8,128)(2,1)S(1)} %copy.15) | copy-start | bytes 1179652
  120.9 12.3 %collective-permute-start.19 = (bf16[27,16,192]{2,1,0:T(8,128)(2,1)S(1)}, bf16[27,16,192]{2,1,0:T(8,128)(2,1)S(1)}, u32[]{:S(2)}, u32[]{:S(2)}) collective-permute-start(bf16[27,16,192]{2,1,0:T(8,128)(2,1)S(1)} %shard_map.146.refs_1_.refs_0_), channel_id=1, source_target_pairs={{0,2},{2,0},{4,6},{6,4},{1,3},{3,1},{5,7},{7,5},{8,10},{10,8},{12,... | collective-permute-start | bytes 497672 | tf_op jit(solution)/shard_map/ppermute | solution.py:315
  122.1 11.2 %collective-permute-start.21 = (bf16[27,16,192]{2,1,0:T(8,128)(2,1)S(1)}, bf16[27,16,192]{2,1,0:T(8,128)(2,1)S(1)}, u32[]{:S(2)}, u32[]{:S(2)}) collective-permute-start(bf16[27,16,192]{2,1,0:T(8,128)(2,1)S(1)} %shard_map.146.refs_1_.refs_0_), channel_id=1, source_target_pairs={{0,6},{2,4},{4,2},{6,0},{1,7},{3,5},{5,3},{7,1},{8,14},{10,12},{12... | collective-permute-start | bytes 497672 | tf_op jit(solution)/shard_map/ppermute | solution.py:315
  126.4 9.4 %collective-permute-start.20 = (bf16[27,16,192]{2,1,0:T(8,128)(2,1)S(1)}, bf16[27,16,192]{2,1,0:T(8,128)(2,1)S(1)}, u32[]{:S(2)}, u32[]{:S(2)}) collective-permute-start(bf16[27,16,192]{2,1,0:T(8,128)(2,1)S(1)} %shard_map.146.refs_1_.refs_0_), channel_id=1, source_target_pairs={{0,4},{2,6},{4,0},{6,2},{1,5},{3,7},{5,1},{7,3},{8,12},{10,14},{12... | collective-permute-start | bytes 497672 | tf_op jit(solution)/shard_map/ppermute | solution.py:315
  133.2 4.0 %collective-permute-start.27 = (bf16[2,27,16,192]{3,2,1,0:T(8,128)(2,1)S(1)}, bf16[2,27,16,192]{3,2,1,0:T(8,128)(2,1)S(1)}, u32[]{:S(2)}, u32[]{:S(2)}) collective-permute-start(bf16[2,27,16,192]{3,2,1,0:T(8,128)(2,1)S(1)} %shard_map.150), channel_id=1, source_target_pairs={{0,1},{1,0},{2,3},{3,2},{4,5},{5,4},{6,7},{7,6},{8,9},{9,8},{10,11... | collective-permute-start | bytes 995336 | tf_op jit(solution)/shard_map/ppermute | solution.py:315
  133.3 2.4 %collective-permute-start.29 = (bf16[27,16,192]{2,1,0:T(8,128)(2,1)S(1)}, bf16[27,16,192]{2,1,0:T(8,128)(2,1)S(1)}, u32[]{:S(2)}, u32[]{:S(2)}) collective-permute-start(bf16[27,16,192]{2,1,0:T(8,128)(2,1)S(1)} %collective-permute-done.21.refs_3_), channel_id=1, source_target_pairs={{0,1},{1,0},{2,3},{3,2},{4,5},{5,4},{6,7},{7,6},{8,9},{9,8},{10,11... | collective-permute-start | bytes 497672 | tf_op jit(solution)/shard_map/ppermute | solution.py:315
  135.7 1.5 %collective-permute-start.28 = (bf16[27,16,192]{2,1,0:T(8,128)(2,1)S(1)}, bf16[27,16,192]{2,1,0:T(8,128)(2,1)S(1)}, u32[]{:S(2)}, u32[]{:S(2)}) collective-permute-start(bf16[27,16,192]{2,1,0:T(8,128)(2,1)S(1)} %collective-permute-done.20.refs_2_), channel_id=1, source_target_pairs={{0,1},{1,0},{2,3},{3,2},{4,5},{5,4},{6,7},{7,6},{8,9},{9,8},{10,11... | collective-permute-start | bytes 497672 | tf_op jit(solution)/shard_map/ppermute | solution.py:315

commit v7 on v6

--- a/solution.py
+++ b/solution.py
@@ -30,8 +30,14 @@
 
 
 def call(body, outs, scratch, flops, *args, after=(), far=0):
-    specs = [pl.BlockSpec(memory_space=pl.ANY)] * len(after)
-    arrays, size = list(after), 0
+    specs, arrays, size = [], [], 0
+    for array in after:
+        if isinstance(array, Far):
+            specs.append(pl.BlockSpec(memory_space=pltpu.HBM))
+            arrays.append(pltpu.with_memory_space_constraint(array.array, pltpu.HBM))
+        else:
+            specs.append(pl.BlockSpec(memory_space=pl.ANY))
+            arrays.append(array)
     buffers = []
     for arg in args:
         if isinstance(arg, Far):
@@ -191,7 +197,7 @@
     return parts[: len(parts) - emit], parts[-1]
 
 
-def tap_products(wide_ref, src_ref, active, step, out_ref):
+def tap_products(wide_ref, src_ref, active, step, out_ref, done=None):
     src = class_flat(arrived(src_ref))
     chan = src.shape[-1]
     if active:
@@ -203,6 +209,8 @@
         out_ref[k * chan : (k + 1) * chan] = jnp.dot(
             turned, window(padded, tap, step), preferred_element_type=F32
         )
+        if done is not None and k % 3 == 2:
+            done(k // 3)
 
 
 def tap_rows(chan):
@@ -210,15 +218,20 @@
 
 
 def weight_grad(wide, source, step, chan, after=()):
-    def body(wide_ref, src_ref, out_ref, total, sem):
-        tap_products(wide_ref, src_ref, True, step, total)
-        copy = pltpu.make_async_copy(total, out_ref, sem)
-        copy.start()
-        copy.wait()
-
     shape = (tap_rows(chan), chan)
+    third = shape[0] // 3
+
+    def body(wide_ref, src_ref, out_ref, total, sems):
+        copies = [
+            pltpu.make_async_copy(total.at[pl.ds(i * third, third)], out_ref.at[pl.ds(i * third, third)], sems.at[i])
+            for i in range(3)
+        ]
+        tap_products(wide_ref, src_ref, True, step, total, lambda i: copies[i].start())
+        for copy in copies:
+            copy.wait()
+
     out = [jax.ShapeDtypeStruct(shape, F32)]
-    scratch = [pltpu.VMEM(shape, F32), pltpu.SemaphoreType.DMA]
+    scratch = [pltpu.VMEM(shape, F32), pltpu.SemaphoreType.DMA((3,))]
     return call(body, out, scratch, conv_flops(chan), Far(wide, None), source, after=after, far=1)[0]
 
 
@@ -465,7 +478,7 @@
     low, high = ring(pre[0], pre[1])
     second_two = weight_grad(wide, act_two, 2, chan)
     field = [low, *pre, high]
-    mid, wide = conv_one(field, [final], second_block_conv_one, 2, thirds, after=[second_two])
+    mid, wide = conv_one(field, [final], second_block_conv_one, 2, thirds, after=[Far(second_two, None)])
     low, high = ring(mid[0], mid[2])
     keep, got = weight_grad_split([wide], entry_two, 2, chan, second_two)
     field = [low, *mid, high]

time: 140 us -> 138 us (0.986)
  local copies, waits for them, and re-layouts: 4.51 us -> 3.03 us
    unnamed x54 -> x52, local copies, waits for them, and re-layouts: 2.68 us -> 1.2 us
where the time goes in v7:
time: 138 us
  starting transfers between devices  50.4 us (37%)
  waiting for transfers between devices  38.9 us (28%)
  Pallas kernels  30.4 us (22%)
  blocking collectives  13.9 us (10%)
  local copies, waits for them, and re-layouts  3.03 us (2%)
    pallas_call x24, Pallas kernels, call(): pl.pallas_call(run, grid=(1,), out_shape=outs[:near] + [pltpu.HBM(o.shape...  30.4 us
    ppermute x22, waiting for transfers between devices, xor(): return lax.ppermute(value, axis, [(i, i ^ k) for i in range(count)])  21.2 us
    ppermute x22, starting transfers between devices, xor(): return lax.ppermute(value, axis, [(i, i ^ k) for i in range(count)])  19.1 us
    all_to_all x1, blocking collectives, swap_classes(): moved = lax.all_to_all(packed, PLANE, 0, 0)  13.9 us
    ppermute x4, starting transfers between devices, ring(): lax.ppermute(left_edge, 'z', down)  11.3 us
    all_to_all x2, starting transfers between devices, swap_classes(): moved = lax.all_to_all(packed, PLANE, 0, 0)  7.79 us
    ppermute x4, waiting for transfers between devices, ring(): lax.ppermute(left_edge, 'z', down)  7.15 us
    ppermute x4, waiting for transfers between devices, ring(): lax.ppermute(right_edge, 'z', up)  4.49 us
  transfers between devices with their start and end apart: 34, of which 17 were waited for; matrix products, arithmetic and copies ran while one was open for 1% of the time, Pallas kernels for 20%

profile of v7, /device:TPU:0, one launch (start us, length us, event | category | flops | bytes accessed | tf_op | source)
XLA Modules:
  0.0 137.8 jit_solution(16968416724726420150)
XLA Ops:
  0.7 1.1 copy-done.6
  1.8 13.9 %all_to_all.25 = bf16[8,1,2,2,2,16,192]{6,5,4,3,2,1,0:T(8,128)(2,1)S(1)} all-to-all(bf16[8,1,2,2,2,16,192]{6,5,4,3,2,1,0:T(8,128)(2,1)S(1)} %shard_map.128), channel_id=1, replica_groups=mesh['z'=4,'x'=2,'y'=2,'c'=2] {'x','y','c'}, dimensions={0} | all-to-all | bytes 786432 | tf_op jit(solution)/shard_map/all_to_all | solution.py:307
  15.7 0.8 shard_map.129.refs_0_
  16.5 3.5 %all-to-all-start.1 = ((bf16[8,1,2,2,2,16,192]{6,5,4,3,2,1,0:T(8,128)(2,1)}), bf16[8,1,2,2,2,16,192]{6,5,4,3,2,1,0:T(8,128)(2,1)S(1)}, u32[]{:S(2)}, u32[]{:S(2)}) async-start(bf16[8,1,2,2,2,16,192]{6,5,4,3,2,1,0:T(8,128)(2,1)} %shard_map.129.refs_0_), calls=%async_computation.1 | async-start | bytes 1048576 | tf_op jit(solution)/shard_map/all_to_all | solution.py:307
  20.0 0.8 fusion
  20.7 1.6 %collective-permute-start = (bf16[2,2,2,2,2,16,192]{6,5,4,3,2,1,0:T(8,128)(2,1)}, bf16[2,2,2,2,2,16,192]{6,5,4,3,2,1,0:T(8,128)(2,1)S(1)}, u32[]{:S(2)}, u32[]{:S(2)}) collective-permute-start(bf16[2,2,2,2,2,16,192]{6,5,4,3,2,1,0:T(8,128)(2,1)} %bitcast.1), channel_id=1, source_target_pairs={{0,8},{8,16},{16,24},{24,0},{1,9},{9,17},{17,25},{25,1},{2,10},{10... | collective-permute-start | bytes 589832 | tf_op jit(solution)/shard_map/ppermute | solution.py:323
  22.3 2.2 %collective-permute-start.1 = (bf16[2,2,2,2,2,16,192]{6,5,4,3,2,1,0:T(8,128)(2,1)S(1)}, bf16[2,2,2,2,2,16,192]{6,5,4,3,2,1,0:T(8,128)(2,1)S(1)}, u32[]{:S(2)}, u32[]{:S(2)}) collective-permute-start(bf16[2,2,2,2,2,16,192]{6,5,4,3,2,1,0:T(8,128)(2,1)S(1)} %bitcast.19), channel_id=1, source_target_pairs={{8,0},{16,8},{24,16},{0,24},{9,1},{17,9},{25,17},{1,25},{10,2},{18... | collective-permute-start | bytes 589832 | tf_op jit(solution)/shard_map/ppermute | solution.py:323
  24.6 1.2 shard_map.130.refs_0_
  25.8 2.9 %all-to-all-done.1 = bf16[8,1,2,2,2,16,192]{6,5,4,3,2,1,0:T(8,128)(2,1)S(1)} async-done(((bf16[8,1,2,2,2,16,192]{6,5,4,3,2,1,0:T(8,128)(2,1)}), bf16[8,1,2,2,2,16,192]{6,5,4,3,2,1,0:T(8,128)(2,1)S(1)}, u32[]{:S(2)}, u32[]{:S(2)}) %all-to-all-start.1) | async-done | bytes 393248 | tf_op jit(solution)/shard_map/all_to_all | solution.py:307
  28.8 4.3 %all-to-all-start.2 = ((bf16[8,3,2,2,2,16,192]{6,5,4,3,2,1,0:T(8,128)(2,1)}), bf16[8,3,2,2,2,16,192]{6,5,4,3,2,1,0:T(8,128)(2,1)}, u32[]{:S(2)}, u32[]{:S(2)}) async-start(bf16[8,3,2,2,2,16,192]{6,5,4,3,2,1,0:T(8,128)(2,1)} %shard_map.130.refs_0_), calls=%async_computation.2 | async-start | bytes 3145728 | tf_op jit(solution)/shard_map/all_to_all | solution.py:307
  33.1 3.2 %collective-permute-done.1.refs_3_ = bf16[2,2,2,2,2,16,192]{6,5,4,3,2,1,0:T(8,128)(2,1)S(1)} collective-permute-done((bf16[2,2,2,2,2,16,192]{6,5,4,3,2,1,0:T(8,128)(2,1)S(1)}, bf16[2,2,2,2,2,16,192]{6,5,4,3,2,1,0:T(8,128)(2,1)S(1)}, u32[]{:S(2)}, u32[]{:S(2)}) %collective-permute-start.1) | collective-permute-done | bytes 196640 | tf_op jit(solution)/shard_map/ppermute | solution.py:323
  36.3 1.8 %shard_map.131 = (bf16[2,8,2,16,192]{4,3,2,1,0:T(8,128)(2,1)S(1)}, bf16[2,8,2,16,192]{4,3,2,1,0:T(8,128)(2,1)S(1)}, bf16[8,12,2,16,192]{4,3,2,1,0:T(8,128)(2,1)}) custom-call(bf16[8,3,2,2,2,16,192]{6,5,4,3,2,1,0:T(8,128)(2,1)} %shard_map.130.refs_0_, bf16[2,2,2,2,2,16,192]{6,5,4,3,2,1,0:T(8,128)(2,1)S(1)} %collective-permute-done.refs_1_, ...), custom_call_target="tpu_custom_call" | custom-call | flops 13589544960 | bytes 3416064 | tf_op jit(solution)/shard_map/pallas_call | solution.py:74
  38.1 1.4 collective-permute-start.2
  39.4 2.5 %collective-permute-start.3 = (bf16[2,8,2,16,192]{4,3,2,1,0:T(8,128)(2,1)S(1)}, bf16[2,8,2,16,192]{4,3,2,1,0:T(8,128)(2,1)S(1)}, u32[]{:S(2)}, u32[]{:S(2)}) collective-permute-start(bf16[2,8,2,16,192]{4,3,2,1,0:T(8,128)(2,1)S(1)} %get-tuple-element.33.refs_2_), channel_id=1, source_target_pairs={{8,0},{16,8},{24,16},{0,24},{9,1},{17,9},{25,17},{1,25},{10,2},{18... | collective-permute-start | bytes 589832 | tf_op jit(solution)/shard_map/ppermute | solution.py:323
  42.0 3.4 %shard_map.132.refs_0_.refs_2_ = f32[1728,192]{1,0:T(8,128)} custom-call(bf16[8,12,2,16,192]{4,3,2,1,0:T(8,128)(2,1)} %get-tuple-element.31.refs_0_, bf16[2,2,2,1,2,2,2,16,192]{8,7,6,5,4,3,2,1,0:T(8,128)(2,1)S(1)} %bitcast.18), custom_call_target="tpu_custom_call" | custom-call | flops 13589544960 | bytes 2899968 | tf_op jit(solution)/shard_map/pallas_call | solution.py:74
  45.4 3.8 %collective-permute-done.2.refs_1_ = bf16[2,8,2,16,192]{4,3,2,1,0:T(8,128)(2,1)S(1)} collective-permute-done((bf16[2,8,2,16,192]{4,3,2,1,0:T(8,128)(2,1)S(1)}, bf16[2,8,2,16,192]{4,3,2,1,0:T(8,128)(2,1)S(1)}, u32[]{:S(2)}, u32[]{:S(2)}) %collective-permute-start.2) | collective-permute-done | bytes 196640 | tf_op jit(solution)/shard_map/ppermute | solution.py:323
  49.2 3.9 %collective-permute-done.3.refs_4_ = bf16[2,8,2,16,192]{4,3,2,1,0:T(8,128)(2,1)S(1)} collective-permute-done((bf16[2,8,2,16,192]{4,3,2,1,0:T(8,128)(2,1)S(1)}, bf16[2,8,2,16,192]{4,3,2,1,0:T(8,128)(2,1)S(1)}, u32[]{:S(2)}, u32[]{:S(2)}) %collective-permute-start.3) | collective-permute-done | bytes 196640 | tf_op jit(solution)/shard_map/ppermute | solution.py:323
  53.0 1.8 %shard_map.133 = (bf16[1,8,2,16,192]{4,3,2,1,0:T(8,128)(2,1)S(1)}, bf16[2,8,2,16,192]{4,3,2,1,0:T(8,128)(2,1)S(1)}, bf16[1,8,2,16,192]{4,3,2,1,0:T(8,128)(2,1)S(1)}, bf16[8,12,2,16,192]{4,3,2,1,0:T(8,128)(2,1)}) custom-call(f32[1728,192]{1,0:T(8,128)} %shard_map.132.refs_0_.refs_2_, bf16[2,8,2,16,192]{4,3,2,1,0:T(8,128)(2,1)S(1)} %collective-permute-done.2.refs_1_, ...), custom_call_target="tpu_custom_call" | custom-call | flops 13589544960 | bytes 3416064 | tf_op jit(solution)/shard_map/pallas_call | solution.py:74
  54.8 0.4 collective-permute-start.6
  55.2 3.5 %collective-permute-start.7 = (bf16[1,8,2,16,192]{4,3,2,1,0:T(8,128)(2,1)S(1)}, bf16[1,8,2,16,192]{4,3,2,1,0:T(8,128)(2,1)S(1)}, u32[]{:S(2)}, u32[]{:S(2)}) collective-permute-start(bf16[1,8,2,16,192]{4,3,2,1,0:T(8,128)(2,1)S(1)} %get-tuple-element.39.refs_2_.refs_6_), channel_id=1, source_target_pairs={{8,0},{16,8},{24,16},{0,24},{9,1},{17,9},{25,17},{1,25},{10,2},{18... | collective-permute-start | bytes 294920 | tf_op jit(solution)/shard_map/ppermute | solution.py:323
  58.7 3.1 %shard_map.134 = (f32[108,16,192]{2,1,0:T(8,128)S(1)}, bf16[2,27,16,192]{3,2,1,0:T(8,128)(2,1)S(1)}, bf16[2,27,16,192]{3,2,1,0:T(8,128)(2,1)S(1)}) custom-call(bf16[8,12,2,16,192]{4,3,2,1,0:T(8,128)(2,1)} %get-tuple-element.34.refs_0_, bf16[2,2,2,3,2,2,2,16,192]{8,7,6,5,4,3,2,1,0:T(8,128)(2,1)} %bitcast.4.refs_1_.refs_6_.refs_2_.refs_5_, ...), custom_call_target="tpu_custom_call" | custom-call | flops 13589544960 | bytes 5677056 | tf_op jit(solution)/shard_map/pallas_call | solution.py:74
  61.8 0.1 collective-permute-start.4
  61.9 0.5 collective-permute-start.5
  62.4 0.7 collective-permute-done.6.refs_1_
  63.2 2.3 %shard_map.137 = (bf16[1,8,2,16,192]{4,3,2,1,0:T(8,128)(2,1)S(1)}, bf16[2,8,2,16,192]{4,3,2,1,0:T(8,128)(2,1)S(1)}, bf16[1,8,2,16,192]{4,3,2,1,0:T(8,128)(2,1)S(1)}, bf16[6,10,2,16,192]{4,3,2,1,0:T(8,128)(2,1)}) custom-call(f32[108,16,192]{2,1,0:T(8,128)S(1)} %get-tuple-element.35.refs_0_, bf16[1,8,2,16,192]{4,3,2,1,0:T(8,128)(2,1)S(1)} %collective-permute-done.6.refs_1_, ...), custom_call_target="tpu_custom_call" | custom-call | flops 13589544960 | bytes 3563520 | tf_op jit(solution)/shard_map/pallas_call | solution.py:74
  65.5 0.8 collective-permute-start.8
  66.3 3.1 %collective-permute-start.9 = (bf16[1,8,2,16,192]{4,3,2,1,0:T(8,128)(2,1)S(1)}, bf16[1,8,2,16,192]{4,3,2,1,0:T(8,128)(2,1)S(1)}, u32[]{:S(2)}, u32[]{:S(2)}) collective-permute-start(bf16[1,8,2,16,192]{4,3,2,1,0:T(8,128)(2,1)S(1)} %get-tuple-element.42.refs_1_.refs_2_), channel_id=1, source_target_pairs={{8,0},{16,8},{24,16},{0,24},{9,1},{17,9},{25,17},{1,25},{10,2},{18... | collective-permute-start | bytes 294920 | tf_op jit(solution)/shard_map/ppermute | solution.py:323
  69.4 1.1 shard_map.135.refs_0_
  70.5 3.9 %all-to-all-start.3 = ((bf16[4,27,16,192]{3,2,1,0:T(8,128)(2,1)}), bf16[4,27,16,192]{3,2,1,0:T(8,128)(2,1)S(1)}, u32[]{:S(2)}, u32[]{:S(2)}) async-start(bf16[4,27,16,192]{3,2,1,0:T(8,128)(2,1)} %shard_map.135.refs_0_), calls=%async_computation.3 | async-start | bytes 1769472 | tf_op jit(solution)/shard_map/all_to_all | solution.py:365
  74.4 3.5 %shard_map.138.refs_6_ = f32[1728,192]{1,0:T(8,128)} custom-call(bf16[4,27,16,192]{3,2,1,0:T(8,128)(2,1)} %shard_map.135.refs_0_, bf16[6,10,2,16,192]{4,3,2,1,0:T(8,128)(2,1)} %get-tuple-element.44.refs_1_, bf16[2,2,2,3,2,2,2,16,192]{8,7,6,5,4,3,2,1,0:T(8,128)(2,1)} %bitcast.4.refs_1_.refs_6_.refs_2_.refs_5_), custom_call_target="tpu_custom_call" | custom-call | flops 13589544960 | bytes 3244032 | tf_op jit(solution)/shard_map/pallas_call | solution.py:74
  77.9 3.6 %shard_map.139 = (f32[108,16,192]{2,1,0:T(8,128)S(1)}, bf16[2,27,16,192]{3,2,1,0:T(8,128)(2,1)}, bf16[2,27,16,192]{3,2,1,0:T(8,128)(2,1)}) custom-call(bf16[1,8,2,16,192]{4,3,2,1,0:T(8,128)(2,1)S(1)} %collective-permute-done.8.refs_0_.refs_1_, bf16[1,8,2,16,192]{4,3,2,1,0:T(8,128)(2,1)S(1)} %get-tuple-element.42.refs_1_.refs_2_, ...), custom_call_target="tpu_custom_call" | custom-call | flops 13589544960 | bytes 5087232 | tf_op jit(solution)/shard_map/pallas_call | solution.py:74
  81.6 0.5 collective-permute-start.11
  82.1 3.1 %all-to-all-done.3.refs_0_ = bf16[4,27,16,192]{3,2,1,0:T(8,128)(2,1)S(1)} async-done(((bf16[4,27,16,192]{3,2,1,0:T(8,128)(2,1)}), bf16[4,27,16,192]{3,2,1,0:T(8,128)(2,1)S(1)}, u32[]{:S(2)}, u32[]{:S(2)}) %all-to-all-start.3) | async-done | bytes 663584 | tf_op jit(solution)/shard_map/all_to_all | solution.py:365
  85.3 0.1 shard_map.136.refs_0_.refs_1_
  85.6 0.9 shard_map.140
  86.5 1.5 %collective-permute-start.13 = (bf16[27,16,192]{2,1,0:T(8,128)(2,1)}, bf16[27,16,192]{2,1,0:T(8,128)(2,1)S(1)}, u32[]{:S(2)}, u32[]{:S(2)}) collective-permute-start(bf16[27,16,192]{2,1,0:T(8,128)(2,1)} %get-tuple-element.49), channel_id=1, source_target_pairs={{0,2},{2,0},{4,6},{6,4},{1,3},{3,1},{5,7},{7,5},{8,10},{10,8},{12,... | collective-permute-start | bytes 497672 | tf_op jit(solution)/shard_map/ppermute | solution.py:328
  88.0 0.8 collective-permute-start.14
  88.7 1.3 collective-permute-start.15
  90.0 1.8 %collective-permute-done.12.refs_2_ = bf16[27,16,192]{2,1,0:T(8,128)(2,1)S(1)} collective-permute-done((bf16[27,16,192]{2,1,0:T(8,128)(2,1)S(1)}, bf16[27,16,192]{2,1,0:T(8,128)(2,1)S(1)}, u32[]{:S(2)}, u32[]{:S(2)}) %collective-permute-start.12) | collective-permute-done | bytes 165920 | tf_op jit(solution)/shard_map/ppermute | solution.py:328
  91.8 0.4 collective-permute-start.16
  92.2 2.2 %shard_map.142.refs_1_ = bf16[2,2,2,2,2,2,16,192]{7,6,5,4,3,2,1,0:T(8,128)(2,1)} custom-call(bf16[27,16,192]{2,1,0:T(8,128)(2,1)S(1)} %shard_map.141.refs_0_.refs_1_, bf16[1,8,2,16,192]{4,3,2,1,0:T(8,128)(2,1)S(1)} %copy-done.20, bf16[1,8,2,16,192]{4,3,2,1,0:T(8,128)(2,1)S(1)} %copy-done.16, bf16[2,8,2,16,192]{4,3,2,1,0:T(8,128)(2,1)S(1)} %copy-done.10, ...), custom_call_target="tpu_custom_call" | custom-call | tf_op jit(solution)/shard_map/pallas_call | solution.py:74
  94.5 4.2 %all-to-all-start.4 = ((bf16[8,2,2,2,16,192]{5,4,3,2,1,0:T(8,128)(2,1)}), bf16[8,2,2,2,16,192]{5,4,3,2,1,0:T(8,128)(2,1)}, u32[]{:S(2)}, u32[]{:S(2)}) async-start(bf16[8,2,2,2,16,192]{5,4,3,2,1,0:T(8,128)(2,1)} %bitcast.5), calls=%async_computation.4 | async-start | bytes 1048576 | tf_op jit(solution)/shard_map/all_to_all | solution.py:315
  98.7 1.0 collective-permute-done.15.refs_5_
  99.6 0.1 shard_map.143.refs_0_.refs_1_
  99.7 1.8 %collective-permute-start.17 = (bf16[27,16,192]{2,1,0:T(8,128)(2,1)S(1)}, bf16[27,16,192]{2,1,0:T(8,128)(2,1)S(1)}, u32[]{:S(2)}, u32[]{:S(2)}) collective-permute-start(bf16[27,16,192]{2,1,0:T(8,128)(2,1)S(1)} %shard_map.143.refs_0_.refs_1_), channel_id=1, source_target_pairs={{0,8},{8,0},{16,24},{24,16},{1,9},{9,1},{17,25},{25,17},{2,10},{10... | collective-permute-start | bytes 497672 | tf_op jit(solution)/shard_map/ppermute | solution.py:328
  101.5 1.5 %collective-permute-done.16.refs_2_ = bf16[27,16,192]{2,1,0:T(8,128)(2,1)S(1)} collective-permute-done((bf16[27,16,192]{2,1,0:T(8,128)(2,1)S(1)}, bf16[27,16,192]{2,1,0:T(8,128)(2,1)S(1)}, u32[]{:S(2)}, u32[]{:S(2)}) %collective-permute-start.16) | collective-permute-done | bytes 165920 | tf_op jit(solution)/shard_map/ppermute | solution.py:328
  103.1 2.9 %collective-permute-start.24 = (bf16[27,16,192]{2,1,0:T(8,128)(2,1)S(1)}, bf16[27,16,192]{2,1,0:T(8,128)(2,1)S(1)}, u32[]{:S(2)}, u32[]{:S(2)}) collective-permute-start(bf16[27,16,192]{2,1,0:T(8,128)(2,1)S(1)} %shard_map.144.refs_0_.refs_1_), channel_id=1, source_target_pairs={{0,6},{2,4},{4,2},{6,0},{1,7},{3,5},{5,3},{7,1},{8,14},{10,12},{12... | collective-permute-start | bytes 497672 | tf_op jit(solution)/shard_map/ppermute | solution.py:328
  106.0 0.7 collective-permute-start.23
  106.8 1.4 %collective-permute-start.22 = (bf16[27,16,192]{2,1,0:T(8,128)(2,1)S(1)}, bf16[27,16,192]{2,1,0:T(8,128)(2,1)S(1)}, u32[]{:S(2)}, u32[]{:S(2)}) collective-permute-start(bf16[27,16,192]{2,1,0:T(8,128)(2,1)S(1)} %shard_map.144.refs_0_.refs_1_), channel_id=1, source_target_pairs={{0,2},{2,0},{4,6},{6,4},{1,3},{3,1},{5,7},{7,5},{8,10},{10,8},{12,... | collective-permute-start | bytes 497672 | tf_op jit(solution)/shard_map/ppermute | solution.py:328
  108.2 1.1 collective-permute-start.18
  109.3 4.2 %collective-permute-done.24.refs_2_.refs_3_ = bf16[27,16,192]{2,1,0:T(8,128)(2,1)S(1)} collective-permute-done((bf16[27,16,192]{2,1,0:T(8,128)(2,1)S(1)}, bf16[27,16,192]{2,1,0:T(8,128)(2,1)S(1)}, u32[]{:S(2)}, u32[]{:S(2)}) %collective-permute-start.24) | collective-permute-done | bytes 165920 | tf_op jit(solution)/shard_map/ppermute | solution.py:328
  113.6 3.5 %collective-permute-done.23.refs_1_.refs_2_ = bf16[27,16,192]{2,1,0:T(8,128)(2,1)S(1)} collective-permute-done((bf16[27,16,192]{2,1,0:T(8,128)(2,1)S(1)}, bf16[27,16,192]{2,1,0:T(8,128)(2,1)S(1)}, u32[]{:S(2)}, u32[]{:S(2)}) %collective-permute-start.23) | collective-permute-done | bytes 165920 | tf_op jit(solution)/shard_map/ppermute | solution.py:328
  117.2 0.6 collective-permute-done.22.refs_2_.refs_1_
  117.8 0.1 collective-permute-start.25
  117.9 1.1 copy.15
  119.0 0.4 collective-permute-done.18.refs_2_
  119.4 1.2 collective-permute-start.19
  120.6 4.3 %collective-permute-start.21 = (bf16[27,16,192]{2,1,0:T(8,128)(2,1)S(1)}, bf16[27,16,192]{2,1,0:T(8,128)(2,1)S(1)}, u32[]{:S(2)}, u32[]{:S(2)}) collective-permute-start(bf16[27,16,192]{2,1,0:T(8,128)(2,1)S(1)} %shard_map.146.refs_1_.refs_0_), channel_id=1, source_target_pairs={{0,6},{2,4},{4,2},{6,0},{1,7},{3,5},{5,3},{7,1},{8,14},{10,12},{12... | collective-permute-start | bytes 497672 | tf_op jit(solution)/shard_map/ppermute | solution.py:328
  124.9 2.0 %shard_map.149 = (f32[1728,192]{1,0:T(8,128)}, f32[1728,192]{1,0:T(8,128)}, f32[8,128]{1,0:T(8,128)S(1)}) custom-call(bf16[27,16,192]{2,1,0:T(8,128)(2,1)S(1)} %shard_map.144.refs_0_.refs_1_, bf16[27,16,192]{2,1,0:T(8,128)(2,1)S(1)} %collective-permute-done.22.refs_2_.refs_1_, bf16[27,16,192]{2,1,0:T(8,128)(2,1)S(1)} %collective-permute-done.23.refs_1_.refs_2_, ...), custom_call_target="tpu_custom_call" | custom-call | tf_op jit(solution)/shard_map/pallas_call | solution.py:74
  126.9 4.8 %collective-permute-done.19.refs_2_.refs_1_ = bf16[27,16,192]{2,1,0:T(8,128)(2,1)S(1)} collective-permute-done((bf16[27,16,192]{2,1,0:T(8,128)(2,1)S(1)}, bf16[27,16,192]{2,1,0:T(8,128)(2,1)S(1)}, u32[]{:S(2)}, u32[]{:S(2)}) %collective-permute-start.19) | collective-permute-done | bytes 165920 | tf_op jit(solution)/shard_map/ppermute | solution.py:328
  131.8 0.5 collective-permute-start.29
  132.3 1.9 %collective-permute-done.20.refs_2_ = bf16[27,16,192]{2,1,0:T(8,128)(2,1)S(1)} collective-permute-done((bf16[27,16,192]{2,1,0:T(8,128)(2,1)S(1)}, bf16[27,16,192]{2,1,0:T(8,128)(2,1)S(1)}, u32[]{:S(2)}, u32[]{:S(2)}) %collective-permute-start.20) | collective-permute-done | bytes 165920 | tf_op jit(solution)/shard_map/ppermute | solution.py:328
  134.3 1.5 %collective-permute-done.28.refs_5_ = bf16[27,16,192]{2,1,0:T(8,128)(2,1)S(1)} collective-permute-done((bf16[27,16,192]{2,1,0:T(8,128)(2,1)S(1)}, bf16[27,16,192]{2,1,0:T(8,128)(2,1)S(1)}, u32[]{:S(2)}, u32[]{:S(2)}) %collective-permute-start.28) | collective-permute-done | bytes 165920 | tf_op jit(solution)/shard_map/ppermute | solution.py:328
  135.7 2.0 %shard_map.151 = (f32[1728,192]{1,0:T(8,128)}, f32[1728,192]{1,0:T(8,128)}, f32[8,128]{1,0:T(8,128)}) custom-call(bf16[27,16,192]{2,1,0:T(8,128)(2,1)S(1)} %shard_map.146.refs_1_.refs_0_, bf16[27,16,192]{2,1,0:T(8,128)(2,1)S(1)} %collective-permute-done.19.refs_2_.refs_1_, bf16[27,16,192]{2,1,0:T(8,128)(2,1)S(1)} %collective-permute-done.20.refs_2_, ...), custom_call_target="tpu_custom_call" | custom-call | tf_op jit(solution)/shard_map/pallas_call | solution.py:74
  (83 shorter events, 0.9 us)
Async XLA Ops:
  0.6 15.0 %copy-start.2 = (bf16[32,32,192]{2,1,0:T(8,128)(2,1)S(1)}, bf16[32,32,192]{2,1,0:T(8,128)(2,1)}, u32[]{:S(2)}) copy-start(bf16[32,32,192]{2,1,0:T(8,128)(2,1)} %refs_1_.2) | copy-start | bytes 1179652
  0.6 1.1 copy-start.6
  15.7 8.9 %copy-start.3 = (bf16[32,32,192]{2,1,0:T(8,128)(2,1)S(1)}, bf16[32,32,192]{2,1,0:T(8,128)(2,1)}, u32[]{:S(2)}) copy-start(bf16[32,32,192]{2,1,0:T(8,128)(2,1)} %refs_1_.3) | copy-start | bytes 1179652
  15.7 8.9 %copy-start.4 = (bf16[32,32,192]{2,1,0:T(8,128)(2,1)S(1)}, bf16[32,32,192]{2,1,0:T(8,128)(2,1)}, u32[]{:S(2)}) copy-start(bf16[32,32,192]{2,1,0:T(8,128)(2,1)} %refs_2_.1) | copy-start | bytes 1179652
  15.7 8.9 %copy-start.5 = (bf16[32,32,192]{2,1,0:T(8,128)(2,1)S(1)}, bf16[32,32,192]{2,1,0:T(8,128)(2,1)}, u32[]{:S(2)}) copy-start(bf16[32,32,192]{2,1,0:T(8,128)(2,1)} %refs_3_.1) | copy-start | bytes 1179652
  16.5 12.3 %all-to-all-start.1 = ((bf16[8,1,2,2,2,16,192]{6,5,4,3,2,1,0:T(8,128)(2,1)}), bf16[8,1,2,2,2,16,192]{6,5,4,3,2,1,0:T(8,128)(2,1)S(1)}, u32[]{:S(2)}, u32[]{:S(2)}) async-start(bf16[8,1,2,2,2,16,192]{6,5,4,3,2,1,0:T(8,128)(2,1)} %shard_map.129.refs_0_), calls=%async_computation.1 | async-start | bytes 1048576 | tf_op jit(solution)/shard_map/all_to_all | solution.py:307
  20.7 12.3 %collective-permute-start = (bf16[2,2,2,2,2,16,192]{6,5,4,3,2,1,0:T(8,128)(2,1)}, bf16[2,2,2,2,2,16,192]{6,5,4,3,2,1,0:T(8,128)(2,1)S(1)}, u32[]{:S(2)}, u32[]{:S(2)}) collective-permute-start(bf16[2,2,2,2,2,16,192]{6,5,4,3,2,1,0:T(8,128)(2,1)} %bitcast.1), channel_id=1, source_target_pairs={{0,8},{8,16},{16,24},{24,0},{1,9},{9,17},{17,25},{25,1},{2,10},{10... | collective-permute-start | bytes 589832 | tf_op jit(solution)/shard_map/ppermute | solution.py:323
  22.3 14.0 %collective-permute-start.1 = (bf16[2,2,2,2,2,16,192]{6,5,4,3,2,1,0:T(8,128)(2,1)S(1)}, bf16[2,2,2,2,2,16,192]{6,5,4,3,2,1,0:T(8,128)(2,1)S(1)}, u32[]{:S(2)}, u32[]{:S(2)}) collective-permute-start(bf16[2,2,2,2,2,16,192]{6,5,4,3,2,1,0:T(8,128)(2,1)S(1)} %bitcast.19), channel_id=1, source_target_pairs={{8,0},{16,8},{24,16},{0,24},{9,1},{17,9},{25,17},{1,25},{10,2},{18... | collective-permute-start | bytes 589832 | tf_op jit(solution)/shard_map/ppermute | solution.py:323
  25.8 10.5 %copy-start.23 = (bf16[9,192,192]{2,1,0:T(8,128)(2,1)S(1)}, bf16[9,192,192]{2,1,0:T(8,128)(2,1)}, u32[]{:S(2)}) copy-start(bf16[9,192,192]{2,1,0:T(8,128)(2,1)} %refs_5_.1) | copy-start | bytes 1990660
  28.8 30.0 %all-to-all-start.2 = ((bf16[8,3,2,2,2,16,192]{6,5,4,3,2,1,0:T(8,128)(2,1)}), bf16[8,3,2,2,2,16,192]{6,5,4,3,2,1,0:T(8,128)(2,1)}, u32[]{:S(2)}, u32[]{:S(2)}) async-start(bf16[8,3,2,2,2,16,192]{6,5,4,3,2,1,0:T(8,128)(2,1)} %shard_map.130.refs_0_), calls=%async_computation.2 | async-start | bytes 3145728 | tf_op jit(solution)/shard_map/all_to_all | solution.py:307
  38.1 11.1 %collective-permute-start.2 = (bf16[2,8,2,16,192]{4,3,2,1,0:T(8,128)(2,1)S(1)}, bf16[2,8,2,16,192]{4,3,2,1,0:T(8,128)(2,1)S(1)}, u32[]{:S(2)}, u32[]{:S(2)}) collective-permute-start(bf16[2,8,2,16,192]{4,3,2,1,0:T(8,128)(2,1)S(1)} %get-tuple-element.32.refs_3_), channel_id=1, source_target_pairs={{0,8},{8,16},{16,24},{24,0},{1,9},{9,17},{17,25},{25,1},{2,10},{10... | collective-permute-start | bytes 589832 | tf_op jit(solution)/shard_map/ppermute | solution.py:323
  39.4 13.6 %collective-permute-start.3 = (bf16[2,8,2,16,192]{4,3,2,1,0:T(8,128)(2,1)S(1)}, bf16[2,8,2,16,192]{4,3,2,1,0:T(8,128)(2,1)S(1)}, u32[]{:S(2)}, u32[]{:S(2)}) collective-permute-start(bf16[2,8,2,16,192]{4,3,2,1,0:T(8,128)(2,1)S(1)} %get-tuple-element.33.refs_2_), channel_id=1, source_target_pairs={{8,0},{16,8},{24,16},{0,24},{9,1},{17,9},{25,17},{1,25},{10,2},{18... | collective-permute-start | bytes 589832 | tf_op jit(solution)/shard_map/ppermute | solution.py:323
  42.0 11.1 %copy-start.24 = (bf16[9,192,192]{2,1,0:T(8,128)(2,1)S(1)}, bf16[9,192,192]{2,1,0:T(8,128)(2,1)}, u32[]{:S(2)}) copy-start(bf16[9,192,192]{2,1,0:T(8,128)(2,1)} %refs_6_.1) | copy-start | bytes 1990660
  54.8 8.4 %copy-start.7 = (bf16[2,8,2,16,192]{4,3,2,1,0:T(8,128)(2,1)}, bf16[2,8,2,16,192]{4,3,2,1,0:T(8,128)(2,1)S(1)}, u32[]{:S(2)}) copy-start(bf16[2,8,2,16,192]{4,3,2,1,0:T(8,128)(2,1)S(1)} %get-tuple-element.40.refs_3_.refs_7_) | copy-start | bytes 589828
  54.8 8.4 %copy-start.11 = (bf16[1,8,2,16,192]{4,3,2,1,0:T(8,128)(2,1)}, bf16[1,8,2,16,192]{4,3,2,1,0:T(8,128)(2,1)S(1)}, u32[]{:S(2)}) copy-start(bf16[1,8,2,16,192]{4,3,2,1,0:T(8,128)(2,1)S(1)} %get-tuple-element.39.refs_2_.refs_6_) | copy-start | bytes 294916
  54.8 8.4 %copy-start.13 = (bf16[1,8,2,16,192]{4,3,2,1,0:T(8,128)(2,1)}, bf16[1,8,2,16,192]{4,3,2,1,0:T(8,128)(2,1)S(1)}, u32[]{:S(2)}) copy-start(bf16[1,8,2,16,192]{4,3,2,1,0:T(8,128)(2,1)S(1)} %get-tuple-element.38.refs_4_.refs_8_) | copy-start | bytes 294916
  54.8 8.3 %collective-permute-start.6 = (bf16[1,8,2,16,192]{4,3,2,1,0:T(8,128)(2,1)S(1)}, bf16[1,8,2,16,192]{4,3,2,1,0:T(8,128)(2,1)S(1)}, u32[]{:S(2)}, u32[]{:S(2)}) collective-permute-start(bf16[1,8,2,16,192]{4,3,2,1,0:T(8,128)(2,1)S(1)} %get-tuple-element.38.refs_4_.refs_8_), channel_id=1, source_target_pairs={{0,8},{8,16},{16,24},{24,0},{1,9},{9,17},{17,25},{25,1},{2,10},{10... | collective-permute-start | bytes 294920 | tf_op jit(solution)/shard_map/ppermute | solution.py:323
  55.2 7.9 %collective-permute-start.7 = (bf16[1,8,2,16,192]{4,3,2,1,0:T(8,128)(2,1)S(1)}, bf16[1,8,2,16,192]{4,3,2,1,0:T(8,128)(2,1)S(1)}, u32[]{:S(2)}, u32[]{:S(2)}) collective-permute-start(bf16[1,8,2,16,192]{4,3,2,1,0:T(8,128)(2,1)S(1)} %get-tuple-element.39.refs_2_.refs_6_), channel_id=1, source_target_pairs={{8,0},{16,8},{24,16},{0,24},{9,1},{17,9},{25,17},{1,25},{10,2},{18... | collective-permute-start | bytes 294920 | tf_op jit(solution)/shard_map/ppermute | solution.py:323
  58.7 4.5 %copy-start.25 = (bf16[9,192,192]{2,1,0:T(8,128)(2,1)S(1)}, bf16[9,192,192]{2,1,0:T(8,128)(2,1)}, u32[]{:S(2)}) copy-start(bf16[9,192,192]{2,1,0:T(8,128)(2,1)} %refs_7_.1) | copy-start | bytes 1990660
  61.8 7.6 %collective-permute-start.4 = (bf16[2,27,16,192]{3,2,1,0:T(8,128)(2,1)S(1)}, bf16[2,27,16,192]{3,2,1,0:T(8,128)(2,1)S(1)}, u32[]{:S(2)}, u32[]{:S(2)}) collective-permute-start(bf16[2,27,16,192]{3,2,1,0:T(8,128)(2,1)S(1)} %get-tuple-element.36), channel_id=1, source_target_pairs={{0,1},{1,0},{2,3},{3,2},{4,5},{5,4},{6,7},{7,6},{8,9},{9,8},{10,11... | collective-permute-start | bytes 995336 | tf_op jit(solution)/shard_map/ppermute | solution.py:328
  61.9 7.5 %collective-permute-start.5 = (bf16[2,27,16,192]{3,2,1,0:T(8,128)(2,1)S(1)}, bf16[2,27,16,192]{3,2,1,0:T(8,128)(2,1)S(1)}, u32[]{:S(2)}, u32[]{:S(2)}) collective-permute-start(bf16[2,27,16,192]{3,2,1,0:T(8,128)(2,1)S(1)} %get-tuple-element.37), channel_id=1, source_target_pairs={{0,1},{1,0},{2,3},{3,2},{4,5},{5,4},{6,7},{7,6},{8,9},{9,8},{10,11... | collective-permute-start | bytes 995336 | tf_op jit(solution)/shard_map/ppermute | solution.py:328
  65.5 12.4 %copy-start.9 = (bf16[2,8,2,16,192]{4,3,2,1,0:T(8,128)(2,1)}, bf16[2,8,2,16,192]{4,3,2,1,0:T(8,128)(2,1)S(1)}, u32[]{:S(2)}) copy-start(bf16[2,8,2,16,192]{4,3,2,1,0:T(8,128)(2,1)S(1)} %get-tuple-element.43.refs_2_.refs_3_) | copy-start | bytes 589828
  65.5 12.4 %copy-start.15 = (bf16[1,8,2,16,192]{4,3,2,1,0:T(8,128)(2,1)}, bf16[1,8,2,16,192]{4,3,2,1,0:T(8,128)(2,1)S(1)}, u32[]{:S(2)}) copy-start(bf16[1,8,2,16,192]{4,3,2,1,0:T(8,128)(2,1)S(1)} %get-tuple-element.42.refs_1_.refs_2_) | copy-start | bytes 294916
  65.5 12.4 %copy-start.17 = (bf16[1,8,2,16,192]{4,3,2,1,0:T(8,128)(2,1)}, bf16[1,8,2,16,192]{4,3,2,1,0:T(8,128)(2,1)S(1)}, u32[]{:S(2)}) copy-start(bf16[1,8,2,16,192]{4,3,2,1,0:T(8,128)(2,1)S(1)} %get-tuple-element.41.refs_3_.refs_4_) | copy-start | bytes 294916
  65.5 12.3 %collective-permute-start.8 = (bf16[1,8,2,16,192]{4,3,2,1,0:T(8,128)(2,1)S(1)}, bf16[1,8,2,16,192]{4,3,2,1,0:T(8,128)(2,1)S(1)}, u32[]{:S(2)}, u32[]{:S(2)}) collective-permute-start(bf16[1,8,2,16,192]{4,3,2,1,0:T(8,128)(2,1)S(1)} %get-tuple-element.41.refs_3_.refs_4_), channel_id=1, source_target_pairs={{0,8},{8,16},{16,24},{24,0},{1,9},{9,17},{17,25},{25,1},{2,10},{10... | collective-permute-start | bytes 294920 | tf_op jit(solution)/shard_map/ppermute | solution.py:323
  66.3 11.6 %collective-permute-start.9 = (bf16[1,8,2,16,192]{4,3,2,1,0:T(8,128)(2,1)S(1)}, bf16[1,8,2,16,192]{4,3,2,1,0:T(8,128)(2,1)S(1)}, u32[]{:S(2)}, u32[]{:S(2)}) collective-permute-start(bf16[1,8,2,16,192]{4,3,2,1,0:T(8,128)(2,1)S(1)} %get-tuple-element.42.refs_1_.refs_2_), channel_id=1, source_target_pairs={{8,0},{16,8},{24,16},{0,24},{9,1},{17,9},{25,17},{1,25},{10,2},{18... | collective-permute-start | bytes 294920 | tf_op jit(solution)/shard_map/ppermute | solution.py:323
  70.5 14.8 %all-to-all-start.3 = ((bf16[4,27,16,192]{3,2,1,0:T(8,128)(2,1)}), bf16[4,27,16,192]{3,2,1,0:T(8,128)(2,1)S(1)}, u32[]{:S(2)}, u32[]{:S(2)}) async-start(bf16[4,27,16,192]{3,2,1,0:T(8,128)(2,1)} %shard_map.135.refs_0_), calls=%async_computation.3 | async-start | bytes 1769472 | tf_op jit(solution)/shard_map/all_to_all | solution.py:365
  77.9 3.6 %copy-start.19 = (bf16[1,8,2,16,192]{4,3,2,1,0:T(8,128)(2,1)}, bf16[1,8,2,16,192]{4,3,2,1,0:T(8,128)(2,1)S(1)}, u32[]{:S(2)}) copy-start(bf16[1,8,2,16,192]{4,3,2,1,0:T(8,128)(2,1)S(1)} %collective-permute-done.8.refs_0_.refs_1_) | copy-start | bytes 294916
  77.9 3.6 %copy-start.21 = (bf16[1,8,2,16,192]{4,3,2,1,0:T(8,128)(2,1)}, bf16[1,8,2,16,192]{4,3,2,1,0:T(8,128)(2,1)S(1)}, u32[]{:S(2)}) copy-start(bf16[1,8,2,16,192]{4,3,2,1,0:T(8,128)(2,1)S(1)} %collective-permute-done.9.refs_4_.refs_5_) | copy-start | bytes 294916
  81.5 3.9 %collective-permute-start.10 = (bf16[2,27,16,192]{3,2,1,0:T(8,128)(2,1)}, bf16[2,27,16,192]{3,2,1,0:T(8,128)(2,1)S(1)}, u32[]{:S(2)}, u32[]{:S(2)}) collective-permute-start(bf16[2,27,16,192]{3,2,1,0:T(8,128)(2,1)} %get-tuple-element.46), channel_id=1, source_target_pairs={{0,1},{1,0},{2,3},{3,2},{4,5},{5,4},{6,7},{7,6},{8,9},{9,8},{10,11... | collective-permute-start | bytes 995336 | tf_op jit(solution)/shard_map/ppermute | solution.py:328
  81.6 3.8 %collective-permute-start.11 = (bf16[2,27,16,192]{3,2,1,0:T(8,128)(2,1)}, bf16[2,27,16,192]{3,2,1,0:T(8,128)(2,1)S(1)}, u32[]{:S(2)}, u32[]{:S(2)}) collective-permute-start(bf16[2,27,16,192]{3,2,1,0:T(8,128)(2,1)} %get-tuple-element.47), channel_id=1, source_target_pairs={{0,1},{1,0},{2,3},{3,2},{4,5},{5,4},{6,7},{7,6},{8,9},{9,8},{10,11... | collective-permute-start | bytes 995336 | tf_op jit(solution)/shard_map/ppermute | solution.py:328
  85.4 6.4 %collective-permute-start.12 = (bf16[27,16,192]{2,1,0:T(8,128)(2,1)S(1)}, bf16[27,16,192]{2,1,0:T(8,128)(2,1)S(1)}, u32[]{:S(2)}, u32[]{:S(2)}) collective-permute-start(bf16[27,16,192]{2,1,0:T(8,128)(2,1)S(1)} %shard_map.136.refs_0_.refs_1_), channel_id=1, source_target_pairs={{0,8},{8,0},{16,24},{24,16},{1,9},{9,1},{17,25},{25,17},{2,10},{10... | collective-permute-start | bytes 497672 | tf_op jit(solution)/shard_map/ppermute | solution.py:328
  85.5 6.7 %copy-start.1 = (bf16[9,192,192]{2,1,0:T(8,128)(2,1)S(1)}, bf16[9,192,192]{2,1,0:T(8,128)(2,1)}, u32[]{:S(2)}) copy-start(bf16[9,192,192]{2,1,0:T(8,128)(2,1)} %refs_9_.1) | copy-start | bytes 1990660
  85.5 6.7 %copy-start.8 = (bf16[2,8,2,16,192]{4,3,2,1,0:T(8,128)(2,1)S(1)}, bf16[2,8,2,16,192]{4,3,2,1,0:T(8,128)(2,1)}, u32[]{:S(2)}) copy-start(bf16[2,8,2,16,192]{4,3,2,1,0:T(8,128)(2,1)} %copy-done.7) | copy-start | bytes 589828
  85.5 6.7 %copy-start.10 = (bf16[2,8,2,16,192]{4,3,2,1,0:T(8,128)(2,1)S(1)}, bf16[2,8,2,16,192]{4,3,2,1,0:T(8,128)(2,1)}, u32[]{:S(2)}) copy-start(bf16[2,8,2,16,192]{4,3,2,1,0:T(8,128)(2,1)} %copy-done.9) | copy-start | bytes 589828
  85.5 6.7 %copy-start.12 = (bf16[1,8,2,16,192]{4,3,2,1,0:T(8,128)(2,1)S(1)}, bf16[1,8,2,16,192]{4,3,2,1,0:T(8,128)(2,1)}, u32[]{:S(2)}) copy-start(bf16[1,8,2,16,192]{4,3,2,1,0:T(8,128)(2,1)} %copy-done.11) | copy-start | bytes 294916
  85.5 6.7 %copy-start.14 = (bf16[1,8,2,16,192]{4,3,2,1,0:T(8,128)(2,1)S(1)}, bf16[1,8,2,16,192]{4,3,2,1,0:T(8,128)(2,1)}, u32[]{:S(2)}) copy-start(bf16[1,8,2,16,192]{4,3,2,1,0:T(8,128)(2,1)} %copy-done.13) | copy-start | bytes 294916
  85.5 6.7 %copy-start.16 = (bf16[1,8,2,16,192]{4,3,2,1,0:T(8,128)(2,1)S(1)}, bf16[1,8,2,16,192]{4,3,2,1,0:T(8,128)(2,1)}, u32[]{:S(2)}) copy-start(bf16[1,8,2,16,192]{4,3,2,1,0:T(8,128)(2,1)} %copy-done.15) | copy-start | bytes 294916
  85.5 6.7 %copy-start.18 = (bf16[1,8,2,16,192]{4,3,2,1,0:T(8,128)(2,1)S(1)}, bf16[1,8,2,16,192]{4,3,2,1,0:T(8,128)(2,1)}, u32[]{:S(2)}) copy-start(bf16[1,8,2,16,192]{4,3,2,1,0:T(8,128)(2,1)} %copy-done.17) | copy-start | bytes 294916
  85.5 6.7 %copy-start.20 = (bf16[1,8,2,16,192]{4,3,2,1,0:T(8,128)(2,1)S(1)}, bf16[1,8,2,16,192]{4,3,2,1,0:T(8,128)(2,1)}, u32[]{:S(2)}) copy-start(bf16[1,8,2,16,192]{4,3,2,1,0:T(8,128)(2,1)} %copy-done.19) | copy-start | bytes 294916
  85.6 6.7 %copy-start.22 = (bf16[1,8,2,16,192]{4,3,2,1,0:T(8,128)(2,1)S(1)}, bf16[1,8,2,16,192]{4,3,2,1,0:T(8,128)(2,1)}, u32[]{:S(2)}) copy-start(bf16[1,8,2,16,192]{4,3,2,1,0:T(8,128)(2,1)} %copy-done.21) | copy-start | bytes 294916
  86.5 12.2 %collective-permute-start.13 = (bf16[27,16,192]{2,1,0:T(8,128)(2,1)}, bf16[27,16,192]{2,1,0:T(8,128)(2,1)S(1)}, u32[]{:S(2)}, u32[]{:S(2)}) collective-permute-start(bf16[27,16,192]{2,1,0:T(8,128)(2,1)} %get-tuple-element.49), channel_id=1, source_target_pairs={{0,2},{2,0},{4,6},{6,4},{1,3},{3,1},{5,7},{7,5},{8,10},{10,8},{12,... | collective-permute-start | bytes 497672 | tf_op jit(solution)/shard_map/ppermute | solution.py:328
  88.0 10.7 %collective-permute-start.14 = (bf16[27,16,192]{2,1,0:T(8,128)(2,1)}, bf16[27,16,192]{2,1,0:T(8,128)(2,1)S(1)}, u32[]{:S(2)}, u32[]{:S(2)}) collective-permute-start(bf16[27,16,192]{2,1,0:T(8,128)(2,1)} %get-tuple-element.50), channel_id=1, source_target_pairs={{0,4},{2,6},{4,0},{6,2},{1,5},{3,7},{5,1},{7,3},{8,12},{10,14},{12... | collective-permute-start | bytes 497672 | tf_op jit(solution)/shard_map/ppermute | solution.py:328
  88.7 10.9 %collective-permute-start.15 = (bf16[27,16,192]{2,1,0:T(8,128)(2,1)}, bf16[27,16,192]{2,1,0:T(8,128)(2,1)S(1)}, u32[]{:S(2)}, u32[]{:S(2)}) collective-permute-start(bf16[27,16,192]{2,1,0:T(8,128)(2,1)} %get-tuple-element.51), channel_id=1, source_target_pairs={{0,6},{2,4},{4,2},{6,0},{1,7},{3,5},{5,3},{7,1},{8,14},{10,12},{12... | collective-permute-start | bytes 497672 | tf_op jit(solution)/shard_map/ppermute | solution.py:328
  91.8 11.2 %collective-permute-start.16 = (bf16[27,16,192]{2,1,0:T(8,128)(2,1)S(1)}, bf16[27,16,192]{2,1,0:T(8,128)(2,1)S(1)}, u32[]{:S(2)}, u32[]{:S(2)}) collective-permute-start(bf16[27,16,192]{2,1,0:T(8,128)(2,1)S(1)} %shard_map.141.refs_0_.refs_1_), channel_id=1, source_target_pairs={{0,16},{8,24},{16,0},{24,8},{1,17},{9,25},{17,1},{25,9},{2,18},{10... | collective-permute-start | bytes 497672 | tf_op jit(solution)/shard_map/ppermute | solution.py:328
  94.5 23.4 %all-to-all-start.4 = ((bf16[8,2,2,2,16,192]{5,4,3,2,1,0:T(8,128)(2,1)}), bf16[8,2,2,2,16,192]{5,4,3,2,1,0:T(8,128)(2,1)}, u32[]{:S(2)}, u32[]{:S(2)}) async-start(bf16[8,2,2,2,16,192]{5,4,3,2,1,0:T(8,128)(2,1)} %bitcast.5), calls=%async_computation.4 | async-start | bytes 1048576 | tf_op jit(solution)/shard_map/all_to_all | solution.py:315
  99.7 8.4 %collective-permute-start.17 = (bf16[27,16,192]{2,1,0:T(8,128)(2,1)S(1)}, bf16[27,16,192]{2,1,0:T(8,128)(2,1)S(1)}, u32[]{:S(2)}, u32[]{:S(2)}) collective-permute-start(bf16[27,16,192]{2,1,0:T(8,128)(2,1)S(1)} %shard_map.143.refs_0_.refs_1_), channel_id=1, source_target_pairs={{0,8},{8,0},{16,24},{24,16},{1,9},{9,1},{17,25},{25,17},{2,10},{10... | collective-permute-start | bytes 497672 | tf_op jit(solution)/shard_map/ppermute | solution.py:328
  103.1 10.4 %collective-permute-start.24 = (bf16[27,16,192]{2,1,0:T(8,128)(2,1)S(1)}, bf16[27,16,192]{2,1,0:T(8,128)(2,1)S(1)}, u32[]{:S(2)}, u32[]{:S(2)}) collective-permute-start(bf16[27,16,192]{2,1,0:T(8,128)(2,1)S(1)} %shard_map.144.refs_0_.refs_1_), channel_id=1, source_target_pairs={{0,6},{2,4},{4,2},{6,0},{1,7},{3,5},{5,3},{7,1},{8,14},{10,12},{12... | collective-permute-start | bytes 497672 | tf_op jit(solution)/shard_map/ppermute | solution.py:328
  106.0 11.1 %collective-permute-start.23 = (bf16[27,16,192]{2,1,0:T(8,128)(2,1)S(1)}, bf16[27,16,192]{2,1,0:T(8,128)(2,1)S(1)}, u32[]{:S(2)}, u32[]{:S(2)}) collective-permute-start(bf16[27,16,192]{2,1,0:T(8,128)(2,1)S(1)} %shard_map.144.refs_0_.refs_1_), channel_id=1, source_target_pairs={{0,4},{2,6},{4,0},{6,2},{1,5},{3,7},{5,1},{7,3},{8,12},{10,14},{12... | collective-permute-start | bytes 497672 | tf_op jit(solution)/shard_map/ppermute | solution.py:328
  106.8 11.0 %collective-permute-start.22 = (bf16[27,16,192]{2,1,0:T(8,128)(2,1)S(1)}, bf16[27,16,192]{2,1,0:T(8,128)(2,1)S(1)}, u32[]{:S(2)}, u32[]{:S(2)}) collective-permute-start(bf16[27,16,192]{2,1,0:T(8,128)(2,1)S(1)} %shard_map.144.refs_0_.refs_1_), channel_id=1, source_target_pairs={{0,2},{2,0},{4,6},{6,4},{1,3},{3,1},{5,7},{7,5},{8,10},{10,8},{12,... | collective-permute-start | bytes 497672 | tf_op jit(solution)/shard_map/ppermute | solution.py:328
  108.2 11.2 %collective-permute-start.18 = (bf16[27,16,192]{2,1,0:T(8,128)(2,1)S(1)}, bf16[27,16,192]{2,1,0:T(8,128)(2,1)S(1)}, u32[]{:S(2)}, u32[]{:S(2)}) collective-permute-start(bf16[27,16,192]{2,1,0:T(8,128)(2,1)S(1)} %shard_map.145.refs_1_.refs_0_), channel_id=1, source_target_pairs={{0,16},{8,24},{16,0},{24,8},{1,17},{9,25},{17,1},{25,9},{2,18},{10... | collective-permute-start | bytes 497672 | tf_op jit(solution)/shard_map/ppermute | solution.py:328
  117.1 7.8 %collective-permute-start.26 = (bf16[2,27,16,192]{3,2,1,0:T(8,128)(2,1)S(1)}, bf16[2,27,16,192]{3,2,1,0:T(8,128)(2,1)S(1)}, u32[]{:S(2)}, u32[]{:S(2)}) collective-permute-start(bf16[2,27,16,192]{3,2,1,0:T(8,128)(2,1)S(1)} %shard_map.148), channel_id=1, source_target_pairs={{0,1},{1,0},{2,3},{3,2},{4,5},{5,4},{6,7},{7,6},{8,9},{9,8},{10,11... | collective-permute-start | bytes 995336 | tf_op jit(solution)/shard_map/ppermute | solution.py:328
  117.8 7.1 %collective-permute-start.25 = (bf16[2,27,16,192]{3,2,1,0:T(8,128)(2,1)S(1)}, bf16[2,27,16,192]{3,2,1,0:T(8,128)(2,1)S(1)}, u32[]{:S(2)}, u32[]{:S(2)}) collective-permute-start(bf16[2,27,16,192]{3,2,1,0:T(8,128)(2,1)S(1)} %shard_map.147), channel_id=1, source_target_pairs={{0,1},{1,0},{2,3},{3,2},{4,5},{5,4},{6,7},{7,6},{8,9},{9,8},{10,11... | collective-permute-start | bytes 995336 | tf_op jit(solution)/shard_map/ppermute | solution.py:328
  119.0 12.7 %copy-start = (bf16[2,8,2,2,16,192]{5,4,3,2,1,0:T(8,128)(2,1)}, bf16[2,8,2,2,16,192]{5,4,3,2,1,0:T(8,128)(2,1)S(1)}, u32[]{:S(2)}) copy-start(bf16[2,8,2,2,16,192]{5,4,3,2,1,0:T(8,128)(2,1)S(1)} %copy.15) | copy-start | bytes 1179652
  119.4 12.3 %collective-permute-start.19 = (bf16[27,16,192]{2,1,0:T(8,128)(2,1)S(1)}, bf16[27,16,192]{2,1,0:T(8,128)(2,1)S(1)}, u32[]{:S(2)}, u32[]{:S(2)}) collective-permute-start(bf16[27,16,192]{2,1,0:T(8,128)(2,1)S(1)} %shard_map.146.refs_1_.refs_0_), channel_id=1, source_target_pairs={{0,2},{2,0},{4,6},{6,4},{1,3},{3,1},{5,7},{7,5},{8,10},{10,8},{12,... | collective-permute-start | bytes 497672 | tf_op jit(solution)/shard_map/ppermute | solution.py:328
  120.6 11.2 %collective-permute-start.21 = (bf16[27,16,192]{2,1,0:T(8,128)(2,1)S(1)}, bf16[27,16,192]{2,1,0:T(8,128)(2,1)S(1)}, u32[]{:S(2)}, u32[]{:S(2)}) collective-permute-start(bf16[27,16,192]{2,1,0:T(8,128)(2,1)S(1)} %shard_map.146.refs_1_.refs_0_), channel_id=1, source_target_pairs={{0,6},{2,4},{4,2},{6,0},{1,7},{3,5},{5,3},{7,1},{8,14},{10,12},{12... | collective-permute-start | bytes 497672 | tf_op jit(solution)/shard_map/ppermute | solution.py:328
  124.9 9.4 %collective-permute-start.20 = (bf16[27,16,192]{2,1,0:T(8,128)(2,1)S(1)}, bf16[27,16,192]{2,1,0:T(8,128)(2,1)S(1)}, u32[]{:S(2)}, u32[]{:S(2)}) collective-permute-start(bf16[27,16,192]{2,1,0:T(8,128)(2,1)S(1)} %shard_map.146.refs_1_.refs_0_), channel_id=1, source_target_pairs={{0,4},{2,6},{4,0},{6,2},{1,5},{3,7},{5,1},{7,3},{8,12},{10,14},{12... | collective-permute-start | bytes 497672 | tf_op jit(solution)/shard_map/ppermute | solution.py:328
  131.7 4.0 %collective-permute-start.27 = (bf16[2,27,16,192]{3,2,1,0:T(8,128)(2,1)S(1)}, bf16[2,27,16,192]{3,2,1,0:T(8,128)(2,1)S(1)}, u32[]{:S(2)}, u32[]{:S(2)}) collective-permute-start(bf16[2,27,16,192]{3,2,1,0:T(8,128)(2,1)S(1)} %shard_map.150), channel_id=1, source_target_pairs={{0,1},{1,0},{2,3},{3,2},{4,5},{5,4},{6,7},{7,6},{8,9},{9,8},{10,11... | collective-permute-start | bytes 995336 | tf_op jit(solution)/shard_map/ppermute | solution.py:328
  131.8 2.4 %collective-permute-start.29 = (bf16[27,16,192]{2,1,0:T(8,128)(2,1)S(1)}, bf16[27,16,192]{2,1,0:T(8,128)(2,1)S(1)}, u32[]{:S(2)}, u32[]{:S(2)}) collective-permute-start(bf16[27,16,192]{2,1,0:T(8,128)(2,1)S(1)} %collective-permute-done.21.refs_3_), channel_id=1, source_target_pairs={{0,1},{1,0},{2,3},{3,2},{4,5},{5,4},{6,7},{7,6},{8,9},{9,8},{10,11... | collective-permute-start | bytes 497672 | tf_op jit(solution)/shard_map/ppermute | solution.py:328
  134.3 1.5 %collective-permute-start.28 = (bf16[27,16,192]{2,1,0:T(8,128)(2,1)S(1)}, bf16[27,16,192]{2,1,0:T(8,128)(2,1)S(1)}, u32[]{:S(2)}, u32[]{:S(2)}) collective-permute-start(bf16[27,16,192]{2,1,0:T(8,128)(2,1)S(1)} %collective-permute-done.20.refs_2_), channel_id=1, source_target_pairs={{0,1},{1,0},{2,3},{3,2},{4,5},{5,4},{6,7},{7,6},{8,9},{9,8},{10,11... | collective-permute-start | bytes 497672 | tf_op jit(solution)/shard_map/ppermute | solution.py:328

commit v8 on v7

--- a/solution.py
+++ b/solution.py
@@ -14,8 +14,8 @@
 STRIDE = 16
 TAPS = [(r, c) for r in (-1, 0, 1) for c in (-1, 0, 1)]
 PLANE = ("x", "y", "c")
-VMEM_LIMIT = 16 * 1024 * 1024
-WEIGHT = 20
+VMEM_LIMIT = 32 * 1024 * 1024
+WEIGHT = 10
 
 
 Far = collections.namedtuple("Far", "array member")
@@ -303,6 +303,35 @@
     return call(body, [jax.ShapeDtypeStruct(shape, BF16)], [], 0, *values, after=after)[0]
 
 
+def pack_direct(value):
+    height, breadth, chan = value.shape
+    group = lax.axis_size(PLANE)
+    size = STRIDE // group
+
+    def body(value_ref, out_ref, sems):
+        copies = []
+        for target in range(group):
+            for ih in range(height // STRIDE):
+                source = value_ref.at[pl.ds(ih * STRIDE + target * size, size)]
+                at = len(copies)
+                copies.append(pltpu.make_async_copy(source, out_ref.at[target, 0, ih], sems.at[at]))
+                copies[at].start()
+        for copy in copies:
+            copy.wait()
+
+    count = group * (height // STRIDE)
+    shape = (group, 1, height // STRIDE, size, breadth, chan)
+    packed = pl.pallas_call(
+        body,
+        out_shape=jax.ShapeDtypeStruct(shape, BF16),
+        in_specs=[pl.BlockSpec(memory_space=pltpu.HBM)],
+        out_specs=pl.BlockSpec(memory_space=pltpu.VMEM),
+        scratch_shapes=[pltpu.SemaphoreType.DMA((count,))],
+        compiler_params=pltpu.CompilerParams(vmem_limit_bytes=VMEM_LIMIT),
+    )(pltpu.with_memory_space_constraint(value, pltpu.HBM))
+    return packed.reshape(shape[:4] + (breadth // STRIDE, STRIDE, chan))
+
+
 def swap_classes(packed):
     moved = lax.all_to_all(packed, PLANE, 0, 0)
     return moved.reshape((2, 2, 2) + moved.shape[1:])
@@ -460,7 +489,7 @@
     second_block_conv_two,
 ):
     height, breadth, chan = output_gradient_final.shape
-    final = swap_classes(pack_classes(output_gradient_final))
+    final = swap_classes(pack_direct(output_gradient_final))
     low, high = ring(final[0, :, :, 0], final[1, :, :, 0])
     packed = pack_classes(second_block_preactivation, after=[final])
     act_two = (swap_classes(packed), 0)

time: 138 us -> 138 us (level)
    pallas_call x24 -> x23, Pallas kernels: 30.4 us -> 30.3 us  [call(): pl.pallas_call(run, grid=(1,), out_shape=outs[:near] + [pltpu.HBM(o.shape...]
where the time goes in v8:
time: 138 us
  starting transfers between devices  50.4 us (37%)
  waiting for transfers between devices  39 us (28%)
  Pallas kernels  31.5 us (23%)
  blocking collectives  13.9 us (10%)
  local copies, waits for them, and re-layouts  1.94 us (1%)
    pallas_call x23, Pallas kernels, call(): pl.pallas_call(run, grid=(1,), out_shape=outs[:near] + [pltpu.HBM(o.shape...  30.3 us
    ppermute x22, waiting for transfers between devices, xor(): return lax.ppermute(value, axis, [(i, i ^ k) for i in range(count)])  21.2 us
    ppermute x22, starting transfers between devices, xor(): return lax.ppermute(value, axis, [(i, i ^ k) for i in range(count)])  19.1 us
    all_to_all x1, blocking collectives, swap_classes(): moved = lax.all_to_all(packed, PLANE, 0, 0)  13.9 us
    ppermute x4, starting transfers between devices, ring(): lax.ppermute(left_edge, 'z', down)  11.3 us
    all_to_all x2, starting transfers between devices, swap_classes(): moved = lax.all_to_all(packed, PLANE, 0, 0)  7.79 us
    ppermute x4, waiting for transfers between devices, ring(): lax.ppermute(left_edge, 'z', down)  7.16 us
    ppermute x4, waiting for transfers between devices, ring(): lax.ppermute(right_edge, 'z', up)  4.49 us
  transfers between devices with their start and end apart: 34, of which 17 were waited for; matrix products, arithmetic and copies ran while one was open for 1% of the time, Pallas kernels for 20%

profile of v8, /device:TPU:0, one launch (start us, length us, event | category | flops | bytes accessed | tf_op | source)
XLA Modules:
  0.0 137.8 jit_solution(14088903837727862828)
XLA Ops:
  0.6 1.2 shard_map.128
  1.8 13.9 %all_to_all.25 = bf16[8,1,2,2,2,16,192]{6,5,4,3,2,1,0:T(8,128)(2,1)S(1)} all-to-all(bf16[8,1,2,2,2,16,192]{6,5,4,3,2,1,0:T(8,128)(2,1)S(1)} %bitcast.20), channel_id=1, replica_groups=mesh['z'=4,'x'=2,'y'=2,'c'=2] {'x','y','c'}, dimensions={0} | all-to-all | bytes 786432 | tf_op jit(solution)/shard_map/all_to_all | solution.py:336
  15.7 0.8 shard_map.129.refs_0_
  16.6 3.5 %all-to-all-start.1 = ((bf16[8,1,2,2,2,16,192]{6,5,4,3,2,1,0:T(8,128)(2,1)}), bf16[8,1,2,2,2,16,192]{6,5,4,3,2,1,0:T(8,128)(2,1)S(1)}, u32[]{:S(2)}, u32[]{:S(2)}) async-start(bf16[8,1,2,2,2,16,192]{6,5,4,3,2,1,0:T(8,128)(2,1)} %shard_map.129.refs_0_), calls=%async_computation.1 | async-start | bytes 1048576 | tf_op jit(solution)/shard_map/all_to_all | solution.py:336
  20.1 0.8 fusion
  20.8 1.6 %collective-permute-start = (bf16[2,2,2,2,2,16,192]{6,5,4,3,2,1,0:T(8,128)(2,1)}, bf16[2,2,2,2,2,16,192]{6,5,4,3,2,1,0:T(8,128)(2,1)S(1)}, u32[]{:S(2)}, u32[]{:S(2)}) collective-permute-start(bf16[2,2,2,2,2,16,192]{6,5,4,3,2,1,0:T(8,128)(2,1)} %bitcast.3), channel_id=1, source_target_pairs={{0,8},{8,16},{16,24},{24,0},{1,9},{9,17},{17,25},{25,1},{2,10},{10... | collective-permute-start | bytes 589832 | tf_op jit(solution)/shard_map/ppermute | solution.py:352
  22.4 2.2 %collective-permute-start.1 = (bf16[2,2,2,2,2,16,192]{6,5,4,3,2,1,0:T(8,128)(2,1)S(1)}, bf16[2,2,2,2,2,16,192]{6,5,4,3,2,1,0:T(8,128)(2,1)S(1)}, u32[]{:S(2)}, u32[]{:S(2)}) collective-permute-start(bf16[2,2,2,2,2,16,192]{6,5,4,3,2,1,0:T(8,128)(2,1)S(1)} %bitcast.23), channel_id=1, source_target_pairs={{8,0},{16,8},{24,16},{0,24},{9,1},{17,9},{25,17},{1,25},{10,2},{18... | collective-permute-start | bytes 589832 | tf_op jit(solution)/shard_map/ppermute | solution.py:352
  24.6 1.2 shard_map.130.refs_0_
  25.9 2.9 %all-to-all-done.1 = bf16[8,1,2,2,2,16,192]{6,5,4,3,2,1,0:T(8,128)(2,1)S(1)} async-done(((bf16[8,1,2,2,2,16,192]{6,5,4,3,2,1,0:T(8,128)(2,1)}), bf16[8,1,2,2,2,16,192]{6,5,4,3,2,1,0:T(8,128)(2,1)S(1)}, u32[]{:S(2)}, u32[]{:S(2)}) %all-to-all-start.1) | async-done | bytes 393248 | tf_op jit(solution)/shard_map/all_to_all | solution.py:336
  28.8 4.3 %all-to-all-start.2 = ((bf16[8,3,2,2,2,16,192]{6,5,4,3,2,1,0:T(8,128)(2,1)}), bf16[8,3,2,2,2,16,192]{6,5,4,3,2,1,0:T(8,128)(2,1)}, u32[]{:S(2)}, u32[]{:S(2)}) async-start(bf16[8,3,2,2,2,16,192]{6,5,4,3,2,1,0:T(8,128)(2,1)} %shard_map.130.refs_0_), calls=%async_computation.2 | async-start | bytes 3145728 | tf_op jit(solution)/shard_map/all_to_all | solution.py:336
  33.1 3.2 %collective-permute-done.1.refs_3_ = bf16[2,2,2,2,2,16,192]{6,5,4,3,2,1,0:T(8,128)(2,1)S(1)} collective-permute-done((bf16[2,2,2,2,2,16,192]{6,5,4,3,2,1,0:T(8,128)(2,1)S(1)}, bf16[2,2,2,2,2,16,192]{6,5,4,3,2,1,0:T(8,128)(2,1)S(1)}, u32[]{:S(2)}, u32[]{:S(2)}) %collective-permute-start.1) | collective-permute-done | bytes 196640 | tf_op jit(solution)/shard_map/ppermute | solution.py:352
  36.4 1.8 %shard_map.131 = (bf16[2,8,2,16,192]{4,3,2,1,0:T(8,128)(2,1)S(1)}, bf16[2,8,2,16,192]{4,3,2,1,0:T(8,128)(2,1)S(1)}, bf16[8,12,2,16,192]{4,3,2,1,0:T(8,128)(2,1)}) custom-call(bf16[8,3,2,2,2,16,192]{6,5,4,3,2,1,0:T(8,128)(2,1)} %shard_map.130.refs_0_, bf16[2,2,2,2,2,16,192]{6,5,4,3,2,1,0:T(8,128)(2,1)S(1)} %collective-permute-done.refs_1_, ...), custom_call_target="tpu_custom_call" | custom-call | flops 6794772480 | bytes 3416064 | tf_op jit(solution)/shard_map/pallas_call | solution.py:74
  38.1 1.4 collective-permute-start.2
  39.5 2.5 %collective-permute-start.3 = (bf16[2,8,2,16,192]{4,3,2,1,0:T(8,128)(2,1)S(1)}, bf16[2,8,2,16,192]{4,3,2,1,0:T(8,128)(2,1)S(1)}, u32[]{:S(2)}, u32[]{:S(2)}) collective-permute-start(bf16[2,8,2,16,192]{4,3,2,1,0:T(8,128)(2,1)S(1)} %get-tuple-element.33.refs_2_), channel_id=1, source_target_pairs={{8,0},{16,8},{24,16},{0,24},{9,1},{17,9},{25,17},{1,25},{10,2},{18... | collective-permute-start | bytes 589832 | tf_op jit(solution)/shard_map/ppermute | solution.py:352
  42.0 3.4 %shard_map.132.refs_0_.refs_2_ = f32[1728,192]{1,0:T(8,128)} custom-call(bf16[8,12,2,16,192]{4,3,2,1,0:T(8,128)(2,1)} %get-tuple-element.31.refs_0_, bf16[2,2,2,1,2,2,2,16,192]{8,7,6,5,4,3,2,1,0:T(8,128)(2,1)S(1)} %bitcast.22), custom_call_target="tpu_custom_call" | custom-call | flops 6794772480 | bytes 2899968 | tf_op jit(solution)/shard_map/pallas_call | solution.py:74
  45.5 3.8 %collective-permute-done.2.refs_1_ = bf16[2,8,2,16,192]{4,3,2,1,0:T(8,128)(2,1)S(1)} collective-permute-done((bf16[2,8,2,16,192]{4,3,2,1,0:T(8,128)(2,1)S(1)}, bf16[2,8,2,16,192]{4,3,2,1,0:T(8,128)(2,1)S(1)}, u32[]{:S(2)}, u32[]{:S(2)}) %collective-permute-start.2) | collective-permute-done | bytes 196640 | tf_op jit(solution)/shard_map/ppermute | solution.py:352
  49.2 3.9 %collective-permute-done.3.refs_4_ = bf16[2,8,2,16,192]{4,3,2,1,0:T(8,128)(2,1)S(1)} collective-permute-done((bf16[2,8,2,16,192]{4,3,2,1,0:T(8,128)(2,1)S(1)}, bf16[2,8,2,16,192]{4,3,2,1,0:T(8,128)(2,1)S(1)}, u32[]{:S(2)}, u32[]{:S(2)}) %collective-permute-start.3) | collective-permute-done | bytes 196640 | tf_op jit(solution)/shard_map/ppermute | solution.py:352
  53.1 1.8 %shard_map.133 = (bf16[1,8,2,16,192]{4,3,2,1,0:T(8,128)(2,1)S(1)}, bf16[2,8,2,16,192]{4,3,2,1,0:T(8,128)(2,1)S(1)}, bf16[1,8,2,16,192]{4,3,2,1,0:T(8,128)(2,1)S(1)}, bf16[8,12,2,16,192]{4,3,2,1,0:T(8,128)(2,1)}) custom-call(f32[1728,192]{1,0:T(8,128)} %shard_map.132.refs_0_.refs_2_, bf16[2,8,2,16,192]{4,3,2,1,0:T(8,128)(2,1)S(1)} %collective-permute-done.2.refs_1_, ...), custom_call_target="tpu_custom_call" | custom-call | flops 6794772480 | bytes 3416064 | tf_op jit(solution)/shard_map/pallas_call | solution.py:74
  54.9 0.4 collective-permute-start.6
  55.3 3.5 %collective-permute-start.7 = (bf16[1,8,2,16,192]{4,3,2,1,0:T(8,128)(2,1)S(1)}, bf16[1,8,2,16,192]{4,3,2,1,0:T(8,128)(2,1)S(1)}, u32[]{:S(2)}, u32[]{:S(2)}) collective-permute-start(bf16[1,8,2,16,192]{4,3,2,1,0:T(8,128)(2,1)S(1)} %get-tuple-element.39.refs_2_.refs_6_), channel_id=1, source_target_pairs={{8,0},{16,8},{24,16},{0,24},{9,1},{17,9},{25,17},{1,25},{10,2},{18... | collective-permute-start | bytes 294920 | tf_op jit(solution)/shard_map/ppermute | solution.py:352
  58.8 3.1 %shard_map.134 = (f32[108,16,192]{2,1,0:T(8,128)S(1)}, bf16[2,27,16,192]{3,2,1,0:T(8,128)(2,1)S(1)}, bf16[2,27,16,192]{3,2,1,0:T(8,128)(2,1)S(1)}) custom-call(bf16[8,12,2,16,192]{4,3,2,1,0:T(8,128)(2,1)} %get-tuple-element.34.refs_0_, bf16[2,2,2,3,2,2,2,16,192]{8,7,6,5,4,3,2,1,0:T(8,128)(2,1)} %bitcast.6.refs_1_.refs_6_.refs_2_.refs_5_, ...), custom_call_target="tpu_custom_call" | custom-call | flops 6794772480 | bytes 5677056 | tf_op jit(solution)/shard_map/pallas_call | solution.py:74
  62.0 0.5 collective-permute-start.5
  62.5 0.7 collective-permute-done.6.refs_1_
  63.3 2.3 %shard_map.137 = (bf16[1,8,2,16,192]{4,3,2,1,0:T(8,128)(2,1)S(1)}, bf16[2,8,2,16,192]{4,3,2,1,0:T(8,128)(2,1)S(1)}, bf16[1,8,2,16,192]{4,3,2,1,0:T(8,128)(2,1)S(1)}, bf16[6,10,2,16,192]{4,3,2,1,0:T(8,128)(2,1)}) custom-call(f32[108,16,192]{2,1,0:T(8,128)S(1)} %get-tuple-element.35.refs_0_, bf16[1,8,2,16,192]{4,3,2,1,0:T(8,128)(2,1)S(1)} %collective-permute-done.6.refs_1_, ...), custom_call_target="tpu_custom_call" | custom-call | flops 6794772480 | bytes 3563520 | tf_op jit(solution)/shard_map/pallas_call | solution.py:74
  65.6 0.8 collective-permute-start.8
  66.4 3.1 %collective-permute-start.9 = (bf16[1,8,2,16,192]{4,3,2,1,0:T(8,128)(2,1)S(1)}, bf16[1,8,2,16,192]{4,3,2,1,0:T(8,128)(2,1)S(1)}, u32[]{:S(2)}, u32[]{:S(2)}) collective-permute-start(bf16[1,8,2,16,192]{4,3,2,1,0:T(8,128)(2,1)S(1)} %get-tuple-element.42.refs_1_.refs_2_), channel_id=1, source_target_pairs={{8,0},{16,8},{24,16},{0,24},{9,1},{17,9},{25,17},{1,25},{10,2},{18... | collective-permute-start | bytes 294920 | tf_op jit(solution)/shard_map/ppermute | solution.py:352
  69.5 1.1 shard_map.135.refs_0_
  70.6 3.9 %all-to-all-start.3 = ((bf16[4,27,16,192]{3,2,1,0:T(8,128)(2,1)}), bf16[4,27,16,192]{3,2,1,0:T(8,128)(2,1)S(1)}, u32[]{:S(2)}, u32[]{:S(2)}) async-start(bf16[4,27,16,192]{3,2,1,0:T(8,128)(2,1)} %shard_map.135.refs_0_), calls=%async_computation.3 | async-start | bytes 1769472 | tf_op jit(solution)/shard_map/all_to_all | solution.py:394
  74.4 3.5 %shard_map.138.refs_6_ = f32[1728,192]{1,0:T(8,128)} custom-call(bf16[4,27,16,192]{3,2,1,0:T(8,128)(2,1)} %shard_map.135.refs_0_, bf16[6,10,2,16,192]{4,3,2,1,0:T(8,128)(2,1)} %get-tuple-element.44.refs_1_, bf16[2,2,2,3,2,2,2,16,192]{8,7,6,5,4,3,2,1,0:T(8,128)(2,1)} %bitcast.6.refs_1_.refs_6_.refs_2_.refs_5_), custom_call_target="tpu_custom_call" | custom-call | flops 6794772480 | bytes 3244032 | tf_op jit(solution)/shard_map/pallas_call | solution.py:74
  78.0 3.6 %shard_map.139 = (f32[108,16,192]{2,1,0:T(8,128)S(1)}, bf16[2,27,16,192]{3,2,1,0:T(8,128)(2,1)}, bf16[2,27,16,192]{3,2,1,0:T(8,128)(2,1)}) custom-call(bf16[1,8,2,16,192]{4,3,2,1,0:T(8,128)(2,1)S(1)} %collective-permute-done.8.refs_0_.refs_1_, bf16[1,8,2,16,192]{4,3,2,1,0:T(8,128)(2,1)S(1)} %get-tuple-element.42.refs_1_.refs_2_, ...), custom_call_target="tpu_custom_call" | custom-call | flops 6794772480 | bytes 5087232 | tf_op jit(solution)/shard_map/pallas_call | solution.py:74
  81.7 0.5 collective-permute-start.11
  82.2 3.1 %all-to-all-done.3.refs_0_ = bf16[4,27,16,192]{3,2,1,0:T(8,128)(2,1)S(1)} async-done(((bf16[4,27,16,192]{3,2,1,0:T(8,128)(2,1)}), bf16[4,27,16,192]{3,2,1,0:T(8,128)(2,1)S(1)}, u32[]{:S(2)}, u32[]{:S(2)}) %all-to-all-start.3) | async-done | bytes 663584 | tf_op jit(solution)/shard_map/all_to_all | solution.py:394
  85.3 0.1 shard_map.136.refs_0_.refs_1_
  85.4 0.1 collective-permute-start.12
  85.6 0.9 shard_map.140
  86.6 1.5 %collective-permute-start.13 = (bf16[27,16,192]{2,1,0:T(8,128)(2,1)}, bf16[27,16,192]{2,1,0:T(8,128)(2,1)S(1)}, u32[]{:S(2)}, u32[]{:S(2)}) collective-permute-start(bf16[27,16,192]{2,1,0:T(8,128)(2,1)} %get-tuple-element.49), channel_id=1, source_target_pairs={{0,2},{2,0},{4,6},{6,4},{1,3},{3,1},{5,7},{7,5},{8,10},{10,8},{12,... | collective-permute-start | bytes 497672 | tf_op jit(solution)/shard_map/ppermute | solution.py:357
  88.0 0.8 collective-permute-start.14
  88.8 1.3 collective-permute-start.15
  90.0 1.8 %collective-permute-done.12.refs_2_ = bf16[27,16,192]{2,1,0:T(8,128)(2,1)S(1)} collective-permute-done((bf16[27,16,192]{2,1,0:T(8,128)(2,1)S(1)}, bf16[27,16,192]{2,1,0:T(8,128)(2,1)S(1)}, u32[]{:S(2)}, u32[]{:S(2)}) %collective-permute-start.12) | collective-permute-done | bytes 165920 | tf_op jit(solution)/shard_map/ppermute | solution.py:357
  91.9 0.4 collective-permute-start.16
  92.3 2.2 %shard_map.142.refs_1_ = bf16[2,2,2,2,2,2,16,192]{7,6,5,4,3,2,1,0:T(8,128)(2,1)} custom-call(bf16[27,16,192]{2,1,0:T(8,128)(2,1)S(1)} %shard_map.141.refs_0_.refs_1_, bf16[1,8,2,16,192]{4,3,2,1,0:T(8,128)(2,1)S(1)} %copy-done.19, bf16[1,8,2,16,192]{4,3,2,1,0:T(8,128)(2,1)S(1)} %copy-done.15, bf16[2,8,2,16,192]{4,3,2,1,0:T(8,128)(2,1)S(1)} %copy-done.9, ...), custom_call_target="tpu_custom_call" | custom-call | tf_op jit(solution)/shard_map/pallas_call | solution.py:74
  94.5 4.2 %all-to-all-start.4 = ((bf16[8,2,2,2,16,192]{5,4,3,2,1,0:T(8,128)(2,1)}), bf16[8,2,2,2,16,192]{5,4,3,2,1,0:T(8,128)(2,1)}, u32[]{:S(2)}, u32[]{:S(2)}) async-start(bf16[8,2,2,2,16,192]{5,4,3,2,1,0:T(8,128)(2,1)} %bitcast.7), calls=%async_computation.4 | async-start | bytes 1048576 | tf_op jit(solution)/shard_map/all_to_all | solution.py:344
  98.7 1.0 collective-permute-done.15.refs_5_
  99.7 0.1 shard_map.143.refs_0_.refs_1_
  99.8 1.8 %collective-permute-start.17 = (bf16[27,16,192]{2,1,0:T(8,128)(2,1)S(1)}, bf16[27,16,192]{2,1,0:T(8,128)(2,1)S(1)}, u32[]{:S(2)}, u32[]{:S(2)}) collective-permute-start(bf16[27,16,192]{2,1,0:T(8,128)(2,1)S(1)} %shard_map.143.refs_0_.refs_1_), channel_id=1, source_target_pairs={{0,8},{8,0},{16,24},{24,16},{1,9},{9,1},{17,25},{25,17},{2,10},{10... | collective-permute-start | bytes 497672 | tf_op jit(solution)/shard_map/ppermute | solution.py:357
  101.6 1.5 %collective-permute-done.16.refs_2_ = bf16[27,16,192]{2,1,0:T(8,128)(2,1)S(1)} collective-permute-done((bf16[27,16,192]{2,1,0:T(8,128)(2,1)S(1)}, bf16[27,16,192]{2,1,0:T(8,128)(2,1)S(1)}, u32[]{:S(2)}, u32[]{:S(2)}) %collective-permute-start.16) | collective-permute-done | bytes 165920 | tf_op jit(solution)/shard_map/ppermute | solution.py:357
  103.2 2.9 %collective-permute-start.24 = (bf16[27,16,192]{2,1,0:T(8,128)(2,1)S(1)}, bf16[27,16,192]{2,1,0:T(8,128)(2,1)S(1)}, u32[]{:S(2)}, u32[]{:S(2)}) collective-permute-start(bf16[27,16,192]{2,1,0:T(8,128)(2,1)S(1)} %shard_map.144.refs_0_.refs_1_), channel_id=1, source_target_pairs={{0,6},{2,4},{4,2},{6,0},{1,7},{3,5},{5,3},{7,1},{8,14},{10,12},{12... | collective-permute-start | bytes 497672 | tf_op jit(solution)/shard_map/ppermute | solution.py:357
  106.1 0.7 collective-permute-start.23
  106.8 1.4 %collective-permute-start.22 = (bf16[27,16,192]{2,1,0:T(8,128)(2,1)S(1)}, bf16[27,16,192]{2,1,0:T(8,128)(2,1)S(1)}, u32[]{:S(2)}, u32[]{:S(2)}) collective-permute-start(bf16[27,16,192]{2,1,0:T(8,128)(2,1)S(1)} %shard_map.144.refs_0_.refs_1_), channel_id=1, source_target_pairs={{0,2},{2,0},{4,6},{6,4},{1,3},{3,1},{5,7},{7,5},{8,10},{10,8},{12,... | collective-permute-start | bytes 497672 | tf_op jit(solution)/shard_map/ppermute | solution.py:357
  108.3 1.1 collective-permute-start.18
  109.4 4.2 %collective-permute-done.24.refs_2_.refs_3_ = bf16[27,16,192]{2,1,0:T(8,128)(2,1)S(1)} collective-permute-done((bf16[27,16,192]{2,1,0:T(8,128)(2,1)S(1)}, bf16[27,16,192]{2,1,0:T(8,128)(2,1)S(1)}, u32[]{:S(2)}, u32[]{:S(2)}) %collective-permute-start.24) | collective-permute-done | bytes 165920 | tf_op jit(solution)/shard_map/ppermute | solution.py:357
  113.6 3.5 %collective-permute-done.23.refs_1_.refs_2_ = bf16[27,16,192]{2,1,0:T(8,128)(2,1)S(1)} collective-permute-done((bf16[27,16,192]{2,1,0:T(8,128)(2,1)S(1)}, bf16[27,16,192]{2,1,0:T(8,128)(2,1)S(1)}, u32[]{:S(2)}, u32[]{:S(2)}) %collective-permute-start.23) | collective-permute-done | bytes 165920 | tf_op jit(solution)/shard_map/ppermute | solution.py:357
  117.3 0.6 collective-permute-done.22.refs_2_.refs_1_
  117.9 0.1 collective-permute-start.25
  118.0 1.1 copy.16
  119.0 0.4 collective-permute-done.18.refs_2_
  119.5 1.2 collective-permute-start.19
  120.7 4.3 %collective-permute-start.21 = (bf16[27,16,192]{2,1,0:T(8,128)(2,1)S(1)}, bf16[27,16,192]{2,1,0:T(8,128)(2,1)S(1)}, u32[]{:S(2)}, u32[]{:S(2)}) collective-permute-start(bf16[27,16,192]{2,1,0:T(8,128)(2,1)S(1)} %shard_map.146.refs_1_.refs_0_), channel_id=1, source_target_pairs={{0,6},{2,4},{4,2},{6,0},{1,7},{3,5},{5,3},{7,1},{8,14},{10,12},{12... | collective-permute-start | bytes 497672 | tf_op jit(solution)/shard_map/ppermute | solution.py:357
  125.0 2.0 %shard_map.149 = (f32[1728,192]{1,0:T(8,128)}, f32[1728,192]{1,0:T(8,128)}, f32[8,128]{1,0:T(8,128)S(1)}) custom-call(bf16[27,16,192]{2,1,0:T(8,128)(2,1)S(1)} %shard_map.144.refs_0_.refs_1_, bf16[27,16,192]{2,1,0:T(8,128)(2,1)S(1)} %collective-permute-done.22.refs_2_.refs_1_, bf16[27,16,192]{2,1,0:T(8,128)(2,1)S(1)} %collective-permute-done.23.refs_1_.refs_2_, ...), custom_call_target="tpu_custom_call" | custom-call | tf_op jit(solution)/shard_map/pallas_call | solution.py:74
  127.0 4.7 %collective-permute-done.19.refs_2_.refs_1_ = bf16[27,16,192]{2,1,0:T(8,128)(2,1)S(1)} collective-permute-done((bf16[27,16,192]{2,1,0:T(8,128)(2,1)S(1)}, bf16[27,16,192]{2,1,0:T(8,128)(2,1)S(1)}, u32[]{:S(2)}, u32[]{:S(2)}) %collective-permute-start.19) | collective-permute-done | bytes 165920 | tf_op jit(solution)/shard_map/ppermute | solution.py:357
  131.9 0.5 collective-permute-start.29
  132.4 2.0 %collective-permute-done.20.refs_2_ = bf16[27,16,192]{2,1,0:T(8,128)(2,1)S(1)} collective-permute-done((bf16[27,16,192]{2,1,0:T(8,128)(2,1)S(1)}, bf16[27,16,192]{2,1,0:T(8,128)(2,1)S(1)}, u32[]{:S(2)}, u32[]{:S(2)}) %collective-permute-start.20) | collective-permute-done | bytes 165920 | tf_op jit(solution)/shard_map/ppermute | solution.py:357
  134.3 1.5 %collective-permute-done.28.refs_5_ = bf16[27,16,192]{2,1,0:T(8,128)(2,1)S(1)} collective-permute-done((bf16[27,16,192]{2,1,0:T(8,128)(2,1)S(1)}, bf16[27,16,192]{2,1,0:T(8,128)(2,1)S(1)}, u32[]{:S(2)}, u32[]{:S(2)}) %collective-permute-start.28) | collective-permute-done | bytes 165920 | tf_op jit(solution)/shard_map/ppermute | solution.py:357
  135.8 2.0 %shard_map.151 = (f32[1728,192]{1,0:T(8,128)}, f32[1728,192]{1,0:T(8,128)}, f32[8,128]{1,0:T(8,128)}) custom-call(bf16[27,16,192]{2,1,0:T(8,128)(2,1)S(1)} %shard_map.146.refs_1_.refs_0_, bf16[27,16,192]{2,1,0:T(8,128)(2,1)S(1)} %collective-permute-done.19.refs_2_.refs_1_, bf16[27,16,192]{2,1,0:T(8,128)(2,1)S(1)} %collective-permute-done.20.refs_2_, ...), custom_call_target="tpu_custom_call" | custom-call | tf_op jit(solution)/shard_map/pallas_call | solution.py:74
  (81 shorter events, 0.8 us)
Async XLA Ops:
  0.6 15.1 %copy-start.2 = (bf16[32,32,192]{2,1,0:T(8,128)(2,1)S(1)}, bf16[32,32,192]{2,1,0:T(8,128)(2,1)}, u32[]{:S(2)}) copy-start(bf16[32,32,192]{2,1,0:T(8,128)(2,1)} %refs_1_.2) | copy-start | bytes 1179652
  15.7 8.9 %copy-start.3 = (bf16[32,32,192]{2,1,0:T(8,128)(2,1)S(1)}, bf16[32,32,192]{2,1,0:T(8,128)(2,1)}, u32[]{:S(2)}) copy-start(bf16[32,32,192]{2,1,0:T(8,128)(2,1)} %refs_1_.3) | copy-start | bytes 1179652
  15.7 8.9 %copy-start.4 = (bf16[32,32,192]{2,1,0:T(8,128)(2,1)S(1)}, bf16[32,32,192]{2,1,0:T(8,128)(2,1)}, u32[]{:S(2)}) copy-start(bf16[32,32,192]{2,1,0:T(8,128)(2,1)} %refs_2_.1) | copy-start | bytes 1179652
  15.7 8.9 %copy-start.5 = (bf16[32,32,192]{2,1,0:T(8,128)(2,1)S(1)}, bf16[32,32,192]{2,1,0:T(8,128)(2,1)}, u32[]{:S(2)}) copy-start(bf16[32,32,192]{2,1,0:T(8,128)(2,1)} %refs_3_.1) | copy-start | bytes 1179652
  16.6 12.3 %all-to-all-start.1 = ((bf16[8,1,2,2,2,16,192]{6,5,4,3,2,1,0:T(8,128)(2,1)}), bf16[8,1,2,2,2,16,192]{6,5,4,3,2,1,0:T(8,128)(2,1)S(1)}, u32[]{:S(2)}, u32[]{:S(2)}) async-start(bf16[8,1,2,2,2,16,192]{6,5,4,3,2,1,0:T(8,128)(2,1)} %shard_map.129.refs_0_), calls=%async_computation.1 | async-start | bytes 1048576 | tf_op jit(solution)/shard_map/all_to_all | solution.py:336
  20.8 12.3 %collective-permute-start = (bf16[2,2,2,2,2,16,192]{6,5,4,3,2,1,0:T(8,128)(2,1)}, bf16[2,2,2,2,2,16,192]{6,5,4,3,2,1,0:T(8,128)(2,1)S(1)}, u32[]{:S(2)}, u32[]{:S(2)}) collective-permute-start(bf16[2,2,2,2,2,16,192]{6,5,4,3,2,1,0:T(8,128)(2,1)} %bitcast.3), channel_id=1, source_target_pairs={{0,8},{8,16},{16,24},{24,0},{1,9},{9,17},{17,25},{25,1},{2,10},{10... | collective-permute-start | bytes 589832 | tf_op jit(solution)/shard_map/ppermute | solution.py:352
  22.4 14.0 %collective-permute-start.1 = (bf16[2,2,2,2,2,16,192]{6,5,4,3,2,1,0:T(8,128)(2,1)S(1)}, bf16[2,2,2,2,2,16,192]{6,5,4,3,2,1,0:T(8,128)(2,1)S(1)}, u32[]{:S(2)}, u32[]{:S(2)}) collective-permute-start(bf16[2,2,2,2,2,16,192]{6,5,4,3,2,1,0:T(8,128)(2,1)S(1)} %bitcast.23), channel_id=1, source_target_pairs={{8,0},{16,8},{24,16},{0,24},{9,1},{17,9},{25,17},{1,25},{10,2},{18... | collective-permute-start | bytes 589832 | tf_op jit(solution)/shard_map/ppermute | solution.py:352
  25.9 10.5 %copy-start.22 = (bf16[9,192,192]{2,1,0:T(8,128)(2,1)S(1)}, bf16[9,192,192]{2,1,0:T(8,128)(2,1)}, u32[]{:S(2)}) copy-start(bf16[9,192,192]{2,1,0:T(8,128)(2,1)} %refs_5_.1) | copy-start | bytes 1990660
  28.8 30.0 %all-to-all-start.2 = ((bf16[8,3,2,2,2,16,192]{6,5,4,3,2,1,0:T(8,128)(2,1)}), bf16[8,3,2,2,2,16,192]{6,5,4,3,2,1,0:T(8,128)(2,1)}, u32[]{:S(2)}, u32[]{:S(2)}) async-start(bf16[8,3,2,2,2,16,192]{6,5,4,3,2,1,0:T(8,128)(2,1)} %shard_map.130.refs_0_), calls=%async_computation.2 | async-start | bytes 3145728 | tf_op jit(solution)/shard_map/all_to_all | solution.py:336
  38.1 11.1 %collective-permute-start.2 = (bf16[2,8,2,16,192]{4,3,2,1,0:T(8,128)(2,1)S(1)}, bf16[2,8,2,16,192]{4,3,2,1,0:T(8,128)(2,1)S(1)}, u32[]{:S(2)}, u32[]{:S(2)}) collective-permute-start(bf16[2,8,2,16,192]{4,3,2,1,0:T(8,128)(2,1)S(1)} %get-tuple-element.32.refs_3_), channel_id=1, source_target_pairs={{0,8},{8,16},{16,24},{24,0},{1,9},{9,17},{17,25},{25,1},{2,10},{10... | collective-permute-start | bytes 589832 | tf_op jit(solution)/shard_map/ppermute | solution.py:352
  39.5 13.6 %collective-permute-start.3 = (bf16[2,8,2,16,192]{4,3,2,1,0:T(8,128)(2,1)S(1)}, bf16[2,8,2,16,192]{4,3,2,1,0:T(8,128)(2,1)S(1)}, u32[]{:S(2)}, u32[]{:S(2)}) collective-permute-start(bf16[2,8,2,16,192]{4,3,2,1,0:T(8,128)(2,1)S(1)} %get-tuple-element.33.refs_2_), channel_id=1, source_target_pairs={{8,0},{16,8},{24,16},{0,24},{9,1},{17,9},{25,17},{1,25},{10,2},{18... | collective-permute-start | bytes 589832 | tf_op jit(solution)/shard_map/ppermute | solution.py:352
  42.0 11.1 %copy-start.23 = (bf16[9,192,192]{2,1,0:T(8,128)(2,1)S(1)}, bf16[9,192,192]{2,1,0:T(8,128)(2,1)}, u32[]{:S(2)}) copy-start(bf16[9,192,192]{2,1,0:T(8,128)(2,1)} %refs_6_.1) | copy-start | bytes 1990660
  54.9 8.4 %copy-start.6 = (bf16[2,8,2,16,192]{4,3,2,1,0:T(8,128)(2,1)}, bf16[2,8,2,16,192]{4,3,2,1,0:T(8,128)(2,1)S(1)}, u32[]{:S(2)}) copy-start(bf16[2,8,2,16,192]{4,3,2,1,0:T(8,128)(2,1)S(1)} %get-tuple-element.40.refs_3_.refs_7_) | copy-start | bytes 589828
  54.9 8.4 %copy-start.10 = (bf16[1,8,2,16,192]{4,3,2,1,0:T(8,128)(2,1)}, bf16[1,8,2,16,192]{4,3,2,1,0:T(8,128)(2,1)S(1)}, u32[]{:S(2)}) copy-start(bf16[1,8,2,16,192]{4,3,2,1,0:T(8,128)(2,1)S(1)} %get-tuple-element.39.refs_2_.refs_6_) | copy-start | bytes 294916
  54.9 8.4 %copy-start.12 = (bf16[1,8,2,16,192]{4,3,2,1,0:T(8,128)(2,1)}, bf16[1,8,2,16,192]{4,3,2,1,0:T(8,128)(2,1)S(1)}, u32[]{:S(2)}) copy-start(bf16[1,8,2,16,192]{4,3,2,1,0:T(8,128)(2,1)S(1)} %get-tuple-element.38.refs_4_.refs_8_) | copy-start | bytes 294916
  54.9 8.3 %collective-permute-start.6 = (bf16[1,8,2,16,192]{4,3,2,1,0:T(8,128)(2,1)S(1)}, bf16[1,8,2,16,192]{4,3,2,1,0:T(8,128)(2,1)S(1)}, u32[]{:S(2)}, u32[]{:S(2)}) collective-permute-start(bf16[1,8,2,16,192]{4,3,2,1,0:T(8,128)(2,1)S(1)} %get-tuple-element.38.refs_4_.refs_8_), channel_id=1, source_target_pairs={{0,8},{8,16},{16,24},{24,0},{1,9},{9,17},{17,25},{25,1},{2,10},{10... | collective-permute-start | bytes 294920 | tf_op jit(solution)/shard_map/ppermute | solution.py:352
  55.3 7.9 %collective-permute-start.7 = (bf16[1,8,2,16,192]{4,3,2,1,0:T(8,128)(2,1)S(1)}, bf16[1,8,2,16,192]{4,3,2,1,0:T(8,128)(2,1)S(1)}, u32[]{:S(2)}, u32[]{:S(2)}) collective-permute-start(bf16[1,8,2,16,192]{4,3,2,1,0:T(8,128)(2,1)S(1)} %get-tuple-element.39.refs_2_.refs_6_), channel_id=1, source_target_pairs={{8,0},{16,8},{24,16},{0,24},{9,1},{17,9},{25,17},{1,25},{10,2},{18... | collective-permute-start | bytes 294920 | tf_op jit(solution)/shard_map/ppermute | solution.py:352
  58.8 4.5 %copy-start.24 = (bf16[9,192,192]{2,1,0:T(8,128)(2,1)S(1)}, bf16[9,192,192]{2,1,0:T(8,128)(2,1)}, u32[]{:S(2)}) copy-start(bf16[9,192,192]{2,1,0:T(8,128)(2,1)} %refs_7_.1) | copy-start | bytes 1990660
  61.9 7.6 %collective-permute-start.4 = (bf16[2,27,16,192]{3,2,1,0:T(8,128)(2,1)S(1)}, bf16[2,27,16,192]{3,2,1,0:T(8,128)(2,1)S(1)}, u32[]{:S(2)}, u32[]{:S(2)}) collective-permute-start(bf16[2,27,16,192]{3,2,1,0:T(8,128)(2,1)S(1)} %get-tuple-element.36), channel_id=1, source_target_pairs={{0,1},{1,0},{2,3},{3,2},{4,5},{5,4},{6,7},{7,6},{8,9},{9,8},{10,11... | collective-permute-start | bytes 995336 | tf_op jit(solution)/shard_map/ppermute | solution.py:357
  62.0 7.5 %collective-permute-start.5 = (bf16[2,27,16,192]{3,2,1,0:T(8,128)(2,1)S(1)}, bf16[2,27,16,192]{3,2,1,0:T(8,128)(2,1)S(1)}, u32[]{:S(2)}, u32[]{:S(2)}) collective-permute-start(bf16[2,27,16,192]{3,2,1,0:T(8,128)(2,1)S(1)} %get-tuple-element.37), channel_id=1, source_target_pairs={{0,1},{1,0},{2,3},{3,2},{4,5},{5,4},{6,7},{7,6},{8,9},{9,8},{10,11... | collective-permute-start | bytes 995336 | tf_op jit(solution)/shard_map/ppermute | solution.py:357
  65.6 12.4 %copy-start.8 = (bf16[2,8,2,16,192]{4,3,2,1,0:T(8,128)(2,1)}, bf16[2,8,2,16,192]{4,3,2,1,0:T(8,128)(2,1)S(1)}, u32[]{:S(2)}) copy-start(bf16[2,8,2,16,192]{4,3,2,1,0:T(8,128)(2,1)S(1)} %get-tuple-element.43.refs_2_.refs_3_) | copy-start | bytes 589828
  65.6 12.4 %copy-start.14 = (bf16[1,8,2,16,192]{4,3,2,1,0:T(8,128)(2,1)}, bf16[1,8,2,16,192]{4,3,2,1,0:T(8,128)(2,1)S(1)}, u32[]{:S(2)}) copy-start(bf16[1,8,2,16,192]{4,3,2,1,0:T(8,128)(2,1)S(1)} %get-tuple-element.42.refs_1_.refs_2_) | copy-start | bytes 294916
  65.6 12.4 %copy-start.16 = (bf16[1,8,2,16,192]{4,3,2,1,0:T(8,128)(2,1)}, bf16[1,8,2,16,192]{4,3,2,1,0:T(8,128)(2,1)S(1)}, u32[]{:S(2)}) copy-start(bf16[1,8,2,16,192]{4,3,2,1,0:T(8,128)(2,1)S(1)} %get-tuple-element.41.refs_3_.refs_4_) | copy-start | bytes 294916
  65.6 12.3 %collective-permute-start.8 = (bf16[1,8,2,16,192]{4,3,2,1,0:T(8,128)(2,1)S(1)}, bf16[1,8,2,16,192]{4,3,2,1,0:T(8,128)(2,1)S(1)}, u32[]{:S(2)}, u32[]{:S(2)}) collective-permute-start(bf16[1,8,2,16,192]{4,3,2,1,0:T(8,128)(2,1)S(1)} %get-tuple-element.41.refs_3_.refs_4_), channel_id=1, source_target_pairs={{0,8},{8,16},{16,24},{24,0},{1,9},{9,17},{17,25},{25,1},{2,10},{10... | collective-permute-start | bytes 294920 | tf_op jit(solution)/shard_map/ppermute | solution.py:352
  66.4 11.6 %collective-permute-start.9 = (bf16[1,8,2,16,192]{4,3,2,1,0:T(8,128)(2,1)S(1)}, bf16[1,8,2,16,192]{4,3,2,1,0:T(8,128)(2,1)S(1)}, u32[]{:S(2)}, u32[]{:S(2)}) collective-permute-start(bf16[1,8,2,16,192]{4,3,2,1,0:T(8,128)(2,1)S(1)} %get-tuple-element.42.refs_1_.refs_2_), channel_id=1, source_target_pairs={{8,0},{16,8},{24,16},{0,24},{9,1},{17,9},{25,17},{1,25},{10,2},{18... | collective-permute-start | bytes 294920 | tf_op jit(solution)/shard_map/ppermute | solution.py:352
  70.6 14.8 %all-to-all-start.3 = ((bf16[4,27,16,192]{3,2,1,0:T(8,128)(2,1)}), bf16[4,27,16,192]{3,2,1,0:T(8,128)(2,1)S(1)}, u32[]{:S(2)}, u32[]{:S(2)}) async-start(bf16[4,27,16,192]{3,2,1,0:T(8,128)(2,1)} %shard_map.135.refs_0_), calls=%async_computation.3 | async-start | bytes 1769472 | tf_op jit(solution)/shard_map/all_to_all | solution.py:394
  77.9 3.6 %copy-start.18 = (bf16[1,8,2,16,192]{4,3,2,1,0:T(8,128)(2,1)}, bf16[1,8,2,16,192]{4,3,2,1,0:T(8,128)(2,1)S(1)}, u32[]{:S(2)}) copy-start(bf16[1,8,2,16,192]{4,3,2,1,0:T(8,128)(2,1)S(1)} %collective-permute-done.8.refs_0_.refs_1_) | copy-start | bytes 294916
  78.0 3.6 %copy-start.20 = (bf16[1,8,2,16,192]{4,3,2,1,0:T(8,128)(2,1)}, bf16[1,8,2,16,192]{4,3,2,1,0:T(8,128)(2,1)S(1)}, u32[]{:S(2)}) copy-start(bf16[1,8,2,16,192]{4,3,2,1,0:T(8,128)(2,1)S(1)} %collective-permute-done.9.refs_4_.refs_5_) | copy-start | bytes 294916
  81.6 3.9 %collective-permute-start.10 = (bf16[2,27,16,192]{3,2,1,0:T(8,128)(2,1)}, bf16[2,27,16,192]{3,2,1,0:T(8,128)(2,1)S(1)}, u32[]{:S(2)}, u32[]{:S(2)}) collective-permute-start(bf16[2,27,16,192]{3,2,1,0:T(8,128)(2,1)} %get-tuple-element.46), channel_id=1, source_target_pairs={{0,1},{1,0},{2,3},{3,2},{4,5},{5,4},{6,7},{7,6},{8,9},{9,8},{10,11... | collective-permute-start | bytes 995336 | tf_op jit(solution)/shard_map/ppermute | solution.py:357
  81.7 3.8 %collective-permute-start.11 = (bf16[2,27,16,192]{3,2,1,0:T(8,128)(2,1)}, bf16[2,27,16,192]{3,2,1,0:T(8,128)(2,1)S(1)}, u32[]{:S(2)}, u32[]{:S(2)}) collective-permute-start(bf16[2,27,16,192]{3,2,1,0:T(8,128)(2,1)} %get-tuple-element.47), channel_id=1, source_target_pairs={{0,1},{1,0},{2,3},{3,2},{4,5},{5,4},{6,7},{7,6},{8,9},{9,8},{10,11... | collective-permute-start | bytes 995336 | tf_op jit(solution)/shard_map/ppermute | solution.py:357
  85.4 6.4 %collective-permute-start.12 = (bf16[27,16,192]{2,1,0:T(8,128)(2,1)S(1)}, bf16[27,16,192]{2,1,0:T(8,128)(2,1)S(1)}, u32[]{:S(2)}, u32[]{:S(2)}) collective-permute-start(bf16[27,16,192]{2,1,0:T(8,128)(2,1)S(1)} %shard_map.136.refs_0_.refs_1_), channel_id=1, source_target_pairs={{0,8},{8,0},{16,24},{24,16},{1,9},{9,1},{17,25},{25,17},{2,10},{10... | collective-permute-start | bytes 497672 | tf_op jit(solution)/shard_map/ppermute | solution.py:357
  85.5 6.7 %copy-start.1 = (bf16[9,192,192]{2,1,0:T(8,128)(2,1)S(1)}, bf16[9,192,192]{2,1,0:T(8,128)(2,1)}, u32[]{:S(2)}) copy-start(bf16[9,192,192]{2,1,0:T(8,128)(2,1)} %refs_9_.1) | copy-start | bytes 1990660
  85.5 6.7 %copy-start.7 = (bf16[2,8,2,16,192]{4,3,2,1,0:T(8,128)(2,1)S(1)}, bf16[2,8,2,16,192]{4,3,2,1,0:T(8,128)(2,1)}, u32[]{:S(2)}) copy-start(bf16[2,8,2,16,192]{4,3,2,1,0:T(8,128)(2,1)} %copy-done.6) | copy-start | bytes 589828
  85.6 6.7 %copy-start.9 = (bf16[2,8,2,16,192]{4,3,2,1,0:T(8,128)(2,1)S(1)}, bf16[2,8,2,16,192]{4,3,2,1,0:T(8,128)(2,1)}, u32[]{:S(2)}) copy-start(bf16[2,8,2,16,192]{4,3,2,1,0:T(8,128)(2,1)} %copy-done.8) | copy-start | bytes 589828
  85.6 6.7 %copy-start.11 = (bf16[1,8,2,16,192]{4,3,2,1,0:T(8,128)(2,1)S(1)}, bf16[1,8,2,16,192]{4,3,2,1,0:T(8,128)(2,1)}, u32[]{:S(2)}) copy-start(bf16[1,8,2,16,192]{4,3,2,1,0:T(8,128)(2,1)} %copy-done.10) | copy-start | bytes 294916
  85.6 6.7 %copy-start.13 = (bf16[1,8,2,16,192]{4,3,2,1,0:T(8,128)(2,1)S(1)}, bf16[1,8,2,16,192]{4,3,2,1,0:T(8,128)(2,1)}, u32[]{:S(2)}) copy-start(bf16[1,8,2,16,192]{4,3,2,1,0:T(8,128)(2,1)} %copy-done.12) | copy-start | bytes 294916
  85.6 6.7 %copy-start.15 = (bf16[1,8,2,16,192]{4,3,2,1,0:T(8,128)(2,1)S(1)}, bf16[1,8,2,16,192]{4,3,2,1,0:T(8,128)(2,1)}, u32[]{:S(2)}) copy-start(bf16[1,8,2,16,192]{4,3,2,1,0:T(8,128)(2,1)} %copy-done.14) | copy-start | bytes 294916
  85.6 6.7 %copy-start.17 = (bf16[1,8,2,16,192]{4,3,2,1,0:T(8,128)(2,1)S(1)}, bf16[1,8,2,16,192]{4,3,2,1,0:T(8,128)(2,1)}, u32[]{:S(2)}) copy-start(bf16[1,8,2,16,192]{4,3,2,1,0:T(8,128)(2,1)} %copy-done.16) | copy-start | bytes 294916
  85.6 6.7 %copy-start.19 = (bf16[1,8,2,16,192]{4,3,2,1,0:T(8,128)(2,1)S(1)}, bf16[1,8,2,16,192]{4,3,2,1,0:T(8,128)(2,1)}, u32[]{:S(2)}) copy-start(bf16[1,8,2,16,192]{4,3,2,1,0:T(8,128)(2,1)} %copy-done.18) | copy-start | bytes 294916
  85.6 6.7 %copy-start.21 = (bf16[1,8,2,16,192]{4,3,2,1,0:T(8,128)(2,1)S(1)}, bf16[1,8,2,16,192]{4,3,2,1,0:T(8,128)(2,1)}, u32[]{:S(2)}) copy-start(bf16[1,8,2,16,192]{4,3,2,1,0:T(8,128)(2,1)} %copy-done.20) | copy-start | bytes 294916
  86.6 12.2 %collective-permute-start.13 = (bf16[27,16,192]{2,1,0:T(8,128)(2,1)}, bf16[27,16,192]{2,1,0:T(8,128)(2,1)S(1)}, u32[]{:S(2)}, u32[]{:S(2)}) collective-permute-start(bf16[27,16,192]{2,1,0:T(8,128)(2,1)} %get-tuple-element.49), channel_id=1, source_target_pairs={{0,2},{2,0},{4,6},{6,4},{1,3},{3,1},{5,7},{7,5},{8,10},{10,8},{12,... | collective-permute-start | bytes 497672 | tf_op jit(solution)/shard_map/ppermute | solution.py:357
  88.0 10.7 %collective-permute-start.14 = (bf16[27,16,192]{2,1,0:T(8,128)(2,1)}, bf16[27,16,192]{2,1,0:T(8,128)(2,1)S(1)}, u32[]{:S(2)}, u32[]{:S(2)}) collective-permute-start(bf16[27,16,192]{2,1,0:T(8,128)(2,1)} %get-tuple-element.50), channel_id=1, source_target_pairs={{0,4},{2,6},{4,0},{6,2},{1,5},{3,7},{5,1},{7,3},{8,12},{10,14},{12... | collective-permute-start | bytes 497672 | tf_op jit(solution)/shard_map/ppermute | solution.py:357
  88.8 10.9 %collective-permute-start.15 = (bf16[27,16,192]{2,1,0:T(8,128)(2,1)}, bf16[27,16,192]{2,1,0:T(8,128)(2,1)S(1)}, u32[]{:S(2)}, u32[]{:S(2)}) collective-permute-start(bf16[27,16,192]{2,1,0:T(8,128)(2,1)} %get-tuple-element.51), channel_id=1, source_target_pairs={{0,6},{2,4},{4,2},{6,0},{1,7},{3,5},{5,3},{7,1},{8,14},{10,12},{12... | collective-permute-start | bytes 497672 | tf_op jit(solution)/shard_map/ppermute | solution.py:357
  91.9 11.2 %collective-permute-start.16 = (bf16[27,16,192]{2,1,0:T(8,128)(2,1)S(1)}, bf16[27,16,192]{2,1,0:T(8,128)(2,1)S(1)}, u32[]{:S(2)}, u32[]{:S(2)}) collective-permute-start(bf16[27,16,192]{2,1,0:T(8,128)(2,1)S(1)} %shard_map.141.refs_0_.refs_1_), channel_id=1, source_target_pairs={{0,16},{8,24},{16,0},{24,8},{1,17},{9,25},{17,1},{25,9},{2,18},{10... | collective-permute-start | bytes 497672 | tf_op jit(solution)/shard_map/ppermute | solution.py:357
  94.5 23.4 %all-to-all-start.4 = ((bf16[8,2,2,2,16,192]{5,4,3,2,1,0:T(8,128)(2,1)}), bf16[8,2,2,2,16,192]{5,4,3,2,1,0:T(8,128)(2,1)}, u32[]{:S(2)}, u32[]{:S(2)}) async-start(bf16[8,2,2,2,16,192]{5,4,3,2,1,0:T(8,128)(2,1)} %bitcast.7), calls=%async_computation.4 | async-start | bytes 1048576 | tf_op jit(solution)/shard_map/all_to_all | solution.py:344
  99.8 8.4 %collective-permute-start.17 = (bf16[27,16,192]{2,1,0:T(8,128)(2,1)S(1)}, bf16[27,16,192]{2,1,0:T(8,128)(2,1)S(1)}, u32[]{:S(2)}, u32[]{:S(2)}) collective-permute-start(bf16[27,16,192]{2,1,0:T(8,128)(2,1)S(1)} %shard_map.143.refs_0_.refs_1_), channel_id=1, source_target_pairs={{0,8},{8,0},{16,24},{24,16},{1,9},{9,1},{17,25},{25,17},{2,10},{10... | collective-permute-start | bytes 497672 | tf_op jit(solution)/shard_map/ppermute | solution.py:357
  103.2 10.4 %collective-permute-start.24 = (bf16[27,16,192]{2,1,0:T(8,128)(2,1)S(1)}, bf16[27,16,192]{2,1,0:T(8,128)(2,1)S(1)}, u32[]{:S(2)}, u32[]{:S(2)}) collective-permute-start(bf16[27,16,192]{2,1,0:T(8,128)(2,1)S(1)} %shard_map.144.refs_0_.refs_1_), channel_id=1, source_target_pairs={{0,6},{2,4},{4,2},{6,0},{1,7},{3,5},{5,3},{7,1},{8,14},{10,12},{12... | collective-permute-start | bytes 497672 | tf_op jit(solution)/shard_map/ppermute | solution.py:357
  106.1 11.1 %collective-permute-start.23 = (bf16[27,16,192]{2,1,0:T(8,128)(2,1)S(1)}, bf16[27,16,192]{2,1,0:T(8,128)(2,1)S(1)}, u32[]{:S(2)}, u32[]{:S(2)}) collective-permute-start(bf16[27,16,192]{2,1,0:T(8,128)(2,1)S(1)} %shard_map.144.refs_0_.refs_1_), channel_id=1, source_target_pairs={{0,4},{2,6},{4,0},{6,2},{1,5},{3,7},{5,1},{7,3},{8,12},{10,14},{12... | collective-permute-start | bytes 497672 | tf_op jit(solution)/shard_map/ppermute | solution.py:357
  106.8 11.0 %collective-permute-start.22 = (bf16[27,16,192]{2,1,0:T(8,128)(2,1)S(1)}, bf16[27,16,192]{2,1,0:T(8,128)(2,1)S(1)}, u32[]{:S(2)}, u32[]{:S(2)}) collective-permute-start(bf16[27,16,192]{2,1,0:T(8,128)(2,1)S(1)} %shard_map.144.refs_0_.refs_1_), channel_id=1, source_target_pairs={{0,2},{2,0},{4,6},{6,4},{1,3},{3,1},{5,7},{7,5},{8,10},{10,8},{12,... | collective-permute-start | bytes 497672 | tf_op jit(solution)/shard_map/ppermute | solution.py:357
  108.3 11.2 %collective-permute-start.18 = (bf16[27,16,192]{2,1,0:T(8,128)(2,1)S(1)}, bf16[27,16,192]{2,1,0:T(8,128)(2,1)S(1)}, u32[]{:S(2)}, u32[]{:S(2)}) collective-permute-start(bf16[27,16,192]{2,1,0:T(8,128)(2,1)S(1)} %shard_map.145.refs_1_.refs_0_), channel_id=1, source_target_pairs={{0,16},{8,24},{16,0},{24,8},{1,17},{9,25},{17,1},{25,9},{2,18},{10... | collective-permute-start | bytes 497672 | tf_op jit(solution)/shard_map/ppermute | solution.py:357
  117.2 7.8 %collective-permute-start.26 = (bf16[2,27,16,192]{3,2,1,0:T(8,128)(2,1)S(1)}, bf16[2,27,16,192]{3,2,1,0:T(8,128)(2,1)S(1)}, u32[]{:S(2)}, u32[]{:S(2)}) collective-permute-start(bf16[2,27,16,192]{3,2,1,0:T(8,128)(2,1)S(1)} %shard_map.148), channel_id=1, source_target_pairs={{0,1},{1,0},{2,3},{3,2},{4,5},{5,4},{6,7},{7,6},{8,9},{9,8},{10,11... | collective-permute-start | bytes 995336 | tf_op jit(solution)/shard_map/ppermute | solution.py:357
  117.9 7.1 %collective-permute-start.25 = (bf16[2,27,16,192]{3,2,1,0:T(8,128)(2,1)S(1)}, bf16[2,27,16,192]{3,2,1,0:T(8,128)(2,1)S(1)}, u32[]{:S(2)}, u32[]{:S(2)}) collective-permute-start(bf16[2,27,16,192]{3,2,1,0:T(8,128)(2,1)S(1)} %shard_map.147), channel_id=1, source_target_pairs={{0,1},{1,0},{2,3},{3,2},{4,5},{5,4},{6,7},{7,6},{8,9},{9,8},{10,11... | collective-permute-start | bytes 995336 | tf_op jit(solution)/shard_map/ppermute | solution.py:357
  119.0 12.7 %copy-start = (bf16[2,8,2,2,16,192]{5,4,3,2,1,0:T(8,128)(2,1)}, bf16[2,8,2,2,16,192]{5,4,3,2,1,0:T(8,128)(2,1)S(1)}, u32[]{:S(2)}) copy-start(bf16[2,8,2,2,16,192]{5,4,3,2,1,0:T(8,128)(2,1)S(1)} %copy.16) | copy-start | bytes 1179652
  119.5 12.3 %collective-permute-start.19 = (bf16[27,16,192]{2,1,0:T(8,128)(2,1)S(1)}, bf16[27,16,192]{2,1,0:T(8,128)(2,1)S(1)}, u32[]{:S(2)}, u32[]{:S(2)}) collective-permute-start(bf16[27,16,192]{2,1,0:T(8,128)(2,1)S(1)} %shard_map.146.refs_1_.refs_0_), channel_id=1, source_target_pairs={{0,2},{2,0},{4,6},{6,4},{1,3},{3,1},{5,7},{7,5},{8,10},{10,8},{12,... | collective-permute-start | bytes 497672 | tf_op jit(solution)/shard_map/ppermute | solution.py:357
  120.7 11.2 %collective-permute-start.21 = (bf16[27,16,192]{2,1,0:T(8,128)(2,1)S(1)}, bf16[27,16,192]{2,1,0:T(8,128)(2,1)S(1)}, u32[]{:S(2)}, u32[]{:S(2)}) collective-permute-start(bf16[27,16,192]{2,1,0:T(8,128)(2,1)S(1)} %shard_map.146.refs_1_.refs_0_), channel_id=1, source_target_pairs={{0,6},{2,4},{4,2},{6,0},{1,7},{3,5},{5,3},{7,1},{8,14},{10,12},{12... | collective-permute-start | bytes 497672 | tf_op jit(solution)/shard_map/ppermute | solution.py:357
  124.9 9.4 %collective-permute-start.20 = (bf16[27,16,192]{2,1,0:T(8,128)(2,1)S(1)}, bf16[27,16,192]{2,1,0:T(8,128)(2,1)S(1)}, u32[]{:S(2)}, u32[]{:S(2)}) collective-permute-start(bf16[27,16,192]{2,1,0:T(8,128)(2,1)S(1)} %shard_map.146.refs_1_.refs_0_), channel_id=1, source_target_pairs={{0,4},{2,6},{4,0},{6,2},{1,5},{3,7},{5,1},{7,3},{8,12},{10,14},{12... | collective-permute-start | bytes 497672 | tf_op jit(solution)/shard_map/ppermute | solution.py:357
  131.8 4.0 %collective-permute-start.27 = (bf16[2,27,16,192]{3,2,1,0:T(8,128)(2,1)S(1)}, bf16[2,27,16,192]{3,2,1,0:T(8,128)(2,1)S(1)}, u32[]{:S(2)}, u32[]{:S(2)}) collective-permute-start(bf16[2,27,16,192]{3,2,1,0:T(8,128)(2,1)S(1)} %shard_map.150), channel_id=1, source_target_pairs={{0,1},{1,0},{2,3},{3,2},{4,5},{5,4},{6,7},{7,6},{8,9},{9,8},{10,11... | collective-permute-start | bytes 995336 | tf_op jit(solution)/shard_map/ppermute | solution.py:357
  131.9 2.5 %collective-permute-start.29 = (bf16[27,16,192]{2,1,0:T(8,128)(2,1)S(1)}, bf16[27,16,192]{2,1,0:T(8,128)(2,1)S(1)}, u32[]{:S(2)}, u32[]{:S(2)}) collective-permute-start(bf16[27,16,192]{2,1,0:T(8,128)(2,1)S(1)} %collective-permute-done.21.refs_3_), channel_id=1, source_target_pairs={{0,1},{1,0},{2,3},{3,2},{4,5},{5,4},{6,7},{7,6},{8,9},{9,8},{10,11... | collective-permute-start | bytes 497672 | tf_op jit(solution)/shard_map/ppermute | solution.py:357
  134.3 1.5 %collective-permute-start.28 = (bf16[27,16,192]{2,1,0:T(8,128)(2,1)S(1)}, bf16[27,16,192]{2,1,0:T(8,128)(2,1)S(1)}, u32[]{:S(2)}, u32[]{:S(2)}) collective-permute-start(bf16[27,16,192]{2,1,0:T(8,128)(2,1)S(1)} %collective-permute-done.20.refs_2_), channel_id=1, source_target_pairs={{0,1},{1,0},{2,3},{3,2},{4,5},{5,4},{6,7},{7,6},{8,9},{9,8},{10,11... | collective-permute-start | bytes 497672 | tf_op jit(solution)/shard_map/ppermute | solution.py:357
